TPU v7x, 512 devices: a whole 4x8x8 slice. The times are simulated.
512 devices in a mesh: dp: 16 (over y_hi, x, core), ctx: 8 (over z), mp: 4 (over y_lo).
Axes of the slice: x: 4, y: 8 (y_hi: 2, y_lo: 4; y = y_hi * 4 + y_lo), z: 8, core: 2. Of those that a mesh axis runs over, the one named last changes fastest.
Arguments:
- queries: bfloat16 [24576, 4096], P(('dp', 'ctx'), 'mp'), may hold values from -96 to 96
- key_states: bfloat16 [24576, 512], P(('dp', 'ctx'), 'mp'), may hold values from -12 to 12
- normed: bfloat16 [24576, 8192], P(('dp', 'ctx'), 'mp'), may hold values from -24 to 24
- value_weight: bfloat16 [8192, 512], P(('dp', 'ctx'), 'mp'), may hold values from -0.0625 to 0.0625
- grad_out: bfloat16 [24576, 4096], P(('dp', 'ctx'), 'mp'), may hold values from -6 to 6
- lengths: int32 [16, 8], P('dp'), may hold values from 1 to 768, 1536 in all within a row
Outputs:
- attended: bfloat16 [24576, 4096], P(('dp', 'ctx'), 'mp')
- grad_query: bfloat16 [24576, 4096], P(('dp', 'ctx'), 'mp')
- grad_key: bfloat16 [24576, 512], P(('dp', 'ctx'), 'mp')
- grad_weight: float32 [8192, 512], P(('dp', 'ctx'), 'mp')
Inputs may be any that keep to these rules, and one draw needn't show every extreme that they name: Each row holds the lengths of one pack's documents and sums to 1536; the longest is exactly 768.
All inputs are finite; a program needn't handle non-finite values.
Results may differ from a plain program's by a relative error of at most 0.04.
Values may be sent and summed in bfloat16 or wider, within the bound.
No kernel may reach another device: no remote copies, remote signals or barrier semaphores. Data moves between devices by JAX's collectives and lax.ppermute only.
A program may use at most 64 MiB of HBM per device.

v0:
```python
import jax
import jax.numpy as jnp
from jax import lax
from jax.sharding import PartitionSpec as P

HEAD_DIM = 128


def passed_along(block, axis, distance):
    devices = range(lax.axis_size(axis))
    route = [((i - distance) % len(devices), i) for i in devices]
    return lax.ppermute(block, axis, route)


def doc_index(positions, doc_ends):
    return jnp.sum((positions[:, None] >= doc_ends[None, :]).astype(jnp.int32), axis=1)


def shards(queries, key_states, normed, value_weight, grad_out, lengths):
    tok_rows = queries.shape[0]
    local_kv = key_states.shape[1] // HEAD_DIM
    kv_group = queries.shape[1] // HEAD_DIM // local_kv
    score_scale = HEAD_DIM ** (-0.5)
    ctx_size = lax.axis_size("ctx")
    ctx_index = lax.axis_index("ctx")
    doc_ends = jnp.cumsum(lengths[0])
    query_pos = ctx_index * tok_rows + jnp.arange(tok_rows, dtype=jnp.int32)
    query_doc = doc_index(query_pos, doc_ends)
    features = lax.all_gather(normed, "mp", axis=1, tiled=True)
    columns = features
    projected = jnp.dot(
        columns,
        lax.all_gather(value_weight, ("dp", "ctx"), axis=0, tiled=True),
        preferred_element_type=jnp.float32,
    ).astype(jnp.bfloat16)
    key_whole, value_whole = (
        lax.all_gather(key_states, "ctx", axis=0, tiled=True),
        lax.all_gather(projected, "ctx", axis=0, tiled=True),
    )
    query_heads = queries.reshape(tok_rows, local_kv, kv_group, HEAD_DIM)
    grad_heads = grad_out.reshape(tok_rows, local_kv, kv_group, HEAD_DIM)

    def key_block(source):
        offset = source * tok_rows
        block_keys = lax.dynamic_slice_in_dim(key_whole, offset, tok_rows, 0).reshape(
            tok_rows, local_kv, HEAD_DIM
        )
        block_values = lax.dynamic_slice_in_dim(value_whole, offset, tok_rows, 0).reshape(
            tok_rows, local_kv, HEAD_DIM
        )
        key_pos = offset + jnp.arange(tok_rows, dtype=jnp.int32)
        allowed = (query_doc[:, None] == doc_index(key_pos, doc_ends)[None, :]) & (
            key_pos[None, :] <= query_pos[:, None]
        )
        scores = (
            jnp.einsum(
                "tlgd,jld->tlgj", query_heads, block_keys, preferred_element_type=jnp.float32
            )
            * score_scale
        )
        return (block_keys, block_values, allowed[:, None, None, :], scores)

    def forward_step(source, loop_state):
        running_max, running_sum, weighted = loop_state
        block_keys, block_values, allowed, scores = key_block(source)
        masked = jnp.where(allowed, scores, jnp.float32(-1e30))
        next_max = jnp.maximum(running_max, jnp.max(masked, axis=-1))
        rescale = jnp.exp(running_max - next_max)
        weights = jnp.exp(masked - next_max[..., None])
        running_sum = running_sum * rescale + jnp.sum(weights, axis=-1)
        weighted = weighted * rescale[..., None] + jnp.einsum(
            "tlgj,jld->tlgd",
            weights,
            block_values.astype(jnp.float32),
            precision=lax.Precision.HIGHEST,
        )
        return (next_max, running_sum, weighted)

    stat_shape = (tok_rows, local_kv, kv_group)
    running_max, running_sum, weighted = lax.fori_loop(
        0,
        ctx_size,
        forward_step,
        (
            jnp.full(stat_shape, -1e30, jnp.float32),
            jnp.zeros(stat_shape, jnp.float32),
            jnp.zeros(stat_shape + (HEAD_DIM,), jnp.float32),
        ),
    )
    log_total = running_max + jnp.log(running_sum)
    attended = (weighted / running_sum[..., None]).astype(jnp.bfloat16)
    row_dots = jnp.sum(grad_heads.astype(jnp.float32) * attended.astype(jnp.float32), axis=-1)

    def backward_step(step_index, loop_state):
        key_acc, value_acc, query_acc = loop_state
        source = (ctx_index - step_index) % ctx_size
        key_part = key_acc
        value_part = value_acc
        query_part = query_acc
        block_keys, block_values, allowed, scores = key_block(source)
        attn_probs = jnp.where(allowed, jnp.exp(scores - log_total[..., None]), jnp.float32(0.0))
        grad_probs = jnp.einsum(
            "tlgd,jld->tlgj", grad_heads, block_values, preferred_element_type=jnp.float32
        )
        grad_scores = (attn_probs * (grad_probs - row_dots[..., None])).astype(jnp.bfloat16)
        probs_half = attn_probs.astype(jnp.bfloat16)
        value_part = value_part + jnp.einsum(
            "tlgj,tlgd->jld", probs_half, grad_heads, preferred_element_type=jnp.float32
        )
        key_part = key_part + jnp.einsum(
            "tlgj,tlgd->jld", grad_scores, query_heads, preferred_element_type=jnp.float32
        )
        query_part = query_part + jnp.einsum(
            "tlgj,jld->tlgd", grad_scores, block_keys, preferred_element_type=jnp.float32
        )
        key_acc = key_part
        value_acc = value_part
        key_acc, value_acc = (
            passed_along(key_acc.astype(jnp.bfloat16), "ctx", 1).astype(key_acc.dtype),
            passed_along(value_acc.astype(jnp.bfloat16), "ctx", 1).astype(value_acc.dtype),
        )
        return (key_acc, value_acc, query_part)

    acc_shape = (tok_rows, local_kv, HEAD_DIM)
    key_acc, value_acc, query_acc = lax.fori_loop(
        0,
        ctx_size,
        backward_step,
        (
            jnp.zeros(acc_shape, jnp.float32),
            jnp.zeros(acc_shape, jnp.float32),
            jnp.zeros(stat_shape + (HEAD_DIM,), jnp.float32),
        ),
    )
    grad_query = (query_acc * score_scale).astype(jnp.bfloat16).reshape(tok_rows, -1)
    grad_key = (key_acc * score_scale).astype(jnp.bfloat16).reshape(tok_rows, -1)
    grad_value = value_acc.astype(jnp.bfloat16).reshape(tok_rows, -1)
    columns = features
    grad_weight = lax.psum_scatter(
        lax.dot_general(
            columns, grad_value, (((0,), (0,)), ((), ())), preferred_element_type=jnp.float32
        ),
        ("dp", "ctx"),
        scatter_dimension=0,
        tiled=True,
    )
    return (attended.reshape(tok_rows, -1), grad_query, grad_key, grad_weight)


def solution(mesh):
    in_specs = (
        P(("dp", "ctx"), "mp"),
        P(("dp", "ctx"), "mp"),
        P(("dp", "ctx"), "mp"),
        P(("dp", "ctx"), "mp"),
        P(("dp", "ctx"), "mp"),
        P("dp", None),
    )
    out_specs = (
        P(("dp", "ctx"), "mp"),
        P(("dp", "ctx"), "mp"),
        P(("dp", "ctx"), "mp"),
        P(("dp", "ctx"), "mp"),
    )
    return jax.shard_map(shards, mesh=mesh, in_specs=in_specs, out_specs=out_specs, check_vma=False)
```

profile of v0, /device:TPU:56, one launch (start us, length us, event | category | flops | bytes accessed | tf_op | source)
XLA Modules:
  0.0 1233.9 jit_solution(18081227807282282920)
XLA Ops:
  11.7 33.6 %all_gather.12 = bf16[1536,128]{1,0:T(8,128)(2,1)} all-gather(bf16[192,128]{1,0:T(8,128)(2,1)S(1)} %copy-done.4), channel_id=1, replica_groups=mesh['dp'=16,'ctx'=8,'mp'=4] {'ctx'}, dimensions={0}, use_global_device_ids=true | all-gather | bytes 442368 | tf_op jit(solution)/shard_map/all_gather | solution.py:37
  45.4 95.9 %all-gather.5.cloned.1.call-done = bf16[8192,128]{1,0:T(8,128)(2,1)} async-done(((bf16[64,128]{1,0:T(8,128)(2,1)}), bf16[8192,128]{1,0:T(8,128)(2,1)}) %all-gather.5.cloned.1.call-update) | async-done | bytes 2097168 | tf_op jit(solution)/shard_map/all_gather | solution.py:33
  141.2 70.7 %all-gather.3.cloned.1.call-done = bf16[192,8192]{1,0:T(8,128)(2,1)} async-done(((bf16[192,2048]{1,0:T(8,128)(2,1)}), bf16[192,8192]{1,0:T(8,128)(2,1)}) %all-gather.3.cloned.1.call-update) | async-done | bytes 3145744 | tf_op jit(solution)/shard_map/all_gather | solution.py:29
  211.9 3.5 convolution_convert_fusion
  215.4 29.2 %all_gather.15 = bf16[1536,128]{1,0:T(8,128)(2,1)} all-gather(bf16[192,128]{1,0:T(8,128)(2,1)S(1)} %convolution_convert_fusion), channel_id=1, replica_groups=mesh['dp'=16,'ctx'=8,'mp'=4] {'ctx'}, dimensions={0}, use_global_device_ids=true | all-gather | bytes 442368 | tf_op jit(solution)/shard_map/all_gather | solution.py:38
  244.6 49.7 %while.38 = (s32[]{:T(128)}, f32[192,1,8]{0,2,1:T(8,128)S(1)}, f32[192,1,8]{0,2,1:T(8,128)S(1)}, f32[192,1,8,128]{3,0,2,1:T(8,128)}, s32[192]{0:T(256)S(1)}, /*i...) while((s32[]{:T(128)}, f32[192,1,8]{0,2,1:T(8,128)S(1)}, ...), condition=%wide.region_6.7_spmd.clone, body=%wide.region_2.6_spmd.clone.sunk | while | flops 530966208 | bytes 12073263 | solution.py:80
  244.8 1.2 fusion.78
  247.2 2.7 fusion.81
  251.0 1.2 fusion.78
  253.4 2.7 fusion.81
  259.6 2.7 fusion.81
  263.5 1.2 fusion.78
  265.8 2.7 fusion.81
  272.1 2.7 fusion.81
  275.9 1.2 fusion.78
  278.3 2.7 fusion.81
  282.1 1.2 fusion.78
  284.5 2.7 fusion.81
  290.7 2.7 fusion.81
  294.4 1.9 multiply_reduce_fusion
  296.4 103.6 %while.39 = (s32[]{:T(128)}, f32[192,1,128]{2,0,1:T(8,128)S(1)}, f32[192,1,128]{2,0,1:T(8,128)S(1)}, f32[192,1,8,128]{3,0,2,1:T(8,128)S(1)}, s32[192]{0:T(256)S(...) while((s32[]{:T(128)}, f32[192,1,128]{2,0,1:T(8,128)S(1)}, ...), condition=%wide.region_10.11_spmd.clone, body=%wide.region_8.10_spmd.clone.sunk | while | flops 380256960 | bytes 9677292 | solution.py:125
  296.7 1.3 bitcast_select_fusion.3
  299.6 2.5 collective-permute-start
  302.4 3.7 collective-permute-start.1
  306.2 1.4 fusion.95
  307.6 2.0 collective-permute-done.1
  309.9 1.3 bitcast_select_fusion.3
  312.8 2.6 collective-permute-start
  315.8 2.7 collective-permute-start.1
  318.5 1.4 fusion.95
  320.0 3.4 collective-permute-done.1
  323.6 1.3 bitcast_select_fusion.3
  326.5 1.9 collective-permute-start
  328.8 3.6 collective-permute-start.1
  332.4 1.4 fusion.95
  333.8 2.2 collective-permute-done.1
  336.3 1.3 bitcast_select_fusion.3
  339.1 2.4 collective-permute-start
  341.9 3.0 collective-permute-start.1
  344.9 1.4 fusion.95
  346.8 2.4 collective-permute-done.1
  349.5 1.3 bitcast_select_fusion.3
  352.3 2.2 collective-permute-start
  354.9 2.9 collective-permute-start.1
  357.8 1.4 fusion.95
  359.5 2.6 collective-permute-done.1
  362.4 1.3 bitcast_select_fusion.3
  365.3 1.9 collective-permute-start
  367.6 3.1 collective-permute-start.1
  370.6 1.4 fusion.95
  373.0 1.8 collective-permute-done.1
  375.0 1.3 bitcast_select_fusion.3
  377.9 1.9 collective-permute-start
  380.2 2.9 collective-permute-start.1
  383.1 1.4 fusion.95
  385.3 2.1 collective-permute-done.1
  387.7 1.3 bitcast_select_fusion.3
  390.6 1.9 collective-permute-start
  392.8 3.7 collective-permute-start.1
  396.5 1.4 fusion.95
  398.0 2.1 collective-permute-done.1
  400.1 4.6 convolution_bitcast_fusion.3
  404.6 5.6 copy.46
  412.2 815.2 %reduce-scatter.4.cloned.1.call-done = f32[64,128]{1,0:T(8,128)} async-done(((f32[8192,128]{1,0:T(8,128)}), f32[64,128]{1,0:T(8,128)}) %reduce-scatter.4.cloned.1.call-update) | async-done | bytes 32784
  (195 shorter events, 47.8 us)
Async XLA Ops:
  7.2 3.6 copy-start.3
  7.2 134.1 %all-gather.5.cloned.1.call-start = ((), (), s32[]{:S(2)}) async-start(), calls=%async_computation.2 | async-start | bytes 2113536 | tf_op jit(solution)/shard_map/all_gather | solution.py:33
  7.9 204.0 %all-gather.3.cloned.1.call-start = ((), (), s32[]{:S(2)}) async-start(), calls=%async_computation.1 | async-start | bytes 3932160 | tf_op jit(solution)/shard_map/all_gather | solution.py:29
  8.7 1218.8 %reduce-scatter.4.cloned.1.call-start = ((), (), s32[]{:S(2)}) async-start(), calls=%async_computation.3 | async-start | bytes 4227072
  9.6 2.1 copy-start.4
  10.8 0.7 copy-start.2
  246.1 1.1 copy-start
  249.9 0.9 copy-start.1
  252.3 1.1 copy-start
  256.1 0.9 copy-start.1
  258.5 1.1 copy-start
  262.3 0.9 copy-start.1
  264.7 1.1 copy-start
  268.5 0.9 copy-start.1
  270.9 1.1 copy-start
  274.7 0.9 copy-start.1
  277.1 1.1 copy-start
  281.0 0.9 copy-start.1
  283.4 1.1 copy-start
  287.2 0.9 copy-start.1
  289.6 1.1 copy-start
  293.4 0.9 copy-start.1
  299.6 8.0 collective-permute-start
  302.4 7.2 collective-permute-start.1
  312.8 7.2 collective-permute-start
  315.8 7.6 collective-permute-start.1
  326.5 7.3 collective-permute-start
  328.8 7.2 collective-permute-start.1
  339.1 7.7 collective-permute-start
  341.9 7.3 collective-permute-start.1
  352.3 7.2 collective-permute-start
  354.9 7.2 collective-permute-start.1
  365.3 7.7 collective-permute-start
  367.6 7.2 collective-permute-start.1
  377.9 7.3 collective-permute-start
  380.2 7.2 collective-permute-start.1
  390.6 7.4 collective-permute-start
  392.8 7.2 collective-permute-start.1
Sparse Core Ops, SparseCore 0:
  12.5 128.7 all-gather.4
  143.3 68.5 all-gather.2
  410.3 817.0 reduce-scatter.3
where the time goes:
time: 1240 us; the launch traced here: 1230 us
  waiting for transfers between devices  1000 us (81%)
  matrix products  76.3 us (6%)
  blocking collectives  62.8 us (5%)
  starting transfers between devices  43.1 us (3%)
  local copies, waits for them, and re-layouts  22.9 us (2%)
  between operations  13.9 us (1%)
    unnamed x4, waiting for transfers between devices  817 us
    all_gather x1, waiting for transfers between devices, shards(): lax.all_gather(value_weight, ('dp', 'ctx'), axis=0, tiled=True)  95.9 us
    all_gather x1, waiting for transfers between devices, shards(): features = lax.all_gather(normed, 'mp', axis=1, tiled=True)  70.7 us
    ppermute x16, starting transfers between devices, passed_along(): return lax.ppermute(block, axis, route)  43 us
    all_gather x1, blocking collectives, shards(): lax.all_gather(key_states, 'ctx', axis=0, tiled=True)  33.6 us
    all_gather x1, blocking collectives, shards(): lax.all_gather(projected, 'ctx', axis=0, tiled=True)  29.2 us
  transfers between devices with their start and end apart: 19, of which 16 were waited for; matrix products, arithmetic and copies ran while one was open for 1% of the time, Pallas kernels for 0%

commit v1 on v0

v1 whole, which is shorter than its diff:
```python
import functools

import jax
import jax.numpy as jnp
from jax import lax
from jax.experimental import pallas as pl
from jax.experimental.pallas import tpu as pltpu
from jax.sharding import Mesh, PartitionSpec as P

HEAD_DIM = 128
TOK = 192
GROUP = 8
WINDOW = 5 * TOK
PACK = 8 * TOK
HEADS_AT_ONCE = 2
LANES = HEADS_AT_ONCE * TOK
CHIPS = ("yh", "x", "ctx")
PAIR_MP = ("core", "mp")
F32 = jnp.float32
BF16 = jnp.bfloat16


def swapped_with_mp(block):
    route = []
    for yh in range(2):
        for x in range(4):
            for mp in range(4):
                source = (yh * 4 + x) * 4 + mp
                target = ((mp >> 1) * 4 + (mp & 1) * 2 + (x & 1)) * 4 + yh * 2 + (x >> 1)
                route.append((source, target))
    return lax.ppermute(block, ("yh", "x", "mp"), route)


def to_all(block, axes, copies):
    return lax.all_to_all(
        jnp.broadcast_to(block[None], (copies,) + block.shape), axes, 0, 0, tiled=True
    )


def project_kernel(x_ref, other_ref, w_ref, out_ref):
    core = lax.axis_index("core")
    weight = jnp.concatenate(
        [w_ref[c].reshape(1024, HEAD_DIM) for c in range(4)], axis=1
    )
    own = jnp.concatenate(
        [x_ref[:, pl.ds(pl.multiple_of((2 * part + core) * 512, 512), 512)] for part in range(2)],
        axis=1,
    )
    for rows, place in ((own, core), (other_ref[...], 1 - core)):
        result = jnp.dot(rows, weight, preferred_element_type=F32)
        for c in range(4):
            out_ref[place * 4 + c] = result[:, c * HEAD_DIM : (c + 1) * HEAD_DIM].astype(BF16)


def project(x, other, weight):
    return pl.pallas_call(
        project_kernel,
        out_shape=jax.ShapeDtypeStruct((8, TOK, HEAD_DIM), BF16),
        in_specs=[pl.BlockSpec(memory_space=pltpu.VMEM)] * 3,
        out_specs=pl.BlockSpec(memory_space=pltpu.VMEM),
        compiler_params=pltpu.CompilerParams(vmem_limit_bytes=48 * 2**20),
        name="project",
    )(x, other, weight)


def weight_grad_kernel(x_ref, other_ref, dv_ref, out_ref):
    core = lax.axis_index("core")
    own_dv = jnp.concatenate([dv_ref[core * 4 + c] for c in range(4)], axis=1)
    other_dv = jnp.concatenate([dv_ref[(1 - core) * 4 + c] for c in range(4)], axis=1)
    contract = (((0,), (0,)), ((), ()))
    for part in range(2):
        own = x_ref[:, pl.ds(pl.multiple_of((2 * part + core) * 512, 512), 512)]
        other = other_ref[:, part * 512 : (part + 1) * 512]
        result = lax.dot_general(own, own_dv, contract, preferred_element_type=F32)
        result += lax.dot_general(other, other_dv, contract, preferred_element_type=F32)
        for c in range(4):
            out_ref[c, part] = result[:, c * HEAD_DIM : (c + 1) * HEAD_DIM].astype(BF16)


def weight_grad(x, other, dv):
    return pl.pallas_call(
        weight_grad_kernel,
        out_shape=jax.ShapeDtypeStruct((4, 2, 512, HEAD_DIM), BF16),
        in_specs=[pl.BlockSpec(memory_space=pltpu.VMEM)] * 3,
        out_specs=pl.BlockSpec(memory_space=pltpu.VMEM),
        compiler_params=pltpu.CompilerParams(vmem_limit_bytes=48 * 2**20),
        name="weight_grad",
    )(x, other, dv)


def attention_kernel(
    len_ref, q_ref, k_ref, v_ref, do_ref, att_ref, dq_ref, dk_ref, dv_ref,
    q_rows, do_rows, bias, probs, dscores,
):
    ctx = lax.axis_index("ctx")
    start = pl.multiple_of(jnp.clip(ctx - 4, 0, 3) * TOK, TOK)
    scale = HEAD_DIM ** -0.5
    for h in range(GROUP):
        q_rows[h * TOK : (h + 1) * TOK] = q_ref[:, h * HEAD_DIM : (h + 1) * HEAD_DIM]
        do_rows[h * TOK : (h + 1) * TOK] = do_ref[:, h * HEAD_DIM : (h + 1) * HEAD_DIM]
    lane = lax.broadcasted_iota(jnp.int32, (1, LANES), 1)
    query = ctx * TOK + lax.rem(lane, TOK)
    first = jnp.zeros_like(query)
    end = jnp.int32(0)
    for d in range(8):
        end = end + len_ref[0, d]
        first = jnp.where(query >= end, end, first)
    key = start + lax.broadcasted_iota(jnp.int32, (WINDOW, LANES), 0)
    bias[...] = jnp.where((key >= first) & (key <= query), F32(0.0), F32(-1e30))

    keys = k_ref[pl.ds(start, WINDOW), :]
    values = v_ref[pl.ds(start, WINDOW), :]
    nt = (((1,), (1,)), ((), ()))
    tn = (((0,), (0,)), ((), ()))
    for i in range(GROUP // HEADS_AT_ONCE):
        cols = slice(i * LANES, (i + 1) * LANES)
        q = q_rows[cols]
        do = do_rows[cols]
        scores = lax.dot_general(keys, q, nt, preferred_element_type=F32)
        scores = scores * F32(scale) + bias[...]
        top = jnp.max(scores, axis=0, keepdims=True)
        weights = jnp.exp(scores - top)
        p = weights * (1.0 / jnp.sum(weights, axis=0, keepdims=True))
        p_half = p.astype(BF16)
        probs[:, cols] = p_half
        att = lax.dot_general(values, p_half, tn, preferred_element_type=F32)
        dp = lax.dot_general(values, do, nt, preferred_element_type=F32)
        dots = jnp.sum(p * dp, axis=0, keepdims=True)
        ds = (p * (dp - dots)).astype(BF16)
        dscores[:, cols] = ds
        dq = lax.dot_general(keys, ds, tn, preferred_element_type=F32) * F32(scale)
        att = att.T.astype(BF16)
        dq = dq.T.astype(BF16)
        for j in range(HEADS_AT_ONCE):
            h = i * HEADS_AT_ONCE + j
            att_ref[:, h * HEAD_DIM : (h + 1) * HEAD_DIM] = att[j * TOK : (j + 1) * TOK]
            dq_ref[:, h * HEAD_DIM : (h + 1) * HEAD_DIM] = dq[j * TOK : (j + 1) * TOK]
    dk_ref[...] = jnp.zeros_like(dk_ref)
    dv_ref[...] = jnp.zeros_like(dv_ref)
    dv_ref[pl.ds(start, WINDOW), :] = jnp.dot(
        probs[...], do_rows[...], preferred_element_type=F32
    ).astype(BF16)
    dk_ref[pl.ds(start, WINDOW), :] = jnp.dot(
        dscores[...], q_rows[...], preferred_element_type=F32
    ).astype(BF16)


def attention(lengths, q, k, v, do):
    vmem = pl.BlockSpec(memory_space=pltpu.VMEM)
    wide = jax.ShapeDtypeStruct((TOK, GROUP * HEAD_DIM), BF16)
    pack = jax.ShapeDtypeStruct((PACK, HEAD_DIM), BF16)
    return pl.pallas_call(
        attention_kernel,
        out_shape=(wide, wide, pack, pack),
        in_specs=[pl.BlockSpec(memory_space=pltpu.SMEM)] + [vmem] * 4,
        out_specs=(vmem,) * 4,
        scratch_shapes=[
            pltpu.VMEM((GROUP * TOK, HEAD_DIM), BF16),
            pltpu.VMEM((GROUP * TOK, HEAD_DIM), BF16),
            pltpu.VMEM((WINDOW, LANES), F32),
            pltpu.VMEM((WINDOW, GROUP * TOK), BF16),
            pltpu.VMEM((WINDOW, GROUP * TOK), BF16),
        ],
        compiler_params=pltpu.CompilerParams(vmem_limit_bytes=56 * 2**20),
        name="attention",
    )(lengths, q, k, v, do)


def summed(parts):
    return jnp.sum(parts.astype(F32), axis=0)


def shards(queries, key_states, normed, value_weight, grad_out, lengths):
    core = lax.axis_index("core")
    quarters = normed.reshape(TOK, 2, 2, 512)
    away = lax.dynamic_index_in_dim(quarters, 1 - core, axis=2, keepdims=False)
    other = lax.ppermute(away.reshape(TOK, 1024), "core", [(0, 1), (1, 0)])

    weight = to_all(swapped_with_mp(value_weight), CHIPS, 64)
    weight = weight.reshape(4, 2, 512, HEAD_DIM)
    parts = project(normed, other, weight)
    projected = summed(
        lax.all_to_all(parts, PAIR_MP, 0, 0, tiled=True)
    ).astype(BF16)
    gathered = to_all(jnp.stack([key_states, projected]), "ctx", 8).reshape(8, 2, TOK, HEAD_DIM)
    keys = gathered[:, 0].reshape(PACK, HEAD_DIM)
    values = gathered[:, 1].reshape(PACK, HEAD_DIM)

    attended, grad_query, dk, dv = attention(lengths, queries, keys, values, grad_out)

    back = jnp.stack([dk.reshape(8, TOK, HEAD_DIM), dv.reshape(8, TOK, HEAD_DIM)], axis=1)
    back = lax.all_to_all(back, "ctx", 0, 0, tiled=True)
    back = summed(back)
    grad_key = (back[0] * F32(HEAD_DIM ** -0.5)).astype(BF16)
    grad_value = back[1].astype(BF16)

    grad_values = to_all(grad_value, PAIR_MP, 8)
    blocks = weight_grad(normed, other, grad_values).reshape(64, 64, HEAD_DIM)
    block = summed(lax.all_to_all(blocks, CHIPS, 0, 0, tiled=True))
    grad_weight = swapped_with_mp(block)
    return attended, grad_query, grad_key, grad_weight


def solution(mesh):
    fine = Mesh(mesh.devices.reshape(2, 4, 2, 8, 4), ("yh", "x", "core", "ctx", "mp"))
    tokens = P(("yh", "x", "core", "ctx"), "mp")
    return jax.shard_map(
        shards,
        mesh=fine,
        in_specs=(tokens,) * 5 + (P(("yh", "x", "core"), None),),
        out_specs=(tokens,) * 4,
        check_vma=False,
    )
```

time: 1240 us -> 209 us (0.17)
  the two profiles are of different devices: /device:TPU:56 before, /device:TPU:22 now
where the time goes in v1:
time: 209 us; the launch traced here: 208 us
  blocking collectives  125 us (60%)
  waiting for transfers between devices  36.2 us (17%)
  starting transfers between devices  25.4 us (12%)
  Pallas kernels  11.9 us (6%)
  local copies, waits for them, and re-layouts  6.36 us (3%)
  other arithmetic  2.18 us (1%)
    all_to_all x1, blocking collectives, shards(): block = summed(lax.all_to_all(blocks, CHIPS, 0, 0, tiled=True))  41.1 us
    all_to_all x2, blocking collectives, to_all(): lax.all_to_all(jnp.broadcast_to(block[None], (copies,) + block.shape), ax...  40.9 us
    all_to_all x1, blocking collectives, shards(): back = lax.all_to_all(back, 'ctx', 0, 0, tiled=True)  25.6 us
    all_to_all x1, waiting for transfers between devices, to_all(): lax.all_to_all(jnp.broadcast_to(block[None], (copies,) + block.shape), ax...  21.7 us
    all_to_all x1, blocking collectives, shards(): lax.all_to_all(parts, PAIR_MP, 0, 0, tiled=True)  17.7 us
    all_to_all x1, starting transfers between devices, to_all(): lax.all_to_all(jnp.broadcast_to(block[None], (copies,) + block.shape), ax...  14.4 us
    ppermute x2, waiting for transfers between devices, swapped_with_mp(): return lax.ppermute(block, ('yh', 'x', 'mp'), route)  12.8 us
    pallas_call x1, Pallas kernels, attention(): pl.pallas_call(attention_kernel, out_shape=(wide, wide, pack, pack), in_s...  10.5 us
  transfers between devices with their start and end apart: 4, of which 4 were waited for; matrix products, arithmetic and copies ran while one was open for 2% of the time, Pallas kernels for 0%

profile of v1, /device:TPU:22, one launch (start us, length us, event | category | flops | bytes accessed | tf_op | source)
XLA Modules:
  0.0 208.0 jit_solution(11879626615936854217)
XLA Ops:
  0.6 6.7 %collective-permute-start.1 = (bf16[64,128]{1,0:T(8,128)(2,1)}, bf16[64,128]{1,0:T(8,128)(2,1)S(1)}, u32[]{:S(2)}, u32[]{:S(2)}) collective-permute-start(bf16[64,128]{1,0:T(8,128)(2,1)} %param.9), channel_id=1, source_target_pairs={{0,0},{1,128},{2,256},{3,384},{64,64},{65,192},{66,320},{67,448},{... | collective-permute-start | bytes 49160 | tf_op jit(solution)/shard_map/ppermute | solution.py:31
  7.3 4.6 %collective-permute-done.1 = bf16[64,128]{1,0:T(8,128)(2,1)S(1)} collective-permute-done((bf16[64,128]{1,0:T(8,128)(2,1)}, bf16[64,128]{1,0:T(8,128)(2,1)S(1)}, u32[]{:S(2)}, u32[]{:S(2)}) %collective-permute-start.1) | collective-permute-done | bytes 16416 | tf_op jit(solution)/shard_map/ppermute | solution.py:31
  11.9 1.2 broadcast_in_dim.8
  13.1 0.0 copy-start
  13.1 14.4 %all-to-all-start = ((bf16[64,64,128]{2,1,0:T(8,128)(2,1)}), bf16[64,64,128]{2,1,0:T(8,128)(2,1)S(1)}, u32[]{:S(2)}, u32[]{:S(2)}) async-start(bf16[64,64,128]{2,1,0:T(8,128)(2,1)} %broadcast_in_dim.8), calls=%async_computation | async-start | bytes 2097152 | tf_op jit(solution)/shard_map/all_to_all | solution.py:35
  27.6 0.0 copy-done
  27.6 0.6 reshape.26
  28.2 2.7 %dynamic-slice_reduce_fusion = bf16[192,2,512]{2,1,0:T(2,128)(2,1)S(1)} fusion(bf16[192,2,2,512]{3,2,1,0:T(2,128)(2,1)S(1)} %reshape.26, s32[]{:T(128)S(6)} %select_n.4), kind=kLoop, calls=%fused_computation.3 | loop fusion | bytes 786436 | tf_op jit(solution)/shard_map/jit(dynamic_index_in_dim)/dynamic_slice | solution.py:176
  31.0 1.9 collective-permute-start
  32.9 1.7 collective-permute-done.other_ref
  34.6 21.7 %all-to-all-done = bf16[64,64,128]{2,1,0:T(8,128)(2,1)S(1)} async-done(((bf16[64,64,128]{2,1,0:T(8,128)(2,1)}), bf16[64,64,128]{2,1,0:T(8,128)(2,1)S(1)}, u32[]{:S(2)}, u32[]{:S(2)}) %all-to-all-start) | async-done | bytes 1048608 | tf_op jit(solution)/shard_map/all_to_all | solution.py:35
  56.2 0.6 project.1
  56.8 0.0 copy-start.1
  56.8 17.7 %all_to_all.30 = bf16[8,192,128]{2,1,0:T(8,128)(2,1)S(1)} all-to-all(bf16[8,192,128]{2,1,0:T(8,128)(2,1)S(1)} %project.1), channel_id=1, replica_groups=mesh['yh'=2,'x'=4,'core'=2,'ctx'=8,'mp'=4] {'core','mp'}, dimensions={0} | all-to-all | bytes 786432 | tf_op jit(solution)/shard_map/all_to_all | solution.py:183
  74.6 0.1 reduce_sum.30
  74.6 0.0 copy-done.1
  74.7 0.1 broadcast_in_dim.9
  74.8 26.0 %all_to_all.31 = bf16[8,2,192,128]{3,2,1,0:T(8,128)(2,1)S(1)} all-to-all(bf16[8,2,192,128]{3,2,1,0:T(8,128)(2,1)S(1)} %broadcast_in_dim.9), channel_id=1, replica_groups=mesh['yh'=2,'x'=4,'core'=2,'ctx'=8,'mp'=4] {'ctx'}, dimensions={0} | all-to-all | bytes 1572864 | tf_op jit(solution)/shard_map/all_to_all | solution.py:35
  100.9 0.9 fusion.3
  101.8 10.5 %attention.1 = (bf16[192,1024]{1,0:T(8,128)(2,1)}, bf16[192,1024]{1,0:T(8,128)(2,1)}, bf16[1536,128]{1,0:T(8,128)(2,1)}, bf16[1536,128]{1,0:T(8,128)(2,1)}) custom-call(s32[1,8]{1,0:T(1,128)} %len_ref.1, bf16[192,1024]{1,0:T(8,128)(2,1)} %q_ref.1, bf16[1536,128]{1,0:T(8,128)(2,1)} %bitcast.22, bf16[1536,128]{1,0:T(8,128)(2,1)} %bitcast.21, ...), custom_call_target="tpu_custom_call" | custom-call | tf_op jit(solution)/shard_map/attention/pallas_call | solution.py:152
  112.3 1.2 pad_maximum_fusion
  113.5 25.6 %all_to_all.32 = bf16[8,2,192,128]{3,2,1,0:T(8,128)(2,1)S(1)} all-to-all(bf16[8,2,192,128]{3,2,1,0:T(8,128)(2,1)S(1)} %pad_maximum_fusion), channel_id=1, replica_groups=mesh['yh'=2,'x'=4,'core'=2,'ctx'=8,'mp'=4] {'ctx'}, dimensions={0} | all-to-all | bytes 1572864 | tf_op jit(solution)/shard_map/all_to_all | solution.py:192
  139.1 0.1 convert_reduce_fusion.1
  139.2 0.1 broadcast_in_dim.11
  139.3 14.8 %all_to_all.33.dv_ref = bf16[8,192,128]{2,1,0:T(8,128)(2,1)S(1)} all-to-all(bf16[8,192,128]{2,1,0:T(8,128)(2,1)S(1)} %broadcast_in_dim.11), channel_id=1, replica_groups=mesh['yh'=2,'x'=4,'core'=2,'ctx'=8,'mp'=4] {'core','mp'}, dimensions={0} | all-to-all | bytes 786432 | tf_op jit(solution)/shard_map/all_to_all | solution.py:35
  154.1 0.8 weight_grad.1
  154.9 41.1 %all_to_all.34 = bf16[64,64,128]{2,1,0:T(8,128)(2,1)S(1)} all-to-all(bf16[64,64,128]{2,1,0:T(8,128)(2,1)S(1)} %bitcast.19), channel_id=1, replica_groups=mesh['yh'=2,'x'=4,'core'=2,'ctx'=8,'mp'=4] {'yh','x','ctx'}, dimensions={0} | all-to-all | bytes 2097152 | tf_op jit(solution)/shard_map/all_to_all | solution.py:199
  196.0 0.2 convert_reduce_fusion
  196.1 2.4 %collective-permute-start.2 = (f32[64,128]{1,0:T(8,128)S(1)}, f32[64,128]{1,0:T(8,128)S(1)}, u32[]{:S(2)}, u32[]{:S(2)}) collective-permute-start(f32[64,128]{1,0:T(8,128)S(1)} %convert_reduce_fusion), channel_id=1, source_target_pairs={{0,0},{1,128},{2,256},{3,384},{64,64},{65,192},{66,320},{67,448},{... | collective-permute-start | bytes 98312 | tf_op jit(solution)/shard_map/ppermute | solution.py:31
  198.5 0.6 fusion.1
  199.1 8.2 %collective-permute-done.2 = f32[64,128]{1,0:T(8,128)S(1)} collective-permute-done((f32[64,128]{1,0:T(8,128)S(1)}, f32[64,128]{1,0:T(8,128)S(1)}, u32[]{:S(2)}, u32[]{:S(2)}) %collective-permute-start.2) | collective-permute-done | bytes 32800 | tf_op jit(solution)/shard_map/ppermute | solution.py:31
  207.3 0.6 copy.17
  (3 shorter events, 0.1 us)
Async XLA Ops:
  0.6 11.3 %collective-permute-start.1 = (bf16[64,128]{1,0:T(8,128)(2,1)}, bf16[64,128]{1,0:T(8,128)(2,1)S(1)}, u32[]{:S(2)}, u32[]{:S(2)}) collective-permute-start(bf16[64,128]{1,0:T(8,128)(2,1)} %param.9), channel_id=1, source_target_pairs={{0,0},{1,128},{2,256},{3,384},{64,64},{65,192},{66,320},{67,448},{... | collective-permute-start | bytes 49160 | tf_op jit(solution)/shard_map/ppermute | solution.py:31
  13.1 14.5 %copy-start = (bf16[192,2048]{1,0:T(8,128)(2,1)S(1)}, bf16[192,2048]{1,0:T(8,128)(2,1)}, u32[]{:S(2)}) copy-start(bf16[192,2048]{1,0:T(8,128)(2,1)} %x_ref.3) | copy-start | bytes 2359300
  13.1 43.1 %all-to-all-start = ((bf16[64,64,128]{2,1,0:T(8,128)(2,1)}), bf16[64,64,128]{2,1,0:T(8,128)(2,1)S(1)}, u32[]{:S(2)}, u32[]{:S(2)}) async-start(bf16[64,64,128]{2,1,0:T(8,128)(2,1)} %broadcast_in_dim.8), calls=%async_computation | async-start | bytes 2097152 | tf_op jit(solution)/shard_map/all_to_all | solution.py:35
  31.0 3.6 %collective-permute-start = (bf16[192,1024]{1,0:T(8,128)(2,1)S(1)}, bf16[192,1024]{1,0:T(8,128)(2,1)S(1)}, u32[]{:S(2)}, u32[]{:S(2)}) collective-permute-start(bf16[192,1024]{1,0:T(8,128)(2,1)S(1)} %bitcast.23), channel_id=1, source_target_pairs={{0,32},{32,0},{1,33},{33,1},{2,34},{34,2},{3,35},{35,3},{4,36},{36... | collective-permute-start | bytes 1179656 | tf_op jit(solution)/shard_map/ppermute | solution.py:177
  56.8 17.8 %copy-start.1 = (bf16[192,128]{1,0:T(8,128)(2,1)S(1)}, bf16[192,128]{1,0:T(8,128)(2,1)}, u32[]{:S(2)}) copy-start(bf16[192,128]{1,0:T(8,128)(2,1)} %param.7) | copy-start | bytes 147460
  196.1 11.2 %collective-permute-start.2 = (f32[64,128]{1,0:T(8,128)S(1)}, f32[64,128]{1,0:T(8,128)S(1)}, u32[]{:S(2)}, u32[]{:S(2)}) collective-permute-start(f32[64,128]{1,0:T(8,128)S(1)} %convert_reduce_fusion), channel_id=1, source_target_pairs={{0,0},{1,128},{2,256},{3,384},{64,64},{65,192},{66,320},{67,448},{... | collective-permute-start | bytes 98312 | tf_op jit(solution)/shard_map/ppermute | solution.py:31

commit v2 on v1

v2 whole, which is shorter than its diff:
```python
import jax
import jax.numpy as jnp
from jax import lax
from jax.experimental import pallas as pl
from jax.experimental.pallas import tpu as pltpu
from jax.sharding import Mesh, PartitionSpec as P

HEAD_DIM = 128
TOK = 192
GROUP = 8
REACH = 4
WINDOW = (REACH + 1) * TOK
HEADS_AT_ONCE = 2
LANES = HEADS_AT_ONCE * TOK
CHUNKS = GROUP // HEADS_AT_ONCE
PLANE = ("yh", "x", "mp")
PAIR_MP = ("core", "mp")
SCALE = HEAD_DIM ** -0.5
F32 = jnp.float32
BF16 = jnp.bfloat16
NT = (((1,), (1,)), ((), ()))
TN = (((0,), (0,)), ((), ()))
VMEM = pl.BlockSpec(memory_space=pltpu.VMEM)
SMEM = pl.BlockSpec(memory_space=pltpu.SMEM)


def shape(dims, dtype=BF16):
    return jax.ShapeDtypeStruct(dims, dtype)


def call(kernel, out_shape, n_in, flops, n_bytes, scratch=(), smem=0, vmem=48):
    outs = out_shape if isinstance(out_shape, tuple) else None
    return pl.pallas_call(
        kernel,
        out_shape=out_shape,
        in_specs=[SMEM] * smem + [VMEM] * n_in,
        out_specs=(VMEM,) * len(outs) if outs else VMEM,
        scratch_shapes=scratch,
        compiler_params=pltpu.CompilerParams(vmem_limit_bytes=vmem * 2**20),
        cost_estimate=pl.CostEstimate(
            flops=flops, bytes_accessed=n_bytes, transcendentals=0
        ),
        name=kernel.__name__,
    )


def to_all(block, axes, copies):
    return lax.all_to_all(
        jnp.broadcast_to(block[None], (copies,) + block.shape), axes, 0, 0, tiled=True
    )


def from_behind(block, distance):
    return lax.ppermute(block, "ctx", [(i, i + distance) for i in range(8 - distance)])


def from_ahead(block, distance):
    return lax.ppermute(block, "ctx", [(i + distance, i) for i in range(8 - distance)])


def own_features(x_ref, part):
    core = lax.axis_index("core")
    return x_ref[:, pl.ds(pl.multiple_of((2 * part + core) * 512, 512), 512)]


def other_half(x_ref, out_ref):
    core = lax.axis_index("core")
    for part in range(2):
        place = pl.multiple_of((2 * part + 1 - core) * 512, 512)
        out_ref[:, part * 512 : (part + 1) * 512] = x_ref[:, pl.ds(place, 512)]


def project(x_ref, other_ref, w_ref, *refs):
    dv_refs, out_ref = refs[:-1], refs[-1]
    core = lax.axis_index("core")
    weight = jnp.concatenate(
        [
            jnp.concatenate([w_ref[ctx, part, c] for c in range(4)], axis=1)
            for part in range(2)
            for ctx in range(8)
        ],
        axis=0,
    )
    own = jnp.concatenate([own_features(x_ref, part) for part in range(2)], axis=1)
    for rows, place in ((own, core), (other_ref[...], 1 - core)):
        result = jnp.dot(rows, weight, preferred_element_type=F32)
        for c in range(4):
            out_ref[place * 4 + c, 0] = result[:, c * HEAD_DIM : (c + 1) * HEAD_DIM].astype(BF16)
    total = dv_refs[0][...]
    for ref in dv_refs[1:]:
        total = total + ref[...].astype(F32)
    total = total.astype(BF16)
    for place in range(8):
        out_ref[place, 1] = total


def spread_sum(parts_ref, out_ref):
    total = parts_ref[0, 0].astype(F32)
    for i in range(1, 8):
        total = total + parts_ref[i, 0].astype(F32)
    total = total.astype(BF16)
    for i in range(8):
        out_ref[i] = total


def weight_grad(x_ref, other_ref, dv_ref, out_ref):
    core = lax.axis_index("core")
    own_dv = jnp.concatenate([dv_ref[core * 4 + c, 1] for c in range(4)], axis=1)
    other_dv = jnp.concatenate([dv_ref[(1 - core) * 4 + c, 1] for c in range(4)], axis=1)
    for part in range(2):
        other = other_ref[:, part * 512 : (part + 1) * 512]
        result = lax.dot_general(own_features(x_ref, part), own_dv, TN, preferred_element_type=F32)
        result += lax.dot_general(other, other_dv, TN, preferred_element_type=F32)
        result = result.astype(BF16)
        for ctx in range(8):
            for c in range(4):
                out_ref[ctx, part, c] = result[
                    ctx * 64 : (ctx + 1) * 64, c * HEAD_DIM : (c + 1) * HEAD_DIM
                ]


def tiled_sum(parts_ref, out_ref):
    total = parts_ref[0].astype(F32)
    for i in range(1, 8):
        total = total + parts_ref[i].astype(F32)
    total = total.astype(BF16)
    for i in range(4):
        out_ref[i] = total


def rows_of_heads(wide_ref, rows_ref):
    for h in range(GROUP):
        rows_ref[h * TOK : (h + 1) * TOK] = wide_ref[:, h * HEAD_DIM : (h + 1) * HEAD_DIM]


def fill_bias(len_ref, bias):
    ctx = lax.axis_index("ctx")
    lane = lax.broadcasted_iota(jnp.int32, (1, LANES), 1)
    query = ctx * TOK + lax.rem(lane, TOK)
    first = jnp.zeros_like(query)
    end = jnp.int32(0)
    for d in range(8):
        end = end + len_ref[0, d]
        first = jnp.where(query >= end, end, first)
    offset = lax.broadcasted_iota(jnp.int32, (TOK, LANES), 0)
    for slot in range(REACH + 1):
        key = lax.rem(ctx - (REACH - slot) + 8, 8) * TOK + offset
        bias[slot * TOK : (slot + 1) * TOK] = jnp.where(
            (key >= first) & (key <= query), F32(0.0), F32(-1e30)
        )


def soft(len_ref, q_ref, do_ref, *refs):
    k_refs, dv_refs, stat_ref = refs[:5], refs[5:10], refs[10]
    q_rows, do_rows, bias, probs, keys = refs[11:]
    rows_of_heads(q_ref, q_rows)
    rows_of_heads(do_ref, do_rows)
    for slot, ref in enumerate(k_refs):
        keys[slot * TOK : (slot + 1) * TOK] = ref[...]
    fill_bias(len_ref, bias)
    for i in range(CHUNKS):
        cols = slice(i * LANES, (i + 1) * LANES)
        scores = lax.dot_general(keys[...], q_rows[cols], NT, preferred_element_type=F32)
        scores = scores * F32(SCALE) + bias[...]
        top = jnp.max(scores, axis=0, keepdims=True)
        weights = jnp.exp(scores - top)
        inverse = 1.0 / jnp.sum(weights, axis=0, keepdims=True)
        probs[:, cols] = (weights * inverse).astype(BF16)
        stat_ref[i : i + 1] = top
        stat_ref[CHUNKS + i : CHUNKS + i + 1] = inverse
    total = jnp.dot(probs[...], do_rows[...], preferred_element_type=F32)
    for slot, ref in enumerate(dv_refs):
        ref[...] = total[slot * TOK : (slot + 1) * TOK].astype(ref.dtype)


def attend(len_ref, q_ref, do_ref, stat_ref, v_ref, *refs):
    k_refs, (att_ref, dq_ref), dk_refs = refs[:5], refs[5:7], refs[7:12]
    q_rows, do_rows, bias, dscores, keys, values = refs[12:]
    ctx = lax.axis_index("ctx")
    rows_of_heads(q_ref, q_rows)
    rows_of_heads(do_ref, do_rows)
    for slot, ref in enumerate(k_refs):
        keys[slot * TOK : (slot + 1) * TOK] = ref[...]
        values[slot * TOK : (slot + 1) * TOK] = v_ref[lax.rem(ctx - (REACH - slot) + 8, 8)]
    fill_bias(len_ref, bias)
    for i in range(CHUNKS):
        cols = slice(i * LANES, (i + 1) * LANES)
        scores = lax.dot_general(keys[...], q_rows[cols], NT, preferred_element_type=F32)
        scores = scores * F32(SCALE) + bias[...]
        p = jnp.exp(scores - stat_ref[i : i + 1]) * stat_ref[CHUNKS + i : CHUNKS + i + 1]
        att = lax.dot_general(values[...], p.astype(BF16), TN, preferred_element_type=F32)
        dp = lax.dot_general(values[...], do_rows[cols], NT, preferred_element_type=F32)
        dots = jnp.sum(p * dp, axis=0, keepdims=True)
        ds = (p * (dp - dots)).astype(BF16)
        dscores[:, cols] = ds
        dq = lax.dot_general(keys[...], ds, TN, preferred_element_type=F32) * F32(SCALE)
        att = att.T.astype(BF16)
        dq = dq.T.astype(BF16)
        for j in range(HEADS_AT_ONCE):
            head = slice((i * HEADS_AT_ONCE + j) * HEAD_DIM, (i * HEADS_AT_ONCE + j + 1) * HEAD_DIM)
            att_ref[:, head] = att[j * TOK : (j + 1) * TOK]
            dq_ref[:, head] = dq[j * TOK : (j + 1) * TOK]
    total = jnp.dot(dscores[...], q_rows[...], preferred_element_type=F32)
    for slot, ref in enumerate(dk_refs):
        ref[...] = total[slot * TOK : (slot + 1) * TOK].astype(ref.dtype)


def shards(queries, key_states, normed, value_weight, grad_out, lengths):
    mp = lax.axis_index("mp")
    plane = to_all(value_weight, PLANE, 32)
    mine = lax.dynamic_slice_in_dim(plane, mp * 8, 8, 0)
    spread = jnp.broadcast_to(mine[None], (8, 8, 64, HEAD_DIM))
    away = call(other_half, shape((TOK, 1024)), 1, 0, 10**6)(normed)
    other = lax.ppermute(away, "core", [(0, 1), (1, 0)])
    keys = [from_behind(key_states, d) for d in range(REACH, 0, -1)] + [key_states]
    spread, keys = lax.optimization_barrier((spread, keys))

    weight = lax.all_to_all(spread, "ctx", 0, 0, tiled=True).reshape(8, 2, 4, 64, HEAD_DIM)
    heads = GROUP * TOK
    rows = pltpu.VMEM((heads, HEAD_DIM), BF16)
    window = pltpu.VMEM((WINDOW, HEAD_DIM), BF16)
    bias = pltpu.VMEM((WINDOW, LANES), F32)
    pairs = pltpu.VMEM((WINDOW, heads), BF16)
    block = shape((TOK, HEAD_DIM))
    own = shape((TOK, HEAD_DIM), F32)
    *dv, stats = call(
        soft, (block,) * REACH + (own, shape((8, LANES), F32)), 7, 3 * 10**9, 2 * 10**6,
        (rows, rows, bias, pairs, window), smem=1, vmem=56,
    )(lengths, queries, grad_out, *keys)
    dv = [dv[REACH]] + [from_ahead(dv[REACH - d], d) for d in range(1, REACH + 1)]

    mixed = call(project, shape((8, 2, TOK, HEAD_DIM)), 3 + len(dv), 4 * 10**8, 3 * 10**6)(
        normed, other, weight, *dv
    )
    mixed = lax.all_to_all(mixed, PAIR_MP, 0, 0, tiled=True)
    values = call(spread_sum, shape((8, TOK, HEAD_DIM)), 1, 0, 10**6)(mixed)
    values = lax.all_to_all(values, "ctx", 0, 0, tiled=True)
    partial = call(weight_grad, shape((8, 2, 4, 64, HEAD_DIM)), 3, 4 * 10**8, 3 * 10**6)(
        normed, other, mixed
    )
    partial, values = lax.optimization_barrier((partial, values))
    partial = lax.all_to_all(partial, "ctx", 0, 0, tiled=True)

    wide = shape((TOK, GROUP * HEAD_DIM))
    attended, grad_query, *dk = call(
        attend, (wide, wide) + (block,) * REACH + (own,), 9, 6 * 10**9, 4 * 10**6,
        (rows, rows, bias, pairs, window, window), smem=1, vmem=56,
    )(lengths, queries, grad_out, stats, values, *keys)
    partial, dk = lax.optimization_barrier((partial, dk))
    dk = [dk[REACH]] + [from_ahead(dk[REACH - d], d) for d in range(1, REACH + 1)]
    grad_key = (sum(part.astype(F32) for part in dk) * F32(SCALE)).astype(BF16)

    partial = call(tiled_sum, shape((4, 8, 64, HEAD_DIM)), 1, 0, 2 * 10**6)(
        partial.reshape(8, 8, 64, HEAD_DIM)
    )
    partial = lax.all_to_all(partial.reshape(32, 64, HEAD_DIM), PLANE, 0, 0, tiled=True)
    quarter = lax.axis_index("yh") * 2 + lax.axis_index("x") // 2
    grad_weight = jnp.sum(
        lax.dynamic_index_in_dim(
            partial.reshape(8, 4, 64, HEAD_DIM), quarter, axis=1, keepdims=False
        ).astype(F32),
        axis=0,
    )
    return attended, grad_query, grad_key, grad_weight


def solution(mesh):
    fine = Mesh(mesh.devices.reshape(2, 4, 2, 8, 4), ("yh", "x", "core", "ctx", "mp"))
    tokens = P(("yh", "x", "core", "ctx"), "mp")
    return jax.shard_map(
        shards,
        mesh=fine,
        in_specs=(tokens,) * 5 + (P(("yh", "x", "core"), None),),
        out_specs=(tokens,) * 4,
        check_vma=False,
    )
```

time: 209 us -> 180 us (0.86)
  the two profiles are of different devices: /device:TPU:22 before, /device:TPU:56 now
where the time goes in v2:
time: 180 us; the launch traced here: 178 us
  starting transfers between devices  69.6 us (39%)
  waiting for transfers between devices  60.9 us (34%)
  blocking collectives  22.5 us (12%)
  Pallas kernels  18.1 us (10%)
  local copies, waits for them, and re-layouts  4.56 us (3%)
    ppermute x8, waiting for transfers between devices, from_ahead(): lax.ppermute(block, 'ctx', [(i + distance, i) for i in range(8 - distance)])  27.6 us
    all_to_all x1, blocking collectives, shards(): mixed = lax.all_to_all(mixed, PAIR_MP, 0, 0, tiled=True)  22.5 us
    ppermute x4, starting transfers between devices, from_behind(): lax.ppermute(block, 'ctx', [(i, i + distance) for i in range(8 - distance)])  19.9 us
    all_to_all x1, waiting for transfers between devices, shards(): partial = lax.all_to_all(partial, 'ctx', 0, 0, tiled=True)  18.6 us
    all_to_all x1, waiting for transfers between devices, shards(): values = lax.all_to_all(values, 'ctx', 0, 0, tiled=True)  13.1 us
    all_to_all x1, starting transfers between devices, shards(): lax.all_to_all(partial.reshape(32, 64, HEAD_DIM), PLANE, 0, 0, tiled=True)  10.4 us
    ppermute x8, starting transfers between devices, from_ahead(): lax.ppermute(block, 'ctx', [(i + distance, i) for i in range(8 - distance)])  10.3 us
    all_to_all x1, starting transfers between devices, to_all(): lax.all_to_all(jnp.broadcast_to(block[None], (copies,) + block.shape), ax...  9.62 us
  transfers between devices with their start and end apart: 18, of which 10 were waited for; matrix products, arithmetic and copies ran while one was open for 0% of the time, Pallas kernels for 9%

profile of v2, /device:TPU:56, one launch (start us, length us, event | category | flops | bytes accessed | tf_op | source)
XLA Modules:
  0.0 177.9 jit_solution(5610719927240099093)
XLA Ops:
  0.6 1.6 broadcast_in_dim.4
  2.3 9.6 %all-to-all-start = ((bf16[32,64,128]{2,1,0:T(8,128)(2,1)}), bf16[32,64,128]{2,1,0:T(8,128)(2,1)S(1)}, u32[]{:S(2)}, u32[]{:S(2)}) async-start(bf16[32,64,128]{2,1,0:T(8,128)(2,1)} %broadcast_in_dim.4), calls=%async_computation | async-start | bytes 1048576 | tf_op jit(solution)/shard_map/all_to_all | solution.py:48
  11.9 0.0 copy-done.4
  11.9 6.1 %collective-permute-start.2 = (bf16[192,128]{1,0:T(8,128)(2,1)S(1)}, bf16[192,128]{1,0:T(8,128)(2,1)S(1)}, u32[]{:S(2)}, u32[]{:S(2)}) collective-permute-start(bf16[192,128]{1,0:T(8,128)(2,1)S(1)} %copy-done.4), channel_id=1, source_target_pairs={{0,8},{4,12},{8,16},{12,20},{16,24},{20,28},{1,9},{5,13},{9,17},{1... | collective-permute-start | bytes 147464 | tf_op jit(solution)/shard_map/ppermute | solution.py:54
  18.0 8.2 %collective-permute-start.1 = (bf16[192,128]{1,0:T(8,128)(2,1)S(1)}, bf16[192,128]{1,0:T(8,128)(2,1)S(1)}, u32[]{:S(2)}, u32[]{:S(2)}) collective-permute-start(bf16[192,128]{1,0:T(8,128)(2,1)S(1)} %copy-done.4), channel_id=1, source_target_pairs={{0,12},{4,16},{8,20},{12,24},{16,28},{1,13},{5,17},{9,21},{13,25},... | collective-permute-start | bytes 147464 | tf_op jit(solution)/shard_map/ppermute | solution.py:54
  26.2 3.1 %collective-permute-start = (bf16[192,128]{1,0:T(8,128)(2,1)S(1)}, bf16[192,128]{1,0:T(8,128)(2,1)S(1)}, u32[]{:S(2)}, u32[]{:S(2)}) collective-permute-start(bf16[192,128]{1,0:T(8,128)(2,1)S(1)} %copy-done.4), channel_id=1, source_target_pairs={{0,16},{4,20},{8,24},{12,28},{1,17},{5,21},{9,25},{13,29},{2,18},{... | collective-permute-start | bytes 147464 | tf_op jit(solution)/shard_map/ppermute | solution.py:54
  29.3 2.5 %collective-permute-start.3 = (bf16[192,128]{1,0:T(8,128)(2,1)S(1)}, bf16[192,128]{1,0:T(8,128)(2,1)S(1)}, u32[]{:S(2)}, u32[]{:S(2)}) collective-permute-start(bf16[192,128]{1,0:T(8,128)(2,1)S(1)} %copy-done.4), channel_id=1, source_target_pairs={{0,4},{4,8},{8,12},{12,16},{16,20},{20,24},{24,28},{1,5},{5,9},{9,... | collective-permute-start | bytes 147464 | tf_op jit(solution)/shard_map/ppermute | solution.py:54
  31.8 0.0 all-to-all-done
  31.8 0.0 collective-permute-done.2.refs_2_
  31.9 0.0 copy-start.5
  31.9 0.0 collective-permute-done.1.refs_1_
  31.9 0.0 copy-start.6
  31.9 0.0 collective-permute-done.refs_0_
  31.9 0.0 copy-start.7
  31.9 1.6 collective-permute-done.3.refs_3_
  33.5 1.2 broadcast_in_dim.5
  34.8 0.0 copy-done.5
  34.8 0.0 copy-done.6
  34.8 0.0 copy-done.7
  34.8 0.0 copy-done.8
  34.8 0.0 copy-start
  34.8 5.5 %all-to-all-start.1 = ((bf16[8,8,64,128]{3,2,1,0:T(8,128)(2,1)}), bf16[8,8,64,128]{3,2,1,0:T(8,128)(2,1)S(1)}, u32[]{:S(2)}, u32[]{:S(2)}) async-start(bf16[8,8,64,128]{3,2,1,0:T(8,128)(2,1)} %broadcast_in_dim.5), calls=%async_computation.1 | async-start | bytes 2097152 | tf_op jit(solution)/shard_map/all_to_all | solution.py:218
  40.3 0.0 copy-done
  40.3 1.9 %collective-permute-start.4 = (bf16[192,1024]{1,0:T(8,128)(2,1)S(1)}, bf16[192,1024]{1,0:T(8,128)(2,1)S(1)}, u32[]{:S(2)}, u32[]{:S(2)}) collective-permute-start(bf16[192,1024]{1,0:T(8,128)(2,1)S(1)} %other_half.1), channel_id=1, source_target_pairs={{0,32},{32,0},{1,33},{33,1},{2,34},{34,2},{3,35},{35,3},{4,36},{36... | collective-permute-start | bytes 1179656 | tf_op jit(solution)/shard_map/ppermute | solution.py:214
  42.3 5.6 %soft.1 = (bf16[192,128]{1,0:T(8,128)(2,1)}, bf16[192,128]{1,0:T(8,128)(2,1)}, bf16[192,128]{1,0:T(8,128)(2,1)}, bf16[192,128]{1,0:T(8,128)(2,1)}, f32[192,128]{1,0:T(8,128)}, /*index=5*/f32[8,384]{1,0:T(8,128)}) custom-call(s32[1,8]{1,0:T(1,128)} %len_ref.3, bf16[192,1024]{1,0:T(8,128)(2,1)} %q_ref.3, bf16[192,1024]{1,0:T(8,128)(2,1)} %do_ref.3, ...), custom_call_target="tpu_custom_call" | custom-call | flops 3000000000 | bytes 2000000 | tf_op jit(solution)/shard_map/soft/pallas_call | solution.py:226
  47.9 1.3 collective-permute-start.5
  49.2 1.3 collective-permute-start.6
  50.5 1.3 collective-permute-start.7
  51.8 1.3 collective-permute-start.8
  53.1 0.0 collective-permute-done.4.other_ref
  53.1 12.2 %collective-permute-done.5.refs_1_ = bf16[192,128]{1,0:T(8,128)(2,1)S(1)} collective-permute-done((bf16[192,128]{1,0:T(8,128)(2,1)}, bf16[192,128]{1,0:T(8,128)(2,1)S(1)}, u32[]{:S(2)}, u32[]{:S(2)}) %collective-permute-start.5) | collective-permute-done | bytes 49184 | tf_op jit(solution)/shard_map/ppermute | solution.py:58
  65.3 1.0 collective-permute-done.6.refs_2_
  66.2 2.9 %collective-permute-done.7.refs_3_ = bf16[192,128]{1,0:T(8,128)(2,1)S(1)} collective-permute-done((bf16[192,128]{1,0:T(8,128)(2,1)}, bf16[192,128]{1,0:T(8,128)(2,1)S(1)}, u32[]{:S(2)}, u32[]{:S(2)}) %collective-permute-start.7) | collective-permute-done | bytes 49184 | tf_op jit(solution)/shard_map/ppermute | solution.py:58
  69.2 0.0 collective-permute-done.8.refs_4_
  69.2 0.0 all-to-all-done.1
  69.2 0.9 copy-done.1
  70.1 0.6 project.1
  70.6 22.5 %all_to_all.30.dv_ref.parts_ref = bf16[8,2,192,128]{3,2,1,0:T(8,128)(2,1)S(1)} all-to-all(bf16[8,2,192,128]{3,2,1,0:T(8,128)(2,1)S(1)} %project.1), channel_id=1, replica_groups=mesh['yh'=2,'x'=4,'core'=2,'ctx'=8,'mp'=4] {'core','mp'}, dimensions={0} | all-to-all | bytes 1572864 | tf_op jit(solution)/shard_map/all_to_all | solution.py:235
  93.1 0.8 spread_sum.1
  93.9 8.2 %all-to-all-start.3 = ((bf16[8,192,128]{2,1,0:T(8,128)(2,1)}), bf16[8,192,128]{2,1,0:T(8,128)(2,1)S(1)}, u32[]{:S(2)}, u32[]{:S(2)}) async-start(bf16[8,192,128]{2,1,0:T(8,128)(2,1)} %spread_sum.1), calls=%async_computation.3 | async-start | bytes 786432 | tf_op jit(solution)/shard_map/all_to_all | solution.py:237
  102.2 1.7 weight_grad.1
  103.9 13.1 %all-to-all-done.3.v_ref = bf16[8,192,128]{2,1,0:T(8,128)(2,1)S(1)} async-done(((bf16[8,192,128]{2,1,0:T(8,128)(2,1)}), bf16[8,192,128]{2,1,0:T(8,128)(2,1)S(1)}, u32[]{:S(2)}, u32[]{:S(2)}) %all-to-all-start.3) | async-done | bytes 393248 | tf_op jit(solution)/shard_map/all_to_all | solution.py:237
  117.0 0.7 copy-done.2
  117.8 3.7 %all-to-all-start.4 = ((bf16[8,2,4,64,128]{4,3,2,1,0:T(8,128)(2,1)}), bf16[8,2,4,64,128]{4,3,2,1,0:T(8,128)(2,1)S(1)}, u32[]{:S(2)}, u32[]{:S(2)}) async-start(bf16[8,2,4,64,128]{4,3,2,1,0:T(8,128)(2,1)} %weight_grad.1), calls=%async_computation.4 | async-start | bytes 2097152 | tf_op jit(solution)/shard_map/all_to_all | solution.py:242
  121.5 8.4 %attend.1 = (bf16[192,1024]{1,0:T(8,128)(2,1)}, bf16[192,1024]{1,0:T(8,128)(2,1)}, bf16[192,128]{1,0:T(8,128)(2,1)}, bf16[192,128]{1,0:T(8,128)(2,1)}, bf16[192,...) custom-call(s32[1,8]{1,0:T(1,128)} %len_ref.3, bf16[192,1024]{1,0:T(8,128)(2,1)} %q_ref.3, ...), custom_call_target="tpu_custom_call" | custom-call | flops 6000000000 | bytes 4000000 | tf_op jit(solution)/shard_map/attend/pallas_call | solution.py:245
  129.9 18.6 %all-to-all-done.4 = bf16[8,2,4,64,128]{4,3,2,1,0:T(8,128)(2,1)S(1)} async-done(((bf16[8,2,4,64,128]{4,3,2,1,0:T(8,128)(2,1)}), bf16[8,2,4,64,128]{4,3,2,1,0:T(8,128)(2,1)S(1)}, u32[]{:S(2)}, u32[]{:S(2)}) %all-to-all-start.4) | async-done | bytes 1048608 | tf_op jit(solution)/shard_map/all_to_all | solution.py:242
  148.5 0.9 tiled_sum.1
  149.4 0.0 copy-start.3
  149.4 10.4 %all-to-all-start.5 = ((bf16[32,64,128]{2,1,0:T(8,128)(2,1)}), bf16[32,64,128]{2,1,0:T(8,128)(2,1)S(1)}, u32[]{:S(2)}, u32[]{:S(2)}) async-start(bf16[32,64,128]{2,1,0:T(8,128)(2,1)} %bitcast.2), calls=%async_computation.5 | async-start | bytes 1048576 | tf_op jit(solution)/shard_map/all_to_all | solution.py:256
  159.8 0.0 copy-done.12
  159.8 1.3 collective-permute-start.9
  161.2 0.0 copy-done.11
  161.2 1.3 collective-permute-start.10
  162.5 0.0 copy-done.10
  162.5 1.3 collective-permute-start.11
  163.8 0.0 copy-done.9
  163.8 1.3 collective-permute-start.12
  165.1 1.2 collective-permute-done.9
  166.3 3.4 %collective-permute-done.10 = bf16[192,128]{1,0:T(8,128)(2,1)S(1)} collective-permute-done((bf16[192,128]{1,0:T(8,128)(2,1)S(1)}, bf16[192,128]{1,0:T(8,128)(2,1)S(1)}, u32[]{:S(2)}, u32[]{:S(2)}) %collective-permute-start.10) | collective-permute-done | bytes 49184 | tf_op jit(solution)/shard_map/ppermute | solution.py:58
  169.7 3.7 %collective-permute-done.11 = bf16[192,128]{1,0:T(8,128)(2,1)S(1)} collective-permute-done((bf16[192,128]{1,0:T(8,128)(2,1)S(1)}, bf16[192,128]{1,0:T(8,128)(2,1)S(1)}, u32[]{:S(2)}, u32[]{:S(2)}) %collective-permute-start.11) | collective-permute-done | bytes 49184 | tf_op jit(solution)/shard_map/ppermute | solution.py:58
  173.4 3.2 %collective-permute-done.12 = bf16[192,128]{1,0:T(8,128)(2,1)S(1)} collective-permute-done((bf16[192,128]{1,0:T(8,128)(2,1)S(1)}, bf16[192,128]{1,0:T(8,128)(2,1)S(1)}, u32[]{:S(2)}, u32[]{:S(2)}) %collective-permute-start.12) | collective-permute-done | bytes 49184 | tf_op jit(solution)/shard_map/ppermute | solution.py:58
  176.6 0.7 multiply_convert_fusion
  177.3 0.0 all-to-all-done.5
  177.3 0.6 convert_reduce_fusion
  (11 shorter events, 0.1 us)
Async XLA Ops:
  2.3 9.6 %copy-start.4 = (bf16[192,128]{1,0:T(8,128)(2,1)S(1)}, bf16[192,128]{1,0:T(8,128)(2,1)}, u32[]{:S(2)}) copy-start(bf16[192,128]{1,0:T(8,128)(2,1)} %refs_4_.1) | copy-start | bytes 147460
  2.3 29.6 %all-to-all-start = ((bf16[32,64,128]{2,1,0:T(8,128)(2,1)}), bf16[32,64,128]{2,1,0:T(8,128)(2,1)S(1)}, u32[]{:S(2)}, u32[]{:S(2)}) async-start(bf16[32,64,128]{2,1,0:T(8,128)(2,1)} %broadcast_in_dim.4), calls=%async_computation | async-start | bytes 1048576 | tf_op jit(solution)/shard_map/all_to_all | solution.py:48
  11.9 19.9 %collective-permute-start.2 = (bf16[192,128]{1,0:T(8,128)(2,1)S(1)}, bf16[192,128]{1,0:T(8,128)(2,1)S(1)}, u32[]{:S(2)}, u32[]{:S(2)}) collective-permute-start(bf16[192,128]{1,0:T(8,128)(2,1)S(1)} %copy-done.4), channel_id=1, source_target_pairs={{0,8},{4,12},{8,16},{12,20},{16,24},{20,28},{1,9},{5,13},{9,17},{1... | collective-permute-start | bytes 147464 | tf_op jit(solution)/shard_map/ppermute | solution.py:54
  18.0 13.9 %collective-permute-start.1 = (bf16[192,128]{1,0:T(8,128)(2,1)S(1)}, bf16[192,128]{1,0:T(8,128)(2,1)S(1)}, u32[]{:S(2)}, u32[]{:S(2)}) collective-permute-start(bf16[192,128]{1,0:T(8,128)(2,1)S(1)} %copy-done.4), channel_id=1, source_target_pairs={{0,12},{4,16},{8,20},{12,24},{16,28},{1,13},{5,17},{9,21},{13,25},... | collective-permute-start | bytes 147464 | tf_op jit(solution)/shard_map/ppermute | solution.py:54
  26.2 5.7 %collective-permute-start = (bf16[192,128]{1,0:T(8,128)(2,1)S(1)}, bf16[192,128]{1,0:T(8,128)(2,1)S(1)}, u32[]{:S(2)}, u32[]{:S(2)}) collective-permute-start(bf16[192,128]{1,0:T(8,128)(2,1)S(1)} %copy-done.4), channel_id=1, source_target_pairs={{0,16},{4,20},{8,24},{12,28},{1,17},{5,21},{9,25},{13,29},{2,18},{... | collective-permute-start | bytes 147464 | tf_op jit(solution)/shard_map/ppermute | solution.py:54
  29.3 4.2 %collective-permute-start.3 = (bf16[192,128]{1,0:T(8,128)(2,1)S(1)}, bf16[192,128]{1,0:T(8,128)(2,1)S(1)}, u32[]{:S(2)}, u32[]{:S(2)}) collective-permute-start(bf16[192,128]{1,0:T(8,128)(2,1)S(1)} %copy-done.4), channel_id=1, source_target_pairs={{0,4},{4,8},{8,12},{12,16},{16,20},{20,24},{24,28},{1,5},{5,9},{9,... | collective-permute-start | bytes 147464 | tf_op jit(solution)/shard_map/ppermute | solution.py:54
  31.9 2.9 %copy-start.5 = (bf16[192,128]{1,0:T(8,128)(2,1)}, bf16[192,128]{1,0:T(8,128)(2,1)S(1)}, u32[]{:S(2)}) copy-start(bf16[192,128]{1,0:T(8,128)(2,1)S(1)} %collective-permute-done.2.refs_2_) | copy-start | bytes 147460
  31.9 2.9 %copy-start.6 = (bf16[192,128]{1,0:T(8,128)(2,1)}, bf16[192,128]{1,0:T(8,128)(2,1)S(1)}, u32[]{:S(2)}) copy-start(bf16[192,128]{1,0:T(8,128)(2,1)S(1)} %collective-permute-done.1.refs_1_) | copy-start | bytes 147460
  31.9 2.9 %copy-start.7 = (bf16[192,128]{1,0:T(8,128)(2,1)}, bf16[192,128]{1,0:T(8,128)(2,1)S(1)}, u32[]{:S(2)}) copy-start(bf16[192,128]{1,0:T(8,128)(2,1)S(1)} %collective-permute-done.refs_0_) | copy-start | bytes 147460
  33.5 1.2 copy-start.8
  34.8 5.5 %copy-start = (bf16[192,2048]{1,0:T(8,128)(2,1)S(1)}, bf16[192,2048]{1,0:T(8,128)(2,1)}, u32[]{:S(2)}) copy-start(bf16[192,2048]{1,0:T(8,128)(2,1)} %x_ref.5) | copy-start | bytes 2359300
  34.8 34.4 %all-to-all-start.1 = ((bf16[8,8,64,128]{3,2,1,0:T(8,128)(2,1)}), bf16[8,8,64,128]{3,2,1,0:T(8,128)(2,1)S(1)}, u32[]{:S(2)}, u32[]{:S(2)}) async-start(bf16[8,8,64,128]{3,2,1,0:T(8,128)(2,1)} %broadcast_in_dim.5), calls=%async_computation.1 | async-start | bytes 2097152 | tf_op jit(solution)/shard_map/all_to_all | solution.py:218
  40.3 12.7 %collective-permute-start.4 = (bf16[192,1024]{1,0:T(8,128)(2,1)S(1)}, bf16[192,1024]{1,0:T(8,128)(2,1)S(1)}, u32[]{:S(2)}, u32[]{:S(2)}) collective-permute-start(bf16[192,1024]{1,0:T(8,128)(2,1)S(1)} %other_half.1), channel_id=1, source_target_pairs={{0,32},{32,0},{1,33},{33,1},{2,34},{34,2},{3,35},{35,3},{4,36},{36... | collective-permute-start | bytes 1179656 | tf_op jit(solution)/shard_map/ppermute | solution.py:214
  47.9 17.4 %collective-permute-start.5 = (bf16[192,128]{1,0:T(8,128)(2,1)}, bf16[192,128]{1,0:T(8,128)(2,1)S(1)}, u32[]{:S(2)}, u32[]{:S(2)}) collective-permute-start(bf16[192,128]{1,0:T(8,128)(2,1)} %get-tuple-element.39), channel_id=1, source_target_pairs={{4,0},{8,4},{12,8},{16,12},{20,16},{24,20},{28,24},{5,1},{9,5},{13... | collective-permute-start | bytes 147464 | tf_op jit(solution)/shard_map/ppermute | solution.py:58
  49.2 17.1 %collective-permute-start.6 = (bf16[192,128]{1,0:T(8,128)(2,1)}, bf16[192,128]{1,0:T(8,128)(2,1)S(1)}, u32[]{:S(2)}, u32[]{:S(2)}) collective-permute-start(bf16[192,128]{1,0:T(8,128)(2,1)} %get-tuple-element.40), channel_id=1, source_target_pairs={{8,0},{12,4},{16,8},{20,12},{24,16},{28,20},{9,1},{13,5},{17,9},{2... | collective-permute-start | bytes 147464 | tf_op jit(solution)/shard_map/ppermute | solution.py:58
  50.5 18.7 %collective-permute-start.7 = (bf16[192,128]{1,0:T(8,128)(2,1)}, bf16[192,128]{1,0:T(8,128)(2,1)S(1)}, u32[]{:S(2)}, u32[]{:S(2)}) collective-permute-start(bf16[192,128]{1,0:T(8,128)(2,1)} %get-tuple-element.41), channel_id=1, source_target_pairs={{12,0},{16,4},{20,8},{24,12},{28,16},{13,1},{17,5},{21,9},{25,13},... | collective-permute-start | bytes 147464 | tf_op jit(solution)/shard_map/ppermute | solution.py:58
  51.8 17.4 %collective-permute-start.8 = (bf16[192,128]{1,0:T(8,128)(2,1)}, bf16[192,128]{1,0:T(8,128)(2,1)S(1)}, u32[]{:S(2)}, u32[]{:S(2)}) collective-permute-start(bf16[192,128]{1,0:T(8,128)(2,1)} %get-tuple-element.42), channel_id=1, source_target_pairs={{16,0},{20,4},{24,8},{28,12},{17,1},{21,5},{25,9},{29,13},{18,2},{... | collective-permute-start | bytes 147464 | tf_op jit(solution)/shard_map/ppermute | solution.py:58
  69.2 0.9 copy-start.1
  93.9 23.1 %all-to-all-start.3 = ((bf16[8,192,128]{2,1,0:T(8,128)(2,1)}), bf16[8,192,128]{2,1,0:T(8,128)(2,1)S(1)}, u32[]{:S(2)}, u32[]{:S(2)}) async-start(bf16[8,192,128]{2,1,0:T(8,128)(2,1)} %spread_sum.1), calls=%async_computation.3 | async-start | bytes 786432 | tf_op jit(solution)/shard_map/all_to_all | solution.py:237
  117.0 0.7 copy-start.2
  117.8 30.7 %all-to-all-start.4 = ((bf16[8,2,4,64,128]{4,3,2,1,0:T(8,128)(2,1)}), bf16[8,2,4,64,128]{4,3,2,1,0:T(8,128)(2,1)S(1)}, u32[]{:S(2)}, u32[]{:S(2)}) async-start(bf16[8,2,4,64,128]{4,3,2,1,0:T(8,128)(2,1)} %weight_grad.1), calls=%async_computation.4 | async-start | bytes 2097152 | tf_op jit(solution)/shard_map/all_to_all | solution.py:242
  149.4 10.4 %copy-start.12 = (bf16[192,128]{1,0:T(8,128)(2,1)S(1)}, bf16[192,128]{1,0:T(8,128)(2,1)}, u32[]{:S(2)}) copy-start(bf16[192,128]{1,0:T(8,128)(2,1)} %get-tuple-element.53) | copy-start | bytes 147460
  149.4 11.7 %copy-start.11 = (bf16[192,128]{1,0:T(8,128)(2,1)S(1)}, bf16[192,128]{1,0:T(8,128)(2,1)}, u32[]{:S(2)}) copy-start(bf16[192,128]{1,0:T(8,128)(2,1)} %get-tuple-element.54) | copy-start | bytes 147460
  149.4 13.1 %copy-start.10 = (bf16[192,128]{1,0:T(8,128)(2,1)S(1)}, bf16[192,128]{1,0:T(8,128)(2,1)}, u32[]{:S(2)}) copy-start(bf16[192,128]{1,0:T(8,128)(2,1)} %get-tuple-element.55) | copy-start | bytes 147460
  149.4 14.4 %copy-start.9 = (bf16[192,128]{1,0:T(8,128)(2,1)S(1)}, bf16[192,128]{1,0:T(8,128)(2,1)}, u32[]{:S(2)}) copy-start(bf16[192,128]{1,0:T(8,128)(2,1)} %get-tuple-element.56) | copy-start | bytes 147460
  149.4 27.2 %copy-start.3 = (f32[192,128]{1,0:T(8,128)S(1)}, f32[192,128]{1,0:T(8,128)}, u32[]{:S(2)}) copy-start(f32[192,128]{1,0:T(8,128)} %get-tuple-element.52) | copy-start | bytes 294916
  149.4 27.9 %all-to-all-start.5 = ((bf16[32,64,128]{2,1,0:T(8,128)(2,1)}), bf16[32,64,128]{2,1,0:T(8,128)(2,1)S(1)}, u32[]{:S(2)}, u32[]{:S(2)}) async-start(bf16[32,64,128]{2,1,0:T(8,128)(2,1)} %bitcast.2), calls=%async_computation.5 | async-start | bytes 1048576 | tf_op jit(solution)/shard_map/all_to_all | solution.py:256
  159.8 6.5 %collective-permute-start.9 = (bf16[192,128]{1,0:T(8,128)(2,1)S(1)}, bf16[192,128]{1,0:T(8,128)(2,1)S(1)}, u32[]{:S(2)}, u32[]{:S(2)}) collective-permute-start(bf16[192,128]{1,0:T(8,128)(2,1)S(1)} %copy-done.12), channel_id=1, source_target_pairs={{4,0},{8,4},{12,8},{16,12},{20,16},{24,20},{28,24},{5,1},{9,5},{13... | collective-permute-start | bytes 147464 | tf_op jit(solution)/shard_map/ppermute | solution.py:58
  161.2 8.5 %collective-permute-start.10 = (bf16[192,128]{1,0:T(8,128)(2,1)S(1)}, bf16[192,128]{1,0:T(8,128)(2,1)S(1)}, u32[]{:S(2)}, u32[]{:S(2)}) collective-permute-start(bf16[192,128]{1,0:T(8,128)(2,1)S(1)} %copy-done.11), channel_id=1, source_target_pairs={{8,0},{12,4},{16,8},{20,12},{24,16},{28,20},{9,1},{13,5},{17,9},{2... | collective-permute-start | bytes 147464 | tf_op jit(solution)/shard_map/ppermute | solution.py:58
  162.5 10.9 %collective-permute-start.11 = (bf16[192,128]{1,0:T(8,128)(2,1)S(1)}, bf16[192,128]{1,0:T(8,128)(2,1)S(1)}, u32[]{:S(2)}, u32[]{:S(2)}) collective-permute-start(bf16[192,128]{1,0:T(8,128)(2,1)S(1)} %copy-done.10), channel_id=1, source_target_pairs={{12,0},{16,4},{20,8},{24,12},{28,16},{13,1},{17,5},{21,9},{25,13},... | collective-permute-start | bytes 147464 | tf_op jit(solution)/shard_map/ppermute | solution.py:58
  163.8 12.8 %collective-permute-start.12 = (bf16[192,128]{1,0:T(8,128)(2,1)S(1)}, bf16[192,128]{1,0:T(8,128)(2,1)S(1)}, u32[]{:S(2)}, u32[]{:S(2)}) collective-permute-start(bf16[192,128]{1,0:T(8,128)(2,1)S(1)} %copy-done.9), channel_id=1, source_target_pairs={{16,0},{20,4},{24,8},{28,12},{17,1},{21,5},{25,9},{29,13},{18,2},{... | collective-permute-start | bytes 147464 | tf_op jit(solution)/shard_map/ppermute | solution.py:58

commit v3 on v2

--- a/solution.py
+++ b/solution.py
@@ -13,8 +13,7 @@
 HEADS_AT_ONCE = 2
 LANES = HEADS_AT_ONCE * TOK
 CHUNKS = GROUP // HEADS_AT_ONCE
-PLANE = ("yh", "x", "mp")
-PAIR_MP = ("core", "mp")
+CHIPS = ("yh", "x")
 SCALE = HEAD_DIM ** -0.5
 F32 = jnp.float32
 BF16 = jnp.bfloat16
@@ -58,74 +57,53 @@
     return lax.ppermute(block, "ctx", [(i + distance, i) for i in range(8 - distance)])
 
 
-def own_features(x_ref, part):
+def weight_rows(w_ref, j):
+    return jnp.concatenate([w_ref[ctx, j] for ctx in range(8)], axis=0)
+
+
+def feature_columns(x_ref, j, core):
+    place = pl.multiple_of(((j % 2) * 2 + core) * 512, 512)
+    return x_ref[j // 2, :, pl.ds(place, 512)]
+
+
+def project(x_ref, own_ref, other_ref, out_ref):
     core = lax.axis_index("core")
-    return x_ref[:, pl.ds(pl.multiple_of((2 * part + core) * 512, 512), 512)]
-
-
-def other_half(x_ref, out_ref):
-    core = lax.axis_index("core")
-    for part in range(2):
-        place = pl.multiple_of((2 * part + 1 - core) * 512, 512)
-        out_ref[:, part * 512 : (part + 1) * 512] = x_ref[:, pl.ds(place, 512)]
-
-
-def project(x_ref, other_ref, w_ref, *refs):
-    dv_refs, out_ref = refs[:-1], refs[-1]
-    core = lax.axis_index("core")
-    weight = jnp.concatenate(
-        [
-            jnp.concatenate([w_ref[ctx, part, c] for c in range(4)], axis=1)
-            for part in range(2)
-            for ctx in range(8)
-        ],
-        axis=0,
-    )
-    own = jnp.concatenate([own_features(x_ref, part) for part in range(2)], axis=1)
-    for rows, place in ((own, core), (other_ref[...], 1 - core)):
-        result = jnp.dot(rows, weight, preferred_element_type=F32)
-        for c in range(4):
-            out_ref[place * 4 + c, 0] = result[:, c * HEAD_DIM : (c + 1) * HEAD_DIM].astype(BF16)
-    total = dv_refs[0][...]
-    for ref in dv_refs[1:]:
-        total = total + ref[...].astype(F32)
+    total = jnp.zeros((TOK, HEAD_DIM), F32)
+    for w_ref, half in ((own_ref, core), (other_ref, 1 - core)):
+        for j in range(8):
+            total += jnp.dot(
+                feature_columns(x_ref, j, half), weight_rows(w_ref, j), preferred_element_type=F32
+            )
     total = total.astype(BF16)
     for place in range(8):
-        out_ref[place, 1] = total
-
-
-def spread_sum(parts_ref, out_ref):
-    total = parts_ref[0, 0].astype(F32)
-    for i in range(1, 8):
-        total = total + parts_ref[i, 0].astype(F32)
-    total = total.astype(BF16)
-    for i in range(8):
-        out_ref[i] = total
-
-
-def weight_grad(x_ref, other_ref, dv_ref, out_ref):
+        out_ref[place] = total
+
+
+def weight_grad(x_ref, *refs):
+    dv_refs, out_refs = refs[:5], refs[5:]
     core = lax.axis_index("core")
-    own_dv = jnp.concatenate([dv_ref[core * 4 + c, 1] for c in range(4)], axis=1)
-    other_dv = jnp.concatenate([dv_ref[(1 - core) * 4 + c, 1] for c in range(4)], axis=1)
-    for part in range(2):
-        other = other_ref[:, part * 512 : (part + 1) * 512]
-        result = lax.dot_general(own_features(x_ref, part), own_dv, TN, preferred_element_type=F32)
-        result += lax.dot_general(other, other_dv, TN, preferred_element_type=F32)
-        result = result.astype(BF16)
-        for ctx in range(8):
-            for c in range(4):
-                out_ref[ctx, part, c] = result[
-                    ctx * 64 : (ctx + 1) * 64, c * HEAD_DIM : (c + 1) * HEAD_DIM
-                ]
-
-
-def tiled_sum(parts_ref, out_ref):
+    dv = dv_refs[0][...]
+    for ref in dv_refs[1:]:
+        dv = dv + ref[...].astype(F32)
+    dv = dv.astype(BF16)
+    for out_ref, half in zip(out_refs, (core, 1 - core)):
+        for j in range(8):
+            rows = lax.dot_general(
+                feature_columns(x_ref, j, half), dv, TN, preferred_element_type=F32
+            ).astype(BF16)
+            for ctx in range(8):
+                out_ref[ctx, j] = rows[ctx * 64 : (ctx + 1) * 64]
+
+
+def add_halves(a_ref, b_ref, out_ref):
+    out_ref[...] = (a_ref[...].astype(F32) + b_ref[...].astype(F32)).astype(BF16)
+
+
+def sum_blocks(parts_ref, out_ref):
     total = parts_ref[0].astype(F32)
     for i in range(1, 8):
         total = total + parts_ref[i].astype(F32)
-    total = total.astype(BF16)
-    for i in range(4):
-        out_ref[i] = total
+    out_ref[...] = total.astype(out_ref.dtype)
 
 
 def rows_of_heads(wide_ref, rows_ref):
@@ -206,16 +184,14 @@
 
 
 def shards(queries, key_states, normed, value_weight, grad_out, lengths):
-    mp = lax.axis_index("mp")
-    plane = to_all(value_weight, PLANE, 32)
-    mine = lax.dynamic_slice_in_dim(plane, mp * 8, 8, 0)
-    spread = jnp.broadcast_to(mine[None], (8, 8, 64, HEAD_DIM))
-    away = call(other_half, shape((TOK, 1024)), 1, 0, 10**6)(normed)
-    other = lax.ppermute(away, "core", [(0, 1), (1, 0)])
+    features = lax.all_gather(normed, "mp", axis=0)
     keys = [from_behind(key_states, d) for d in range(REACH, 0, -1)] + [key_states]
+    chips = to_all(value_weight, CHIPS, 8)
+    spread = jnp.broadcast_to(chips[None], (8, 8, 64, HEAD_DIM))
     spread, keys = lax.optimization_barrier((spread, keys))
 
-    weight = lax.all_to_all(spread, "ctx", 0, 0, tiled=True).reshape(8, 2, 4, 64, HEAD_DIM)
+    weight = lax.all_to_all(spread, "ctx", 0, 0, tiled=True)
+    other = lax.ppermute(weight, "core", [(0, 1), (1, 0)])
     heads = GROUP * TOK
     rows = pltpu.VMEM((heads, HEAD_DIM), BF16)
     window = pltpu.VMEM((WINDOW, HEAD_DIM), BF16)
@@ -223,21 +199,20 @@
     pairs = pltpu.VMEM((WINDOW, heads), BF16)
     block = shape((TOK, HEAD_DIM))
     own = shape((TOK, HEAD_DIM), F32)
+    whole = shape((8, 8, 64, HEAD_DIM))
     *dv, stats = call(
         soft, (block,) * REACH + (own, shape((8, LANES), F32)), 7, 3 * 10**9, 2 * 10**6,
         (rows, rows, bias, pairs, window), smem=1, vmem=56,
     )(lengths, queries, grad_out, *keys)
     dv = [dv[REACH]] + [from_ahead(dv[REACH - d], d) for d in range(1, REACH + 1)]
 
-    mixed = call(project, shape((8, 2, TOK, HEAD_DIM)), 3 + len(dv), 4 * 10**8, 3 * 10**6)(
-        normed, other, weight, *dv
-    )
-    mixed = lax.all_to_all(mixed, PAIR_MP, 0, 0, tiled=True)
-    values = call(spread_sum, shape((8, TOK, HEAD_DIM)), 1, 0, 10**6)(mixed)
+    values = call(project, shape((8, TOK, HEAD_DIM)), 3, 4 * 10**8, 5 * 10**6)(
+        features, weight, other
+    )
     values = lax.all_to_all(values, "ctx", 0, 0, tiled=True)
-    partial = call(weight_grad, shape((8, 2, 4, 64, HEAD_DIM)), 3, 4 * 10**8, 3 * 10**6)(
-        normed, other, mixed
-    )
+    partial, given = call(weight_grad, (whole, whole), 6, 4 * 10**8, 5 * 10**6)(features, *dv)
+    taken = lax.ppermute(given, "core", [(0, 1), (1, 0)])
+    partial = call(add_halves, whole, 2, 10**6, 3 * 10**6)(partial, taken)
     partial, values = lax.optimization_barrier((partial, values))
     partial = lax.all_to_all(partial, "ctx", 0, 0, tiled=True)
 
@@ -250,17 +225,9 @@
     dk = [dk[REACH]] + [from_ahead(dk[REACH - d], d) for d in range(1, REACH + 1)]
     grad_key = (sum(part.astype(F32) for part in dk) * F32(SCALE)).astype(BF16)
 
-    partial = call(tiled_sum, shape((4, 8, 64, HEAD_DIM)), 1, 0, 2 * 10**6)(
-        partial.reshape(8, 8, 64, HEAD_DIM)
-    )
-    partial = lax.all_to_all(partial.reshape(32, 64, HEAD_DIM), PLANE, 0, 0, tiled=True)
-    quarter = lax.axis_index("yh") * 2 + lax.axis_index("x") // 2
-    grad_weight = jnp.sum(
-        lax.dynamic_index_in_dim(
-            partial.reshape(8, 4, 64, HEAD_DIM), quarter, axis=1, keepdims=False
-        ).astype(F32),
-        axis=0,
-    )
+    partial = call(sum_blocks, shape((8, 64, HEAD_DIM)), 1, 10**6, 10**6)(partial)
+    partial = lax.all_to_all(partial, CHIPS, 0, 0, tiled=True)
+    grad_weight = call(sum_blocks, shape((64, HEAD_DIM), F32), 1, 10**5, 10**5)(partial)
     return attended, grad_query, grad_key, grad_weight
 
 

time: 180 us -> 194 us (1.078)
  the two profiles are of different devices: /device:TPU:56 before, /device:TPU:128 now
where the time goes in v3:
time: 194 us; the launch traced here: 192 us
  starting transfers between devices  66.5 us (34%)
  waiting for transfers between devices  53.6 us (28%)
  blocking collectives  30.2 us (16%)
  Pallas kernels  22 us (11%)
  between operations  14.3 us (7%)
  local copies, waits for them, and re-layouts  4.44 us (2%)
    all_to_all x1, blocking collectives, shards(): weight = lax.all_to_all(spread, 'ctx', 0, 0, tiled=True)  30.2 us
    all_to_all x1, waiting for transfers between devices, shards(): partial = lax.all_to_all(partial, 'ctx', 0, 0, tiled=True)  18.5 us
    ppermute x8, starting transfers between devices, from_ahead(): lax.ppermute(block, 'ctx', [(i + distance, i) for i in range(8 - distance)])  16.3 us
    ppermute x4, starting transfers between devices, from_behind(): lax.ppermute(block, 'ctx', [(i, i + distance) for i in range(8 - distance)])  15.7 us
    all_to_all x1, waiting for transfers between devices, shards(): values = lax.all_to_all(values, 'ctx', 0, 0, tiled=True)  11.2 us
    ppermute x8, waiting for transfers between devices, from_ahead(): lax.ppermute(block, 'ctx', [(i + distance, i) for i in range(8 - distance)])  9.98 us
    all_to_all x1, starting transfers between devices, to_all(): lax.all_to_all(jnp.broadcast_to(block[None], (copies,) + block.shape), ax...  9.56 us
    all_to_all x1, starting transfers between devices, shards(): partial = lax.all_to_all(partial, CHIPS, 0, 0, tiled=True)  9 us
  transfers between devices with their start and end apart: 19, of which 9 were waited for; matrix products, arithmetic and copies ran while one was open for 2% of the time, Pallas kernels for 11%

profile of v3, /device:TPU:128, one launch (start us, length us, event | category | flops | bytes accessed | tf_op | source)
XLA Modules:
  0.0 192.5 jit_solution(12821634157535200437)
XLA Ops:
  7.2 0.0 all-gather.3.cloned.1.call-start
  7.2 0.7 all-gather.3.cloned.1.call-update
  7.9 1.4 broadcast_in_dim.4
  9.3 9.6 %all-to-all-start = ((bf16[8,64,128]{2,1,0:T(8,128)(2,1)}), bf16[8,64,128]{2,1,0:T(8,128)(2,1)S(1)}, u32[]{:S(2)}, u32[]{:S(2)}) async-start(bf16[8,64,128]{2,1,0:T(8,128)(2,1)} %broadcast_in_dim.4), calls=%async_computation | async-start | bytes 262144 | tf_op jit(solution)/shard_map/all_to_all | solution.py:47
  18.9 7.3 %collective-permute-start.2 = (bf16[192,128]{1,0:T(8,128)(2,1)}, bf16[192,128]{1,0:T(8,128)(2,1)S(1)}, u32[]{:S(2)}, u32[]{:S(2)}) collective-permute-start(bf16[192,128]{1,0:T(8,128)(2,1)} %refs_4_.1), channel_id=1, source_target_pairs={{0,8},{4,12},{8,16},{12,20},{16,24},{20,28},{1,9},{5,13},{9,17},{1... | collective-permute-start | bytes 147464 | tf_op jit(solution)/shard_map/ppermute | solution.py:53
  26.1 5.2 %collective-permute-start.1 = (bf16[192,128]{1,0:T(8,128)(2,1)}, bf16[192,128]{1,0:T(8,128)(2,1)S(1)}, u32[]{:S(2)}, u32[]{:S(2)}) collective-permute-start(bf16[192,128]{1,0:T(8,128)(2,1)} %refs_4_.1), channel_id=1, source_target_pairs={{0,12},{4,16},{8,20},{12,24},{16,28},{1,13},{5,17},{9,21},{13,25},... | collective-permute-start | bytes 147464 | tf_op jit(solution)/shard_map/ppermute | solution.py:53
  31.4 1.3 collective-permute-start
  32.7 1.9 collective-permute-start.3
  34.6 0.0 collective-permute-done.2.refs_2_
  34.6 0.0 copy-start.4
  34.6 0.7 collective-permute-done.1.refs_1_
  35.3 0.0 copy-start.5
  35.3 1.6 collective-permute-done.refs_0_
  36.8 0.0 copy-start.6
  36.8 2.0 %collective-permute-done.3.refs_3_ = bf16[192,128]{1,0:T(8,128)(2,1)S(1)} collective-permute-done((bf16[192,128]{1,0:T(8,128)(2,1)}, bf16[192,128]{1,0:T(8,128)(2,1)S(1)}, u32[]{:S(2)}, u32[]{:S(2)}) %collective-permute-start.3) | collective-permute-done | bytes 49184 | tf_op jit(solution)/shard_map/ppermute | solution.py:53
  38.9 0.0 copy-start.7
  38.9 0.0 all-to-all-done
  38.9 0.2 broadcast_in_dim.5
  39.1 30.2 %all_to_all.25.own_ref = bf16[8,8,64,128]{3,2,1,0:T(8,128)(2,1)S(1)} all-to-all(bf16[8,8,64,128]{3,2,1,0:T(8,128)(2,1)S(1)} %broadcast_in_dim.5), channel_id=1, replica_groups=mesh['yh'=2,'x'=4,'core'=2,'ctx'=8,'mp'=4] {'ctx'}, dimensions={0} | all-to-all | bytes 2097152 | tf_op jit(solution)/shard_map/all_to_all | solution.py:193
  69.3 1.9 collective-permute-start.9
  71.2 0.0 copy-done.4
  71.2 0.0 copy-done.5
  71.2 0.0 copy-done.6
  71.2 0.0 copy-done.7
  71.2 5.6 %soft.1 = (bf16[192,128]{1,0:T(8,128)(2,1)}, bf16[192,128]{1,0:T(8,128)(2,1)}, bf16[192,128]{1,0:T(8,128)(2,1)}, bf16[192,128]{1,0:T(8,128)(2,1)}, f32[192,128]{1,0:T(8,128)}, /*index=5*/f32[8,384]{1,0:T(8,128)}) custom-call(s32[1,8]{1,0:T(1,128)} %len_ref.3, bf16[192,1024]{1,0:T(8,128)(2,1)} %q_ref.3, bf16[192,1024]{1,0:T(8,128)(2,1)} %do_ref.3, ...), custom_call_target="tpu_custom_call" | custom-call | flops 3000000000 | bytes 2000000 | tf_op jit(solution)/shard_map/soft/pallas_call | solution.py:203
  76.8 3.7 %collective-permute-start.4 = (bf16[192,128]{1,0:T(8,128)(2,1)}, bf16[192,128]{1,0:T(8,128)(2,1)S(1)}, u32[]{:S(2)}, u32[]{:S(2)}) collective-permute-start(bf16[192,128]{1,0:T(8,128)(2,1)} %get-tuple-element.40), channel_id=1, source_target_pairs={{4,0},{8,4},{12,8},{16,12},{20,16},{24,20},{28,24},{5,1},{9,5},{13... | collective-permute-start | bytes 147464 | tf_op jit(solution)/shard_map/ppermute | solution.py:57
  80.6 2.2 %collective-permute-start.5 = (bf16[192,128]{1,0:T(8,128)(2,1)}, bf16[192,128]{1,0:T(8,128)(2,1)S(1)}, u32[]{:S(2)}, u32[]{:S(2)}) collective-permute-start(bf16[192,128]{1,0:T(8,128)(2,1)} %get-tuple-element.41), channel_id=1, source_target_pairs={{8,0},{12,4},{16,8},{20,12},{24,16},{28,20},{9,1},{13,5},{17,9},{2... | collective-permute-start | bytes 147464 | tf_op jit(solution)/shard_map/ppermute | solution.py:57
  82.8 1.3 collective-permute-start.6
  84.1 1.3 collective-permute-start.7
  85.4 0.0 collective-permute-done.4.refs_1_
  85.4 4.0 %collective-permute-done.5.refs_2_ = bf16[192,128]{1,0:T(8,128)(2,1)S(1)} collective-permute-done((bf16[192,128]{1,0:T(8,128)(2,1)}, bf16[192,128]{1,0:T(8,128)(2,1)S(1)}, u32[]{:S(2)}, u32[]{:S(2)}) %collective-permute-start.5) | collective-permute-done | bytes 49184 | tf_op jit(solution)/shard_map/ppermute | solution.py:57
  89.4 2.6 %collective-permute-done.6.refs_3_ = bf16[192,128]{1,0:T(8,128)(2,1)S(1)} collective-permute-done((bf16[192,128]{1,0:T(8,128)(2,1)}, bf16[192,128]{1,0:T(8,128)(2,1)S(1)}, u32[]{:S(2)}, u32[]{:S(2)}) %collective-permute-start.6) | collective-permute-done | bytes 49184 | tf_op jit(solution)/shard_map/ppermute | solution.py:57
  92.0 3.4 %collective-permute-done.7.refs_4_ = bf16[192,128]{1,0:T(8,128)(2,1)S(1)} collective-permute-done((bf16[192,128]{1,0:T(8,128)(2,1)}, bf16[192,128]{1,0:T(8,128)(2,1)S(1)}, u32[]{:S(2)}, u32[]{:S(2)}) %collective-permute-start.7) | collective-permute-done | bytes 49184 | tf_op jit(solution)/shard_map/ppermute | solution.py:57
  95.3 0.0 all-gather.3.cloned.1.call-done
  95.3 0.0 copy-start
  95.3 1.9 copy-done
  97.2 0.0 copy-start.2
  97.2 0.9 copy-done.2
  98.1 2.4 %weight_grad.1 = (bf16[8,8,64,128]{3,2,1,0:T(8,128)(2,1)S(1)}, bf16[8,8,64,128]{3,2,1,0:T(8,128)(2,1)}) custom-call(bf16[4,192,2048]{2,1,0:T(8,128)(2,1)S(1)} %bitcast.1, f32[192,128]{1,0:T(8,128)S(1)} %copy-done.2, bf16[192,128]{1,0:T(8,128)(2,1)S(1)} %collective-permute-done.4.refs_1_, bf16[192,128]{1,0:T(8,128)(2,1)S(1)} %collective-permute-done.5.refs_2_, ...), custom_call_target="tpu_custom_call" | custom-call | flops 400000000 | bytes 5000000 | tf_op jit(solution)/shard_map/weight_grad/pallas_call | solution.py:213
  100.5 1.9 collective-permute-start.8
  102.4 0.0 collective-permute-done.9.other_ref
  102.4 0.0 copy-done.1
  102.5 3.0 %project.1 = bf16[8,192,128]{2,1,0:T(8,128)(2,1)} custom-call(bf16[4,192,2048]{2,1,0:T(8,128)(2,1)S(1)} %bitcast.2, bf16[8,8,64,128]{3,2,1,0:T(8,128)(2,1)S(1)} %all_to_all.25.own_ref, bf16[8,8,64,128]{3,2,1,0:T(8,128)(2,1)} %collective-permute-done.9.other_ref), custom_call_target="tpu_custom_call" | custom-call | flops 400000000 | bytes 5000000 | tf_op jit(solution)/shard_map/project/pallas_call | solution.py:209
  105.4 5.7 %all-to-all-start.2 = ((bf16[8,192,128]{2,1,0:T(8,128)(2,1)}), bf16[8,192,128]{2,1,0:T(8,128)(2,1)S(1)}, u32[]{:S(2)}, u32[]{:S(2)}) async-start(bf16[8,192,128]{2,1,0:T(8,128)(2,1)} %project.1), calls=%async_computation.2 | async-start | bytes 786432 | tf_op jit(solution)/shard_map/all_to_all | solution.py:212
  111.1 0.0 collective-permute-done.8.b_ref
  111.1 1.2 add_halves.1
  112.4 11.2 %all-to-all-done.2.v_ref = bf16[8,192,128]{2,1,0:T(8,128)(2,1)S(1)} async-done(((bf16[8,192,128]{2,1,0:T(8,128)(2,1)}), bf16[8,192,128]{2,1,0:T(8,128)(2,1)S(1)}, u32[]{:S(2)}, u32[]{:S(2)}) %all-to-all-start.2) | async-done | bytes 393248 | tf_op jit(solution)/shard_map/all_to_all | solution.py:212
  123.6 6.4 %all-to-all-start.3 = ((bf16[8,8,64,128]{3,2,1,0:T(8,128)(2,1)}), bf16[8,8,64,128]{3,2,1,0:T(8,128)(2,1)S(1)}, u32[]{:S(2)}, u32[]{:S(2)}) async-start(bf16[8,8,64,128]{3,2,1,0:T(8,128)(2,1)} %add_halves.1), calls=%async_computation.3 | async-start | bytes 2097152 | tf_op jit(solution)/shard_map/all_to_all | solution.py:217
  130.0 0.0 copy-done.3
  130.0 8.4 %attend.1 = (bf16[192,1024]{1,0:T(8,128)(2,1)}, bf16[192,1024]{1,0:T(8,128)(2,1)}, bf16[192,128]{1,0:T(8,128)(2,1)}, bf16[192,128]{1,0:T(8,128)(2,1)}, bf16[192,...) custom-call(s32[1,8]{1,0:T(1,128)} %len_ref.3, bf16[192,1024]{1,0:T(8,128)(2,1)} %q_ref.3, ...), custom_call_target="tpu_custom_call" | custom-call | flops 6000000000 | bytes 4000000 | tf_op jit(solution)/shard_map/attend/pallas_call | solution.py:220
  138.4 18.5 %all-to-all-done.3.parts_ref = bf16[8,8,64,128]{3,2,1,0:T(8,128)(2,1)S(1)} async-done(((bf16[8,8,64,128]{3,2,1,0:T(8,128)(2,1)}), bf16[8,8,64,128]{3,2,1,0:T(8,128)(2,1)S(1)}, u32[]{:S(2)}, u32[]{:S(2)}) %all-to-all-start.3) | async-done | bytes 1048608 | tf_op jit(solution)/shard_map/all_to_all | solution.py:217
  156.9 3.3 %collective-permute-start.10 = (bf16[192,128]{1,0:T(8,128)(2,1)}, bf16[192,128]{1,0:T(8,128)(2,1)S(1)}, u32[]{:S(2)}, u32[]{:S(2)}) collective-permute-start(bf16[192,128]{1,0:T(8,128)(2,1)} %get-tuple-element.57), channel_id=1, source_target_pairs={{4,0},{8,4},{12,8},{16,12},{20,16},{24,20},{28,24},{5,1},{9,5},{13... | collective-permute-start | bytes 147464 | tf_op jit(solution)/shard_map/ppermute | solution.py:57
  160.2 1.9 collective-permute-start.11
  162.1 1.3 collective-permute-start.12
  163.4 1.3 collective-permute-start.13
  164.7 0.8 sum_blocks.2
  165.5 9.0 %all-to-all-start.4 = ((bf16[8,64,128]{2,1,0:T(8,128)(2,1)}), bf16[8,64,128]{2,1,0:T(8,128)(2,1)S(1)}, u32[]{:S(2)}, u32[]{:S(2)}) async-start(bf16[8,64,128]{2,1,0:T(8,128)(2,1)} %sum_blocks.2), calls=%async_computation.4 | async-start | bytes 262144 | tf_op jit(solution)/shard_map/all_to_all | solution.py:229
  174.5 0.0 collective-permute-done.10
  174.5 0.0 collective-permute-done.11
  174.5 0.0 collective-permute-done.12
  174.5 0.0 collective-permute-done.13
  174.5 1.6 multiply_convert_fusion
  176.1 8.9 %all-to-all-done.4.parts_ref = bf16[8,64,128]{2,1,0:T(8,128)(2,1)S(1)} async-done(((bf16[8,64,128]{2,1,0:T(8,128)(2,1)}), bf16[8,64,128]{2,1,0:T(8,128)(2,1)S(1)}, u32[]{:S(2)}, u32[]{:S(2)}) %all-to-all-start.4) | async-done | bytes 131104 | tf_op jit(solution)/shard_map/all_to_all | solution.py:229
  185.0 0.6 sum_blocks.3
  (2 shorter events, 0.0 us)
Async XLA Ops:
  7.2 88.2 %all-gather.3.cloned.1.call-start = ((), (), s32[]{:S(2)}) async-start(), calls=%async_computation.5 | async-start | bytes 3932160 | tf_op jit(solution)/shard_map/all_gather | solution.py:187
  9.3 29.6 %all-to-all-start = ((bf16[8,64,128]{2,1,0:T(8,128)(2,1)}), bf16[8,64,128]{2,1,0:T(8,128)(2,1)S(1)}, u32[]{:S(2)}, u32[]{:S(2)}) async-start(bf16[8,64,128]{2,1,0:T(8,128)(2,1)} %broadcast_in_dim.4), calls=%async_computation | async-start | bytes 262144 | tf_op jit(solution)/shard_map/all_to_all | solution.py:47
  18.9 15.7 %collective-permute-start.2 = (bf16[192,128]{1,0:T(8,128)(2,1)}, bf16[192,128]{1,0:T(8,128)(2,1)S(1)}, u32[]{:S(2)}, u32[]{:S(2)}) collective-permute-start(bf16[192,128]{1,0:T(8,128)(2,1)} %refs_4_.1), channel_id=1, source_target_pairs={{0,8},{4,12},{8,16},{12,20},{16,24},{20,28},{1,9},{5,13},{9,17},{1... | collective-permute-start | bytes 147464 | tf_op jit(solution)/shard_map/ppermute | solution.py:53
  26.1 9.1 %collective-permute-start.1 = (bf16[192,128]{1,0:T(8,128)(2,1)}, bf16[192,128]{1,0:T(8,128)(2,1)S(1)}, u32[]{:S(2)}, u32[]{:S(2)}) collective-permute-start(bf16[192,128]{1,0:T(8,128)(2,1)} %refs_4_.1), channel_id=1, source_target_pairs={{0,12},{4,16},{8,20},{12,24},{16,28},{1,13},{5,17},{9,21},{13,25},... | collective-permute-start | bytes 147464 | tf_op jit(solution)/shard_map/ppermute | solution.py:53
  31.4 5.5 %collective-permute-start = (bf16[192,128]{1,0:T(8,128)(2,1)}, bf16[192,128]{1,0:T(8,128)(2,1)S(1)}, u32[]{:S(2)}, u32[]{:S(2)}) collective-permute-start(bf16[192,128]{1,0:T(8,128)(2,1)} %refs_4_.1), channel_id=1, source_target_pairs={{0,16},{4,20},{8,24},{12,28},{1,17},{5,21},{9,25},{13,29},{2,18},{... | collective-permute-start | bytes 147464 | tf_op jit(solution)/shard_map/ppermute | solution.py:53
  32.7 6.2 %collective-permute-start.3 = (bf16[192,128]{1,0:T(8,128)(2,1)}, bf16[192,128]{1,0:T(8,128)(2,1)S(1)}, u32[]{:S(2)}, u32[]{:S(2)}) collective-permute-start(bf16[192,128]{1,0:T(8,128)(2,1)} %refs_4_.1), channel_id=1, source_target_pairs={{0,4},{4,8},{8,12},{12,16},{16,20},{20,24},{24,28},{1,5},{5,9},{9,... | collective-permute-start | bytes 147464 | tf_op jit(solution)/shard_map/ppermute | solution.py:53
  34.6 36.6 %copy-start.4 = (bf16[192,128]{1,0:T(8,128)(2,1)}, bf16[192,128]{1,0:T(8,128)(2,1)S(1)}, u32[]{:S(2)}) copy-start(bf16[192,128]{1,0:T(8,128)(2,1)S(1)} %collective-permute-done.2.refs_2_) | copy-start | bytes 147460
  35.3 35.9 %copy-start.5 = (bf16[192,128]{1,0:T(8,128)(2,1)}, bf16[192,128]{1,0:T(8,128)(2,1)S(1)}, u32[]{:S(2)}) copy-start(bf16[192,128]{1,0:T(8,128)(2,1)S(1)} %collective-permute-done.1.refs_1_) | copy-start | bytes 147460
  36.8 34.4 %copy-start.6 = (bf16[192,128]{1,0:T(8,128)(2,1)}, bf16[192,128]{1,0:T(8,128)(2,1)S(1)}, u32[]{:S(2)}) copy-start(bf16[192,128]{1,0:T(8,128)(2,1)S(1)} %collective-permute-done.refs_0_) | copy-start | bytes 147460
  38.9 32.4 %copy-start.7 = (bf16[192,128]{1,0:T(8,128)(2,1)}, bf16[192,128]{1,0:T(8,128)(2,1)S(1)}, u32[]{:S(2)}) copy-start(bf16[192,128]{1,0:T(8,128)(2,1)S(1)} %collective-permute-done.3.refs_3_) | copy-start | bytes 147460
  69.3 33.2 %collective-permute-start.9 = (bf16[8,8,64,128]{3,2,1,0:T(8,128)(2,1)S(1)}, bf16[8,8,64,128]{3,2,1,0:T(8,128)(2,1)}, u32[]{:S(2)}, u32[]{:S(2)}) collective-permute-start(bf16[8,8,64,128]{3,2,1,0:T(8,128)(2,1)S(1)} %all_to_all.25.own_ref), channel_id=1, source_target_pairs={{0,32},{32,0},{1,33},{33,1},{2,34},{34,2},{3,35},{35,3},{4,36},{36... | collective-permute-start | bytes 3145736 | tf_op jit(solution)/shard_map/ppermute | solution.py:194
  76.8 8.5 %collective-permute-start.4 = (bf16[192,128]{1,0:T(8,128)(2,1)}, bf16[192,128]{1,0:T(8,128)(2,1)S(1)}, u32[]{:S(2)}, u32[]{:S(2)}) collective-permute-start(bf16[192,128]{1,0:T(8,128)(2,1)} %get-tuple-element.40), channel_id=1, source_target_pairs={{4,0},{8,4},{12,8},{16,12},{20,16},{24,20},{28,24},{5,1},{9,5},{13... | collective-permute-start | bytes 147464 | tf_op jit(solution)/shard_map/ppermute | solution.py:57
  80.6 8.8 %collective-permute-start.5 = (bf16[192,128]{1,0:T(8,128)(2,1)}, bf16[192,128]{1,0:T(8,128)(2,1)S(1)}, u32[]{:S(2)}, u32[]{:S(2)}) collective-permute-start(bf16[192,128]{1,0:T(8,128)(2,1)} %get-tuple-element.41), channel_id=1, source_target_pairs={{8,0},{12,4},{16,8},{20,12},{24,16},{28,20},{9,1},{13,5},{17,9},{2... | collective-permute-start | bytes 147464 | tf_op jit(solution)/shard_map/ppermute | solution.py:57
  82.8 9.2 %collective-permute-start.6 = (bf16[192,128]{1,0:T(8,128)(2,1)}, bf16[192,128]{1,0:T(8,128)(2,1)S(1)}, u32[]{:S(2)}, u32[]{:S(2)}) collective-permute-start(bf16[192,128]{1,0:T(8,128)(2,1)} %get-tuple-element.42), channel_id=1, source_target_pairs={{12,0},{16,4},{20,8},{24,12},{28,16},{13,1},{17,5},{21,9},{25,13},... | collective-permute-start | bytes 147464 | tf_op jit(solution)/shard_map/ppermute | solution.py:57
  84.1 11.3 %collective-permute-start.7 = (bf16[192,128]{1,0:T(8,128)(2,1)}, bf16[192,128]{1,0:T(8,128)(2,1)S(1)}, u32[]{:S(2)}, u32[]{:S(2)}) collective-permute-start(bf16[192,128]{1,0:T(8,128)(2,1)} %get-tuple-element.43), channel_id=1, source_target_pairs={{16,0},{20,4},{24,8},{28,12},{17,1},{21,5},{25,9},{29,13},{18,2},{... | collective-permute-start | bytes 147464 | tf_op jit(solution)/shard_map/ppermute | solution.py:57
  95.3 1.9 copy-start
  97.2 0.9 copy-start.2
  98.1 4.3 %copy-start.1 = (bf16[768,2048]{1,0:T(8,128)(2,1)S(1)}, bf16[768,2048]{1,0:T(8,128)(2,1)}, u32[]{:S(2)}) copy-start(bf16[768,2048]{1,0:T(8,128)(2,1)} %all-gather.3.cloned.1.call-done) | copy-start | bytes 9437188
  100.5 10.6 %collective-permute-start.8 = (bf16[8,8,64,128]{3,2,1,0:T(8,128)(2,1)}, bf16[8,8,64,128]{3,2,1,0:T(8,128)(2,1)S(1)}, u32[]{:S(2)}, u32[]{:S(2)}) collective-permute-start(bf16[8,8,64,128]{3,2,1,0:T(8,128)(2,1)} %get-tuple-element.45), channel_id=1, source_target_pairs={{0,32},{32,0},{1,33},{33,1},{2,34},{34,2},{3,35},{35,3},{4,36},{36... | collective-permute-start | bytes 3145736 | tf_op jit(solution)/shard_map/ppermute | solution.py:214
  105.4 18.2 %all-to-all-start.2 = ((bf16[8,192,128]{2,1,0:T(8,128)(2,1)}), bf16[8,192,128]{2,1,0:T(8,128)(2,1)S(1)}, u32[]{:S(2)}, u32[]{:S(2)}) async-start(bf16[8,192,128]{2,1,0:T(8,128)(2,1)} %project.1), calls=%async_computation.2 | async-start | bytes 786432 | tf_op jit(solution)/shard_map/all_to_all | solution.py:212
  123.6 6.4 %copy-start.3 = (bf16[8,192,128]{2,1,0:T(8,128)(2,1)}, bf16[8,192,128]{2,1,0:T(8,128)(2,1)S(1)}, u32[]{:S(2)}) copy-start(bf16[8,192,128]{2,1,0:T(8,128)(2,1)S(1)} %all-to-all-done.2.v_ref) | copy-start | bytes 1179652
  123.6 33.3 %all-to-all-start.3 = ((bf16[8,8,64,128]{3,2,1,0:T(8,128)(2,1)}), bf16[8,8,64,128]{3,2,1,0:T(8,128)(2,1)S(1)}, u32[]{:S(2)}, u32[]{:S(2)}) async-start(bf16[8,8,64,128]{3,2,1,0:T(8,128)(2,1)} %add_halves.1), calls=%async_computation.3 | async-start | bytes 2097152 | tf_op jit(solution)/shard_map/all_to_all | solution.py:217
  156.9 17.6 %collective-permute-start.10 = (bf16[192,128]{1,0:T(8,128)(2,1)}, bf16[192,128]{1,0:T(8,128)(2,1)S(1)}, u32[]{:S(2)}, u32[]{:S(2)}) collective-permute-start(bf16[192,128]{1,0:T(8,128)(2,1)} %get-tuple-element.57), channel_id=1, source_target_pairs={{4,0},{8,4},{12,8},{16,12},{20,16},{24,20},{28,24},{5,1},{9,5},{13... | collective-permute-start | bytes 147464 | tf_op jit(solution)/shard_map/ppermute | solution.py:57
  160.2 14.3 %collective-permute-start.11 = (bf16[192,128]{1,0:T(8,128)(2,1)}, bf16[192,128]{1,0:T(8,128)(2,1)S(1)}, u32[]{:S(2)}, u32[]{:S(2)}) collective-permute-start(bf16[192,128]{1,0:T(8,128)(2,1)} %get-tuple-element.58), channel_id=1, source_target_pairs={{8,0},{12,4},{16,8},{20,12},{24,16},{28,20},{9,1},{13,5},{17,9},{2... | collective-permute-start | bytes 147464 | tf_op jit(solution)/shard_map/ppermute | solution.py:57
  162.1 12.4 %collective-permute-start.12 = (bf16[192,128]{1,0:T(8,128)(2,1)}, bf16[192,128]{1,0:T(8,128)(2,1)S(1)}, u32[]{:S(2)}, u32[]{:S(2)}) collective-permute-start(bf16[192,128]{1,0:T(8,128)(2,1)} %get-tuple-element.59), channel_id=1, source_target_pairs={{12,0},{16,4},{20,8},{24,12},{28,16},{13,1},{17,5},{21,9},{25,13},... | collective-permute-start | bytes 147464 | tf_op jit(solution)/shard_map/ppermute | solution.py:57
  163.4 11.1 %collective-permute-start.13 = (bf16[192,128]{1,0:T(8,128)(2,1)}, bf16[192,128]{1,0:T(8,128)(2,1)S(1)}, u32[]{:S(2)}, u32[]{:S(2)}) collective-permute-start(bf16[192,128]{1,0:T(8,128)(2,1)} %get-tuple-element.60), channel_id=1, source_target_pairs={{16,0},{20,4},{24,8},{28,12},{17,1},{21,5},{25,9},{29,13},{18,2},{... | collective-permute-start | bytes 147464 | tf_op jit(solution)/shard_map/ppermute | solution.py:57
  165.5 19.5 %all-to-all-start.4 = ((bf16[8,64,128]{2,1,0:T(8,128)(2,1)}), bf16[8,64,128]{2,1,0:T(8,128)(2,1)S(1)}, u32[]{:S(2)}, u32[]{:S(2)}) async-start(bf16[8,64,128]{2,1,0:T(8,128)(2,1)} %sum_blocks.2), calls=%async_computation.4 | async-start | bytes 262144 | tf_op jit(solution)/shard_map/all_to_all | solution.py:229
Sparse Core Ops, SparseCore 0:
  10.1 72.6 all-gather.2

commit v4 on v2

--- a/solution.py
+++ b/solution.py
@@ -13,8 +13,7 @@
 HEADS_AT_ONCE = 2
 LANES = HEADS_AT_ONCE * TOK
 CHUNKS = GROUP // HEADS_AT_ONCE
-PLANE = ("yh", "x", "mp")
-PAIR_MP = ("core", "mp")
+PLANE = ("yh", "x1", "mp")
 SCALE = HEAD_DIM ** -0.5
 F32 = jnp.float32
 BF16 = jnp.bfloat16
@@ -58,65 +57,76 @@
     return lax.ppermute(block, "ctx", [(i + distance, i) for i in range(8 - distance)])
 
 
-def own_features(x_ref, part):
-    core = lax.axis_index("core")
-    return x_ref[:, pl.ds(pl.multiple_of((2 * part + core) * 512, 512), 512)]
-
-
-def other_half(x_ref, out_ref):
-    core = lax.axis_index("core")
-    for part in range(2):
-        place = pl.multiple_of((2 * part + 1 - core) * 512, 512)
-        out_ref[:, part * 512 : (part + 1) * 512] = x_ref[:, pl.ds(place, 512)]
-
-
-def project(x_ref, other_ref, w_ref, *refs):
-    dv_refs, out_ref = refs[:-1], refs[-1]
-    core = lax.axis_index("core")
+def traded(blocks):
+    both = [(0, 3), (1, 2), (2, 1), (3, 0)]
+    pair = [(0, 1), (1, 0)]
+    return [
+        lax.ppermute(blocks[0], "core", pair),
+        lax.ppermute(blocks[1], "x0", pair),
+        lax.ppermute(blocks[2], ("x0", "core"), both),
+    ]
+
+
+def piece(x_ref, step):
+    x0, core = lax.axis_index("x0"), lax.axis_index("core")
+    x0 = 1 - x0 if step >= 2 else x0
+    core = 1 - core if step % 2 else core
+    return x_ref[:, pl.ds(pl.multiple_of((2 * x0 + core) * 512, 512), 512)]
+
+
+def pieces(x_ref, *out_refs):
+    for step, ref in enumerate(out_refs):
+        ref[...] = piece(x_ref, step + 1)
+
+
+def project(x_ref, *refs):
+    others, w_ref, outs = refs[:3], refs[3], refs[4:]
     weight = jnp.concatenate(
-        [
-            jnp.concatenate([w_ref[ctx, part, c] for c in range(4)], axis=1)
-            for part in range(2)
-            for ctx in range(8)
-        ],
-        axis=0,
-    )
-    own = jnp.concatenate([own_features(x_ref, part) for part in range(2)], axis=1)
-    for rows, place in ((own, core), (other_ref[...], 1 - core)):
-        result = jnp.dot(rows, weight, preferred_element_type=F32)
+        [jnp.concatenate([w_ref[ctx, c] for c in range(4)], axis=1) for ctx in range(8)], axis=0
+    )
+    rows = [piece(x_ref, 0)] + [ref[...] for ref in others]
+    for x, out_ref in zip(rows, outs):
+        result = jnp.dot(x, weight, preferred_element_type=F32)
         for c in range(4):
-            out_ref[place * 4 + c, 0] = result[:, c * HEAD_DIM : (c + 1) * HEAD_DIM].astype(BF16)
+            out_ref[c] = result[:, c * HEAD_DIM : (c + 1) * HEAD_DIM].astype(out_ref.dtype)
+
+
+def mix(*refs):
+    parts, dv_refs, out_ref = refs[:4], refs[4:9], refs[9]
     total = dv_refs[0][...]
     for ref in dv_refs[1:]:
         total = total + ref[...].astype(F32)
     total = total.astype(BF16)
-    for place in range(8):
-        out_ref[place, 1] = total
-
-
-def spread_sum(parts_ref, out_ref):
+    for c in range(4):
+        value = parts[0][c]
+        for ref in parts[1:]:
+            value = value + ref[c].astype(F32)
+        out_ref[c, 0] = value.astype(BF16)
+        out_ref[c, 1] = total
+
+
+def spread_sum(parts_ref, values_ref, dv_ref):
     total = parts_ref[0, 0].astype(F32)
-    for i in range(1, 8):
+    for i in range(1, 4):
         total = total + parts_ref[i, 0].astype(F32)
     total = total.astype(BF16)
     for i in range(8):
-        out_ref[i] = total
-
-
-def weight_grad(x_ref, other_ref, dv_ref, out_ref):
-    core = lax.axis_index("core")
-    own_dv = jnp.concatenate([dv_ref[core * 4 + c, 1] for c in range(4)], axis=1)
-    other_dv = jnp.concatenate([dv_ref[(1 - core) * 4 + c, 1] for c in range(4)], axis=1)
-    for part in range(2):
-        other = other_ref[:, part * 512 : (part + 1) * 512]
-        result = lax.dot_general(own_features(x_ref, part), own_dv, TN, preferred_element_type=F32)
-        result += lax.dot_general(other, other_dv, TN, preferred_element_type=F32)
-        result = result.astype(BF16)
-        for ctx in range(8):
-            for c in range(4):
-                out_ref[ctx, part, c] = result[
-                    ctx * 64 : (ctx + 1) * 64, c * HEAD_DIM : (c + 1) * HEAD_DIM
-                ]
+        values_ref[i] = total
+    for i in range(4):
+        dv_ref[i] = parts_ref[i, 1]
+
+
+def weight_grad(x_ref, *refs):
+    others, dv_refs, out_ref = refs[:3], refs[3:7], refs[7]
+    rows = [piece(x_ref, 0)] + [ref[...] for ref in others]
+    result = jnp.zeros((512, 512), F32)
+    for x, dv_ref in zip(rows, dv_refs):
+        dv = jnp.concatenate([dv_ref[c] for c in range(4)], axis=1)
+        result += lax.dot_general(x, dv, TN, preferred_element_type=F32)
+    result = result.astype(BF16)
+    for ctx in range(8):
+        for c in range(4):
+            out_ref[ctx, c] = result[ctx * 64 : (ctx + 1) * 64, c * HEAD_DIM : (c + 1) * HEAD_DIM]
 
 
 def tiled_sum(parts_ref, out_ref):
@@ -207,15 +217,15 @@
 
 def shards(queries, key_states, normed, value_weight, grad_out, lengths):
     mp = lax.axis_index("mp")
-    plane = to_all(value_weight, PLANE, 32)
-    mine = lax.dynamic_slice_in_dim(plane, mp * 8, 8, 0)
-    spread = jnp.broadcast_to(mine[None], (8, 8, 64, HEAD_DIM))
-    away = call(other_half, shape((TOK, 1024)), 1, 0, 10**6)(normed)
-    other = lax.ppermute(away, "core", [(0, 1), (1, 0)])
+    plane = to_all(value_weight, PLANE, 16)
+    mine = lax.dynamic_slice_in_dim(plane, mp * 4, 4, 0)
+    spread = jnp.broadcast_to(mine[None], (8, 4, 64, HEAD_DIM))
+    quarter = shape((TOK, 512))
+    others = traded(call(pieces, (quarter,) * 3, 1, 0, 10**6)(normed))
     keys = [from_behind(key_states, d) for d in range(REACH, 0, -1)] + [key_states]
     spread, keys = lax.optimization_barrier((spread, keys))
 
-    weight = lax.all_to_all(spread, "ctx", 0, 0, tiled=True).reshape(8, 2, 4, 64, HEAD_DIM)
+    weight = lax.all_to_all(spread, "ctx", 0, 0, tiled=True)
     heads = GROUP * TOK
     rows = pltpu.VMEM((heads, HEAD_DIM), BF16)
     window = pltpu.VMEM((WINDOW, HEAD_DIM), BF16)
@@ -228,15 +238,20 @@
         (rows, rows, bias, pairs, window), smem=1, vmem=56,
     )(lengths, queries, grad_out, *keys)
     dv = [dv[REACH]] + [from_ahead(dv[REACH - d], d) for d in range(1, REACH + 1)]
-
-    mixed = call(project, shape((8, 2, TOK, HEAD_DIM)), 3 + len(dv), 4 * 10**8, 3 * 10**6)(
-        normed, other, weight, *dv
-    )
-    mixed = lax.all_to_all(mixed, PAIR_MP, 0, 0, tiled=True)
-    values = call(spread_sum, shape((8, TOK, HEAD_DIM)), 1, 0, 10**6)(mixed)
+    weight, stats = lax.optimization_barrier((weight, stats))
+
+    four = shape((4, TOK, HEAD_DIM))
+    projected, *away = call(
+        project, (shape((4, TOK, HEAD_DIM), F32),) + (four,) * 3, 5, 4 * 10**8, 3 * 10**6
+    )(normed, *others, weight)
+    mixed = call(mix, shape((4, 2, TOK, HEAD_DIM)), 9, 10**6, 2 * 10**6)(
+        projected, *traded(away), *dv
+    )
+    mixed = lax.all_to_all(mixed, "mp", 0, 0, tiled=True)
+    values, grad_value = call(spread_sum, (shape((8, TOK, HEAD_DIM)), four), 1, 10**6, 10**6)(mixed)
     values = lax.all_to_all(values, "ctx", 0, 0, tiled=True)
-    partial = call(weight_grad, shape((8, 2, 4, 64, HEAD_DIM)), 3, 4 * 10**8, 3 * 10**6)(
-        normed, other, mixed
+    partial = call(weight_grad, shape((8, 4, 64, HEAD_DIM)), 8, 4 * 10**8, 3 * 10**6)(
+        normed, *others, grad_value, *traded([grad_value] * 3)
     )
     partial, values = lax.optimization_barrier((partial, values))
     partial = lax.all_to_all(partial, "ctx", 0, 0, tiled=True)
@@ -250,14 +265,12 @@
     dk = [dk[REACH]] + [from_ahead(dk[REACH - d], d) for d in range(1, REACH + 1)]
     grad_key = (sum(part.astype(F32) for part in dk) * F32(SCALE)).astype(BF16)
 
-    partial = call(tiled_sum, shape((4, 8, 64, HEAD_DIM)), 1, 0, 2 * 10**6)(
-        partial.reshape(8, 8, 64, HEAD_DIM)
-    )
-    partial = lax.all_to_all(partial.reshape(32, 64, HEAD_DIM), PLANE, 0, 0, tiled=True)
-    quarter = lax.axis_index("yh") * 2 + lax.axis_index("x") // 2
+    partial = call(tiled_sum, shape((4, 4, 64, HEAD_DIM)), 1, 10**6, 10**6)(partial)
+    partial = lax.all_to_all(partial.reshape(16, 64, HEAD_DIM), PLANE, 0, 0, tiled=True)
+    place = lax.axis_index("yh") * 2 + lax.axis_index("x1")
     grad_weight = jnp.sum(
         lax.dynamic_index_in_dim(
-            partial.reshape(8, 4, 64, HEAD_DIM), quarter, axis=1, keepdims=False
+            partial.reshape(4, 4, 64, HEAD_DIM), place, axis=1, keepdims=False
         ).astype(F32),
         axis=0,
     )
@@ -265,12 +278,13 @@
 
 
 def solution(mesh):
-    fine = Mesh(mesh.devices.reshape(2, 4, 2, 8, 4), ("yh", "x", "core", "ctx", "mp"))
-    tokens = P(("yh", "x", "core", "ctx"), "mp")
+    axes = ("yh", "x1", "x0", "core", "ctx", "mp")
+    fine = Mesh(mesh.devices.reshape(2, 2, 2, 2, 8, 4), axes)
+    tokens = P(axes[:5], "mp")
     return jax.shard_map(
         shards,
         mesh=fine,
-        in_specs=(tokens,) * 5 + (P(("yh", "x", "core"), None),),
+        in_specs=(tokens,) * 5 + (P(axes[:4], None),),
         out_specs=(tokens,) * 4,
         check_vma=False,
     )

time: 180 us -> 171 us (0.950)
  starting transfers between devices: 69.6 us -> 90 us
  waiting for transfers between devices: 60.9 us -> 41.9 us
  blocking collectives: 22.5 us -> 13.5 us
    ppermute x1 -> x9, starting transfers between devices: 1.92 us -> 22.7 us  [the longest x3 8.19 us: traded(): lax.ppermute(blocks[2], ('x0', 'core'), both)]
    all_to_all x1, waiting for transfers between devices: 13.1 us -> 0.2 us  [shards(): values = lax.all_to_all(values, 'ctx', 0, 0, tiled=True)]
    all_to_all x1, blocking collectives: 22.5 us -> 13.5 us  [shards(): mixed = lax.all_to_all(mixed, 'mp', 0, 0, tiled=True)]
    all_to_all x1, waiting for transfers between devices: 18.6 us -> 9.95 us  [shards(): partial = lax.all_to_all(partial, 'ctx', 0, 0, tiled=True)]
    ppermute x1 -> x9, waiting for transfers between devices: 0.01 us -> 4.04 us  [the longest x3 2.57 us: traded(): lax.ppermute(blocks[1], 'x0', pair)]
    ppermute x8, waiting for transfers between devices: 27.6 us -> 24.1 us  [from_ahead(): lax.ppermute(block, 'ctx', [(i + distance, i) for i in range(8 - distance)])]
    all_to_all x1, starting transfers between devices: 3.74 us -> 7.01 us  [shards(): partial = lax.all_to_all(partial, 'ctx', 0, 0, tiled=True)]
    all_to_all x1, starting transfers between devices: 8.23 us -> 5.69 us  [shards(): values = lax.all_to_all(values, 'ctx', 0, 0, tiled=True)]
  transfers between devices with their start and end apart: 18 -> 26, of which waited for: 10 -> 14; matrix products, arithmetic and copies ran while one was open for 0% -> 0% of each run, Pallas kernels for 9% -> 9%
where the time goes in v4:
time: 171 us; the launch traced here: 169 us
  starting transfers between devices  90 us (53%)
  waiting for transfers between devices  41.9 us (25%)
  Pallas kernels  17.9 us (10%)
  blocking collectives  13.5 us (8%)
  local copies, waits for them, and re-layouts  3.25 us (2%)
    ppermute x8, waiting for transfers between devices, from_ahead(): lax.ppermute(block, 'ctx', [(i + distance, i) for i in range(8 - distance)])  24.1 us
    ppermute x4, starting transfers between devices, from_behind(): lax.ppermute(block, 'ctx', [(i, i + distance) for i in range(8 - distance)])  19.9 us
    all_to_all x1, blocking collectives, shards(): mixed = lax.all_to_all(mixed, 'mp', 0, 0, tiled=True)  13.5 us
    ppermute x8, starting transfers between devices, from_ahead(): lax.ppermute(block, 'ctx', [(i + distance, i) for i in range(8 - distance)])  10.3 us
    all_to_all x1, waiting for transfers between devices, shards(): partial = lax.all_to_all(partial, 'ctx', 0, 0, tiled=True)  9.95 us
    all_to_all x1, starting transfers between devices, shards(): lax.all_to_all(partial.reshape(16, 64, HEAD_DIM), PLANE, 0, 0, tiled=True)  9.5 us
    all_to_all x1, starting transfers between devices, to_all(): lax.all_to_all(jnp.broadcast_to(block[None], (copies,) + block.shape), ax...  9.48 us
    pallas_call x1, Pallas kernels, shards(): call(attend, (wide, wide) + (block,) * REACH + (own,), 9, 6 * 10 ** 9, 4...  8.41 us
  transfers between devices with their start and end apart: 26, of which 14 were waited for; matrix products, arithmetic and copies ran while one was open for 0% of the time, Pallas kernels for 9%

profile of v4, /device:TPU:56, one launch (start us, length us, event | category | flops | bytes accessed | tf_op | source)
XLA Modules:
  0.0 168.8 jit_solution(2232420015652266144)
XLA Ops:
  0.6 1.5 broadcast_in_dim.4
  2.1 9.5 %all-to-all-start = ((bf16[16,64,128]{2,1,0:T(8,128)(2,1)}), bf16[16,64,128]{2,1,0:T(8,128)(2,1)S(1)}, u32[]{:S(2)}, u32[]{:S(2)}) async-start(bf16[16,64,128]{2,1,0:T(8,128)(2,1)} %broadcast_in_dim.4), calls=%async_computation | async-start | bytes 524288 | tf_op jit(solution)/shard_map/all_to_all | solution.py:47
  11.6 6.1 %collective-permute-start.2 = (bf16[192,128]{1,0:T(8,128)(2,1)S(1)}, bf16[192,128]{1,0:T(8,128)(2,1)S(1)}, u32[]{:S(2)}, u32[]{:S(2)}) collective-permute-start(bf16[192,128]{1,0:T(8,128)(2,1)S(1)} %copy-done.4), channel_id=1, source_target_pairs={{0,8},{4,12},{8,16},{12,20},{16,24},{20,28},{1,9},{5,13},{9,17},{1... | collective-permute-start | bytes 147464 | tf_op jit(solution)/shard_map/ppermute | solution.py:53
  17.7 8.2 %collective-permute-start.1 = (bf16[192,128]{1,0:T(8,128)(2,1)S(1)}, bf16[192,128]{1,0:T(8,128)(2,1)S(1)}, u32[]{:S(2)}, u32[]{:S(2)}) collective-permute-start(bf16[192,128]{1,0:T(8,128)(2,1)S(1)} %copy-done.4), channel_id=1, source_target_pairs={{0,12},{4,16},{8,20},{12,24},{16,28},{1,13},{5,17},{9,21},{13,25},... | collective-permute-start | bytes 147464 | tf_op jit(solution)/shard_map/ppermute | solution.py:53
  25.9 3.1 %collective-permute-start = (bf16[192,128]{1,0:T(8,128)(2,1)S(1)}, bf16[192,128]{1,0:T(8,128)(2,1)S(1)}, u32[]{:S(2)}, u32[]{:S(2)}) collective-permute-start(bf16[192,128]{1,0:T(8,128)(2,1)S(1)} %copy-done.4), channel_id=1, source_target_pairs={{0,16},{4,20},{8,24},{12,28},{1,17},{5,21},{9,25},{13,29},{2,18},{... | collective-permute-start | bytes 147464 | tf_op jit(solution)/shard_map/ppermute | solution.py:53
  29.0 2.5 %collective-permute-start.3 = (bf16[192,128]{1,0:T(8,128)(2,1)S(1)}, bf16[192,128]{1,0:T(8,128)(2,1)S(1)}, u32[]{:S(2)}, u32[]{:S(2)}) collective-permute-start(bf16[192,128]{1,0:T(8,128)(2,1)S(1)} %copy-done.4), channel_id=1, source_target_pairs={{0,4},{4,8},{8,12},{12,16},{16,20},{20,24},{24,28},{1,5},{5,9},{9,... | collective-permute-start | bytes 147464 | tf_op jit(solution)/shard_map/ppermute | solution.py:53
  31.5 0.0 all-to-all-done
  31.5 0.0 copy-start
  31.5 0.0 collective-permute-done.2.refs_2_
  31.6 0.0 collective-permute-done.refs_0_
  31.6 0.0 copy-start.7
  31.6 1.6 collective-permute-done.3.refs_3_
  33.2 0.9 broadcast_in_dim.5
  34.2 5.4 %all-to-all-start.1 = ((bf16[8,4,64,128]{3,2,1,0:T(8,128)(2,1)}), bf16[8,4,64,128]{3,2,1,0:T(8,128)(2,1)S(1)}, u32[]{:S(2)}, u32[]{:S(2)}) async-start(bf16[8,4,64,128]{3,2,1,0:T(8,128)(2,1)} %broadcast_in_dim.5), calls=%async_computation.1 | async-start | bytes 1048576 | tf_op jit(solution)/shard_map/all_to_all | solution.py:228
  39.5 0.1 pieces.1
  39.6 1.9 %collective-permute-start.4 = (bf16[192,512]{1,0:T(8,128)(2,1)S(1)}, bf16[192,512]{1,0:T(8,128)(2,1)S(1)}, u32[]{:S(2)}, u32[]{:S(2)}) collective-permute-start(bf16[192,512]{1,0:T(8,128)(2,1)S(1)} %get-tuple-element.50), channel_id=1, source_target_pairs={{0,32},{32,0},{1,33},{33,1},{2,34},{34,2},{3,35},{35,3},{4,36},{36... | collective-permute-start | bytes 589832 | tf_op jit(solution)/shard_map/ppermute | solution.py:64
  41.5 2.5 %collective-permute-start.5 = (bf16[192,512]{1,0:T(8,128)(2,1)S(1)}, bf16[192,512]{1,0:T(8,128)(2,1)S(1)}, u32[]{:S(2)}, u32[]{:S(2)}) collective-permute-start(bf16[192,512]{1,0:T(8,128)(2,1)S(1)} %get-tuple-element.51), channel_id=1, source_target_pairs={{0,64},{64,0},{1,65},{65,1},{2,66},{66,2},{3,67},{67,3},{4,68},{68... | collective-permute-start | bytes 589832 | tf_op jit(solution)/shard_map/ppermute | solution.py:65
  44.0 3.2 %collective-permute-start.6 = (bf16[192,512]{1,0:T(8,128)(2,1)S(1)}, bf16[192,512]{1,0:T(8,128)(2,1)S(1)}, u32[]{:S(2)}, u32[]{:S(2)}) collective-permute-start(bf16[192,512]{1,0:T(8,128)(2,1)S(1)} %get-tuple-element.52), channel_id=1, source_target_pairs={{0,96},{32,64},{64,32},{96,0},{1,97},{33,65},{65,33},{97,1},{2,98}... | collective-permute-start | bytes 589832 | tf_op jit(solution)/shard_map/ppermute | solution.py:66
  47.2 5.6 %soft.1 = (bf16[192,128]{1,0:T(8,128)(2,1)}, bf16[192,128]{1,0:T(8,128)(2,1)}, bf16[192,128]{1,0:T(8,128)(2,1)}, bf16[192,128]{1,0:T(8,128)(2,1)}, f32[192,128]{1,0:T(8,128)}, /*index=5*/f32[8,384]{1,0:T(8,128)}) custom-call(s32[1,8]{1,0:T(1,128)} %len_ref.3, bf16[192,1024]{1,0:T(8,128)(2,1)} %q_ref.3, bf16[192,1024]{1,0:T(8,128)(2,1)} %do_ref.3, ...), custom_call_target="tpu_custom_call" | custom-call | flops 3000000000 | bytes 2000000 | tf_op jit(solution)/shard_map/soft/pallas_call | solution.py:236
  52.8 2.0 %all-to-all-done.1.refs_3_ = bf16[8,4,64,128]{3,2,1,0:T(8,128)(2,1)S(1)} async-done(((bf16[8,4,64,128]{3,2,1,0:T(8,128)(2,1)}), bf16[8,4,64,128]{3,2,1,0:T(8,128)(2,1)S(1)}, u32[]{:S(2)}, u32[]{:S(2)}) %all-to-all-start.1) | async-done | bytes 524320 | tf_op jit(solution)/shard_map/all_to_all | solution.py:228
  54.8 0.0 copy-start.1
  54.9 0.0 collective-permute-done.4.refs_0_
  54.9 0.0 collective-permute-done.6.refs_2_
  54.9 0.6 project.1
  55.5 2.0 %collective-permute-start.7 = (bf16[4,192,128]{2,1,0:T(8,128)(2,1)S(1)}, bf16[4,192,128]{2,1,0:T(8,128)(2,1)S(1)}, u32[]{:S(2)}, u32[]{:S(2)}) collective-permute-start(bf16[4,192,128]{2,1,0:T(8,128)(2,1)S(1)} %get-tuple-element.55), channel_id=1, source_target_pairs={{0,32},{32,0},{1,33},{33,1},{2,34},{34,2},{3,35},{35,3},{4,36},{36... | collective-permute-start | bytes 589832 | tf_op jit(solution)/shard_map/ppermute | solution.py:64
  57.5 2.5 %collective-permute-start.8 = (bf16[4,192,128]{2,1,0:T(8,128)(2,1)S(1)}, bf16[4,192,128]{2,1,0:T(8,128)(2,1)S(1)}, u32[]{:S(2)}, u32[]{:S(2)}) collective-permute-start(bf16[4,192,128]{2,1,0:T(8,128)(2,1)S(1)} %get-tuple-element.56), channel_id=1, source_target_pairs={{0,64},{64,0},{1,65},{65,1},{2,66},{66,2},{3,67},{67,3},{4,68},{68... | collective-permute-start | bytes 589832 | tf_op jit(solution)/shard_map/ppermute | solution.py:65
  60.0 3.1 %collective-permute-start.9 = (bf16[4,192,128]{2,1,0:T(8,128)(2,1)S(1)}, bf16[4,192,128]{2,1,0:T(8,128)(2,1)S(1)}, u32[]{:S(2)}, u32[]{:S(2)}) collective-permute-start(bf16[4,192,128]{2,1,0:T(8,128)(2,1)S(1)} %get-tuple-element.57), channel_id=1, source_target_pairs={{0,96},{32,64},{64,32},{96,0},{1,97},{33,65},{65,33},{97,1},{2,98}... | collective-permute-start | bytes 589832 | tf_op jit(solution)/shard_map/ppermute | solution.py:66
  63.1 1.3 collective-permute-start.10
  64.4 1.3 collective-permute-start.11
  65.7 3.4 %collective-permute-done.10.refs_5_ = bf16[192,128]{1,0:T(8,128)(2,1)S(1)} collective-permute-done((bf16[192,128]{1,0:T(8,128)(2,1)S(1)}, bf16[192,128]{1,0:T(8,128)(2,1)S(1)}, u32[]{:S(2)}, u32[]{:S(2)}) %collective-permute-start.10) | collective-permute-done | bytes 49184 | tf_op jit(solution)/shard_map/ppermute | solution.py:57
  69.1 1.3 collective-permute-start.12
  70.4 2.3 %collective-permute-done.11.refs_6_ = bf16[192,128]{1,0:T(8,128)(2,1)S(1)} collective-permute-done((bf16[192,128]{1,0:T(8,128)(2,1)S(1)}, bf16[192,128]{1,0:T(8,128)(2,1)S(1)}, u32[]{:S(2)}, u32[]{:S(2)}) %collective-permute-start.11) | collective-permute-done | bytes 49184 | tf_op jit(solution)/shard_map/ppermute | solution.py:57
  72.7 1.3 collective-permute-start.13
  74.0 4.3 %collective-permute-done.12.refs_7_ = bf16[192,128]{1,0:T(8,128)(2,1)S(1)} collective-permute-done((bf16[192,128]{1,0:T(8,128)(2,1)S(1)}, bf16[192,128]{1,0:T(8,128)(2,1)S(1)}, u32[]{:S(2)}, u32[]{:S(2)}) %collective-permute-start.12) | collective-permute-done | bytes 49184 | tf_op jit(solution)/shard_map/ppermute | solution.py:57
  78.3 4.3 %collective-permute-done.13.refs_8_ = bf16[192,128]{1,0:T(8,128)(2,1)S(1)} collective-permute-done((bf16[192,128]{1,0:T(8,128)(2,1)S(1)}, bf16[192,128]{1,0:T(8,128)(2,1)S(1)}, u32[]{:S(2)}, u32[]{:S(2)}) %collective-permute-start.13) | collective-permute-done | bytes 49184 | tf_op jit(solution)/shard_map/ppermute | solution.py:57
  82.6 0.0 collective-permute-done.7.refs_1_
  82.6 0.0 collective-permute-done.8.refs_2_
  82.6 0.1 mix.1
  82.7 13.5 %all_to_all.30.parts_ref = bf16[4,2,192,128]{3,2,1,0:T(8,128)(2,1)S(1)} all-to-all(bf16[4,2,192,128]{3,2,1,0:T(8,128)(2,1)S(1)} %mix.1), channel_id=1, replica_groups=mesh['yh'=2,'x1'=2,'x0'=2,'core'=2,'ctx'=8,'mp'=4] {'mp'}, dimensions={0} | all-to-all | bytes 786432 | tf_op jit(solution)/shard_map/all_to_all | solution.py:250
  96.2 0.8 spread_sum.1
  97.0 5.7 %all-to-all-start.3 = ((bf16[8,192,128]{2,1,0:T(8,128)(2,1)}), bf16[8,192,128]{2,1,0:T(8,128)(2,1)S(1)}, u32[]{:S(2)}, u32[]{:S(2)}) async-start(bf16[8,192,128]{2,1,0:T(8,128)(2,1)} %get-tuple-element.64), calls=%async_computation.3 | async-start | bytes 786432 | tf_op jit(solution)/shard_map/all_to_all | solution.py:252
  102.7 1.9 %collective-permute-start.16 = (bf16[4,192,128]{2,1,0:T(8,128)(2,1)S(1)}, bf16[4,192,128]{2,1,0:T(8,128)(2,1)S(1)}, u32[]{:S(2)}, u32[]{:S(2)}) collective-permute-start(bf16[4,192,128]{2,1,0:T(8,128)(2,1)S(1)} %get-tuple-element.63.refs_3_), channel_id=1, source_target_pairs={{0,96},{32,64},{64,32},{96,0},{1,97},{33,65},{65,33},{97,1},{2,98}... | collective-permute-start | bytes 589832 | tf_op jit(solution)/shard_map/ppermute | solution.py:66
  104.6 2.5 %collective-permute-start.15 = (bf16[4,192,128]{2,1,0:T(8,128)(2,1)S(1)}, bf16[4,192,128]{2,1,0:T(8,128)(2,1)S(1)}, u32[]{:S(2)}, u32[]{:S(2)}) collective-permute-start(bf16[4,192,128]{2,1,0:T(8,128)(2,1)S(1)} %get-tuple-element.63.refs_3_), channel_id=1, source_target_pairs={{0,64},{64,0},{1,65},{65,1},{2,66},{66,2},{3,67},{67,3},{4,68},{68... | collective-permute-start | bytes 589832 | tf_op jit(solution)/shard_map/ppermute | solution.py:65
  107.1 3.2 %collective-permute-start.14 = (bf16[4,192,128]{2,1,0:T(8,128)(2,1)S(1)}, bf16[4,192,128]{2,1,0:T(8,128)(2,1)S(1)}, u32[]{:S(2)}, u32[]{:S(2)}) collective-permute-start(bf16[4,192,128]{2,1,0:T(8,128)(2,1)S(1)} %get-tuple-element.63.refs_3_), channel_id=1, source_target_pairs={{0,32},{32,0},{1,33},{33,1},{2,34},{34,2},{3,35},{35,3},{4,36},{36... | collective-permute-start | bytes 589832 | tf_op jit(solution)/shard_map/ppermute | solution.py:64
  110.3 1.5 collective-permute-done.16.refs_6_
  111.7 2.6 %collective-permute-done.15.refs_5_ = bf16[4,192,128]{2,1,0:T(8,128)(2,1)S(1)} collective-permute-done((bf16[4,192,128]{2,1,0:T(8,128)(2,1)S(1)}, bf16[4,192,128]{2,1,0:T(8,128)(2,1)S(1)}, u32[]{:S(2)}, u32[]{:S(2)}) %collective-permute-start.15) | collective-permute-done | bytes 196640 | tf_op jit(solution)/shard_map/ppermute | solution.py:65
  114.3 1.5 weight_grad.1
  115.8 0.2 all-to-all-done.3.v_ref
  116.0 0.8 copy-done.2
  116.8 7.0 %all-to-all-start.4 = ((bf16[8,4,64,128]{3,2,1,0:T(8,128)(2,1)}), bf16[8,4,64,128]{3,2,1,0:T(8,128)(2,1)S(1)}, u32[]{:S(2)}, u32[]{:S(2)}) async-start(bf16[8,4,64,128]{3,2,1,0:T(8,128)(2,1)} %weight_grad.1), calls=%async_computation.4 | async-start | bytes 1048576 | tf_op jit(solution)/shard_map/all_to_all | solution.py:257
  123.8 8.4 %attend.1 = (bf16[192,1024]{1,0:T(8,128)(2,1)}, bf16[192,1024]{1,0:T(8,128)(2,1)}, bf16[192,128]{1,0:T(8,128)(2,1)}, bf16[192,128]{1,0:T(8,128)(2,1)}, bf16[192,...) custom-call(s32[1,8]{1,0:T(1,128)} %len_ref.3, bf16[192,1024]{1,0:T(8,128)(2,1)} %q_ref.3, ...), custom_call_target="tpu_custom_call" | custom-call | flops 6000000000 | bytes 4000000 | tf_op jit(solution)/shard_map/attend/pallas_call | solution.py:260
  132.3 10.0 %all-to-all-done.4.parts_ref = bf16[8,4,64,128]{3,2,1,0:T(8,128)(2,1)S(1)} async-done(((bf16[8,4,64,128]{3,2,1,0:T(8,128)(2,1)}), bf16[8,4,64,128]{3,2,1,0:T(8,128)(2,1)S(1)}, u32[]{:S(2)}, u32[]{:S(2)}) %all-to-all-start.4) | async-done | bytes 524320 | tf_op jit(solution)/shard_map/all_to_all | solution.py:257
  142.2 0.8 tiled_sum.1
  143.0 9.5 %all-to-all-start.5 = ((bf16[16,64,128]{2,1,0:T(8,128)(2,1)}), bf16[16,64,128]{2,1,0:T(8,128)(2,1)S(1)}, u32[]{:S(2)}, u32[]{:S(2)}) async-start(bf16[16,64,128]{2,1,0:T(8,128)(2,1)} %bitcast), calls=%async_computation.5 | async-start | bytes 524288 | tf_op jit(solution)/shard_map/all_to_all | solution.py:269
  152.5 1.3 collective-permute-start.17
  153.8 1.3 collective-permute-start.18
  155.1 1.3 collective-permute-start.19
  156.4 1.3 collective-permute-start.20
  157.7 0.7 collective-permute-done.17
  158.5 2.2 %collective-permute-done.18 = bf16[192,128]{1,0:T(8,128)(2,1)S(1)} collective-permute-done((bf16[192,128]{1,0:T(8,128)(2,1)S(1)}, bf16[192,128]{1,0:T(8,128)(2,1)S(1)}, u32[]{:S(2)}, u32[]{:S(2)}) %collective-permute-start.18) | collective-permute-done | bytes 49184 | tf_op jit(solution)/shard_map/ppermute | solution.py:57
  160.7 6.0 %collective-permute-done.19 = bf16[192,128]{1,0:T(8,128)(2,1)S(1)} collective-permute-done((bf16[192,128]{1,0:T(8,128)(2,1)S(1)}, bf16[192,128]{1,0:T(8,128)(2,1)S(1)}, u32[]{:S(2)}, u32[]{:S(2)}) %collective-permute-start.19) | collective-permute-done | bytes 49184 | tf_op jit(solution)/shard_map/ppermute | solution.py:57
  166.8 0.7 collective-permute-done.20
  167.5 0.7 multiply_convert_fusion
  168.2 0.6 convert_reduce_fusion
  (36 shorter events, 0.1 us)
Async XLA Ops:
  2.1 9.5 %copy-start.4 = (bf16[192,128]{1,0:T(8,128)(2,1)S(1)}, bf16[192,128]{1,0:T(8,128)(2,1)}, u32[]{:S(2)}) copy-start(bf16[192,128]{1,0:T(8,128)(2,1)} %refs_4_.1) | copy-start | bytes 147460
  2.1 29.4 %all-to-all-start = ((bf16[16,64,128]{2,1,0:T(8,128)(2,1)}), bf16[16,64,128]{2,1,0:T(8,128)(2,1)S(1)}, u32[]{:S(2)}, u32[]{:S(2)}) async-start(bf16[16,64,128]{2,1,0:T(8,128)(2,1)} %broadcast_in_dim.4), calls=%async_computation | async-start | bytes 524288 | tf_op jit(solution)/shard_map/all_to_all | solution.py:47
  11.6 20.0 %collective-permute-start.2 = (bf16[192,128]{1,0:T(8,128)(2,1)S(1)}, bf16[192,128]{1,0:T(8,128)(2,1)S(1)}, u32[]{:S(2)}, u32[]{:S(2)}) collective-permute-start(bf16[192,128]{1,0:T(8,128)(2,1)S(1)} %copy-done.4), channel_id=1, source_target_pairs={{0,8},{4,12},{8,16},{12,20},{16,24},{20,28},{1,9},{5,13},{9,17},{1... | collective-permute-start | bytes 147464 | tf_op jit(solution)/shard_map/ppermute | solution.py:53
  17.7 13.9 %collective-permute-start.1 = (bf16[192,128]{1,0:T(8,128)(2,1)S(1)}, bf16[192,128]{1,0:T(8,128)(2,1)S(1)}, u32[]{:S(2)}, u32[]{:S(2)}) collective-permute-start(bf16[192,128]{1,0:T(8,128)(2,1)S(1)} %copy-done.4), channel_id=1, source_target_pairs={{0,12},{4,16},{8,20},{12,24},{16,28},{1,13},{5,17},{9,21},{13,25},... | collective-permute-start | bytes 147464 | tf_op jit(solution)/shard_map/ppermute | solution.py:53
  25.9 5.7 %collective-permute-start = (bf16[192,128]{1,0:T(8,128)(2,1)S(1)}, bf16[192,128]{1,0:T(8,128)(2,1)S(1)}, u32[]{:S(2)}, u32[]{:S(2)}) collective-permute-start(bf16[192,128]{1,0:T(8,128)(2,1)S(1)} %copy-done.4), channel_id=1, source_target_pairs={{0,16},{4,20},{8,24},{12,28},{1,17},{5,21},{9,25},{13,29},{2,18},{... | collective-permute-start | bytes 147464 | tf_op jit(solution)/shard_map/ppermute | solution.py:53
  29.0 4.2 %collective-permute-start.3 = (bf16[192,128]{1,0:T(8,128)(2,1)S(1)}, bf16[192,128]{1,0:T(8,128)(2,1)S(1)}, u32[]{:S(2)}, u32[]{:S(2)}) collective-permute-start(bf16[192,128]{1,0:T(8,128)(2,1)S(1)} %copy-done.4), channel_id=1, source_target_pairs={{0,4},{4,8},{8,12},{12,16},{16,20},{20,24},{24,28},{1,5},{5,9},{9,... | collective-permute-start | bytes 147464 | tf_op jit(solution)/shard_map/ppermute | solution.py:53
  31.5 8.0 %copy-start = (bf16[192,2048]{1,0:T(8,128)(2,1)S(1)}, bf16[192,2048]{1,0:T(8,128)(2,1)}, u32[]{:S(2)}) copy-start(bf16[192,2048]{1,0:T(8,128)(2,1)} %x_ref.5) | copy-start | bytes 2359300
  31.6 2.6 %copy-start.5 = (bf16[192,128]{1,0:T(8,128)(2,1)}, bf16[192,128]{1,0:T(8,128)(2,1)S(1)}, u32[]{:S(2)}) copy-start(bf16[192,128]{1,0:T(8,128)(2,1)S(1)} %collective-permute-done.2.refs_2_) | copy-start | bytes 147460
  31.6 2.6 %copy-start.6 = (bf16[192,128]{1,0:T(8,128)(2,1)}, bf16[192,128]{1,0:T(8,128)(2,1)S(1)}, u32[]{:S(2)}) copy-start(bf16[192,128]{1,0:T(8,128)(2,1)S(1)} %collective-permute-done.1.refs_1_) | copy-start | bytes 147460
  31.6 2.6 %copy-start.7 = (bf16[192,128]{1,0:T(8,128)(2,1)}, bf16[192,128]{1,0:T(8,128)(2,1)S(1)}, u32[]{:S(2)}) copy-start(bf16[192,128]{1,0:T(8,128)(2,1)S(1)} %collective-permute-done.refs_0_) | copy-start | bytes 147460
  33.2 0.9 copy-start.8
  34.2 20.7 %all-to-all-start.1 = ((bf16[8,4,64,128]{3,2,1,0:T(8,128)(2,1)}), bf16[8,4,64,128]{3,2,1,0:T(8,128)(2,1)S(1)}, u32[]{:S(2)}, u32[]{:S(2)}) async-start(bf16[8,4,64,128]{3,2,1,0:T(8,128)(2,1)} %broadcast_in_dim.5), calls=%async_computation.1 | async-start | bytes 1048576 | tf_op jit(solution)/shard_map/all_to_all | solution.py:228
  39.6 15.3 %collective-permute-start.4 = (bf16[192,512]{1,0:T(8,128)(2,1)S(1)}, bf16[192,512]{1,0:T(8,128)(2,1)S(1)}, u32[]{:S(2)}, u32[]{:S(2)}) collective-permute-start(bf16[192,512]{1,0:T(8,128)(2,1)S(1)} %get-tuple-element.50), channel_id=1, source_target_pairs={{0,32},{32,0},{1,33},{33,1},{2,34},{34,2},{3,35},{35,3},{4,36},{36... | collective-permute-start | bytes 589832 | tf_op jit(solution)/shard_map/ppermute | solution.py:64
  41.5 13.3 %collective-permute-start.5 = (bf16[192,512]{1,0:T(8,128)(2,1)S(1)}, bf16[192,512]{1,0:T(8,128)(2,1)S(1)}, u32[]{:S(2)}, u32[]{:S(2)}) collective-permute-start(bf16[192,512]{1,0:T(8,128)(2,1)S(1)} %get-tuple-element.51), channel_id=1, source_target_pairs={{0,64},{64,0},{1,65},{65,1},{2,66},{66,2},{3,67},{67,3},{4,68},{68... | collective-permute-start | bytes 589832 | tf_op jit(solution)/shard_map/ppermute | solution.py:65
  44.0 10.8 %collective-permute-start.6 = (bf16[192,512]{1,0:T(8,128)(2,1)S(1)}, bf16[192,512]{1,0:T(8,128)(2,1)S(1)}, u32[]{:S(2)}, u32[]{:S(2)}) collective-permute-start(bf16[192,512]{1,0:T(8,128)(2,1)S(1)} %get-tuple-element.52), channel_id=1, source_target_pairs={{0,96},{32,64},{64,32},{96,0},{1,97},{33,65},{65,33},{97,1},{2,98}... | collective-permute-start | bytes 589832 | tf_op jit(solution)/shard_map/ppermute | solution.py:66
  54.8 8.3 %copy-start.16 = (bf16[192,128]{1,0:T(8,128)(2,1)S(1)}, bf16[192,128]{1,0:T(8,128)(2,1)}, u32[]{:S(2)}) copy-start(bf16[192,128]{1,0:T(8,128)(2,1)} %get-tuple-element.59) | copy-start | bytes 147460
  54.8 9.6 %copy-start.15 = (bf16[192,128]{1,0:T(8,128)(2,1)S(1)}, bf16[192,128]{1,0:T(8,128)(2,1)}, u32[]{:S(2)}) copy-start(bf16[192,128]{1,0:T(8,128)(2,1)} %get-tuple-element.60) | copy-start | bytes 147460
  54.8 14.2 %copy-start.14 = (bf16[192,128]{1,0:T(8,128)(2,1)S(1)}, bf16[192,128]{1,0:T(8,128)(2,1)}, u32[]{:S(2)}) copy-start(bf16[192,128]{1,0:T(8,128)(2,1)} %get-tuple-element.61) | copy-start | bytes 147460
  54.8 17.9 %copy-start.13 = (bf16[192,128]{1,0:T(8,128)(2,1)S(1)}, bf16[192,128]{1,0:T(8,128)(2,1)}, u32[]{:S(2)}) copy-start(bf16[192,128]{1,0:T(8,128)(2,1)} %get-tuple-element.62) | copy-start | bytes 147460
  54.8 27.8 %copy-start.1 = (f32[192,128]{1,0:T(8,128)S(1)}, f32[192,128]{1,0:T(8,128)}, u32[]{:S(2)}) copy-start(f32[192,128]{1,0:T(8,128)} %get-tuple-element.58.refs_4_) | copy-start | bytes 294916
  55.5 27.1 %collective-permute-start.7 = (bf16[4,192,128]{2,1,0:T(8,128)(2,1)S(1)}, bf16[4,192,128]{2,1,0:T(8,128)(2,1)S(1)}, u32[]{:S(2)}, u32[]{:S(2)}) collective-permute-start(bf16[4,192,128]{2,1,0:T(8,128)(2,1)S(1)} %get-tuple-element.55), channel_id=1, source_target_pairs={{0,32},{32,0},{1,33},{33,1},{2,34},{34,2},{3,35},{35,3},{4,36},{36... | collective-permute-start | bytes 589832 | tf_op jit(solution)/shard_map/ppermute | solution.py:64
  57.5 25.1 %collective-permute-start.8 = (bf16[4,192,128]{2,1,0:T(8,128)(2,1)S(1)}, bf16[4,192,128]{2,1,0:T(8,128)(2,1)S(1)}, u32[]{:S(2)}, u32[]{:S(2)}) collective-permute-start(bf16[4,192,128]{2,1,0:T(8,128)(2,1)S(1)} %get-tuple-element.56), channel_id=1, source_target_pairs={{0,64},{64,0},{1,65},{65,1},{2,66},{66,2},{3,67},{67,3},{4,68},{68... | collective-permute-start | bytes 589832 | tf_op jit(solution)/shard_map/ppermute | solution.py:65
  60.0 22.6 %collective-permute-start.9 = (bf16[4,192,128]{2,1,0:T(8,128)(2,1)S(1)}, bf16[4,192,128]{2,1,0:T(8,128)(2,1)S(1)}, u32[]{:S(2)}, u32[]{:S(2)}) collective-permute-start(bf16[4,192,128]{2,1,0:T(8,128)(2,1)S(1)} %get-tuple-element.57), channel_id=1, source_target_pairs={{0,96},{32,64},{64,32},{96,0},{1,97},{33,65},{65,33},{97,1},{2,98}... | collective-permute-start | bytes 589832 | tf_op jit(solution)/shard_map/ppermute | solution.py:66
  63.1 6.0 %collective-permute-start.10 = (bf16[192,128]{1,0:T(8,128)(2,1)S(1)}, bf16[192,128]{1,0:T(8,128)(2,1)S(1)}, u32[]{:S(2)}, u32[]{:S(2)}) collective-permute-start(bf16[192,128]{1,0:T(8,128)(2,1)S(1)} %copy-done.16), channel_id=1, source_target_pairs={{4,0},{8,4},{12,8},{16,12},{20,16},{24,20},{28,24},{5,1},{9,5},{13... | collective-permute-start | bytes 147464 | tf_op jit(solution)/shard_map/ppermute | solution.py:57
  64.4 8.3 %collective-permute-start.11 = (bf16[192,128]{1,0:T(8,128)(2,1)S(1)}, bf16[192,128]{1,0:T(8,128)(2,1)S(1)}, u32[]{:S(2)}, u32[]{:S(2)}) collective-permute-start(bf16[192,128]{1,0:T(8,128)(2,1)S(1)} %copy-done.15), channel_id=1, source_target_pairs={{8,0},{12,4},{16,8},{20,12},{24,16},{28,20},{9,1},{13,5},{17,9},{2... | collective-permute-start | bytes 147464 | tf_op jit(solution)/shard_map/ppermute | solution.py:57
  69.1 9.2 %collective-permute-start.12 = (bf16[192,128]{1,0:T(8,128)(2,1)S(1)}, bf16[192,128]{1,0:T(8,128)(2,1)S(1)}, u32[]{:S(2)}, u32[]{:S(2)}) collective-permute-start(bf16[192,128]{1,0:T(8,128)(2,1)S(1)} %copy-done.14), channel_id=1, source_target_pairs={{12,0},{16,4},{20,8},{24,12},{28,16},{13,1},{17,5},{21,9},{25,13},... | collective-permute-start | bytes 147464 | tf_op jit(solution)/shard_map/ppermute | solution.py:57
  72.7 9.9 %collective-permute-start.13 = (bf16[192,128]{1,0:T(8,128)(2,1)S(1)}, bf16[192,128]{1,0:T(8,128)(2,1)S(1)}, u32[]{:S(2)}, u32[]{:S(2)}) collective-permute-start(bf16[192,128]{1,0:T(8,128)(2,1)S(1)} %copy-done.13), channel_id=1, source_target_pairs={{16,0},{20,4},{24,8},{28,12},{17,1},{21,5},{25,9},{29,13},{18,2},{... | collective-permute-start | bytes 147464 | tf_op jit(solution)/shard_map/ppermute | solution.py:57
  97.0 19.1 %all-to-all-start.3 = ((bf16[8,192,128]{2,1,0:T(8,128)(2,1)}), bf16[8,192,128]{2,1,0:T(8,128)(2,1)S(1)}, u32[]{:S(2)}, u32[]{:S(2)}) async-start(bf16[8,192,128]{2,1,0:T(8,128)(2,1)} %get-tuple-element.64), calls=%async_computation.3 | async-start | bytes 786432 | tf_op jit(solution)/shard_map/all_to_all | solution.py:252
  102.7 9.1 %collective-permute-start.16 = (bf16[4,192,128]{2,1,0:T(8,128)(2,1)S(1)}, bf16[4,192,128]{2,1,0:T(8,128)(2,1)S(1)}, u32[]{:S(2)}, u32[]{:S(2)}) collective-permute-start(bf16[4,192,128]{2,1,0:T(8,128)(2,1)S(1)} %get-tuple-element.63.refs_3_), channel_id=1, source_target_pairs={{0,96},{32,64},{64,32},{96,0},{1,97},{33,65},{65,33},{97,1},{2,98}... | collective-permute-start | bytes 589832 | tf_op jit(solution)/shard_map/ppermute | solution.py:66
  104.6 9.7 %collective-permute-start.15 = (bf16[4,192,128]{2,1,0:T(8,128)(2,1)S(1)}, bf16[4,192,128]{2,1,0:T(8,128)(2,1)S(1)}, u32[]{:S(2)}, u32[]{:S(2)}) collective-permute-start(bf16[4,192,128]{2,1,0:T(8,128)(2,1)S(1)} %get-tuple-element.63.refs_3_), channel_id=1, source_target_pairs={{0,64},{64,0},{1,65},{65,1},{2,66},{66,2},{3,67},{67,3},{4,68},{68... | collective-permute-start | bytes 589832 | tf_op jit(solution)/shard_map/ppermute | solution.py:65
  107.1 7.2 %collective-permute-start.14 = (bf16[4,192,128]{2,1,0:T(8,128)(2,1)S(1)}, bf16[4,192,128]{2,1,0:T(8,128)(2,1)S(1)}, u32[]{:S(2)}, u32[]{:S(2)}) collective-permute-start(bf16[4,192,128]{2,1,0:T(8,128)(2,1)S(1)} %get-tuple-element.63.refs_3_), channel_id=1, source_target_pairs={{0,32},{32,0},{1,33},{33,1},{2,34},{34,2},{3,35},{35,3},{4,36},{36... | collective-permute-start | bytes 589832 | tf_op jit(solution)/shard_map/ppermute | solution.py:64
  116.0 0.8 copy-start.2
  116.8 25.4 %all-to-all-start.4 = ((bf16[8,4,64,128]{3,2,1,0:T(8,128)(2,1)}), bf16[8,4,64,128]{3,2,1,0:T(8,128)(2,1)S(1)}, u32[]{:S(2)}, u32[]{:S(2)}) async-start(bf16[8,4,64,128]{3,2,1,0:T(8,128)(2,1)} %weight_grad.1), calls=%async_computation.4 | async-start | bytes 1048576 | tf_op jit(solution)/shard_map/all_to_all | solution.py:257
  143.0 9.5 %copy-start.12 = (bf16[192,128]{1,0:T(8,128)(2,1)S(1)}, bf16[192,128]{1,0:T(8,128)(2,1)}, u32[]{:S(2)}) copy-start(bf16[192,128]{1,0:T(8,128)(2,1)} %get-tuple-element.75) | copy-start | bytes 147460
  143.0 10.8 %copy-start.11 = (bf16[192,128]{1,0:T(8,128)(2,1)S(1)}, bf16[192,128]{1,0:T(8,128)(2,1)}, u32[]{:S(2)}) copy-start(bf16[192,128]{1,0:T(8,128)(2,1)} %get-tuple-element.76) | copy-start | bytes 147460
  143.0 12.1 %copy-start.10 = (bf16[192,128]{1,0:T(8,128)(2,1)S(1)}, bf16[192,128]{1,0:T(8,128)(2,1)}, u32[]{:S(2)}) copy-start(bf16[192,128]{1,0:T(8,128)(2,1)} %get-tuple-element.77) | copy-start | bytes 147460
  143.0 13.4 %copy-start.9 = (bf16[192,128]{1,0:T(8,128)(2,1)S(1)}, bf16[192,128]{1,0:T(8,128)(2,1)}, u32[]{:S(2)}) copy-start(bf16[192,128]{1,0:T(8,128)(2,1)} %get-tuple-element.78) | copy-start | bytes 147460
  143.0 24.5 %copy-start.3 = (f32[192,128]{1,0:T(8,128)S(1)}, f32[192,128]{1,0:T(8,128)}, u32[]{:S(2)}) copy-start(f32[192,128]{1,0:T(8,128)} %get-tuple-element.74) | copy-start | bytes 294916
  143.0 25.2 %all-to-all-start.5 = ((bf16[16,64,128]{2,1,0:T(8,128)(2,1)}), bf16[16,64,128]{2,1,0:T(8,128)(2,1)S(1)}, u32[]{:S(2)}, u32[]{:S(2)}) async-start(bf16[16,64,128]{2,1,0:T(8,128)(2,1)} %bitcast), calls=%async_computation.5 | async-start | bytes 524288 | tf_op jit(solution)/shard_map/all_to_all | solution.py:269
  152.5 6.0 %collective-permute-start.17 = (bf16[192,128]{1,0:T(8,128)(2,1)S(1)}, bf16[192,128]{1,0:T(8,128)(2,1)S(1)}, u32[]{:S(2)}, u32[]{:S(2)}) collective-permute-start(bf16[192,128]{1,0:T(8,128)(2,1)S(1)} %copy-done.12), channel_id=1, source_target_pairs={{4,0},{8,4},{12,8},{16,12},{20,16},{24,20},{28,24},{5,1},{9,5},{13... | collective-permute-start | bytes 147464 | tf_op jit(solution)/shard_map/ppermute | solution.py:57
  153.8 6.9 %collective-permute-start.18 = (bf16[192,128]{1,0:T(8,128)(2,1)S(1)}, bf16[192,128]{1,0:T(8,128)(2,1)S(1)}, u32[]{:S(2)}, u32[]{:S(2)}) collective-permute-start(bf16[192,128]{1,0:T(8,128)(2,1)S(1)} %copy-done.11), channel_id=1, source_target_pairs={{8,0},{12,4},{16,8},{20,12},{24,16},{28,20},{9,1},{13,5},{17,9},{2... | collective-permute-start | bytes 147464 | tf_op jit(solution)/shard_map/ppermute | solution.py:57
  155.1 11.6 %collective-permute-start.19 = (bf16[192,128]{1,0:T(8,128)(2,1)S(1)}, bf16[192,128]{1,0:T(8,128)(2,1)S(1)}, u32[]{:S(2)}, u32[]{:S(2)}) collective-permute-start(bf16[192,128]{1,0:T(8,128)(2,1)S(1)} %copy-done.10), channel_id=1, source_target_pairs={{12,0},{16,4},{20,8},{24,12},{28,16},{13,1},{17,5},{21,9},{25,13},... | collective-permute-start | bytes 147464 | tf_op jit(solution)/shard_map/ppermute | solution.py:57
  156.4 11.1 %collective-permute-start.20 = (bf16[192,128]{1,0:T(8,128)(2,1)S(1)}, bf16[192,128]{1,0:T(8,128)(2,1)S(1)}, u32[]{:S(2)}, u32[]{:S(2)}) collective-permute-start(bf16[192,128]{1,0:T(8,128)(2,1)S(1)} %copy-done.9), channel_id=1, source_target_pairs={{16,0},{20,4},{24,8},{28,12},{17,1},{21,5},{25,9},{29,13},{18,2},{... | collective-permute-start | bytes 147464 | tf_op jit(solution)/shard_map/ppermute | solution.py:57

commit v5 on v4

v5 whole, which is shorter than its diff:
```python
import jax
import jax.numpy as jnp
from jax import lax
from jax.experimental import pallas as pl
from jax.experimental.pallas import tpu as pltpu
from jax.sharding import Mesh, PartitionSpec as P

HEAD_DIM = 128
TOK = 192
GROUP = 8
REACH = 4
WINDOW = (REACH + 1) * TOK
HEADS_AT_ONCE = 2
LANES = HEADS_AT_ONCE * TOK
CHUNKS = GROUP // HEADS_AT_ONCE
PLANE = ("yh", "x1", "ctx")
SCALE = HEAD_DIM ** -0.5
F32 = jnp.float32
BF16 = jnp.bfloat16
NT = (((1,), (1,)), ((), ()))
TN = (((0,), (0,)), ((), ()))
VMEM = pl.BlockSpec(memory_space=pltpu.VMEM)
SMEM = pl.BlockSpec(memory_space=pltpu.SMEM)


def shape(dims, dtype=BF16):
    return jax.ShapeDtypeStruct(dims, dtype)


def call(kernel, out_shape, n_in, flops, n_bytes, scratch=(), smem=0, vmem=48):
    outs = out_shape if isinstance(out_shape, tuple) else None
    return pl.pallas_call(
        kernel,
        out_shape=out_shape,
        in_specs=[SMEM] * smem + [VMEM] * n_in,
        out_specs=(VMEM,) * len(outs) if outs else VMEM,
        scratch_shapes=scratch,
        compiler_params=pltpu.CompilerParams(vmem_limit_bytes=vmem * 2**20),
        cost_estimate=pl.CostEstimate(
            flops=flops, bytes_accessed=n_bytes, transcendentals=0
        ),
        name=kernel.__name__,
    )


def to_all(block, axes, copies):
    return lax.all_to_all(
        jnp.broadcast_to(block[None], (copies,) + block.shape), axes, 0, 0, tiled=True
    )


def from_behind(block, distance):
    return lax.ppermute(block, "ctx", [(i, i + distance) for i in range(8 - distance)])


def swapped_with_mp(block):
    route = [(q * 4 + mp, mp * 4 + q) for q in range(4) for mp in range(4)]
    return lax.ppermute(block, ("yh", "x1", "mp"), route)


def summed_over_ctx(parts):
    return lax.psum_scatter(
        parts.reshape(8 * TOK, HEAD_DIM), "ctx", scatter_dimension=0, tiled=True
    )


def traded(blocks):
    both = [(0, 3), (1, 2), (2, 1), (3, 0)]
    pair = [(0, 1), (1, 0)]
    return [
        lax.ppermute(blocks[0], "core", pair),
        lax.ppermute(blocks[1], "x0", pair),
        lax.ppermute(blocks[2], ("x0", "core"), both),
    ]


def piece(x_ref, step):
    x0, core = lax.axis_index("x0"), lax.axis_index("core")
    x0 = 1 - x0 if step >= 2 else x0
    core = 1 - core if step % 2 else core
    return x_ref[:, pl.ds(pl.multiple_of((2 * x0 + core) * 512, 512), 512)]


def pieces(x_ref, *out_refs):
    for step, ref in enumerate(out_refs):
        ref[...] = piece(x_ref, step + 1)


def project(x_ref, *refs):
    others, w_ref, outs = refs[:3], refs[3], refs[4:]
    weight = jnp.concatenate(
        [jnp.concatenate([w_ref[c, ctx] for c in range(4)], axis=1) for ctx in range(8)], axis=0
    )
    rows = [piece(x_ref, 0)] + [ref[...] for ref in others]
    for x, out_ref in zip(rows, outs):
        result = jnp.dot(x, weight, preferred_element_type=F32)
        for c in range(4):
            out_ref[c] = result[:, c * HEAD_DIM : (c + 1) * HEAD_DIM].astype(out_ref.dtype)


def mix(*refs):
    parts, out_ref = refs[:4], refs[4]
    for c in range(4):
        value = parts[0][c]
        for ref in parts[1:]:
            value = value + ref[c].astype(F32)
        out_ref[c] = value.astype(BF16)


def sum_of(parts_ref):
    total = parts_ref[0].astype(F32)
    for i in range(1, parts_ref.shape[0]):
        total = total + parts_ref[i].astype(F32)
    return total


def spread_sum(parts_ref, out_ref):
    total = sum_of(parts_ref).astype(BF16)
    for i in range(8):
        out_ref[i] = total


def sum_blocks(parts_ref, out_ref):
    out_ref[...] = sum_of(parts_ref)


def weight_grad(x_ref, *refs):
    others, dv_refs, out_ref = refs[:3], refs[3:7], refs[7]
    rows = [piece(x_ref, 0)] + [ref[...] for ref in others]
    result = jnp.zeros((512, 512), F32)
    for x, dv_ref in zip(rows, dv_refs):
        dv = jnp.concatenate([dv_ref[c] for c in range(4)], axis=1)
        result += lax.dot_general(x, dv, TN, preferred_element_type=F32)
    result = result.astype(BF16)
    for ctx in range(8):
        for c in range(4):
            out_ref[c, ctx] = result[ctx * 64 : (ctx + 1) * 64, c * HEAD_DIM : (c + 1) * HEAD_DIM]


def rows_of_heads(wide_ref, rows_ref):
    for h in range(GROUP):
        rows_ref[h * TOK : (h + 1) * TOK] = wide_ref[:, h * HEAD_DIM : (h + 1) * HEAD_DIM]


def slot_owner(slot):
    return lax.rem(lax.axis_index("ctx") - (REACH - slot) + 8, 8)


def place_slots(total, out_ref):
    out_ref[...] = jnp.zeros_like(out_ref)
    for slot in range(REACH + 1):
        out_ref[slot_owner(slot)] = total[slot * TOK : (slot + 1) * TOK]


def fill_bias(len_ref, bias):
    ctx = lax.axis_index("ctx")
    lane = lax.broadcasted_iota(jnp.int32, (1, LANES), 1)
    query = ctx * TOK + lax.rem(lane, TOK)
    first = jnp.zeros_like(query)
    end = jnp.int32(0)
    for d in range(8):
        end = end + len_ref[0, d]
        first = jnp.where(query >= end, end, first)
    offset = lax.broadcasted_iota(jnp.int32, (TOK, LANES), 0)
    for slot in range(REACH + 1):
        key = slot_owner(slot) * TOK + offset
        bias[slot * TOK : (slot + 1) * TOK] = jnp.where(
            (key >= first) & (key <= query), F32(0.0), F32(-1e30)
        )


def soft(len_ref, q_ref, do_ref, *refs):
    k_refs, dv_ref, stat_ref = refs[:5], refs[5], refs[6]
    q_rows, do_rows, bias, probs, keys = refs[7:]
    rows_of_heads(q_ref, q_rows)
    rows_of_heads(do_ref, do_rows)
    for slot, ref in enumerate(k_refs):
        keys[slot * TOK : (slot + 1) * TOK] = ref[...]
    fill_bias(len_ref, bias)
    for i in range(CHUNKS):
        cols = slice(i * LANES, (i + 1) * LANES)
        scores = lax.dot_general(keys[...], q_rows[cols], NT, preferred_element_type=F32)
        scores = scores * F32(SCALE) + bias[...]
        top = jnp.max(scores, axis=0, keepdims=True)
        weights = jnp.exp(scores - top)
        inverse = 1.0 / jnp.sum(weights, axis=0, keepdims=True)
        probs[:, cols] = (weights * inverse).astype(BF16)
        stat_ref[i : i + 1] = top
        stat_ref[CHUNKS + i : CHUNKS + i + 1] = inverse
    place_slots(jnp.dot(probs[...], do_rows[...], preferred_element_type=F32), dv_ref)


def attend(len_ref, q_ref, do_ref, stat_ref, v_ref, *refs):
    k_refs, (att_ref, dq_ref, dk_ref) = refs[:5], refs[5:8]
    q_rows, do_rows, bias, dscores, keys, values = refs[8:]
    rows_of_heads(q_ref, q_rows)
    rows_of_heads(do_ref, do_rows)
    for slot, ref in enumerate(k_refs):
        keys[slot * TOK : (slot + 1) * TOK] = ref[...]
        values[slot * TOK : (slot + 1) * TOK] = v_ref[slot_owner(slot)]
    fill_bias(len_ref, bias)
    for i in range(CHUNKS):
        cols = slice(i * LANES, (i + 1) * LANES)
        scores = lax.dot_general(keys[...], q_rows[cols], NT, preferred_element_type=F32)
        scores = scores * F32(SCALE) + bias[...]
        p = jnp.exp(scores - stat_ref[i : i + 1]) * stat_ref[CHUNKS + i : CHUNKS + i + 1]
        att = lax.dot_general(values[...], p.astype(BF16), TN, preferred_element_type=F32)
        dp = lax.dot_general(values[...], do_rows[cols], NT, preferred_element_type=F32)
        dots = jnp.sum(p * dp, axis=0, keepdims=True)
        ds = (p * (dp - dots)).astype(BF16)
        dscores[:, cols] = ds
        dq = lax.dot_general(keys[...], ds, TN, preferred_element_type=F32) * F32(SCALE)
        att = att.T.astype(BF16)
        dq = dq.T.astype(BF16)
        for j in range(HEADS_AT_ONCE):
            head = slice((i * HEADS_AT_ONCE + j) * HEAD_DIM, (i * HEADS_AT_ONCE + j + 1) * HEAD_DIM)
            att_ref[:, head] = att[j * TOK : (j + 1) * TOK]
            dq_ref[:, head] = dq[j * TOK : (j + 1) * TOK]
    place_slots(jnp.dot(dscores[...], q_rows[...], preferred_element_type=F32), dk_ref)


def shards(queries, key_states, normed, value_weight, grad_out, lengths):
    turned = swapped_with_mp(value_weight)
    keys = [from_behind(key_states, d) for d in range(REACH, 0, -1)] + [key_states]
    weight = to_all(turned, PLANE, 32).reshape(4, 8, 64, HEAD_DIM)
    quarter = shape((TOK, 512))
    others = traded(call(pieces, (quarter,) * 3, 1, 0, 10**6)(normed))
    others, lengths = lax.optimization_barrier((others, lengths))

    heads = GROUP * TOK
    rows = pltpu.VMEM((heads, HEAD_DIM), BF16)
    window = pltpu.VMEM((WINDOW, HEAD_DIM), BF16)
    bias = pltpu.VMEM((WINDOW, LANES), F32)
    pairs = pltpu.VMEM((WINDOW, heads), BF16)
    slots = shape((8, TOK, HEAD_DIM), F32)
    dv, stats = call(
        soft, (slots, shape((8, LANES), F32)), 7, 3 * 10**9, 2 * 10**6,
        (rows, rows, bias, pairs, window), smem=1, vmem=56,
    )(lengths, queries, grad_out, *keys)
    weight, stats = lax.optimization_barrier((weight, stats))
    dv = summed_over_ctx(dv)

    four = shape((4, TOK, HEAD_DIM))
    projected, *away = call(
        project, (shape((4, TOK, HEAD_DIM), F32),) + (four,) * 3, 5, 4 * 10**8, 3 * 10**6
    )(normed, *others, weight)
    mixed = call(mix, four, 4, 10**6, 2 * 10**6)(projected, *traded(away))
    mixed = lax.all_to_all(mixed, "mp", 0, 0, tiled=True)
    values = call(spread_sum, shape((8, TOK, HEAD_DIM)), 1, 10**6, 10**6)(mixed)
    values = lax.all_to_all(values, "ctx", 0, 0, tiled=True)

    dv, values = lax.optimization_barrier((dv, values))
    grad_value = to_all(dv.astype(BF16), "mp", 4)
    wide = shape((TOK, GROUP * HEAD_DIM))
    attended, grad_query, dk = call(
        attend, (wide, wide, slots), 9, 6 * 10**9, 4 * 10**6,
        (rows, rows, bias, pairs, window, window), smem=1, vmem=56,
    )(lengths, queries, grad_out, stats, values, *keys)
    grad_key = (summed_over_ctx(dk) * F32(SCALE)).astype(BF16)

    partial = call(weight_grad, shape((4, 8, 64, HEAD_DIM)), 8, 4 * 10**8, 3 * 10**6)(
        normed, *others, grad_value, *traded([grad_value] * 3)
    )
    partial = lax.all_to_all(partial.reshape(32, 64, HEAD_DIM), PLANE, 0, 0, tiled=True)
    total = call(sum_blocks, shape((64, HEAD_DIM), F32), 1, 10**6, 10**6)(partial)
    return attended, grad_query, grad_key, swapped_with_mp(total)


def solution(mesh):
    axes = ("yh", "x1", "x0", "core", "ctx", "mp")
    fine = Mesh(mesh.devices.reshape(2, 2, 2, 2, 8, 4), axes)
    tokens = P(axes[:5], "mp")
    return jax.shard_map(
        shards,
        mesh=fine,
        in_specs=(tokens,) * 5 + (P(axes[:4], None),),
        out_specs=(tokens,) * 4,
        check_vma=False,
    )
```

time: 171 us -> 195 us (1.14)
  blocking collectives: 13.5 us -> 44.5 us
  starting transfers between devices: 90 us -> 75.6 us
  between operations: 1.04 us -> 14.3 us
  waiting for transfers between devices: 41.9 us -> 34.7 us
    all_to_all x0 -> x1, blocking collectives: none -> 29.8 us  [shards(): lax.all_to_all(partial.reshape(32, 64, HEAD_DIM), PLANE, 0, 0, tiled=True)]
    all_to_all x3 -> x0, starting transfers between devices: 21.9 us -> none  [the longest x1 9.5 us: shards(): lax.all_to_all(partial.reshape(16, 64, HEAD_DIM), PLANE, 0, 0, tiled=True)]
    ppermute x8 -> x2, waiting for transfers between devices: 24.1 us -> 6.48 us  [swapped_with_mp(): return lax.ppermute(block, ('yh', 'x1', 'mp'), route)]
    all_to_all x3 -> x0, waiting for transfers between devices: 12 us -> none  [the longest x1 9.95 us: shards(): partial = lax.all_to_all(partial, 'ctx', 0, 0, tiled=True)]
    all_to_all x1 -> x2, starting transfers between devices: 9.48 us -> 20.9 us  [to_all(): lax.all_to_all(jnp.broadcast_to(block[None], (copies,) + block.shape), ax...]
    reduce_scatter x0 -> x2, waiting for transfers between devices: none -> 9 us  [summed_over_ctx(): lax.psum_scatter(parts.reshape(8 * TOK, HEAD_DIM), 'ctx', scatter_dimensi...]
    all_to_all x1, waiting for transfers between devices: 0.2 us -> 6.14 us  [shards(): values = lax.all_to_all(values, 'ctx', 0, 0, tiled=True)]
    ppermute x4, starting transfers between devices: 19.9 us -> 14.2 us  [from_behind(): lax.ppermute(block, 'ctx', [(i, i + distance) for i in range(8 - distance)])]
  transfers between devices with their start and end apart: 26 -> 20, of which waited for: 14 -> 9; matrix products, arithmetic and copies ran while one was open for 0% -> 0% of each run, Pallas kernels for 9% -> 9%
where the time goes in v5:
time: 195 us; the launch traced here: 191 us
  starting transfers between devices  75.6 us (39%)
  blocking collectives  44.5 us (23%)
  waiting for transfers between devices  34.7 us (18%)
  Pallas kernels  16.8 us (9%)
  between operations  14.3 us (7%)
  local copies, waits for them, and re-layouts  2.91 us (1%)
  other arithmetic  2.49 us (1%)
    all_to_all x1, blocking collectives, shards(): lax.all_to_all(partial.reshape(32, 64, HEAD_DIM), PLANE, 0, 0, tiled=True)  29.8 us
    all_to_all x2, starting transfers between devices, to_all(): lax.all_to_all(jnp.broadcast_to(block[None], (copies,) + block.shape), ax...  20.9 us
    all_to_all x1, blocking collectives, shards(): mixed = lax.all_to_all(mixed, 'mp', 0, 0, tiled=True)  14.7 us
    ppermute x4, starting transfers between devices, from_behind(): lax.ppermute(block, 'ctx', [(i, i + distance) for i in range(8 - distance)])  14.2 us
    ppermute x2, starting transfers between devices, swapped_with_mp(): return lax.ppermute(block, ('yh', 'x1', 'mp'), route)  10.1 us
    reduce_scatter x2, waiting for transfers between devices, summed_over_ctx(): lax.psum_scatter(parts.reshape(8 * TOK, HEAD_DIM), 'ctx', scatter_dimensi...  9 us
    ppermute x3, starting transfers between devices, traded(): lax.ppermute(blocks[1], 'x0', pair)  8.85 us
    pallas_call x1, Pallas kernels, shards(): call(attend, (wide, wide, slots), 9, 6 * 10 ** 9, 4 * 10 ** 6, (rows, row...  8.66 us
  transfers between devices with their start and end apart: 20, of which 9 were waited for; matrix products, arithmetic and copies ran while one was open for 0% of the time, Pallas kernels for 9%

profile of v5, /device:TPU:56, one launch (start us, length us, event | category | flops | bytes accessed | tf_op | source)
XLA Modules:
  0.0 191.4 jit_solution(17554563341495598413)
XLA Ops:
  7.2 0.0 copy-start
  7.2 5.8 %collective-permute-start.3 = (bf16[64,128]{1,0:T(8,128)(2,1)}, bf16[64,128]{1,0:T(8,128)(2,1)S(1)}, u32[]{:S(2)}, u32[]{:S(2)}) collective-permute-start(bf16[64,128]{1,0:T(8,128)(2,1)} %param.9), channel_id=1, source_target_pairs={{0,0},{1,128},{2,256},{3,384},{128,1},{129,129},{130,257},{131,385... | collective-permute-start | bytes 49160 | tf_op jit(solution)/shard_map/ppermute | solution.py:58
  13.0 2.5 %collective-permute-done.3 = bf16[64,128]{1,0:T(8,128)(2,1)S(1)} collective-permute-done((bf16[64,128]{1,0:T(8,128)(2,1)}, bf16[64,128]{1,0:T(8,128)(2,1)S(1)}, u32[]{:S(2)}, u32[]{:S(2)}) %collective-permute-start.3) | collective-permute-done | bytes 16416 | tf_op jit(solution)/shard_map/ppermute | solution.py:58
  15.6 0.9 broadcast_in_dim.4
  16.5 15.8 %all-to-all-start = ((bf16[32,64,128]{2,1,0:T(8,128)(2,1)}), bf16[32,64,128]{2,1,0:T(8,128)(2,1)S(1)}, u32[]{:S(2)}, u32[]{:S(2)}) async-start(bf16[32,64,128]{2,1,0:T(8,128)(2,1)} %broadcast_in_dim.4), calls=%async_computation | async-start | bytes 1048576 | tf_op jit(solution)/shard_map/all_to_all | solution.py:47
  32.3 0.0 copy-start.2
  32.4 0.0 reduce-scatter.3.cloned.1.call-start
  32.4 0.0 copy-done
  32.4 0.1 pieces.1
  32.5 1.9 %collective-permute-start = (bf16[192,512]{1,0:T(8,128)(2,1)S(1)}, bf16[192,512]{1,0:T(8,128)(2,1)S(1)}, u32[]{:S(2)}, u32[]{:S(2)}) collective-permute-start(bf16[192,512]{1,0:T(8,128)(2,1)S(1)} %get-tuple-element.24), channel_id=1, source_target_pairs={{0,32},{32,0},{1,33},{33,1},{2,34},{34,2},{3,35},{35,3},{4,36},{36... | collective-permute-start | bytes 589832 | tf_op jit(solution)/shard_map/ppermute | solution.py:71
  34.4 3.4 %collective-permute-start.1 = (bf16[192,512]{1,0:T(8,128)(2,1)S(1)}, bf16[192,512]{1,0:T(8,128)(2,1)S(1)}, u32[]{:S(2)}, u32[]{:S(2)}) collective-permute-start(bf16[192,512]{1,0:T(8,128)(2,1)S(1)} %get-tuple-element.25), channel_id=1, source_target_pairs={{0,64},{64,0},{1,65},{65,1},{2,66},{66,2},{3,67},{67,3},{4,68},{68... | collective-permute-start | bytes 589832 | tf_op jit(solution)/shard_map/ppermute | solution.py:72
  37.8 2.3 %collective-permute-start.2 = (bf16[192,512]{1,0:T(8,128)(2,1)S(1)}, bf16[192,512]{1,0:T(8,128)(2,1)S(1)}, u32[]{:S(2)}, u32[]{:S(2)}) collective-permute-start(bf16[192,512]{1,0:T(8,128)(2,1)S(1)} %get-tuple-element.26), channel_id=1, source_target_pairs={{0,96},{32,64},{64,32},{96,0},{1,97},{33,65},{65,33},{97,1},{2,98}... | collective-permute-start | bytes 589832 | tf_op jit(solution)/shard_map/ppermute | solution.py:73
  40.1 0.0 copy-done.2
  40.1 3.4 %collective-permute-start.7 = (bf16[192,128]{1,0:T(8,128)(2,1)S(1)}, bf16[192,128]{1,0:T(8,128)(2,1)S(1)}, u32[]{:S(2)}, u32[]{:S(2)}) collective-permute-start(bf16[192,128]{1,0:T(8,128)(2,1)S(1)} %copy-done.2), channel_id=1, source_target_pairs={{0,4},{4,8},{8,12},{12,16},{16,20},{20,24},{24,28},{1,5},{5,9},{9,... | collective-permute-start | bytes 147464 | tf_op jit(solution)/shard_map/ppermute | solution.py:53
  43.5 4.3 %collective-permute-start.6 = (bf16[192,128]{1,0:T(8,128)(2,1)S(1)}, bf16[192,128]{1,0:T(8,128)(2,1)S(1)}, u32[]{:S(2)}, u32[]{:S(2)}) collective-permute-start(bf16[192,128]{1,0:T(8,128)(2,1)S(1)} %copy-done.2), channel_id=1, source_target_pairs={{0,8},{4,12},{8,16},{12,20},{16,24},{20,28},{1,9},{5,13},{9,17},{1... | collective-permute-start | bytes 147464 | tf_op jit(solution)/shard_map/ppermute | solution.py:53
  47.8 0.0 collective-permute-done.refs_0_
  47.8 4.6 %collective-permute-start.5 = (bf16[192,128]{1,0:T(8,128)(2,1)S(1)}, bf16[192,128]{1,0:T(8,128)(2,1)S(1)}, u32[]{:S(2)}, u32[]{:S(2)}) collective-permute-start(bf16[192,128]{1,0:T(8,128)(2,1)S(1)} %copy-done.2), channel_id=1, source_target_pairs={{0,12},{4,16},{8,20},{12,24},{16,28},{1,13},{5,17},{9,21},{13,25},... | collective-permute-start | bytes 147464 | tf_op jit(solution)/shard_map/ppermute | solution.py:53
  52.4 0.0 collective-permute-done.1.refs_1_
  52.4 1.9 %collective-permute-start.4 = (bf16[192,128]{1,0:T(8,128)(2,1)S(1)}, bf16[192,128]{1,0:T(8,128)(2,1)S(1)}, u32[]{:S(2)}, u32[]{:S(2)}) collective-permute-start(bf16[192,128]{1,0:T(8,128)(2,1)S(1)} %copy-done.2), channel_id=1, source_target_pairs={{0,16},{4,20},{8,24},{12,28},{1,17},{5,21},{9,25},{13,29},{2,18},{... | collective-permute-start | bytes 147464 | tf_op jit(solution)/shard_map/ppermute | solution.py:53
  54.3 0.0 collective-permute-done.2.refs_2_
  54.3 0.0 collective-permute-done.7.refs_3_
  54.3 0.0 copy-start.3
  54.4 0.0 collective-permute-done.6.refs_2_
  54.4 0.0 copy-start.4
  54.4 0.0 collective-permute-done.5.refs_1_
  54.4 1.7 collective-permute-done.4.refs_0_
  56.1 0.0 copy-done.4
  56.1 0.6 copy-done.6
  56.7 5.8 %soft.1 = (f32[8,192,128]{2,1,0:T(8,128)}, f32[8,384]{1,0:T(8,128)}) custom-call(s32[1,8]{1,0:T(1,128)} %len_ref.1, bf16[192,1024]{1,0:T(8,128)(2,1)} %q_ref.3, bf16[192,1024]{1,0:T(8,128)(2,1)} %do_ref.3, bf16[192,128]{1,0:T(8,128)(2,1)} %copy-done.6, bf16[192,128]{1,0:T(8,128)(2,1)} %copy-done.5, bf16[192,128]{1,0:T(8,128)(2,1)} %copy-done.4, ...), custom_call_target="tpu_custom_call" | custom-call | flops 3000000000 | bytes 2000000 | tf_op jit(solution)/shard_map/soft/pallas_call | solution.py:236
  62.5 0.0 reduce-scatter.3.cloned.1.call-update
  62.6 0.0 all-to-all-done
  62.6 0.6 project.1
  63.2 1.9 %collective-permute-start.8 = (bf16[4,192,128]{2,1,0:T(8,128)(2,1)S(1)}, bf16[4,192,128]{2,1,0:T(8,128)(2,1)S(1)}, u32[]{:S(2)}, u32[]{:S(2)}) collective-permute-start(bf16[4,192,128]{2,1,0:T(8,128)(2,1)S(1)} %get-tuple-element.36), channel_id=1, source_target_pairs={{0,32},{32,0},{1,33},{33,1},{2,34},{34,2},{3,35},{35,3},{4,36},{36... | collective-permute-start | bytes 589832 | tf_op jit(solution)/shard_map/ppermute | solution.py:71
  65.1 3.4 %collective-permute-start.9 = (bf16[4,192,128]{2,1,0:T(8,128)(2,1)S(1)}, bf16[4,192,128]{2,1,0:T(8,128)(2,1)S(1)}, u32[]{:S(2)}, u32[]{:S(2)}) collective-permute-start(bf16[4,192,128]{2,1,0:T(8,128)(2,1)S(1)} %get-tuple-element.37), channel_id=1, source_target_pairs={{0,64},{64,0},{1,65},{65,1},{2,66},{66,2},{3,67},{67,3},{4,68},{68... | collective-permute-start | bytes 589832 | tf_op jit(solution)/shard_map/ppermute | solution.py:72
  68.5 2.3 %collective-permute-start.10 = (bf16[4,192,128]{2,1,0:T(8,128)(2,1)S(1)}, bf16[4,192,128]{2,1,0:T(8,128)(2,1)S(1)}, u32[]{:S(2)}, u32[]{:S(2)}) collective-permute-start(bf16[4,192,128]{2,1,0:T(8,128)(2,1)S(1)} %get-tuple-element.38), channel_id=1, source_target_pairs={{0,96},{32,64},{64,32},{96,0},{1,97},{33,65},{65,33},{97,1},{2,98}... | collective-permute-start | bytes 589832 | tf_op jit(solution)/shard_map/ppermute | solution.py:73
  70.8 0.0 collective-permute-done.8.refs_1_
  70.8 3.9 %collective-permute-done.9.refs_2_ = bf16[4,192,128]{2,1,0:T(8,128)(2,1)S(1)} collective-permute-done((bf16[4,192,128]{2,1,0:T(8,128)(2,1)S(1)}, bf16[4,192,128]{2,1,0:T(8,128)(2,1)S(1)}, u32[]{:S(2)}, u32[]{:S(2)}) %collective-permute-start.9) | collective-permute-done | bytes 196640 | tf_op jit(solution)/shard_map/ppermute | solution.py:72
  74.7 3.4 %collective-permute-done.10.refs_3_ = bf16[4,192,128]{2,1,0:T(8,128)(2,1)S(1)} collective-permute-done((bf16[4,192,128]{2,1,0:T(8,128)(2,1)S(1)}, bf16[4,192,128]{2,1,0:T(8,128)(2,1)S(1)}, u32[]{:S(2)}, u32[]{:S(2)}) %collective-permute-start.10) | collective-permute-done | bytes 196640 | tf_op jit(solution)/shard_map/ppermute | solution.py:73
  78.1 0.1 mix.1
  78.2 14.7 %all_to_all.25.parts_ref = bf16[4,192,128]{2,1,0:T(8,128)(2,1)S(1)} all-to-all(bf16[4,192,128]{2,1,0:T(8,128)(2,1)S(1)} %mix.1), channel_id=1, replica_groups=mesh['yh'=2,'x1'=2,'x0'=2,'core'=2,'ctx'=8,'mp'=4] {'mp'}, dimensions={0} | all-to-all | bytes 393216 | tf_op jit(solution)/shard_map/all_to_all | solution.py:248
  92.9 0.8 spread_sum.1
  93.7 7.6 %all-to-all-start.2 = ((bf16[8,192,128]{2,1,0:T(8,128)(2,1)}), bf16[8,192,128]{2,1,0:T(8,128)(2,1)S(1)}, u32[]{:S(2)}, u32[]{:S(2)}) async-start(bf16[8,192,128]{2,1,0:T(8,128)(2,1)} %spread_sum.1), calls=%async_computation.3 | async-start | bytes 786432 | tf_op jit(solution)/shard_map/all_to_all | solution.py:250
  101.3 9.0 %reduce-scatter.3.cloned.1.call-done = f32[192,128]{1,0:T(8,128)} async-done(((f32[1536,128]{1,0:T(8,128)}), f32[192,128]{1,0:T(8,128)}) %reduce-scatter.3.cloned.1.call-update) | async-done | bytes 98320 | tf_op jit(solution)/shard_map/reduce_scatter | solution.py:62
  110.3 6.1 %all-to-all-done.2.v_ref = bf16[8,192,128]{2,1,0:T(8,128)(2,1)S(1)} async-done(((bf16[8,192,128]{2,1,0:T(8,128)(2,1)}), bf16[8,192,128]{2,1,0:T(8,128)(2,1)S(1)}, u32[]{:S(2)}, u32[]{:S(2)}) %all-to-all-start.2) | async-done | bytes 393248 | tf_op jit(solution)/shard_map/all_to_all | solution.py:250
  116.4 1.0 convert_element_type.7
  117.4 0.7 broadcast_in_dim.5
  118.1 5.1 %all-to-all-start.3 = ((bf16[4,192,128]{2,1,0:T(8,128)(2,1)}), bf16[4,192,128]{2,1,0:T(8,128)(2,1)S(1)}, u32[]{:S(2)}, u32[]{:S(2)}) async-start(bf16[4,192,128]{2,1,0:T(8,128)(2,1)} %broadcast_in_dim.5), calls=%async_computation.5 | async-start | bytes 393216 | tf_op jit(solution)/shard_map/all_to_all | solution.py:47
  123.2 0.0 reduce-scatter.5.cloned.1.call-start
  123.2 8.7 %attend.1 = (bf16[192,1024]{1,0:T(8,128)(2,1)}, bf16[192,1024]{1,0:T(8,128)(2,1)}, f32[8,192,128]{2,1,0:T(8,128)}) custom-call(s32[1,8]{1,0:T(1,128)} %len_ref.1, bf16[192,1024]{1,0:T(8,128)(2,1)} %q_ref.3, bf16[192,1024]{1,0:T(8,128)(2,1)} %do_ref.3, f32[8,384]{1,0:T(8,128)} %get-tuple-element.29.stat_ref, bf16[8,192,128]{2,1,0:T(8,128)(2,1)} %copy-done.1, ...), custom_call_target="tpu_custom_call" | custom-call | flops 6000000000 | bytes 4000000 | tf_op jit(solution)/shard_map/attend/pallas_call | solution.py:255
  131.9 0.0 reduce-scatter.5.cloned.1.call-update
  131.9 0.0 all-to-all-done.3.refs_3_
  131.9 1.9 %collective-permute-start.13 = (bf16[4,192,128]{2,1,0:T(8,128)(2,1)S(1)}, bf16[4,192,128]{2,1,0:T(8,128)(2,1)S(1)}, u32[]{:S(2)}, u32[]{:S(2)}) collective-permute-start(bf16[4,192,128]{2,1,0:T(8,128)(2,1)S(1)} %all-to-all-done.3.refs_3_), channel_id=1, source_target_pairs={{0,96},{32,64},{64,32},{96,0},{1,97},{33,65},{65,33},{97,1},{2,98}... | collective-permute-start | bytes 589832 | tf_op jit(solution)/shard_map/ppermute | solution.py:73
  133.8 2.1 %collective-permute-start.12 = (bf16[4,192,128]{2,1,0:T(8,128)(2,1)S(1)}, bf16[4,192,128]{2,1,0:T(8,128)(2,1)S(1)}, u32[]{:S(2)}, u32[]{:S(2)}) collective-permute-start(bf16[4,192,128]{2,1,0:T(8,128)(2,1)S(1)} %all-to-all-done.3.refs_3_), channel_id=1, source_target_pairs={{0,64},{64,0},{1,65},{65,1},{2,66},{66,2},{3,67},{67,3},{4,68},{68... | collective-permute-start | bytes 589832 | tf_op jit(solution)/shard_map/ppermute | solution.py:72
  135.9 3.6 %collective-permute-start.11 = (bf16[4,192,128]{2,1,0:T(8,128)(2,1)S(1)}, bf16[4,192,128]{2,1,0:T(8,128)(2,1)S(1)}, u32[]{:S(2)}, u32[]{:S(2)}) collective-permute-start(bf16[4,192,128]{2,1,0:T(8,128)(2,1)S(1)} %all-to-all-done.3.refs_3_), channel_id=1, source_target_pairs={{0,32},{32,0},{1,33},{33,1},{2,34},{34,2},{3,35},{35,3},{4,36},{36... | collective-permute-start | bytes 589832 | tf_op jit(solution)/shard_map/ppermute | solution.py:71
  139.5 0.5 collective-permute-done.13.refs_6_
  140.0 3.5 %collective-permute-done.12.refs_5_ = bf16[4,192,128]{2,1,0:T(8,128)(2,1)S(1)} collective-permute-done((bf16[4,192,128]{2,1,0:T(8,128)(2,1)S(1)}, bf16[4,192,128]{2,1,0:T(8,128)(2,1)S(1)}, u32[]{:S(2)}, u32[]{:S(2)}) %collective-permute-start.12) | collective-permute-done | bytes 196640 | tf_op jit(solution)/shard_map/ppermute | solution.py:72
  143.6 0.0 collective-permute-done.11.refs_4_
  143.6 0.7 weight_grad.1
  144.3 29.8 %all_to_all.26.parts_ref = bf16[32,64,128]{2,1,0:T(8,128)(2,1)S(1)} all-to-all(bf16[32,64,128]{2,1,0:T(8,128)(2,1)S(1)} %bitcast.5), channel_id=1, replica_groups=mesh['yh'=2,'x1'=2,'x0'=2,'core'=2,'ctx'=8,'mp'=4] {'yh','x1','ctx'}, dimensions={0} | all-to-all | bytes 1048576 | tf_op jit(solution)/shard_map/all_to_all | solution.py:264
  174.1 0.1 sum_blocks.1
  174.2 4.2 %collective-permute-start.14 = (f32[64,128]{1,0:T(8,128)S(1)}, f32[64,128]{1,0:T(8,128)S(1)}, u32[]{:S(2)}, u32[]{:S(2)}) collective-permute-start(f32[64,128]{1,0:T(8,128)S(1)} %sum_blocks.1), channel_id=1, source_target_pairs={{0,0},{1,128},{2,256},{3,384},{128,1},{129,129},{130,257},{131,385... | collective-permute-start | bytes 98312 | tf_op jit(solution)/shard_map/ppermute | solution.py:58
  178.5 4.0 %collective-permute-done.14 = f32[64,128]{1,0:T(8,128)S(1)} collective-permute-done((f32[64,128]{1,0:T(8,128)S(1)}, f32[64,128]{1,0:T(8,128)S(1)}, u32[]{:S(2)}, u32[]{:S(2)}) %collective-permute-start.14) | collective-permute-done | bytes 32800 | tf_op jit(solution)/shard_map/ppermute | solution.py:58
  182.4 1.5 multiply_convert_fusion
  183.9 0.6 copy.11
  (7 shorter events, 0.0 us)
Async XLA Ops:
  7.2 25.2 %copy-start = (bf16[192,2048]{1,0:T(8,128)(2,1)S(1)}, bf16[192,2048]{1,0:T(8,128)(2,1)}, u32[]{:S(2)}) copy-start(bf16[192,2048]{1,0:T(8,128)(2,1)} %x_ref.5) | copy-start | bytes 2359300
  7.2 8.4 %collective-permute-start.3 = (bf16[64,128]{1,0:T(8,128)(2,1)}, bf16[64,128]{1,0:T(8,128)(2,1)S(1)}, u32[]{:S(2)}, u32[]{:S(2)}) collective-permute-start(bf16[64,128]{1,0:T(8,128)(2,1)} %param.9), channel_id=1, source_target_pairs={{0,0},{1,128},{2,256},{3,384},{128,1},{129,129},{130,257},{131,385... | collective-permute-start | bytes 49160 | tf_op jit(solution)/shard_map/ppermute | solution.py:58
  16.5 46.1 %all-to-all-start = ((bf16[32,64,128]{2,1,0:T(8,128)(2,1)}), bf16[32,64,128]{2,1,0:T(8,128)(2,1)S(1)}, u32[]{:S(2)}, u32[]{:S(2)}) async-start(bf16[32,64,128]{2,1,0:T(8,128)(2,1)} %broadcast_in_dim.4), calls=%async_computation | async-start | bytes 1048576 | tf_op jit(solution)/shard_map/all_to_all | solution.py:47
  32.3 7.7 %copy-start.2 = (bf16[192,128]{1,0:T(8,128)(2,1)S(1)}, bf16[192,128]{1,0:T(8,128)(2,1)}, u32[]{:S(2)}) copy-start(bf16[192,128]{1,0:T(8,128)(2,1)} %refs_4_.3) | copy-start | bytes 147460
  32.4 77.9 %reduce-scatter.3.cloned.1.call-start = ((), (), s32[]{:S(2)}) async-start(), calls=%async_computation.7 | async-start | bytes 884736 | tf_op jit(solution)/shard_map/reduce_scatter | solution.py:62
  32.5 15.3 %collective-permute-start = (bf16[192,512]{1,0:T(8,128)(2,1)S(1)}, bf16[192,512]{1,0:T(8,128)(2,1)S(1)}, u32[]{:S(2)}, u32[]{:S(2)}) collective-permute-start(bf16[192,512]{1,0:T(8,128)(2,1)S(1)} %get-tuple-element.24), channel_id=1, source_target_pairs={{0,32},{32,0},{1,33},{33,1},{2,34},{34,2},{3,35},{35,3},{4,36},{36... | collective-permute-start | bytes 589832 | tf_op jit(solution)/shard_map/ppermute | solution.py:71
  34.4 18.0 %collective-permute-start.1 = (bf16[192,512]{1,0:T(8,128)(2,1)S(1)}, bf16[192,512]{1,0:T(8,128)(2,1)S(1)}, u32[]{:S(2)}, u32[]{:S(2)}) collective-permute-start(bf16[192,512]{1,0:T(8,128)(2,1)S(1)} %get-tuple-element.25), channel_id=1, source_target_pairs={{0,64},{64,0},{1,65},{65,1},{2,66},{66,2},{3,67},{67,3},{4,68},{68... | collective-permute-start | bytes 589832 | tf_op jit(solution)/shard_map/ppermute | solution.py:72
  37.8 16.5 %collective-permute-start.2 = (bf16[192,512]{1,0:T(8,128)(2,1)S(1)}, bf16[192,512]{1,0:T(8,128)(2,1)S(1)}, u32[]{:S(2)}, u32[]{:S(2)}) collective-permute-start(bf16[192,512]{1,0:T(8,128)(2,1)S(1)} %get-tuple-element.26), channel_id=1, source_target_pairs={{0,96},{32,64},{64,32},{96,0},{1,97},{33,65},{65,33},{97,1},{2,98}... | collective-permute-start | bytes 589832 | tf_op jit(solution)/shard_map/ppermute | solution.py:73
  40.1 14.2 %collective-permute-start.7 = (bf16[192,128]{1,0:T(8,128)(2,1)S(1)}, bf16[192,128]{1,0:T(8,128)(2,1)S(1)}, u32[]{:S(2)}, u32[]{:S(2)}) collective-permute-start(bf16[192,128]{1,0:T(8,128)(2,1)S(1)} %copy-done.2), channel_id=1, source_target_pairs={{0,4},{4,8},{8,12},{12,16},{16,20},{20,24},{24,28},{1,5},{5,9},{9,... | collective-permute-start | bytes 147464 | tf_op jit(solution)/shard_map/ppermute | solution.py:53
  43.5 10.9 %collective-permute-start.6 = (bf16[192,128]{1,0:T(8,128)(2,1)S(1)}, bf16[192,128]{1,0:T(8,128)(2,1)S(1)}, u32[]{:S(2)}, u32[]{:S(2)}) collective-permute-start(bf16[192,128]{1,0:T(8,128)(2,1)S(1)} %copy-done.2), channel_id=1, source_target_pairs={{0,8},{4,12},{8,16},{12,20},{16,24},{20,28},{1,9},{5,13},{9,17},{1... | collective-permute-start | bytes 147464 | tf_op jit(solution)/shard_map/ppermute | solution.py:53
  47.8 6.6 %collective-permute-start.5 = (bf16[192,128]{1,0:T(8,128)(2,1)S(1)}, bf16[192,128]{1,0:T(8,128)(2,1)S(1)}, u32[]{:S(2)}, u32[]{:S(2)}) collective-permute-start(bf16[192,128]{1,0:T(8,128)(2,1)S(1)} %copy-done.2), channel_id=1, source_target_pairs={{0,12},{4,16},{8,20},{12,24},{16,28},{1,13},{5,17},{9,21},{13,25},... | collective-permute-start | bytes 147464 | tf_op jit(solution)/shard_map/ppermute | solution.py:53
  52.4 3.7 %collective-permute-start.4 = (bf16[192,128]{1,0:T(8,128)(2,1)S(1)}, bf16[192,128]{1,0:T(8,128)(2,1)S(1)}, u32[]{:S(2)}, u32[]{:S(2)}) collective-permute-start(bf16[192,128]{1,0:T(8,128)(2,1)S(1)} %copy-done.2), channel_id=1, source_target_pairs={{0,16},{4,20},{8,24},{12,28},{1,17},{5,21},{9,25},{13,29},{2,18},{... | collective-permute-start | bytes 147464 | tf_op jit(solution)/shard_map/ppermute | solution.py:53
  54.3 1.7 copy-start.3
  54.4 1.7 copy-start.4
  54.4 1.7 copy-start.5
  56.1 0.6 copy-start.6
  63.2 7.6 %collective-permute-start.8 = (bf16[4,192,128]{2,1,0:T(8,128)(2,1)S(1)}, bf16[4,192,128]{2,1,0:T(8,128)(2,1)S(1)}, u32[]{:S(2)}, u32[]{:S(2)}) collective-permute-start(bf16[4,192,128]{2,1,0:T(8,128)(2,1)S(1)} %get-tuple-element.36), channel_id=1, source_target_pairs={{0,32},{32,0},{1,33},{33,1},{2,34},{34,2},{3,35},{35,3},{4,36},{36... | collective-permute-start | bytes 589832 | tf_op jit(solution)/shard_map/ppermute | solution.py:71
  65.1 9.6 %collective-permute-start.9 = (bf16[4,192,128]{2,1,0:T(8,128)(2,1)S(1)}, bf16[4,192,128]{2,1,0:T(8,128)(2,1)S(1)}, u32[]{:S(2)}, u32[]{:S(2)}) collective-permute-start(bf16[4,192,128]{2,1,0:T(8,128)(2,1)S(1)} %get-tuple-element.37), channel_id=1, source_target_pairs={{0,64},{64,0},{1,65},{65,1},{2,66},{66,2},{3,67},{67,3},{4,68},{68... | collective-permute-start | bytes 589832 | tf_op jit(solution)/shard_map/ppermute | solution.py:72
  68.5 9.6 %collective-permute-start.10 = (bf16[4,192,128]{2,1,0:T(8,128)(2,1)S(1)}, bf16[4,192,128]{2,1,0:T(8,128)(2,1)S(1)}, u32[]{:S(2)}, u32[]{:S(2)}) collective-permute-start(bf16[4,192,128]{2,1,0:T(8,128)(2,1)S(1)} %get-tuple-element.38), channel_id=1, source_target_pairs={{0,96},{32,64},{64,32},{96,0},{1,97},{33,65},{65,33},{97,1},{2,98}... | collective-permute-start | bytes 589832 | tf_op jit(solution)/shard_map/ppermute | solution.py:73
  93.7 22.7 %all-to-all-start.2 = ((bf16[8,192,128]{2,1,0:T(8,128)(2,1)}), bf16[8,192,128]{2,1,0:T(8,128)(2,1)S(1)}, u32[]{:S(2)}, u32[]{:S(2)}) async-start(bf16[8,192,128]{2,1,0:T(8,128)(2,1)} %spread_sum.1), calls=%async_computation.3 | async-start | bytes 786432 | tf_op jit(solution)/shard_map/all_to_all | solution.py:250
  116.4 6.8 %copy-start.1 = (bf16[8,192,128]{2,1,0:T(8,128)(2,1)}, bf16[8,192,128]{2,1,0:T(8,128)(2,1)S(1)}, u32[]{:S(2)}) copy-start(bf16[8,192,128]{2,1,0:T(8,128)(2,1)S(1)} %all-to-all-done.2.v_ref) | copy-start | bytes 1179652
  118.1 13.8 %all-to-all-start.3 = ((bf16[4,192,128]{2,1,0:T(8,128)(2,1)}), bf16[4,192,128]{2,1,0:T(8,128)(2,1)S(1)}, u32[]{:S(2)}, u32[]{:S(2)}) async-start(bf16[4,192,128]{2,1,0:T(8,128)(2,1)} %broadcast_in_dim.5), calls=%async_computation.5 | async-start | bytes 393216 | tf_op jit(solution)/shard_map/all_to_all | solution.py:47
  123.2 59.2 %reduce-scatter.5.cloned.1.call-start = ((), (), s32[]{:S(2)}) async-start(), calls=%async_computation.8 | async-start | bytes 884736 | tf_op jit(solution)/shard_map/reduce_scatter | solution.py:62
  131.9 8.1 %collective-permute-start.13 = (bf16[4,192,128]{2,1,0:T(8,128)(2,1)S(1)}, bf16[4,192,128]{2,1,0:T(8,128)(2,1)S(1)}, u32[]{:S(2)}, u32[]{:S(2)}) collective-permute-start(bf16[4,192,128]{2,1,0:T(8,128)(2,1)S(1)} %all-to-all-done.3.refs_3_), channel_id=1, source_target_pairs={{0,96},{32,64},{64,32},{96,0},{1,97},{33,65},{65,33},{97,1},{2,98}... | collective-permute-start | bytes 589832 | tf_op jit(solution)/shard_map/ppermute | solution.py:73
  133.8 9.7 %collective-permute-start.12 = (bf16[4,192,128]{2,1,0:T(8,128)(2,1)S(1)}, bf16[4,192,128]{2,1,0:T(8,128)(2,1)S(1)}, u32[]{:S(2)}, u32[]{:S(2)}) collective-permute-start(bf16[4,192,128]{2,1,0:T(8,128)(2,1)S(1)} %all-to-all-done.3.refs_3_), channel_id=1, source_target_pairs={{0,64},{64,0},{1,65},{65,1},{2,66},{66,2},{3,67},{67,3},{4,68},{68... | collective-permute-start | bytes 589832 | tf_op jit(solution)/shard_map/ppermute | solution.py:72
  135.9 7.7 %collective-permute-start.11 = (bf16[4,192,128]{2,1,0:T(8,128)(2,1)S(1)}, bf16[4,192,128]{2,1,0:T(8,128)(2,1)S(1)}, u32[]{:S(2)}, u32[]{:S(2)}) collective-permute-start(bf16[4,192,128]{2,1,0:T(8,128)(2,1)S(1)} %all-to-all-done.3.refs_3_), channel_id=1, source_target_pairs={{0,32},{32,0},{1,33},{33,1},{2,34},{34,2},{3,35},{35,3},{4,36},{36... | collective-permute-start | bytes 589832 | tf_op jit(solution)/shard_map/ppermute | solution.py:71
  174.2 8.2 %collective-permute-start.14 = (f32[64,128]{1,0:T(8,128)S(1)}, f32[64,128]{1,0:T(8,128)S(1)}, u32[]{:S(2)}, u32[]{:S(2)}) collective-permute-start(f32[64,128]{1,0:T(8,128)S(1)} %sum_blocks.1), channel_id=1, source_target_pairs={{0,0},{1,128},{2,256},{3,384},{128,1},{129,129},{130,257},{131,385... | collective-permute-start | bytes 98312 | tf_op jit(solution)/shard_map/ppermute | solution.py:58
Sparse Core Ops, SparseCore 0:
  62.7 47.5 reduce-scatter.2
  132.0 40.7 reduce-scatter.4

commit v6 on v3

--- a/solution.py
+++ b/solution.py
@@ -74,9 +74,7 @@
             total += jnp.dot(
                 feature_columns(x_ref, j, half), weight_rows(w_ref, j), preferred_element_type=F32
             )
-    total = total.astype(BF16)
-    for place in range(8):
-        out_ref[place] = total
+    out_ref[...] = total.astype(BF16)
 
 
 def weight_grad(x_ref, *refs):
@@ -92,7 +90,7 @@
                 feature_columns(x_ref, j, half), dv, TN, preferred_element_type=F32
             ).astype(BF16)
             for ctx in range(8):
-                out_ref[ctx, j] = rows[ctx * 64 : (ctx + 1) * 64]
+                out_ref[j, ctx] = rows[ctx * 64 : (ctx + 1) * 64]
 
 
 def add_halves(a_ref, b_ref, out_ref):
@@ -101,9 +99,9 @@
 
 def sum_blocks(parts_ref, out_ref):
     total = parts_ref[0].astype(F32)
-    for i in range(1, 8):
+    for i in range(1, parts_ref.shape[0]):
         total = total + parts_ref[i].astype(F32)
-    out_ref[...] = total.astype(out_ref.dtype)
+    out_ref[...] = total
 
 
 def rows_of_heads(wide_ref, rows_ref):
@@ -151,15 +149,14 @@
         ref[...] = total[slot * TOK : (slot + 1) * TOK].astype(ref.dtype)
 
 
-def attend(len_ref, q_ref, do_ref, stat_ref, v_ref, *refs):
-    k_refs, (att_ref, dq_ref), dk_refs = refs[:5], refs[5:7], refs[7:12]
-    q_rows, do_rows, bias, dscores, keys, values = refs[12:]
-    ctx = lax.axis_index("ctx")
+def attend(len_ref, q_ref, do_ref, stat_ref, *refs):
+    k_refs, v_refs, (att_ref, dq_ref), dk_refs = refs[:5], refs[5:10], refs[10:12], refs[12:17]
+    q_rows, do_rows, bias, dscores, keys, values = refs[17:]
     rows_of_heads(q_ref, q_rows)
     rows_of_heads(do_ref, do_rows)
-    for slot, ref in enumerate(k_refs):
-        keys[slot * TOK : (slot + 1) * TOK] = ref[...]
-        values[slot * TOK : (slot + 1) * TOK] = v_ref[lax.rem(ctx - (REACH - slot) + 8, 8)]
+    for slot in range(REACH + 1):
+        keys[slot * TOK : (slot + 1) * TOK] = k_refs[slot][...]
+        values[slot * TOK : (slot + 1) * TOK] = v_refs[slot][...]
     fill_bias(len_ref, bias)
     for i in range(CHUNKS):
         cols = slice(i * LANES, (i + 1) * LANES)
@@ -191,7 +188,6 @@
     spread, keys = lax.optimization_barrier((spread, keys))
 
     weight = lax.all_to_all(spread, "ctx", 0, 0, tiled=True)
-    other = lax.ppermute(weight, "core", [(0, 1), (1, 0)])
     heads = GROUP * TOK
     rows = pltpu.VMEM((heads, HEAD_DIM), BF16)
     window = pltpu.VMEM((WINDOW, HEAD_DIM), BF16)
@@ -206,28 +202,30 @@
     )(lengths, queries, grad_out, *keys)
     dv = [dv[REACH]] + [from_ahead(dv[REACH - d], d) for d in range(1, REACH + 1)]
 
-    values = call(project, shape((8, TOK, HEAD_DIM)), 3, 4 * 10**8, 5 * 10**6)(
-        features, weight, other
-    )
-    values = lax.all_to_all(values, "ctx", 0, 0, tiled=True)
+    weight, dv = lax.optimization_barrier((weight, dv))
+    other = lax.ppermute(weight, "core", [(0, 1), (1, 0)])
+    other, dv = lax.optimization_barrier((other, dv))
+
     partial, given = call(weight_grad, (whole, whole), 6, 4 * 10**8, 5 * 10**6)(features, *dv)
     taken = lax.ppermute(given, "core", [(0, 1), (1, 0)])
+    projected = call(project, block, 3, 4 * 10**8, 5 * 10**6)(features, weight, other)
+    taken, projected = lax.optimization_barrier((taken, projected))
+    values = [from_behind(projected, d) for d in range(REACH, 0, -1)] + [projected]
     partial = call(add_halves, whole, 2, 10**6, 3 * 10**6)(partial, taken)
-    partial, values = lax.optimization_barrier((partial, values))
-    partial = lax.all_to_all(partial, "ctx", 0, 0, tiled=True)
+    partial = lax.all_to_all(
+        partial.reshape(64, 64, HEAD_DIM), ("yh", "x", "ctx"), 0, 0, tiled=True
+    )
 
     wide = shape((TOK, GROUP * HEAD_DIM))
     attended, grad_query, *dk = call(
-        attend, (wide, wide) + (block,) * REACH + (own,), 9, 6 * 10**9, 4 * 10**6,
+        attend, (wide, wide) + (block,) * REACH + (own,), 13, 6 * 10**9, 4 * 10**6,
         (rows, rows, bias, pairs, window, window), smem=1, vmem=56,
-    )(lengths, queries, grad_out, stats, values, *keys)
-    partial, dk = lax.optimization_barrier((partial, dk))
+    )(lengths, queries, grad_out, stats, *keys, *values)
     dk = [dk[REACH]] + [from_ahead(dk[REACH - d], d) for d in range(1, REACH + 1)]
     grad_key = (sum(part.astype(F32) for part in dk) * F32(SCALE)).astype(BF16)
 
-    partial = call(sum_blocks, shape((8, 64, HEAD_DIM)), 1, 10**6, 10**6)(partial)
-    partial = lax.all_to_all(partial, CHIPS, 0, 0, tiled=True)
-    grad_weight = call(sum_blocks, shape((64, HEAD_DIM), F32), 1, 10**5, 10**5)(partial)
+    partial, grad_key = lax.optimization_barrier((partial, grad_key))
+    grad_weight = call(sum_blocks, shape((64, HEAD_DIM), F32), 1, 10**6, 10**6)(partial)
     return attended, grad_query, grad_key, grad_weight
 
 

time: 194 us -> 178 us (0.918)
  the two profiles are of different devices: /device:TPU:128 before, /device:TPU:56 now
where the time goes in v6:
time: 178 us; the launch traced here: 175 us
  starting transfers between devices  79.2 us (44%)
  waiting for transfers between devices  55.7 us (31%)
  Pallas kernels  18.3 us (10%)
  between operations  14.3 us (8%)
  local copies, waits for them, and re-layouts  6.06 us (3%)
    ppermute x8, starting transfers between devices, from_behind(): lax.ppermute(block, 'ctx', [(i, i + distance) for i in range(8 - distance)])  34.2 us
    ppermute x8, waiting for transfers between devices, from_ahead(): lax.ppermute(block, 'ctx', [(i + distance, i) for i in range(8 - distance)])  31.9 us
    all_to_all x1, starting transfers between devices, shards(): lax.all_to_all(partial.reshape(64, 64, HEAD_DIM), ('yh', 'x', 'ctx'), 0,...  15.8 us
    ppermute x8, waiting for transfers between devices, from_behind(): lax.ppermute(block, 'ctx', [(i, i + distance) for i in range(8 - distance)])  14.3 us
    ppermute x8, starting transfers between devices, from_ahead(): lax.ppermute(block, 'ctx', [(i + distance, i) for i in range(8 - distance)])  10.3 us
    all_to_all x1, starting transfers between devices, to_all(): lax.all_to_all(jnp.broadcast_to(block[None], (copies,) + block.shape), ax...  9.67 us
    pallas_call x1, Pallas kernels, shards(): call(attend, (wide, wide) + (block,) * REACH + (own,), 13, 6 * 10 ** 9, 4...  8.36 us
    pallas_call x1, Pallas kernels, shards(): call(soft, (block,) * REACH + (own, shape((8, LANES), F32)), 7, 3 * 10 **...  5.62 us
  transfers between devices with their start and end apart: 22, of which 15 were waited for; matrix products, arithmetic and copies ran while one was open for 2% of the time, Pallas kernels for 9%

profile of v6, /device:TPU:56, one launch (start us, length us, event | category | flops | bytes accessed | tf_op | source)
XLA Modules:
  0.0 175.2 jit_solution(16242588499696456043)
XLA Ops:
  7.2 0.0 all-gather.3.cloned.1.call-start
  7.2 0.7 all-gather.3.cloned.1.call-update
  7.9 1.4 broadcast_in_dim.4
  9.3 9.7 %all-to-all-start = ((bf16[8,64,128]{2,1,0:T(8,128)(2,1)}), bf16[8,64,128]{2,1,0:T(8,128)(2,1)S(1)}, u32[]{:S(2)}, u32[]{:S(2)}) async-start(bf16[8,64,128]{2,1,0:T(8,128)(2,1)} %broadcast_in_dim.4), calls=%async_computation | async-start | bytes 262144 | tf_op jit(solution)/shard_map/all_to_all | solution.py:47
  19.0 6.1 %collective-permute-start.2 = (bf16[192,128]{1,0:T(8,128)(2,1)}, bf16[192,128]{1,0:T(8,128)(2,1)S(1)}, u32[]{:S(2)}, u32[]{:S(2)}) collective-permute-start(bf16[192,128]{1,0:T(8,128)(2,1)} %refs_4_.1), channel_id=1, source_target_pairs={{0,8},{4,12},{8,16},{12,20},{16,24},{20,28},{1,9},{5,13},{9,17},{1... | collective-permute-start | bytes 147464 | tf_op jit(solution)/shard_map/ppermute | solution.py:53
  25.0 8.2 %collective-permute-start.1 = (bf16[192,128]{1,0:T(8,128)(2,1)}, bf16[192,128]{1,0:T(8,128)(2,1)S(1)}, u32[]{:S(2)}, u32[]{:S(2)}) collective-permute-start(bf16[192,128]{1,0:T(8,128)(2,1)} %refs_4_.1), channel_id=1, source_target_pairs={{0,12},{4,16},{8,20},{12,24},{16,28},{1,13},{5,17},{9,21},{13,25},... | collective-permute-start | bytes 147464 | tf_op jit(solution)/shard_map/ppermute | solution.py:53
  33.3 3.1 %collective-permute-start = (bf16[192,128]{1,0:T(8,128)(2,1)}, bf16[192,128]{1,0:T(8,128)(2,1)S(1)}, u32[]{:S(2)}, u32[]{:S(2)}) collective-permute-start(bf16[192,128]{1,0:T(8,128)(2,1)} %refs_4_.1), channel_id=1, source_target_pairs={{0,16},{4,20},{8,24},{12,28},{1,17},{5,21},{9,25},{13,29},{2,18},{... | collective-permute-start | bytes 147464 | tf_op jit(solution)/shard_map/ppermute | solution.py:53
  36.4 2.5 %collective-permute-start.3 = (bf16[192,128]{1,0:T(8,128)(2,1)}, bf16[192,128]{1,0:T(8,128)(2,1)S(1)}, u32[]{:S(2)}, u32[]{:S(2)}) collective-permute-start(bf16[192,128]{1,0:T(8,128)(2,1)} %refs_4_.1), channel_id=1, source_target_pairs={{0,4},{4,8},{8,12},{12,16},{16,20},{20,24},{24,28},{1,5},{5,9},{9,... | collective-permute-start | bytes 147464 | tf_op jit(solution)/shard_map/ppermute | solution.py:53
  38.9 0.0 collective-permute-done.2.refs_2_
  38.9 0.0 copy-start.4
  38.9 0.0 collective-permute-done.1.refs_1_
  38.9 0.0 copy-start.5
  38.9 0.0 collective-permute-done.refs_0_
  38.9 0.0 copy-start.6
  38.9 2.0 %collective-permute-done.3.refs_3_ = bf16[192,128]{1,0:T(8,128)(2,1)S(1)} collective-permute-done((bf16[192,128]{1,0:T(8,128)(2,1)}, bf16[192,128]{1,0:T(8,128)(2,1)S(1)}, u32[]{:S(2)}, u32[]{:S(2)}) %collective-permute-start.3) | collective-permute-done | bytes 49184 | tf_op jit(solution)/shard_map/ppermute | solution.py:53
  40.9 0.0 all-to-all-done
  40.9 1.3 broadcast_in_dim.5
  42.2 5.2 %all-to-all-start.1 = ((bf16[8,8,64,128]{3,2,1,0:T(8,128)(2,1)}), bf16[8,8,64,128]{3,2,1,0:T(8,128)(2,1)S(1)}, u32[]{:S(2)}, u32[]{:S(2)}) async-start(bf16[8,8,64,128]{3,2,1,0:T(8,128)(2,1)} %broadcast_in_dim.5), calls=%async_computation.1 | async-start | bytes 2097152 | tf_op jit(solution)/shard_map/all_to_all | solution.py:190
  47.4 0.0 copy-done.4
  47.4 0.0 copy-done.5
  47.5 5.6 %soft.1 = (bf16[192,128]{1,0:T(8,128)(2,1)}, bf16[192,128]{1,0:T(8,128)(2,1)}, bf16[192,128]{1,0:T(8,128)(2,1)}, bf16[192,128]{1,0:T(8,128)(2,1)}, f32[192,128]{1,0:T(8,128)}, /*index=5*/f32[8,384]{1,0:T(8,128)}) custom-call(s32[1,8]{1,0:T(1,128)} %len_ref.3, bf16[192,1024]{1,0:T(8,128)(2,1)} %q_ref.3, bf16[192,1024]{1,0:T(8,128)(2,1)} %do_ref.3, ...), custom_call_target="tpu_custom_call" | custom-call | flops 3000000000 | bytes 2000000 | tf_op jit(solution)/shard_map/soft/pallas_call | solution.py:199
  53.1 1.3 collective-permute-start.4
  54.4 1.3 collective-permute-start.5
  55.7 1.3 collective-permute-start.6
  57.0 1.3 collective-permute-start.7
  58.3 13.7 %collective-permute-done.4.refs_1_ = bf16[192,128]{1,0:T(8,128)(2,1)S(1)} collective-permute-done((bf16[192,128]{1,0:T(8,128)(2,1)}, bf16[192,128]{1,0:T(8,128)(2,1)S(1)}, u32[]{:S(2)}, u32[]{:S(2)}) %collective-permute-start.4) | collective-permute-done | bytes 49184 | tf_op jit(solution)/shard_map/ppermute | solution.py:57
  72.0 1.2 collective-permute-done.5.refs_2_
  73.2 3.0 %collective-permute-done.6.refs_3_ = bf16[192,128]{1,0:T(8,128)(2,1)S(1)} collective-permute-done((bf16[192,128]{1,0:T(8,128)(2,1)}, bf16[192,128]{1,0:T(8,128)(2,1)S(1)}, u32[]{:S(2)}, u32[]{:S(2)}) %collective-permute-start.6) | collective-permute-done | bytes 49184 | tf_op jit(solution)/shard_map/ppermute | solution.py:57
  76.1 0.0 collective-permute-done.7.refs_4_
  76.2 0.0 all-to-all-done.1.own_ref
  76.2 1.9 %collective-permute-start.8 = (bf16[8,8,64,128]{3,2,1,0:T(8,128)(2,1)S(1)}, bf16[8,8,64,128]{3,2,1,0:T(8,128)(2,1)S(1)}, u32[]{:S(2)}, u32[]{:S(2)}) collective-permute-start(bf16[8,8,64,128]{3,2,1,0:T(8,128)(2,1)S(1)} %all-to-all-done.1.own_ref), channel_id=1, source_target_pairs={{0,32},{32,0},{1,33},{33,1},{2,34},{34,2},{3,35},{35,3},{4,36},{36... | collective-permute-start | bytes 3145736 | tf_op jit(solution)/shard_map/ppermute | solution.py:206
  78.1 2.6 %collective-permute-done.8.other_ref = bf16[8,8,64,128]{3,2,1,0:T(8,128)(2,1)S(1)} collective-permute-done((bf16[8,8,64,128]{3,2,1,0:T(8,128)(2,1)S(1)}, bf16[8,8,64,128]{3,2,1,0:T(8,128)(2,1)S(1)}, u32[]{:S(2)}, u32[]{:S(2)}) %collective-permute-start.8) | collective-permute-done | bytes 1048608 | tf_op jit(solution)/shard_map/ppermute | solution.py:206
  80.7 4.6 %all-gather.3.cloned.1.call-done = bf16[768,2048]{1,0:T(8,128)(2,1)} async-done(((bf16[192,2048]{1,0:T(8,128)(2,1)}), bf16[768,2048]{1,0:T(8,128)(2,1)}) %all-gather.3.cloned.1.call-update) | async-done | bytes 3145744 | tf_op jit(solution)/shard_map/all_gather | solution.py:184
  85.3 1.9 %copy-done = bf16[768,2048]{1,0:T(8,128)(2,1)S(1)} copy-done((bf16[768,2048]{1,0:T(8,128)(2,1)S(1)}, bf16[768,2048]{1,0:T(8,128)(2,1)}, u32[]{:S(2)}) %copy-start) | copy-done | bytes 3145752
  87.2 0.9 copy-done.2
  88.1 1.4 weight_grad.1
  89.4 1.9 %collective-permute-start.9 = (bf16[8,8,64,128]{3,2,1,0:T(8,128)(2,1)S(1)}, bf16[8,8,64,128]{3,2,1,0:T(8,128)(2,1)S(1)}, u32[]{:S(2)}, u32[]{:S(2)}) collective-permute-start(bf16[8,8,64,128]{3,2,1,0:T(8,128)(2,1)S(1)} %get-tuple-element.64), channel_id=1, source_target_pairs={{0,32},{32,0},{1,33},{33,1},{2,34},{34,2},{3,35},{35,3},{4,36},{36... | collective-permute-start | bytes 3145736 | tf_op jit(solution)/shard_map/ppermute | solution.py:210
  91.4 1.0 project.1.refs_9_
  92.4 1.6 collective-permute-done.9.b_ref
  94.0 1.2 add_halves.1
  95.2 15.8 %all-to-all-start.2 = ((bf16[64,64,128]{2,1,0:T(8,128)(2,1)}), bf16[64,64,128]{2,1,0:T(8,128)(2,1)S(1)}, u32[]{:S(2)}, u32[]{:S(2)}) async-start(bf16[64,64,128]{2,1,0:T(8,128)(2,1)} %bitcast.1), calls=%async_computation.2 | async-start | bytes 2097152 | tf_op jit(solution)/shard_map/all_to_all | solution.py:215
  111.0 3.4 %collective-permute-start.13 = (bf16[192,128]{1,0:T(8,128)(2,1)S(1)}, bf16[192,128]{1,0:T(8,128)(2,1)S(1)}, u32[]{:S(2)}, u32[]{:S(2)}) collective-permute-start(bf16[192,128]{1,0:T(8,128)(2,1)S(1)} %project.1.refs_9_), channel_id=1, source_target_pairs={{0,4},{4,8},{8,12},{12,16},{16,20},{20,24},{24,28},{1,5},{5,9},{9,... | collective-permute-start | bytes 147464 | tf_op jit(solution)/shard_map/ppermute | solution.py:53
  114.4 4.3 %collective-permute-start.12 = (bf16[192,128]{1,0:T(8,128)(2,1)S(1)}, bf16[192,128]{1,0:T(8,128)(2,1)S(1)}, u32[]{:S(2)}, u32[]{:S(2)}) collective-permute-start(bf16[192,128]{1,0:T(8,128)(2,1)S(1)} %project.1.refs_9_), channel_id=1, source_target_pairs={{0,8},{4,12},{8,16},{12,20},{16,24},{20,28},{1,9},{5,13},{9,17},{1... | collective-permute-start | bytes 147464 | tf_op jit(solution)/shard_map/ppermute | solution.py:53
  118.7 4.6 %collective-permute-start.11 = (bf16[192,128]{1,0:T(8,128)(2,1)S(1)}, bf16[192,128]{1,0:T(8,128)(2,1)S(1)}, u32[]{:S(2)}, u32[]{:S(2)}) collective-permute-start(bf16[192,128]{1,0:T(8,128)(2,1)S(1)} %project.1.refs_9_), channel_id=1, source_target_pairs={{0,12},{4,16},{8,20},{12,24},{16,28},{1,13},{5,17},{9,21},{13,25},... | collective-permute-start | bytes 147464 | tf_op jit(solution)/shard_map/ppermute | solution.py:53
  123.3 2.1 %collective-permute-start.10 = (bf16[192,128]{1,0:T(8,128)(2,1)S(1)}, bf16[192,128]{1,0:T(8,128)(2,1)S(1)}, u32[]{:S(2)}, u32[]{:S(2)}) collective-permute-start(bf16[192,128]{1,0:T(8,128)(2,1)S(1)} %project.1.refs_9_), channel_id=1, source_target_pairs={{0,16},{4,20},{8,24},{12,28},{1,17},{5,21},{9,25},{13,29},{2,18},{... | collective-permute-start | bytes 147464 | tf_op jit(solution)/shard_map/ppermute | solution.py:53
  125.4 8.5 %collective-permute-done.13.refs_8_ = bf16[192,128]{1,0:T(8,128)(2,1)S(1)} collective-permute-done((bf16[192,128]{1,0:T(8,128)(2,1)S(1)}, bf16[192,128]{1,0:T(8,128)(2,1)S(1)}, u32[]{:S(2)}, u32[]{:S(2)}) %collective-permute-start.13) | collective-permute-done | bytes 49184 | tf_op jit(solution)/shard_map/ppermute | solution.py:53
  133.9 1.9 %collective-permute-done.12.refs_7_ = bf16[192,128]{1,0:T(8,128)(2,1)S(1)} collective-permute-done((bf16[192,128]{1,0:T(8,128)(2,1)S(1)}, bf16[192,128]{1,0:T(8,128)(2,1)S(1)}, u32[]{:S(2)}, u32[]{:S(2)}) %collective-permute-start.12) | collective-permute-done | bytes 49184 | tf_op jit(solution)/shard_map/ppermute | solution.py:53
  135.9 1.4 collective-permute-done.11.refs_6_
  137.2 0.5 collective-permute-done.10.refs_5_
  137.8 0.0 copy-done.8
  137.8 0.1 copy-done.10
  137.9 0.5 copy-done.11
  138.4 8.4 %attend.1 = (bf16[192,1024]{1,0:T(8,128)(2,1)}, bf16[192,1024]{1,0:T(8,128)(2,1)}, bf16[192,128]{1,0:T(8,128)(2,1)}, bf16[192,128]{1,0:T(8,128)(2,1)}, bf16[192,...) custom-call(s32[1,8]{1,0:T(1,128)} %len_ref.3, bf16[192,1024]{1,0:T(8,128)(2,1)} %q_ref.3, ...), custom_call_target="tpu_custom_call" | custom-call | flops 6000000000 | bytes 4000000 | tf_op jit(solution)/shard_map/attend/pallas_call | solution.py:220
  146.7 1.3 collective-permute-start.14
  148.0 1.3 collective-permute-start.15
  149.3 1.3 collective-permute-start.16
  150.6 1.3 collective-permute-start.17
  151.9 2.3 %collective-permute-done.14 = bf16[192,128]{1,0:T(8,128)(2,1)S(1)} collective-permute-done((bf16[192,128]{1,0:T(8,128)(2,1)}, bf16[192,128]{1,0:T(8,128)(2,1)S(1)}, u32[]{:S(2)}, u32[]{:S(2)}) %collective-permute-start.14) | collective-permute-done | bytes 49184 | tf_op jit(solution)/shard_map/ppermute | solution.py:57
  154.3 4.9 %collective-permute-done.15 = bf16[192,128]{1,0:T(8,128)(2,1)S(1)} collective-permute-done((bf16[192,128]{1,0:T(8,128)(2,1)}, bf16[192,128]{1,0:T(8,128)(2,1)S(1)}, u32[]{:S(2)}, u32[]{:S(2)}) %collective-permute-start.15) | collective-permute-done | bytes 49184 | tf_op jit(solution)/shard_map/ppermute | solution.py:57
  159.2 3.8 %collective-permute-done.16 = bf16[192,128]{1,0:T(8,128)(2,1)S(1)} collective-permute-done((bf16[192,128]{1,0:T(8,128)(2,1)}, bf16[192,128]{1,0:T(8,128)(2,1)S(1)}, u32[]{:S(2)}, u32[]{:S(2)}) %collective-permute-start.16) | collective-permute-done | bytes 49184 | tf_op jit(solution)/shard_map/ppermute | solution.py:57
  163.0 3.0 %collective-permute-done.17 = bf16[192,128]{1,0:T(8,128)(2,1)S(1)} collective-permute-done((bf16[192,128]{1,0:T(8,128)(2,1)}, bf16[192,128]{1,0:T(8,128)(2,1)S(1)}, u32[]{:S(2)}, u32[]{:S(2)}) %collective-permute-start.17) | collective-permute-done | bytes 49184 | tf_op jit(solution)/shard_map/ppermute | solution.py:57
  166.0 1.6 multiply_convert_fusion
  167.5 0.0 all-to-all-done.2.parts_ref
  167.5 0.8 sum_blocks.1
  (14 shorter events, 0.0 us)
Async XLA Ops:
  7.2 78.1 %all-gather.3.cloned.1.call-start = ((), (), s32[]{:S(2)}) async-start(), calls=%async_computation.3 | async-start | bytes 3932160 | tf_op jit(solution)/shard_map/all_gather | solution.py:184
  9.3 31.6 %all-to-all-start = ((bf16[8,64,128]{2,1,0:T(8,128)(2,1)}), bf16[8,64,128]{2,1,0:T(8,128)(2,1)S(1)}, u32[]{:S(2)}, u32[]{:S(2)}) async-start(bf16[8,64,128]{2,1,0:T(8,128)(2,1)} %broadcast_in_dim.4), calls=%async_computation | async-start | bytes 262144 | tf_op jit(solution)/shard_map/all_to_all | solution.py:47
  19.0 19.9 %collective-permute-start.2 = (bf16[192,128]{1,0:T(8,128)(2,1)}, bf16[192,128]{1,0:T(8,128)(2,1)S(1)}, u32[]{:S(2)}, u32[]{:S(2)}) collective-permute-start(bf16[192,128]{1,0:T(8,128)(2,1)} %refs_4_.1), channel_id=1, source_target_pairs={{0,8},{4,12},{8,16},{12,20},{16,24},{20,28},{1,9},{5,13},{9,17},{1... | collective-permute-start | bytes 147464 | tf_op jit(solution)/shard_map/ppermute | solution.py:53
  25.0 13.8 %collective-permute-start.1 = (bf16[192,128]{1,0:T(8,128)(2,1)}, bf16[192,128]{1,0:T(8,128)(2,1)S(1)}, u32[]{:S(2)}, u32[]{:S(2)}) collective-permute-start(bf16[192,128]{1,0:T(8,128)(2,1)} %refs_4_.1), channel_id=1, source_target_pairs={{0,12},{4,16},{8,20},{12,24},{16,28},{1,13},{5,17},{9,21},{13,25},... | collective-permute-start | bytes 147464 | tf_op jit(solution)/shard_map/ppermute | solution.py:53
  33.3 5.6 %collective-permute-start = (bf16[192,128]{1,0:T(8,128)(2,1)}, bf16[192,128]{1,0:T(8,128)(2,1)S(1)}, u32[]{:S(2)}, u32[]{:S(2)}) collective-permute-start(bf16[192,128]{1,0:T(8,128)(2,1)} %refs_4_.1), channel_id=1, source_target_pairs={{0,16},{4,20},{8,24},{12,28},{1,17},{5,21},{9,25},{13,29},{2,18},{... | collective-permute-start | bytes 147464 | tf_op jit(solution)/shard_map/ppermute | solution.py:53
  36.4 4.5 %collective-permute-start.3 = (bf16[192,128]{1,0:T(8,128)(2,1)}, bf16[192,128]{1,0:T(8,128)(2,1)S(1)}, u32[]{:S(2)}, u32[]{:S(2)}) collective-permute-start(bf16[192,128]{1,0:T(8,128)(2,1)} %refs_4_.1), channel_id=1, source_target_pairs={{0,4},{4,8},{8,12},{12,16},{16,20},{20,24},{24,28},{1,5},{5,9},{9,... | collective-permute-start | bytes 147464 | tf_op jit(solution)/shard_map/ppermute | solution.py:53
  38.9 8.6 %copy-start.4 = (bf16[192,128]{1,0:T(8,128)(2,1)}, bf16[192,128]{1,0:T(8,128)(2,1)S(1)}, u32[]{:S(2)}) copy-start(bf16[192,128]{1,0:T(8,128)(2,1)S(1)} %collective-permute-done.2.refs_2_) | copy-start | bytes 147460
  38.9 8.5 %copy-start.5 = (bf16[192,128]{1,0:T(8,128)(2,1)}, bf16[192,128]{1,0:T(8,128)(2,1)S(1)}, u32[]{:S(2)}) copy-start(bf16[192,128]{1,0:T(8,128)(2,1)S(1)} %collective-permute-done.1.refs_1_) | copy-start | bytes 147460
  38.9 8.5 %copy-start.6 = (bf16[192,128]{1,0:T(8,128)(2,1)}, bf16[192,128]{1,0:T(8,128)(2,1)S(1)}, u32[]{:S(2)}) copy-start(bf16[192,128]{1,0:T(8,128)(2,1)S(1)} %collective-permute-done.refs_0_) | copy-start | bytes 147460
  40.9 6.5 %copy-start.7 = (bf16[192,128]{1,0:T(8,128)(2,1)}, bf16[192,128]{1,0:T(8,128)(2,1)S(1)}, u32[]{:S(2)}) copy-start(bf16[192,128]{1,0:T(8,128)(2,1)S(1)} %collective-permute-done.3.refs_3_) | copy-start | bytes 147460
  42.2 34.0 %all-to-all-start.1 = ((bf16[8,8,64,128]{3,2,1,0:T(8,128)(2,1)}), bf16[8,8,64,128]{3,2,1,0:T(8,128)(2,1)S(1)}, u32[]{:S(2)}, u32[]{:S(2)}) async-start(bf16[8,8,64,128]{3,2,1,0:T(8,128)(2,1)} %broadcast_in_dim.5), calls=%async_computation.1 | async-start | bytes 2097152 | tf_op jit(solution)/shard_map/all_to_all | solution.py:190
  53.1 18.9 %collective-permute-start.4 = (bf16[192,128]{1,0:T(8,128)(2,1)}, bf16[192,128]{1,0:T(8,128)(2,1)S(1)}, u32[]{:S(2)}, u32[]{:S(2)}) collective-permute-start(bf16[192,128]{1,0:T(8,128)(2,1)} %get-tuple-element.49), channel_id=1, source_target_pairs={{4,0},{8,4},{12,8},{16,12},{20,16},{24,20},{28,24},{5,1},{9,5},{13... | collective-permute-start | bytes 147464 | tf_op jit(solution)/shard_map/ppermute | solution.py:57
  54.4 18.8 %collective-permute-start.5 = (bf16[192,128]{1,0:T(8,128)(2,1)}, bf16[192,128]{1,0:T(8,128)(2,1)S(1)}, u32[]{:S(2)}, u32[]{:S(2)}) collective-permute-start(bf16[192,128]{1,0:T(8,128)(2,1)} %get-tuple-element.50), channel_id=1, source_target_pairs={{8,0},{12,4},{16,8},{20,12},{24,16},{28,20},{9,1},{13,5},{17,9},{2... | collective-permute-start | bytes 147464 | tf_op jit(solution)/shard_map/ppermute | solution.py:57
  55.7 20.5 %collective-permute-start.6 = (bf16[192,128]{1,0:T(8,128)(2,1)}, bf16[192,128]{1,0:T(8,128)(2,1)S(1)}, u32[]{:S(2)}, u32[]{:S(2)}) collective-permute-start(bf16[192,128]{1,0:T(8,128)(2,1)} %get-tuple-element.51), channel_id=1, source_target_pairs={{12,0},{16,4},{20,8},{24,12},{28,16},{13,1},{17,5},{21,9},{25,13},... | collective-permute-start | bytes 147464 | tf_op jit(solution)/shard_map/ppermute | solution.py:57
  57.0 19.2 %collective-permute-start.7 = (bf16[192,128]{1,0:T(8,128)(2,1)}, bf16[192,128]{1,0:T(8,128)(2,1)S(1)}, u32[]{:S(2)}, u32[]{:S(2)}) collective-permute-start(bf16[192,128]{1,0:T(8,128)(2,1)} %get-tuple-element.52), channel_id=1, source_target_pairs={{16,0},{20,4},{24,8},{28,12},{17,1},{21,5},{25,9},{29,13},{18,2},{... | collective-permute-start | bytes 147464 | tf_op jit(solution)/shard_map/ppermute | solution.py:57
  76.2 4.5 %collective-permute-start.8 = (bf16[8,8,64,128]{3,2,1,0:T(8,128)(2,1)S(1)}, bf16[8,8,64,128]{3,2,1,0:T(8,128)(2,1)S(1)}, u32[]{:S(2)}, u32[]{:S(2)}) collective-permute-start(bf16[8,8,64,128]{3,2,1,0:T(8,128)(2,1)S(1)} %all-to-all-done.1.own_ref), channel_id=1, source_target_pairs={{0,32},{32,0},{1,33},{33,1},{2,34},{34,2},{3,35},{35,3},{4,36},{36... | collective-permute-start | bytes 3145736 | tf_op jit(solution)/shard_map/ppermute | solution.py:206
  85.3 1.9 %copy-start = (bf16[768,2048]{1,0:T(8,128)(2,1)S(1)}, bf16[768,2048]{1,0:T(8,128)(2,1)}, u32[]{:S(2)}) copy-start(bf16[768,2048]{1,0:T(8,128)(2,1)} %all-gather.3.cloned.1.call-done) | copy-start | bytes 9437188
  87.2 0.9 copy-start.2
  88.1 3.3 %copy-start.1 = (bf16[768,2048]{1,0:T(8,128)(2,1)S(1)}, bf16[768,2048]{1,0:T(8,128)(2,1)}, u32[]{:S(2)}) copy-start(bf16[768,2048]{1,0:T(8,128)(2,1)} %all-gather.3.cloned.1.call-done) | copy-start | bytes 9437188
  89.4 4.6 %collective-permute-start.9 = (bf16[8,8,64,128]{3,2,1,0:T(8,128)(2,1)S(1)}, bf16[8,8,64,128]{3,2,1,0:T(8,128)(2,1)S(1)}, u32[]{:S(2)}, u32[]{:S(2)}) collective-permute-start(bf16[8,8,64,128]{3,2,1,0:T(8,128)(2,1)S(1)} %get-tuple-element.64), channel_id=1, source_target_pairs={{0,32},{32,0},{1,33},{33,1},{2,34},{34,2},{3,35},{35,3},{4,36},{36... | collective-permute-start | bytes 3145736 | tf_op jit(solution)/shard_map/ppermute | solution.py:210
  92.3 45.4 %copy-start.3 = (bf16[192,128]{1,0:T(8,128)(2,1)}, bf16[192,128]{1,0:T(8,128)(2,1)S(1)}, u32[]{:S(2)}) copy-start(bf16[192,128]{1,0:T(8,128)(2,1)S(1)} %project.1.refs_9_) | copy-start | bytes 147460
  95.2 72.3 %all-to-all-start.2 = ((bf16[64,64,128]{2,1,0:T(8,128)(2,1)}), bf16[64,64,128]{2,1,0:T(8,128)(2,1)S(1)}, u32[]{:S(2)}, u32[]{:S(2)}) async-start(bf16[64,64,128]{2,1,0:T(8,128)(2,1)} %bitcast.1), calls=%async_computation.2 | async-start | bytes 2097152 | tf_op jit(solution)/shard_map/all_to_all | solution.py:215
  111.0 22.9 %collective-permute-start.13 = (bf16[192,128]{1,0:T(8,128)(2,1)S(1)}, bf16[192,128]{1,0:T(8,128)(2,1)S(1)}, u32[]{:S(2)}, u32[]{:S(2)}) collective-permute-start(bf16[192,128]{1,0:T(8,128)(2,1)S(1)} %project.1.refs_9_), channel_id=1, source_target_pairs={{0,4},{4,8},{8,12},{12,16},{16,20},{20,24},{24,28},{1,5},{5,9},{9,... | collective-permute-start | bytes 147464 | tf_op jit(solution)/shard_map/ppermute | solution.py:53
  114.4 21.5 %collective-permute-start.12 = (bf16[192,128]{1,0:T(8,128)(2,1)S(1)}, bf16[192,128]{1,0:T(8,128)(2,1)S(1)}, u32[]{:S(2)}, u32[]{:S(2)}) collective-permute-start(bf16[192,128]{1,0:T(8,128)(2,1)S(1)} %project.1.refs_9_), channel_id=1, source_target_pairs={{0,8},{4,12},{8,16},{12,20},{16,24},{20,28},{1,9},{5,13},{9,17},{1... | collective-permute-start | bytes 147464 | tf_op jit(solution)/shard_map/ppermute | solution.py:53
  118.7 18.5 %collective-permute-start.11 = (bf16[192,128]{1,0:T(8,128)(2,1)S(1)}, bf16[192,128]{1,0:T(8,128)(2,1)S(1)}, u32[]{:S(2)}, u32[]{:S(2)}) collective-permute-start(bf16[192,128]{1,0:T(8,128)(2,1)S(1)} %project.1.refs_9_), channel_id=1, source_target_pairs={{0,12},{4,16},{8,20},{12,24},{16,28},{1,13},{5,17},{9,21},{13,25},... | collective-permute-start | bytes 147464 | tf_op jit(solution)/shard_map/ppermute | solution.py:53
  123.3 14.4 %collective-permute-start.10 = (bf16[192,128]{1,0:T(8,128)(2,1)S(1)}, bf16[192,128]{1,0:T(8,128)(2,1)S(1)}, u32[]{:S(2)}, u32[]{:S(2)}) collective-permute-start(bf16[192,128]{1,0:T(8,128)(2,1)S(1)} %project.1.refs_9_), channel_id=1, source_target_pairs={{0,16},{4,20},{8,24},{12,28},{1,17},{5,21},{9,25},{13,29},{2,18},{... | collective-permute-start | bytes 147464 | tf_op jit(solution)/shard_map/ppermute | solution.py:53
  133.9 3.8 %copy-start.8 = (bf16[192,128]{1,0:T(8,128)(2,1)}, bf16[192,128]{1,0:T(8,128)(2,1)S(1)}, u32[]{:S(2)}) copy-start(bf16[192,128]{1,0:T(8,128)(2,1)S(1)} %collective-permute-done.13.refs_8_) | copy-start | bytes 147460
  135.9 1.9 %copy-start.9 = (bf16[192,128]{1,0:T(8,128)(2,1)}, bf16[192,128]{1,0:T(8,128)(2,1)S(1)}, u32[]{:S(2)}) copy-start(bf16[192,128]{1,0:T(8,128)(2,1)S(1)} %collective-permute-done.12.refs_7_) | copy-start | bytes 147460
  137.2 0.6 copy-start.10
  137.8 0.6 copy-start.11
  146.7 7.5 %collective-permute-start.14 = (bf16[192,128]{1,0:T(8,128)(2,1)}, bf16[192,128]{1,0:T(8,128)(2,1)S(1)}, u32[]{:S(2)}, u32[]{:S(2)}) collective-permute-start(bf16[192,128]{1,0:T(8,128)(2,1)} %get-tuple-element.72), channel_id=1, source_target_pairs={{4,0},{8,4},{12,8},{16,12},{20,16},{24,20},{28,24},{5,1},{9,5},{13... | collective-permute-start | bytes 147464 | tf_op jit(solution)/shard_map/ppermute | solution.py:57
  148.0 11.2 %collective-permute-start.15 = (bf16[192,128]{1,0:T(8,128)(2,1)}, bf16[192,128]{1,0:T(8,128)(2,1)S(1)}, u32[]{:S(2)}, u32[]{:S(2)}) collective-permute-start(bf16[192,128]{1,0:T(8,128)(2,1)} %get-tuple-element.73), channel_id=1, source_target_pairs={{8,0},{12,4},{16,8},{20,12},{24,16},{28,20},{9,1},{13,5},{17,9},{2... | collective-permute-start | bytes 147464 | tf_op jit(solution)/shard_map/ppermute | solution.py:57
  149.3 13.6 %collective-permute-start.16 = (bf16[192,128]{1,0:T(8,128)(2,1)}, bf16[192,128]{1,0:T(8,128)(2,1)S(1)}, u32[]{:S(2)}, u32[]{:S(2)}) collective-permute-start(bf16[192,128]{1,0:T(8,128)(2,1)} %get-tuple-element.74), channel_id=1, source_target_pairs={{12,0},{16,4},{20,8},{24,12},{28,16},{13,1},{17,5},{21,9},{25,13},... | collective-permute-start | bytes 147464 | tf_op jit(solution)/shard_map/ppermute | solution.py:57
  150.6 15.3 %collective-permute-start.17 = (bf16[192,128]{1,0:T(8,128)(2,1)}, bf16[192,128]{1,0:T(8,128)(2,1)S(1)}, u32[]{:S(2)}, u32[]{:S(2)}) collective-permute-start(bf16[192,128]{1,0:T(8,128)(2,1)} %get-tuple-element.75), channel_id=1, source_target_pairs={{16,0},{20,4},{24,8},{28,12},{17,1},{21,5},{25,9},{29,13},{18,2},{... | collective-permute-start | bytes 147464 | tf_op jit(solution)/shard_map/ppermute | solution.py:57
Sparse Core Ops, SparseCore 0:
  10.1 75.1 all-gather.2

commit v7 on v6

--- a/solution.py
+++ b/solution.py
@@ -101,7 +101,7 @@
     total = parts_ref[0].astype(F32)
     for i in range(1, parts_ref.shape[0]):
         total = total + parts_ref[i].astype(F32)
-    out_ref[...] = total
+    out_ref[...] = total.astype(out_ref.dtype)
 
 
 def rows_of_heads(wide_ref, rows_ref):
@@ -212,19 +212,19 @@
     taken, projected = lax.optimization_barrier((taken, projected))
     values = [from_behind(projected, d) for d in range(REACH, 0, -1)] + [projected]
     partial = call(add_halves, whole, 2, 10**6, 3 * 10**6)(partial, taken)
-    partial = lax.all_to_all(
-        partial.reshape(64, 64, HEAD_DIM), ("yh", "x", "ctx"), 0, 0, tiled=True
-    )
+    partial = lax.all_to_all(partial, CHIPS, 0, 0, tiled=True)
 
     wide = shape((TOK, GROUP * HEAD_DIM))
     attended, grad_query, *dk = call(
         attend, (wide, wide) + (block,) * REACH + (own,), 13, 6 * 10**9, 4 * 10**6,
         (rows, rows, bias, pairs, window, window), smem=1, vmem=56,
     )(lengths, queries, grad_out, stats, *keys, *values)
+    partial, dk = lax.optimization_barrier((partial, dk))
     dk = [dk[REACH]] + [from_ahead(dk[REACH - d], d) for d in range(1, REACH + 1)]
     grad_key = (sum(part.astype(F32) for part in dk) * F32(SCALE)).astype(BF16)
 
-    partial, grad_key = lax.optimization_barrier((partial, grad_key))
+    partial = call(sum_blocks, shape((8, 64, HEAD_DIM)), 1, 10**6, 10**6)(partial)
+    partial = lax.all_to_all(partial, "ctx", 0, 0, tiled=True)
     grad_weight = call(sum_blocks, shape((64, HEAD_DIM), F32), 1, 10**6, 10**6)(partial)
     return attended, grad_query, grad_key, grad_weight
 

time: 178 us -> 168 us (0.944)
  waiting for transfers between devices: 55.7 us -> 38.4 us
  starting transfers between devices: 79.2 us -> 85 us
    ppermute x8, waiting for transfers between devices: 31.9 us -> 17.9 us  [from_ahead(): lax.ppermute(block, 'ctx', [(i + distance, i) for i in range(8 - distance)])]
    ppermute x8, waiting for transfers between devices: 14.3 us -> 3.49 us  [from_behind(): lax.ppermute(block, 'ctx', [(i, i + distance) for i in range(8 - distance)])]
    all_to_all x1 -> x2, waiting for transfers between devices: 0.01 us -> 7.49 us  [the longest x1 7.49 us: shards(): partial = lax.all_to_all(partial, 'ctx', 0, 0, tiled=True)]
    all_to_all x1 -> x2, starting transfers between devices: 15.8 us -> 20.4 us  [the longest x1 10.8 us: shards(): partial = lax.all_to_all(partial, 'ctx', 0, 0, tiled=True)]
  transfers between devices with their start and end apart: 22 -> 23, of which waited for: 15 -> 9; matrix products, arithmetic and copies ran while one was open for 2% -> 3% of each run, Pallas kernels for 9% -> 10%
where the time goes in v7:
time: 168 us; the launch traced here: 164 us
  starting transfers between devices  85 us (51%)
  waiting for transfers between devices  38.4 us (23%)
  Pallas kernels  19 us (11%)
  between operations  14.4 us (9%)
  local copies, waits for them, and re-layouts  6.05 us (4%)
    ppermute x8, starting transfers between devices, from_behind(): lax.ppermute(block, 'ctx', [(i, i + distance) for i in range(8 - distance)])  35.5 us
    ppermute x8, waiting for transfers between devices, from_ahead(): lax.ppermute(block, 'ctx', [(i + distance, i) for i in range(8 - distance)])  17.9 us
    all_to_all x1, starting transfers between devices, shards(): partial = lax.all_to_all(partial, 'ctx', 0, 0, tiled=True)  10.8 us
    ppermute x8, starting transfers between devices, from_ahead(): lax.ppermute(block, 'ctx', [(i + distance, i) for i in range(8 - distance)])  10.3 us
    all_to_all x1, starting transfers between devices, to_all(): lax.all_to_all(jnp.broadcast_to(block[None], (copies,) + block.shape), ax...  9.67 us
    all_to_all x1, starting transfers between devices, shards(): partial = lax.all_to_all(partial, CHIPS, 0, 0, tiled=True)  9.62 us
    pallas_call x1, Pallas kernels, shards(): call(attend, (wide, wide) + (block,) * REACH + (own,), 13, 6 * 10 ** 9, 4...  8.36 us
    all_to_all x1, waiting for transfers between devices, shards(): partial = lax.all_to_all(partial, 'ctx', 0, 0, tiled=True)  7.49 us
  transfers between devices with their start and end apart: 23, of which 9 were waited for; matrix products, arithmetic and copies ran while one was open for 3% of the time, Pallas kernels for 10%

profile of v7, /device:TPU:56, one launch (start us, length us, event | category | flops | bytes accessed | tf_op | source)
XLA Modules:
  0.0 164.3 jit_solution(12132001336303645923)
XLA Ops:
  7.2 0.0 all-gather.3.cloned.1.call-start
  7.2 0.7 all-gather.3.cloned.1.call-update
  7.9 1.4 broadcast_in_dim.4
  9.3 9.7 %all-to-all-start = ((bf16[8,64,128]{2,1,0:T(8,128)(2,1)}), bf16[8,64,128]{2,1,0:T(8,128)(2,1)S(1)}, u32[]{:S(2)}, u32[]{:S(2)}) async-start(bf16[8,64,128]{2,1,0:T(8,128)(2,1)} %broadcast_in_dim.4), calls=%async_computation | async-start | bytes 262144 | tf_op jit(solution)/shard_map/all_to_all | solution.py:47
  19.0 6.1 %collective-permute-start.2 = (bf16[192,128]{1,0:T(8,128)(2,1)}, bf16[192,128]{1,0:T(8,128)(2,1)S(1)}, u32[]{:S(2)}, u32[]{:S(2)}) collective-permute-start(bf16[192,128]{1,0:T(8,128)(2,1)} %refs_4_.1), channel_id=1, source_target_pairs={{0,8},{4,12},{8,16},{12,20},{16,24},{20,28},{1,9},{5,13},{9,17},{1... | collective-permute-start | bytes 147464 | tf_op jit(solution)/shard_map/ppermute | solution.py:53
  25.0 8.2 %collective-permute-start.1 = (bf16[192,128]{1,0:T(8,128)(2,1)}, bf16[192,128]{1,0:T(8,128)(2,1)S(1)}, u32[]{:S(2)}, u32[]{:S(2)}) collective-permute-start(bf16[192,128]{1,0:T(8,128)(2,1)} %refs_4_.1), channel_id=1, source_target_pairs={{0,12},{4,16},{8,20},{12,24},{16,28},{1,13},{5,17},{9,21},{13,25},... | collective-permute-start | bytes 147464 | tf_op jit(solution)/shard_map/ppermute | solution.py:53
  33.3 3.1 %collective-permute-start = (bf16[192,128]{1,0:T(8,128)(2,1)}, bf16[192,128]{1,0:T(8,128)(2,1)S(1)}, u32[]{:S(2)}, u32[]{:S(2)}) collective-permute-start(bf16[192,128]{1,0:T(8,128)(2,1)} %refs_4_.1), channel_id=1, source_target_pairs={{0,16},{4,20},{8,24},{12,28},{1,17},{5,21},{9,25},{13,29},{2,18},{... | collective-permute-start | bytes 147464 | tf_op jit(solution)/shard_map/ppermute | solution.py:53
  36.4 2.5 %collective-permute-start.3 = (bf16[192,128]{1,0:T(8,128)(2,1)}, bf16[192,128]{1,0:T(8,128)(2,1)S(1)}, u32[]{:S(2)}, u32[]{:S(2)}) collective-permute-start(bf16[192,128]{1,0:T(8,128)(2,1)} %refs_4_.1), channel_id=1, source_target_pairs={{0,4},{4,8},{8,12},{12,16},{16,20},{20,24},{24,28},{1,5},{5,9},{9,... | collective-permute-start | bytes 147464 | tf_op jit(solution)/shard_map/ppermute | solution.py:53
  38.9 0.0 collective-permute-done.2.refs_2_
  38.9 0.0 copy-start.4
  38.9 0.0 collective-permute-done.1.refs_1_
  38.9 0.0 copy-start.5
  38.9 0.0 collective-permute-done.refs_0_
  38.9 0.0 copy-start.6
  38.9 2.0 %collective-permute-done.3.refs_3_ = bf16[192,128]{1,0:T(8,128)(2,1)S(1)} collective-permute-done((bf16[192,128]{1,0:T(8,128)(2,1)}, bf16[192,128]{1,0:T(8,128)(2,1)S(1)}, u32[]{:S(2)}, u32[]{:S(2)}) %collective-permute-start.3) | collective-permute-done | bytes 49184 | tf_op jit(solution)/shard_map/ppermute | solution.py:53
  40.9 0.0 all-to-all-done
  40.9 1.2 broadcast_in_dim.5
  42.2 5.2 %all-to-all-start.1 = ((bf16[8,8,64,128]{3,2,1,0:T(8,128)(2,1)}), bf16[8,8,64,128]{3,2,1,0:T(8,128)(2,1)S(1)}, u32[]{:S(2)}, u32[]{:S(2)}) async-start(bf16[8,8,64,128]{3,2,1,0:T(8,128)(2,1)} %broadcast_in_dim.5), calls=%async_computation.1 | async-start | bytes 2097152 | tf_op jit(solution)/shard_map/all_to_all | solution.py:190
  47.4 5.6 %soft.1 = (bf16[192,128]{1,0:T(8,128)(2,1)}, bf16[192,128]{1,0:T(8,128)(2,1)}, bf16[192,128]{1,0:T(8,128)(2,1)}, bf16[192,128]{1,0:T(8,128)(2,1)}, f32[192,128]{1,0:T(8,128)}, /*index=5*/f32[8,384]{1,0:T(8,128)}) custom-call(s32[1,8]{1,0:T(1,128)} %len_ref.3, bf16[192,1024]{1,0:T(8,128)(2,1)} %q_ref.3, bf16[192,1024]{1,0:T(8,128)(2,1)} %do_ref.3, ...), custom_call_target="tpu_custom_call" | custom-call | flops 3000000000 | bytes 2000000 | tf_op jit(solution)/shard_map/soft/pallas_call | solution.py:199
  53.1 1.3 collective-permute-start.4
  54.3 1.3 collective-permute-start.5
  55.6 1.3 collective-permute-start.6
  56.9 1.3 collective-permute-start.7
  58.2 13.7 %collective-permute-done.4.refs_1_ = bf16[192,128]{1,0:T(8,128)(2,1)S(1)} collective-permute-done((bf16[192,128]{1,0:T(8,128)(2,1)}, bf16[192,128]{1,0:T(8,128)(2,1)S(1)}, u32[]{:S(2)}, u32[]{:S(2)}) %collective-permute-start.4) | collective-permute-done | bytes 49184 | tf_op jit(solution)/shard_map/ppermute | solution.py:57
  72.0 1.2 collective-permute-done.5.refs_2_
  73.2 3.0 %collective-permute-done.6.refs_3_ = bf16[192,128]{1,0:T(8,128)(2,1)S(1)} collective-permute-done((bf16[192,128]{1,0:T(8,128)(2,1)}, bf16[192,128]{1,0:T(8,128)(2,1)S(1)}, u32[]{:S(2)}, u32[]{:S(2)}) %collective-permute-start.6) | collective-permute-done | bytes 49184 | tf_op jit(solution)/shard_map/ppermute | solution.py:57
  76.1 0.0 collective-permute-done.7.refs_4_
  76.1 0.0 all-to-all-done.1.own_ref
  76.1 1.9 %collective-permute-start.8 = (bf16[8,8,64,128]{3,2,1,0:T(8,128)(2,1)S(1)}, bf16[8,8,64,128]{3,2,1,0:T(8,128)(2,1)S(1)}, u32[]{:S(2)}, u32[]{:S(2)}) collective-permute-start(bf16[8,8,64,128]{3,2,1,0:T(8,128)(2,1)S(1)} %all-to-all-done.1.own_ref), channel_id=1, source_target_pairs={{0,32},{32,0},{1,33},{33,1},{2,34},{34,2},{3,35},{35,3},{4,36},{36... | collective-permute-start | bytes 3145736 | tf_op jit(solution)/shard_map/ppermute | solution.py:206
  78.1 2.6 %collective-permute-done.8.other_ref = bf16[8,8,64,128]{3,2,1,0:T(8,128)(2,1)S(1)} collective-permute-done((bf16[8,8,64,128]{3,2,1,0:T(8,128)(2,1)S(1)}, bf16[8,8,64,128]{3,2,1,0:T(8,128)(2,1)S(1)}, u32[]{:S(2)}, u32[]{:S(2)}) %collective-permute-start.8) | collective-permute-done | bytes 1048608 | tf_op jit(solution)/shard_map/ppermute | solution.py:206
  80.7 4.6 %all-gather.3.cloned.1.call-done = bf16[768,2048]{1,0:T(8,128)(2,1)} async-done(((bf16[192,2048]{1,0:T(8,128)(2,1)}), bf16[768,2048]{1,0:T(8,128)(2,1)}) %all-gather.3.cloned.1.call-update) | async-done | bytes 3145744 | tf_op jit(solution)/shard_map/all_gather | solution.py:184
  85.3 1.9 %copy-done = bf16[768,2048]{1,0:T(8,128)(2,1)S(1)} copy-done((bf16[768,2048]{1,0:T(8,128)(2,1)S(1)}, bf16[768,2048]{1,0:T(8,128)(2,1)}, u32[]{:S(2)}) %copy-start) | copy-done | bytes 3145752
  87.2 0.9 copy-done.2
  88.1 1.4 weight_grad.1
  89.4 1.9 %collective-permute-start.9 = (bf16[8,8,64,128]{3,2,1,0:T(8,128)(2,1)S(1)}, bf16[8,8,64,128]{3,2,1,0:T(8,128)(2,1)S(1)}, u32[]{:S(2)}, u32[]{:S(2)}) collective-permute-start(bf16[8,8,64,128]{3,2,1,0:T(8,128)(2,1)S(1)} %get-tuple-element.68), channel_id=1, source_target_pairs={{0,32},{32,0},{1,33},{33,1},{2,34},{34,2},{3,35},{35,3},{4,36},{36... | collective-permute-start | bytes 3145736 | tf_op jit(solution)/shard_map/ppermute | solution.py:210
  91.4 1.0 project.1.refs_9_
  92.4 1.6 collective-permute-done.9.b_ref
  94.0 1.2 add_halves.1
  95.2 9.6 %all-to-all-start.2 = ((bf16[8,8,64,128]{3,2,1,0:T(8,128)(2,1)}), bf16[8,8,64,128]{3,2,1,0:T(8,128)(2,1)S(1)}, u32[]{:S(2)}, u32[]{:S(2)}) async-start(bf16[8,8,64,128]{3,2,1,0:T(8,128)(2,1)} %add_halves.1), calls=%async_computation.2 | async-start | bytes 2097152 | tf_op jit(solution)/shard_map/all_to_all | solution.py:215
  104.8 4.1 %collective-permute-start.13 = (bf16[192,128]{1,0:T(8,128)(2,1)S(1)}, bf16[192,128]{1,0:T(8,128)(2,1)S(1)}, u32[]{:S(2)}, u32[]{:S(2)}) collective-permute-start(bf16[192,128]{1,0:T(8,128)(2,1)S(1)} %project.1.refs_9_), channel_id=1, source_target_pairs={{0,4},{4,8},{8,12},{12,16},{16,20},{20,24},{24,28},{1,5},{5,9},{9,... | collective-permute-start | bytes 147464 | tf_op jit(solution)/shard_map/ppermute | solution.py:53
  108.9 4.1 %collective-permute-start.12 = (bf16[192,128]{1,0:T(8,128)(2,1)S(1)}, bf16[192,128]{1,0:T(8,128)(2,1)S(1)}, u32[]{:S(2)}, u32[]{:S(2)}) collective-permute-start(bf16[192,128]{1,0:T(8,128)(2,1)S(1)} %project.1.refs_9_), channel_id=1, source_target_pairs={{0,8},{4,12},{8,16},{12,20},{16,24},{20,28},{1,9},{5,13},{9,17},{1... | collective-permute-start | bytes 147464 | tf_op jit(solution)/shard_map/ppermute | solution.py:53
  113.0 5.1 %collective-permute-start.11 = (bf16[192,128]{1,0:T(8,128)(2,1)S(1)}, bf16[192,128]{1,0:T(8,128)(2,1)S(1)}, u32[]{:S(2)}, u32[]{:S(2)}) collective-permute-start(bf16[192,128]{1,0:T(8,128)(2,1)S(1)} %project.1.refs_9_), channel_id=1, source_target_pairs={{0,12},{4,16},{8,20},{12,24},{16,28},{1,13},{5,17},{9,21},{13,25},... | collective-permute-start | bytes 147464 | tf_op jit(solution)/shard_map/ppermute | solution.py:53
  118.2 2.3 %collective-permute-start.10 = (bf16[192,128]{1,0:T(8,128)(2,1)S(1)}, bf16[192,128]{1,0:T(8,128)(2,1)S(1)}, u32[]{:S(2)}, u32[]{:S(2)}) collective-permute-start(bf16[192,128]{1,0:T(8,128)(2,1)S(1)} %project.1.refs_9_), channel_id=1, source_target_pairs={{0,16},{4,20},{8,24},{12,28},{1,17},{5,21},{9,25},{13,29},{2,18},{... | collective-permute-start | bytes 147464 | tf_op jit(solution)/shard_map/ppermute | solution.py:53
  120.4 0.0 collective-permute-done.13.refs_8_
  120.5 0.0 collective-permute-done.12.refs_7_
  120.5 0.0 collective-permute-done.11.refs_6_
  120.5 1.5 collective-permute-done.10.refs_5_
  122.0 0.0 copy-done.8
  122.0 0.6 copy-done.11
  122.6 8.4 %attend.1 = (bf16[192,1024]{1,0:T(8,128)(2,1)}, bf16[192,1024]{1,0:T(8,128)(2,1)}, bf16[192,128]{1,0:T(8,128)(2,1)}, bf16[192,128]{1,0:T(8,128)(2,1)}, bf16[192,...) custom-call(s32[1,8]{1,0:T(1,128)} %len_ref.3, bf16[192,1024]{1,0:T(8,128)(2,1)} %q_ref.3, ...), custom_call_target="tpu_custom_call" | custom-call | flops 6000000000 | bytes 4000000 | tf_op jit(solution)/shard_map/attend/pallas_call | solution.py:218
  131.0 0.0 all-to-all-done.2.parts_ref
  131.0 1.3 collective-permute-start.14
  132.3 1.3 collective-permute-start.15
  133.6 1.3 collective-permute-start.16
  134.9 1.3 collective-permute-start.17
  136.2 0.8 sum_blocks.2
  137.0 10.8 %all-to-all-start.3 = ((bf16[8,64,128]{2,1,0:T(8,128)(2,1)}), bf16[8,64,128]{2,1,0:T(8,128)(2,1)S(1)}, u32[]{:S(2)}, u32[]{:S(2)}) async-start(bf16[8,64,128]{2,1,0:T(8,128)(2,1)} %sum_blocks.2), calls=%async_computation.3 | async-start | bytes 262144 | tf_op jit(solution)/shard_map/all_to_all | solution.py:227
  147.8 0.0 collective-permute-done.14
  147.8 0.0 collective-permute-done.15
  147.8 0.0 collective-permute-done.16
  147.8 0.0 collective-permute-done.17
  147.8 1.6 multiply_convert_fusion
  149.4 7.5 %all-to-all-done.3.parts_ref = bf16[8,64,128]{2,1,0:T(8,128)(2,1)S(1)} async-done(((bf16[8,64,128]{2,1,0:T(8,128)(2,1)}), bf16[8,64,128]{2,1,0:T(8,128)(2,1)S(1)}, u32[]{:S(2)}, u32[]{:S(2)}) %all-to-all-start.3) | async-done | bytes 131104 | tf_op jit(solution)/shard_map/all_to_all | solution.py:227
  156.8 0.6 sum_blocks.3
  (17 shorter events, 0.0 us)
Async XLA Ops:
  7.2 78.1 %all-gather.3.cloned.1.call-start = ((), (), s32[]{:S(2)}) async-start(), calls=%async_computation.4 | async-start | bytes 3932160 | tf_op jit(solution)/shard_map/all_gather | solution.py:184
  9.3 31.6 %all-to-all-start = ((bf16[8,64,128]{2,1,0:T(8,128)(2,1)}), bf16[8,64,128]{2,1,0:T(8,128)(2,1)S(1)}, u32[]{:S(2)}, u32[]{:S(2)}) async-start(bf16[8,64,128]{2,1,0:T(8,128)(2,1)} %broadcast_in_dim.4), calls=%async_computation | async-start | bytes 262144 | tf_op jit(solution)/shard_map/all_to_all | solution.py:47
  19.0 19.9 %collective-permute-start.2 = (bf16[192,128]{1,0:T(8,128)(2,1)}, bf16[192,128]{1,0:T(8,128)(2,1)S(1)}, u32[]{:S(2)}, u32[]{:S(2)}) collective-permute-start(bf16[192,128]{1,0:T(8,128)(2,1)} %refs_4_.1), channel_id=1, source_target_pairs={{0,8},{4,12},{8,16},{12,20},{16,24},{20,28},{1,9},{5,13},{9,17},{1... | collective-permute-start | bytes 147464 | tf_op jit(solution)/shard_map/ppermute | solution.py:53
  25.0 13.8 %collective-permute-start.1 = (bf16[192,128]{1,0:T(8,128)(2,1)}, bf16[192,128]{1,0:T(8,128)(2,1)S(1)}, u32[]{:S(2)}, u32[]{:S(2)}) collective-permute-start(bf16[192,128]{1,0:T(8,128)(2,1)} %refs_4_.1), channel_id=1, source_target_pairs={{0,12},{4,16},{8,20},{12,24},{16,28},{1,13},{5,17},{9,21},{13,25},... | collective-permute-start | bytes 147464 | tf_op jit(solution)/shard_map/ppermute | solution.py:53
  33.3 5.6 %collective-permute-start = (bf16[192,128]{1,0:T(8,128)(2,1)}, bf16[192,128]{1,0:T(8,128)(2,1)S(1)}, u32[]{:S(2)}, u32[]{:S(2)}) collective-permute-start(bf16[192,128]{1,0:T(8,128)(2,1)} %refs_4_.1), channel_id=1, source_target_pairs={{0,16},{4,20},{8,24},{12,28},{1,17},{5,21},{9,25},{13,29},{2,18},{... | collective-permute-start | bytes 147464 | tf_op jit(solution)/shard_map/ppermute | solution.py:53
  36.4 4.5 %collective-permute-start.3 = (bf16[192,128]{1,0:T(8,128)(2,1)}, bf16[192,128]{1,0:T(8,128)(2,1)S(1)}, u32[]{:S(2)}, u32[]{:S(2)}) collective-permute-start(bf16[192,128]{1,0:T(8,128)(2,1)} %refs_4_.1), channel_id=1, source_target_pairs={{0,4},{4,8},{8,12},{12,16},{16,20},{20,24},{24,28},{1,5},{5,9},{9,... | collective-permute-start | bytes 147464 | tf_op jit(solution)/shard_map/ppermute | solution.py:53
  38.9 8.5 %copy-start.4 = (bf16[192,128]{1,0:T(8,128)(2,1)}, bf16[192,128]{1,0:T(8,128)(2,1)S(1)}, u32[]{:S(2)}) copy-start(bf16[192,128]{1,0:T(8,128)(2,1)S(1)} %collective-permute-done.2.refs_2_) | copy-start | bytes 147460
  38.9 8.5 %copy-start.5 = (bf16[192,128]{1,0:T(8,128)(2,1)}, bf16[192,128]{1,0:T(8,128)(2,1)S(1)}, u32[]{:S(2)}) copy-start(bf16[192,128]{1,0:T(8,128)(2,1)S(1)} %collective-permute-done.1.refs_1_) | copy-start | bytes 147460
  38.9 8.5 %copy-start.6 = (bf16[192,128]{1,0:T(8,128)(2,1)}, bf16[192,128]{1,0:T(8,128)(2,1)S(1)}, u32[]{:S(2)}) copy-start(bf16[192,128]{1,0:T(8,128)(2,1)S(1)} %collective-permute-done.refs_0_) | copy-start | bytes 147460
  40.9 6.5 %copy-start.7 = (bf16[192,128]{1,0:T(8,128)(2,1)}, bf16[192,128]{1,0:T(8,128)(2,1)S(1)}, u32[]{:S(2)}) copy-start(bf16[192,128]{1,0:T(8,128)(2,1)S(1)} %collective-permute-done.3.refs_3_) | copy-start | bytes 147460
  42.2 34.0 %all-to-all-start.1 = ((bf16[8,8,64,128]{3,2,1,0:T(8,128)(2,1)}), bf16[8,8,64,128]{3,2,1,0:T(8,128)(2,1)S(1)}, u32[]{:S(2)}, u32[]{:S(2)}) async-start(bf16[8,8,64,128]{3,2,1,0:T(8,128)(2,1)} %broadcast_in_dim.5), calls=%async_computation.1 | async-start | bytes 2097152 | tf_op jit(solution)/shard_map/all_to_all | solution.py:190
  53.1 18.9 %collective-permute-start.4 = (bf16[192,128]{1,0:T(8,128)(2,1)}, bf16[192,128]{1,0:T(8,128)(2,1)S(1)}, u32[]{:S(2)}, u32[]{:S(2)}) collective-permute-start(bf16[192,128]{1,0:T(8,128)(2,1)} %get-tuple-element.53), channel_id=1, source_target_pairs={{4,0},{8,4},{12,8},{16,12},{20,16},{24,20},{28,24},{5,1},{9,5},{13... | collective-permute-start | bytes 147464 | tf_op jit(solution)/shard_map/ppermute | solution.py:57
  54.3 18.8 %collective-permute-start.5 = (bf16[192,128]{1,0:T(8,128)(2,1)}, bf16[192,128]{1,0:T(8,128)(2,1)S(1)}, u32[]{:S(2)}, u32[]{:S(2)}) collective-permute-start(bf16[192,128]{1,0:T(8,128)(2,1)} %get-tuple-element.54), channel_id=1, source_target_pairs={{8,0},{12,4},{16,8},{20,12},{24,16},{28,20},{9,1},{13,5},{17,9},{2... | collective-permute-start | bytes 147464 | tf_op jit(solution)/shard_map/ppermute | solution.py:57
  55.6 20.5 %collective-permute-start.6 = (bf16[192,128]{1,0:T(8,128)(2,1)}, bf16[192,128]{1,0:T(8,128)(2,1)S(1)}, u32[]{:S(2)}, u32[]{:S(2)}) collective-permute-start(bf16[192,128]{1,0:T(8,128)(2,1)} %get-tuple-element.55), channel_id=1, source_target_pairs={{12,0},{16,4},{20,8},{24,12},{28,16},{13,1},{17,5},{21,9},{25,13},... | collective-permute-start | bytes 147464 | tf_op jit(solution)/shard_map/ppermute | solution.py:57
  56.9 19.2 %collective-permute-start.7 = (bf16[192,128]{1,0:T(8,128)(2,1)}, bf16[192,128]{1,0:T(8,128)(2,1)S(1)}, u32[]{:S(2)}, u32[]{:S(2)}) collective-permute-start(bf16[192,128]{1,0:T(8,128)(2,1)} %get-tuple-element.56), channel_id=1, source_target_pairs={{16,0},{20,4},{24,8},{28,12},{17,1},{21,5},{25,9},{29,13},{18,2},{... | collective-permute-start | bytes 147464 | tf_op jit(solution)/shard_map/ppermute | solution.py:57
  76.1 4.5 %collective-permute-start.8 = (bf16[8,8,64,128]{3,2,1,0:T(8,128)(2,1)S(1)}, bf16[8,8,64,128]{3,2,1,0:T(8,128)(2,1)S(1)}, u32[]{:S(2)}, u32[]{:S(2)}) collective-permute-start(bf16[8,8,64,128]{3,2,1,0:T(8,128)(2,1)S(1)} %all-to-all-done.1.own_ref), channel_id=1, source_target_pairs={{0,32},{32,0},{1,33},{33,1},{2,34},{34,2},{3,35},{35,3},{4,36},{36... | collective-permute-start | bytes 3145736 | tf_op jit(solution)/shard_map/ppermute | solution.py:206
  85.3 1.9 %copy-start = (bf16[768,2048]{1,0:T(8,128)(2,1)S(1)}, bf16[768,2048]{1,0:T(8,128)(2,1)}, u32[]{:S(2)}) copy-start(bf16[768,2048]{1,0:T(8,128)(2,1)} %all-gather.3.cloned.1.call-done) | copy-start | bytes 9437188
  87.2 0.9 copy-start.2
  88.1 3.3 %copy-start.1 = (bf16[768,2048]{1,0:T(8,128)(2,1)S(1)}, bf16[768,2048]{1,0:T(8,128)(2,1)}, u32[]{:S(2)}) copy-start(bf16[768,2048]{1,0:T(8,128)(2,1)} %all-gather.3.cloned.1.call-done) | copy-start | bytes 9437188
  89.4 4.6 %collective-permute-start.9 = (bf16[8,8,64,128]{3,2,1,0:T(8,128)(2,1)S(1)}, bf16[8,8,64,128]{3,2,1,0:T(8,128)(2,1)S(1)}, u32[]{:S(2)}, u32[]{:S(2)}) collective-permute-start(bf16[8,8,64,128]{3,2,1,0:T(8,128)(2,1)S(1)} %get-tuple-element.68), channel_id=1, source_target_pairs={{0,32},{32,0},{1,33},{33,1},{2,34},{34,2},{3,35},{35,3},{4,36},{36... | collective-permute-start | bytes 3145736 | tf_op jit(solution)/shard_map/ppermute | solution.py:210
  92.3 29.7 %copy-start.3 = (bf16[192,128]{1,0:T(8,128)(2,1)}, bf16[192,128]{1,0:T(8,128)(2,1)S(1)}, u32[]{:S(2)}) copy-start(bf16[192,128]{1,0:T(8,128)(2,1)S(1)} %project.1.refs_9_) | copy-start | bytes 147460
  95.2 35.8 %all-to-all-start.2 = ((bf16[8,8,64,128]{3,2,1,0:T(8,128)(2,1)}), bf16[8,8,64,128]{3,2,1,0:T(8,128)(2,1)S(1)}, u32[]{:S(2)}, u32[]{:S(2)}) async-start(bf16[8,8,64,128]{3,2,1,0:T(8,128)(2,1)} %add_halves.1), calls=%async_computation.2 | async-start | bytes 2097152 | tf_op jit(solution)/shard_map/all_to_all | solution.py:215
  104.8 15.6 %collective-permute-start.13 = (bf16[192,128]{1,0:T(8,128)(2,1)S(1)}, bf16[192,128]{1,0:T(8,128)(2,1)S(1)}, u32[]{:S(2)}, u32[]{:S(2)}) collective-permute-start(bf16[192,128]{1,0:T(8,128)(2,1)S(1)} %project.1.refs_9_), channel_id=1, source_target_pairs={{0,4},{4,8},{8,12},{12,16},{16,20},{20,24},{24,28},{1,5},{5,9},{9,... | collective-permute-start | bytes 147464 | tf_op jit(solution)/shard_map/ppermute | solution.py:53
  108.9 11.5 %collective-permute-start.12 = (bf16[192,128]{1,0:T(8,128)(2,1)S(1)}, bf16[192,128]{1,0:T(8,128)(2,1)S(1)}, u32[]{:S(2)}, u32[]{:S(2)}) collective-permute-start(bf16[192,128]{1,0:T(8,128)(2,1)S(1)} %project.1.refs_9_), channel_id=1, source_target_pairs={{0,8},{4,12},{8,16},{12,20},{16,24},{20,28},{1,9},{5,13},{9,17},{1... | collective-permute-start | bytes 147464 | tf_op jit(solution)/shard_map/ppermute | solution.py:53
  113.0 7.5 %collective-permute-start.11 = (bf16[192,128]{1,0:T(8,128)(2,1)S(1)}, bf16[192,128]{1,0:T(8,128)(2,1)S(1)}, u32[]{:S(2)}, u32[]{:S(2)}) collective-permute-start(bf16[192,128]{1,0:T(8,128)(2,1)S(1)} %project.1.refs_9_), channel_id=1, source_target_pairs={{0,12},{4,16},{8,20},{12,24},{16,28},{1,13},{5,17},{9,21},{13,25},... | collective-permute-start | bytes 147464 | tf_op jit(solution)/shard_map/ppermute | solution.py:53
  118.2 3.8 %collective-permute-start.10 = (bf16[192,128]{1,0:T(8,128)(2,1)S(1)}, bf16[192,128]{1,0:T(8,128)(2,1)S(1)}, u32[]{:S(2)}, u32[]{:S(2)}) collective-permute-start(bf16[192,128]{1,0:T(8,128)(2,1)S(1)} %project.1.refs_9_), channel_id=1, source_target_pairs={{0,16},{4,20},{8,24},{12,28},{1,17},{5,21},{9,25},{13,29},{2,18},{... | collective-permute-start | bytes 147464 | tf_op jit(solution)/shard_map/ppermute | solution.py:53
  120.5 1.5 copy-start.8
  120.5 1.5 copy-start.9
  120.5 1.5 copy-start.10
  122.0 0.6 copy-start.11
  131.0 16.8 %collective-permute-start.14 = (bf16[192,128]{1,0:T(8,128)(2,1)}, bf16[192,128]{1,0:T(8,128)(2,1)S(1)}, u32[]{:S(2)}, u32[]{:S(2)}) collective-permute-start(bf16[192,128]{1,0:T(8,128)(2,1)} %get-tuple-element.81), channel_id=1, source_target_pairs={{4,0},{8,4},{12,8},{16,12},{20,16},{24,20},{28,24},{5,1},{9,5},{13... | collective-permute-start | bytes 147464 | tf_op jit(solution)/shard_map/ppermute | solution.py:57
  132.3 15.5 %collective-permute-start.15 = (bf16[192,128]{1,0:T(8,128)(2,1)}, bf16[192,128]{1,0:T(8,128)(2,1)S(1)}, u32[]{:S(2)}, u32[]{:S(2)}) collective-permute-start(bf16[192,128]{1,0:T(8,128)(2,1)} %get-tuple-element.82), channel_id=1, source_target_pairs={{8,0},{12,4},{16,8},{20,12},{24,16},{28,20},{9,1},{13,5},{17,9},{2... | collective-permute-start | bytes 147464 | tf_op jit(solution)/shard_map/ppermute | solution.py:57
  133.6 14.2 %collective-permute-start.16 = (bf16[192,128]{1,0:T(8,128)(2,1)}, bf16[192,128]{1,0:T(8,128)(2,1)S(1)}, u32[]{:S(2)}, u32[]{:S(2)}) collective-permute-start(bf16[192,128]{1,0:T(8,128)(2,1)} %get-tuple-element.83), channel_id=1, source_target_pairs={{12,0},{16,4},{20,8},{24,12},{28,16},{13,1},{17,5},{21,9},{25,13},... | collective-permute-start | bytes 147464 | tf_op jit(solution)/shard_map/ppermute | solution.py:57
  134.9 12.9 %collective-permute-start.17 = (bf16[192,128]{1,0:T(8,128)(2,1)}, bf16[192,128]{1,0:T(8,128)(2,1)S(1)}, u32[]{:S(2)}, u32[]{:S(2)}) collective-permute-start(bf16[192,128]{1,0:T(8,128)(2,1)} %get-tuple-element.84), channel_id=1, source_target_pairs={{16,0},{20,4},{24,8},{28,12},{17,1},{21,5},{25,9},{29,13},{18,2},{... | collective-permute-start | bytes 147464 | tf_op jit(solution)/shard_map/ppermute | solution.py:57
  137.0 19.9 %all-to-all-start.3 = ((bf16[8,64,128]{2,1,0:T(8,128)(2,1)}), bf16[8,64,128]{2,1,0:T(8,128)(2,1)S(1)}, u32[]{:S(2)}, u32[]{:S(2)}) async-start(bf16[8,64,128]{2,1,0:T(8,128)(2,1)} %sum_blocks.2), calls=%async_computation.3 | async-start | bytes 262144 | tf_op jit(solution)/shard_map/all_to_all | solution.py:227
Sparse Core Ops, SparseCore 0:
  10.1 75.1 all-gather.2

commit v8 on v7

--- a/solution.py
+++ b/solution.py
@@ -97,16 +97,31 @@
     out_ref[...] = (a_ref[...].astype(F32) + b_ref[...].astype(F32)).astype(BF16)
 
 
-def sum_blocks(parts_ref, out_ref):
-    total = parts_ref[0].astype(F32)
-    for i in range(1, parts_ref.shape[0]):
-        total = total + parts_ref[i].astype(F32)
-    out_ref[...] = total.astype(out_ref.dtype)
+def sum_of(parts):
+    total = parts[0].astype(F32)
+    for part in parts[1:]:
+        total = total + part.astype(F32)
+    return total
+
+
+def pack(parts_ref, dk_ref, out_ref):
+    for ctx in range(8):
+        out_ref[ctx, :64] = sum_of([parts_ref[i, ctx] for i in range(8)]).astype(BF16)
+        out_ref[ctx, 64:] = dk_ref[ctx]
+
+
+def unpack(parts_ref, weight_ref, key_ref):
+    weight_ref[...] = sum_of([parts_ref[i, :64] for i in range(8)])
+    key_ref[...] = (sum_of([parts_ref[i, 64:] for i in range(8)]) * F32(SCALE)).astype(BF16)
 
 
 def rows_of_heads(wide_ref, rows_ref):
     for h in range(GROUP):
         rows_ref[h * TOK : (h + 1) * TOK] = wide_ref[:, h * HEAD_DIM : (h + 1) * HEAD_DIM]
+
+
+def slot_owner(slot):
+    return lax.rem(lax.axis_index("ctx") - (REACH - slot) + 8, 8)
 
 
 def fill_bias(len_ref, bias):
@@ -120,7 +135,7 @@
         first = jnp.where(query >= end, end, first)
     offset = lax.broadcasted_iota(jnp.int32, (TOK, LANES), 0)
     for slot in range(REACH + 1):
-        key = lax.rem(ctx - (REACH - slot) + 8, 8) * TOK + offset
+        key = slot_owner(slot) * TOK + offset
         bias[slot * TOK : (slot + 1) * TOK] = jnp.where(
             (key >= first) & (key <= query), F32(0.0), F32(-1e30)
         )
@@ -150,8 +165,8 @@
 
 
 def attend(len_ref, q_ref, do_ref, stat_ref, *refs):
-    k_refs, v_refs, (att_ref, dq_ref), dk_refs = refs[:5], refs[5:10], refs[10:12], refs[12:17]
-    q_rows, do_rows, bias, dscores, keys, values = refs[17:]
+    k_refs, v_refs, (att_ref, dq_ref, dk_ref) = refs[:5], refs[5:10], refs[10:13]
+    q_rows, do_rows, bias, dscores, keys, values = refs[13:]
     rows_of_heads(q_ref, q_rows)
     rows_of_heads(do_ref, do_rows)
     for slot in range(REACH + 1):
@@ -175,9 +190,10 @@
             head = slice((i * HEADS_AT_ONCE + j) * HEAD_DIM, (i * HEADS_AT_ONCE + j + 1) * HEAD_DIM)
             att_ref[:, head] = att[j * TOK : (j + 1) * TOK]
             dq_ref[:, head] = dq[j * TOK : (j + 1) * TOK]
-    total = jnp.dot(dscores[...], q_rows[...], preferred_element_type=F32)
-    for slot, ref in enumerate(dk_refs):
-        ref[...] = total[slot * TOK : (slot + 1) * TOK].astype(ref.dtype)
+    total = jnp.dot(dscores[...], q_rows[...], preferred_element_type=F32).astype(BF16)
+    dk_ref[...] = jnp.zeros_like(dk_ref)
+    for slot in range(REACH + 1):
+        dk_ref[slot_owner(slot)] = total[slot * TOK : (slot + 1) * TOK]
 
 
 def shards(queries, key_states, normed, value_weight, grad_out, lengths):
@@ -215,17 +231,15 @@
     partial = lax.all_to_all(partial, CHIPS, 0, 0, tiled=True)
 
     wide = shape((TOK, GROUP * HEAD_DIM))
-    attended, grad_query, *dk = call(
-        attend, (wide, wide) + (block,) * REACH + (own,), 13, 6 * 10**9, 4 * 10**6,
+    attended, grad_query, dk = call(
+        attend, (wide, wide, shape((8, TOK, HEAD_DIM))), 13, 6 * 10**9, 4 * 10**6,
         (rows, rows, bias, pairs, window, window), smem=1, vmem=56,
     )(lengths, queries, grad_out, stats, *keys, *values)
-    partial, dk = lax.optimization_barrier((partial, dk))
-    dk = [dk[REACH]] + [from_ahead(dk[REACH - d], d) for d in range(1, REACH + 1)]
-    grad_key = (sum(part.astype(F32) for part in dk) * F32(SCALE)).astype(BF16)
-
-    partial = call(sum_blocks, shape((8, 64, HEAD_DIM)), 1, 10**6, 10**6)(partial)
-    partial = lax.all_to_all(partial, "ctx", 0, 0, tiled=True)
-    grad_weight = call(sum_blocks, shape((64, HEAD_DIM), F32), 1, 10**6, 10**6)(partial)
+    parts = call(pack, shape((8, 64 + TOK, HEAD_DIM)), 2, 10**6, 2 * 10**6)(partial, dk)
+    parts = lax.all_to_all(parts, "ctx", 0, 0, tiled=True)
+    grad_weight, grad_key = call(
+        unpack, (shape((64, HEAD_DIM), F32), block), 1, 10**6, 10**6
+    )(parts)
     return attended, grad_query, grad_key, grad_weight
 
 

time: 168 us -> 164 us (0.976); the launches traced: 164 us -> 163 us
  blocking collectives: 0 us -> 23.5 us
  starting transfers between devices: 85 us -> 69 us
  waiting for transfers between devices: 38.4 us -> 30.9 us
    all_to_all x0 -> x1, blocking collectives: none -> 23.5 us  [shards(): parts = lax.all_to_all(parts, 'ctx', 0, 0, tiled=True)]
    all_to_all x1 -> x0, starting transfers between devices: 10.8 us -> none  [shards(): partial = lax.all_to_all(partial, 'ctx', 0, 0, tiled=True)]
    all_to_all x1 -> x0, waiting for transfers between devices: 7.49 us -> none  [shards(): partial = lax.all_to_all(partial, 'ctx', 0, 0, tiled=True)]
    ppermute x8 -> x4, starting transfers between devices: 10.3 us -> 5.16 us  [from_ahead(): lax.ppermute(block, 'ctx', [(i + distance, i) for i in range(8 - distance)])]
    unnamed x24 -> x26, local copies, waits for them, and re-layouts: 3.41 us -> 4.41 us
    ppermute x8 -> x4, waiting for transfers between devices: 17.9 us -> 17.9 us  [from_ahead(): lax.ppermute(block, 'ctx', [(i + distance, i) for i in range(8 - distance)])]
  transfers between devices with their start and end apart: 23 -> 18, of which waited for: 9 -> 8; matrix products, arithmetic and copies ran while one was open for 3% -> 2% of each run, Pallas kernels for 10% -> 9%
where the time goes in v8:
time: 164 us; the launch traced here: 163 us
  starting transfers between devices  69 us (42%)
  waiting for transfers between devices  30.9 us (19%)
  blocking collectives  23.5 us (14%)
  Pallas kernels  18.5 us (11%)
  between operations  14.3 us (9%)
  local copies, waits for them, and re-layouts  7.04 us (4%)
    ppermute x8, starting transfers between devices, from_behind(): lax.ppermute(block, 'ctx', [(i, i + distance) for i in range(8 - distance)])  35.5 us
    all_to_all x1, blocking collectives, shards(): parts = lax.all_to_all(parts, 'ctx', 0, 0, tiled=True)  23.5 us
    ppermute x4, waiting for transfers between devices, from_ahead(): lax.ppermute(block, 'ctx', [(i + distance, i) for i in range(8 - distance)])  17.9 us
    all_to_all x1, starting transfers between devices, to_all(): lax.all_to_all(jnp.broadcast_to(block[None], (copies,) + block.shape), ax...  9.67 us
    all_to_all x1, starting transfers between devices, shards(): partial = lax.all_to_all(partial, CHIPS, 0, 0, tiled=True)  9.62 us
    pallas_call x1, Pallas kernels, shards(): call(attend, (wide, wide, shape((8, TOK, HEAD_DIM))), 13, 6 * 10 ** 9, 4...  8.53 us
    pallas_call x1, Pallas kernels, shards(): call(soft, (block,) * REACH + (own, shape((8, LANES), F32)), 7, 3 * 10 **...  5.62 us
    all_to_all x1, starting transfers between devices, shards(): weight = lax.all_to_all(spread, 'ctx', 0, 0, tiled=True)  5.25 us
  transfers between devices with their start and end apart: 18, of which 8 were waited for; matrix products, arithmetic and copies ran while one was open for 2% of the time, Pallas kernels for 9%

profile of v8, /device:TPU:56, one launch (start us, length us, event | category | flops | bytes accessed | tf_op | source)
XLA Modules:
  0.0 163.3 jit_solution(11629511467540880976)
XLA Ops:
  7.2 0.0 all-gather.3.cloned.1.call-start
  7.2 0.7 all-gather.3.cloned.1.call-update
  7.9 1.4 broadcast_in_dim.4
  9.3 9.7 %all-to-all-start = ((bf16[8,64,128]{2,1,0:T(8,128)(2,1)}), bf16[8,64,128]{2,1,0:T(8,128)(2,1)S(1)}, u32[]{:S(2)}, u32[]{:S(2)}) async-start(bf16[8,64,128]{2,1,0:T(8,128)(2,1)} %broadcast_in_dim.4), calls=%async_computation | async-start | bytes 262144 | tf_op jit(solution)/shard_map/all_to_all | solution.py:47
  19.0 6.1 %collective-permute-start.2 = (bf16[192,128]{1,0:T(8,128)(2,1)}, bf16[192,128]{1,0:T(8,128)(2,1)S(1)}, u32[]{:S(2)}, u32[]{:S(2)}) collective-permute-start(bf16[192,128]{1,0:T(8,128)(2,1)} %refs_4_.1), channel_id=1, source_target_pairs={{0,8},{4,12},{8,16},{12,20},{16,24},{20,28},{1,9},{5,13},{9,17},{1... | collective-permute-start | bytes 147464 | tf_op jit(solution)/shard_map/ppermute | solution.py:53
  25.0 8.2 %collective-permute-start.1 = (bf16[192,128]{1,0:T(8,128)(2,1)}, bf16[192,128]{1,0:T(8,128)(2,1)S(1)}, u32[]{:S(2)}, u32[]{:S(2)}) collective-permute-start(bf16[192,128]{1,0:T(8,128)(2,1)} %refs_4_.1), channel_id=1, source_target_pairs={{0,12},{4,16},{8,20},{12,24},{16,28},{1,13},{5,17},{9,21},{13,25},... | collective-permute-start | bytes 147464 | tf_op jit(solution)/shard_map/ppermute | solution.py:53
  33.3 3.1 %collective-permute-start = (bf16[192,128]{1,0:T(8,128)(2,1)}, bf16[192,128]{1,0:T(8,128)(2,1)S(1)}, u32[]{:S(2)}, u32[]{:S(2)}) collective-permute-start(bf16[192,128]{1,0:T(8,128)(2,1)} %refs_4_.1), channel_id=1, source_target_pairs={{0,16},{4,20},{8,24},{12,28},{1,17},{5,21},{9,25},{13,29},{2,18},{... | collective-permute-start | bytes 147464 | tf_op jit(solution)/shard_map/ppermute | solution.py:53
  36.4 2.5 %collective-permute-start.3 = (bf16[192,128]{1,0:T(8,128)(2,1)}, bf16[192,128]{1,0:T(8,128)(2,1)S(1)}, u32[]{:S(2)}, u32[]{:S(2)}) collective-permute-start(bf16[192,128]{1,0:T(8,128)(2,1)} %refs_4_.1), channel_id=1, source_target_pairs={{0,4},{4,8},{8,12},{12,16},{16,20},{20,24},{24,28},{1,5},{5,9},{9,... | collective-permute-start | bytes 147464 | tf_op jit(solution)/shard_map/ppermute | solution.py:53
  38.9 0.0 collective-permute-done.2.refs_2_
  38.9 0.0 copy-start.5
  38.9 0.0 collective-permute-done.1.refs_1_
  38.9 0.0 copy-start.6
  38.9 0.0 collective-permute-done.refs_0_
  38.9 0.0 copy-start.7
  38.9 2.0 %collective-permute-done.3.refs_3_ = bf16[192,128]{1,0:T(8,128)(2,1)S(1)} collective-permute-done((bf16[192,128]{1,0:T(8,128)(2,1)}, bf16[192,128]{1,0:T(8,128)(2,1)S(1)}, u32[]{:S(2)}, u32[]{:S(2)}) %collective-permute-start.3) | collective-permute-done | bytes 49184 | tf_op jit(solution)/shard_map/ppermute | solution.py:53
  40.9 0.0 all-to-all-done
  40.9 1.2 broadcast_in_dim.5
  42.2 5.2 %all-to-all-start.1 = ((bf16[8,8,64,128]{3,2,1,0:T(8,128)(2,1)}), bf16[8,8,64,128]{3,2,1,0:T(8,128)(2,1)S(1)}, u32[]{:S(2)}, u32[]{:S(2)}) async-start(bf16[8,8,64,128]{3,2,1,0:T(8,128)(2,1)} %broadcast_in_dim.5), calls=%async_computation.1 | async-start | bytes 2097152 | tf_op jit(solution)/shard_map/all_to_all | solution.py:206
  47.4 0.0 copy-done.5
  47.4 0.0 copy-done.6
  47.4 0.0 copy-done.7
  47.4 0.0 copy-done.8
  47.4 5.6 %soft.1 = (bf16[192,128]{1,0:T(8,128)(2,1)}, bf16[192,128]{1,0:T(8,128)(2,1)}, bf16[192,128]{1,0:T(8,128)(2,1)}, bf16[192,128]{1,0:T(8,128)(2,1)}, f32[192,128]{1,0:T(8,128)}, /*index=5*/f32[8,384]{1,0:T(8,128)}) custom-call(s32[1,8]{1,0:T(1,128)} %len_ref.3, bf16[192,1024]{1,0:T(8,128)(2,1)} %q_ref.3, bf16[192,1024]{1,0:T(8,128)(2,1)} %do_ref.3, ...), custom_call_target="tpu_custom_call" | custom-call | flops 3000000000 | bytes 2000000 | tf_op jit(solution)/shard_map/soft/pallas_call | solution.py:215
  53.1 1.3 collective-permute-start.4
  54.4 1.3 collective-permute-start.5
  55.7 1.3 collective-permute-start.6
  57.0 1.3 collective-permute-start.7
  58.3 13.7 %collective-permute-done.4.refs_1_ = bf16[192,128]{1,0:T(8,128)(2,1)S(1)} collective-permute-done((bf16[192,128]{1,0:T(8,128)(2,1)}, bf16[192,128]{1,0:T(8,128)(2,1)S(1)}, u32[]{:S(2)}, u32[]{:S(2)}) %collective-permute-start.4) | collective-permute-done | bytes 49184 | tf_op jit(solution)/shard_map/ppermute | solution.py:57
  72.0 1.2 collective-permute-done.5.refs_2_
  73.2 3.0 %collective-permute-done.6.refs_3_ = bf16[192,128]{1,0:T(8,128)(2,1)S(1)} collective-permute-done((bf16[192,128]{1,0:T(8,128)(2,1)}, bf16[192,128]{1,0:T(8,128)(2,1)S(1)}, u32[]{:S(2)}, u32[]{:S(2)}) %collective-permute-start.6) | collective-permute-done | bytes 49184 | tf_op jit(solution)/shard_map/ppermute | solution.py:57
  76.1 0.0 collective-permute-done.7.refs_4_
  76.1 0.0 all-to-all-done.1.own_ref
  76.1 1.9 %collective-permute-start.8 = (bf16[8,8,64,128]{3,2,1,0:T(8,128)(2,1)S(1)}, bf16[8,8,64,128]{3,2,1,0:T(8,128)(2,1)S(1)}, u32[]{:S(2)}, u32[]{:S(2)}) collective-permute-start(bf16[8,8,64,128]{3,2,1,0:T(8,128)(2,1)S(1)} %all-to-all-done.1.own_ref), channel_id=1, source_target_pairs={{0,32},{32,0},{1,33},{33,1},{2,34},{34,2},{3,35},{35,3},{4,36},{36... | collective-permute-start | bytes 3145736 | tf_op jit(solution)/shard_map/ppermute | solution.py:222
  78.1 2.6 %collective-permute-done.8.other_ref = bf16[8,8,64,128]{3,2,1,0:T(8,128)(2,1)S(1)} collective-permute-done((bf16[8,8,64,128]{3,2,1,0:T(8,128)(2,1)S(1)}, bf16[8,8,64,128]{3,2,1,0:T(8,128)(2,1)S(1)}, u32[]{:S(2)}, u32[]{:S(2)}) %collective-permute-start.8) | collective-permute-done | bytes 1048608 | tf_op jit(solution)/shard_map/ppermute | solution.py:222
  80.7 4.6 %all-gather.3.cloned.1.call-done = bf16[768,2048]{1,0:T(8,128)(2,1)} async-done(((bf16[192,2048]{1,0:T(8,128)(2,1)}), bf16[768,2048]{1,0:T(8,128)(2,1)}) %all-gather.3.cloned.1.call-update) | async-done | bytes 3145744 | tf_op jit(solution)/shard_map/all_gather | solution.py:200
  85.3 1.9 %copy-done = bf16[768,2048]{1,0:T(8,128)(2,1)S(1)} copy-done((bf16[768,2048]{1,0:T(8,128)(2,1)S(1)}, bf16[768,2048]{1,0:T(8,128)(2,1)}, u32[]{:S(2)}) %copy-start) | copy-done | bytes 3145752
  87.2 0.9 copy-done.3
  88.1 1.4 weight_grad.1
  89.4 1.9 %collective-permute-start.9 = (bf16[8,8,64,128]{3,2,1,0:T(8,128)(2,1)S(1)}, bf16[8,8,64,128]{3,2,1,0:T(8,128)(2,1)S(1)}, u32[]{:S(2)}, u32[]{:S(2)}) collective-permute-start(bf16[8,8,64,128]{3,2,1,0:T(8,128)(2,1)S(1)} %get-tuple-element.60), channel_id=1, source_target_pairs={{0,32},{32,0},{1,33},{33,1},{2,34},{34,2},{3,35},{35,3},{4,36},{36... | collective-permute-start | bytes 3145736 | tf_op jit(solution)/shard_map/ppermute | solution.py:226
  91.3 0.0 copy-done.1
  91.4 1.0 project.1.refs_9_
  92.3 0.0 copy-start.4
  92.4 1.6 collective-permute-done.9.b_ref
  94.0 1.2 add_halves.1
  95.2 9.6 %all-to-all-start.2 = ((bf16[8,8,64,128]{3,2,1,0:T(8,128)(2,1)}), bf16[8,8,64,128]{3,2,1,0:T(8,128)(2,1)S(1)}, u32[]{:S(2)}, u32[]{:S(2)}) async-start(bf16[8,8,64,128]{3,2,1,0:T(8,128)(2,1)} %add_halves.1), calls=%async_computation.2 | async-start | bytes 2097152 | tf_op jit(solution)/shard_map/all_to_all | solution.py:231
  104.8 4.1 %collective-permute-start.13 = (bf16[192,128]{1,0:T(8,128)(2,1)S(1)}, bf16[192,128]{1,0:T(8,128)(2,1)S(1)}, u32[]{:S(2)}, u32[]{:S(2)}) collective-permute-start(bf16[192,128]{1,0:T(8,128)(2,1)S(1)} %project.1.refs_9_), channel_id=1, source_target_pairs={{0,4},{4,8},{8,12},{12,16},{16,20},{20,24},{24,28},{1,5},{5,9},{9,... | collective-permute-start | bytes 147464 | tf_op jit(solution)/shard_map/ppermute | solution.py:53
  108.9 4.1 %collective-permute-start.12 = (bf16[192,128]{1,0:T(8,128)(2,1)S(1)}, bf16[192,128]{1,0:T(8,128)(2,1)S(1)}, u32[]{:S(2)}, u32[]{:S(2)}) collective-permute-start(bf16[192,128]{1,0:T(8,128)(2,1)S(1)} %project.1.refs_9_), channel_id=1, source_target_pairs={{0,8},{4,12},{8,16},{12,20},{16,24},{20,28},{1,9},{5,13},{9,17},{1... | collective-permute-start | bytes 147464 | tf_op jit(solution)/shard_map/ppermute | solution.py:53
  113.0 5.1 %collective-permute-start.11 = (bf16[192,128]{1,0:T(8,128)(2,1)S(1)}, bf16[192,128]{1,0:T(8,128)(2,1)S(1)}, u32[]{:S(2)}, u32[]{:S(2)}) collective-permute-start(bf16[192,128]{1,0:T(8,128)(2,1)S(1)} %project.1.refs_9_), channel_id=1, source_target_pairs={{0,12},{4,16},{8,20},{12,24},{16,28},{1,13},{5,17},{9,21},{13,25},... | collective-permute-start | bytes 147464 | tf_op jit(solution)/shard_map/ppermute | solution.py:53
  118.1 2.3 %collective-permute-start.10 = (bf16[192,128]{1,0:T(8,128)(2,1)S(1)}, bf16[192,128]{1,0:T(8,128)(2,1)S(1)}, u32[]{:S(2)}, u32[]{:S(2)}) collective-permute-start(bf16[192,128]{1,0:T(8,128)(2,1)S(1)} %project.1.refs_9_), channel_id=1, source_target_pairs={{0,16},{4,20},{8,24},{12,28},{1,17},{5,21},{9,25},{13,29},{2,18},{... | collective-permute-start | bytes 147464 | tf_op jit(solution)/shard_map/ppermute | solution.py:53
  120.4 0.0 collective-permute-done.13.refs_8_
  120.4 0.0 copy-start.9
  120.5 0.0 collective-permute-done.12.refs_7_
  120.5 0.0 copy-start.10
  120.5 0.0 collective-permute-done.11.refs_6_
  120.5 0.0 copy-start.11
  120.5 1.5 collective-permute-done.10.refs_5_
  122.0 0.0 copy-done.4
  122.0 0.6 copy-done.12
  122.6 8.5 %attend.1 = (bf16[192,1024]{1,0:T(8,128)(2,1)}, bf16[192,1024]{1,0:T(8,128)(2,1)}, bf16[8,192,128]{2,1,0:T(8,128)(2,1)}) custom-call(s32[1,8]{1,0:T(1,128)} %len_ref.3, bf16[192,1024]{1,0:T(8,128)(2,1)} %q_ref.3, bf16[192,1024]{1,0:T(8,128)(2,1)} %do_ref.3, f32[8,384]{1,0:T(8,128)} %get-tuple-element.42.stat_ref, bf16[192,128]{1,0:T(8,128)(2,1)} %copy-done.7, ...), custom_call_target="tpu_custom_call" | custom-call | flops 6000000000 | bytes 4000000 | tf_op jit(solution)/shard_map/attend/pallas_call | solution.py:234
  131.1 0.0 all-to-all-done.2.parts_ref
  131.1 1.0 copy-done.2
  132.1 0.1 pack.1
  132.3 23.5 %all_to_all.20.parts_ref = bf16[8,256,128]{2,1,0:T(8,128)(2,1)S(1)} all-to-all(bf16[8,256,128]{2,1,0:T(8,128)(2,1)S(1)} %pack.1), channel_id=1, replica_groups=mesh['yh'=2,'x'=4,'core'=2,'ctx'=8,'mp'=4] {'ctx'}, dimensions={0} | all-to-all | bytes 1048576 | tf_op jit(solution)/shard_map/all_to_all | solution.py:239
  155.8 0.7 unpack.1
  (9 shorter events, 0.0 us)
Async XLA Ops:
  7.2 78.1 %all-gather.3.cloned.1.call-start = ((), (), s32[]{:S(2)}) async-start(), calls=%async_computation.4 | async-start | bytes 3932160 | tf_op jit(solution)/shard_map/all_gather | solution.py:200
  9.3 31.6 %all-to-all-start = ((bf16[8,64,128]{2,1,0:T(8,128)(2,1)}), bf16[8,64,128]{2,1,0:T(8,128)(2,1)S(1)}, u32[]{:S(2)}, u32[]{:S(2)}) async-start(bf16[8,64,128]{2,1,0:T(8,128)(2,1)} %broadcast_in_dim.4), calls=%async_computation | async-start | bytes 262144 | tf_op jit(solution)/shard_map/all_to_all | solution.py:47
  19.0 19.9 %collective-permute-start.2 = (bf16[192,128]{1,0:T(8,128)(2,1)}, bf16[192,128]{1,0:T(8,128)(2,1)S(1)}, u32[]{:S(2)}, u32[]{:S(2)}) collective-permute-start(bf16[192,128]{1,0:T(8,128)(2,1)} %refs_4_.1), channel_id=1, source_target_pairs={{0,8},{4,12},{8,16},{12,20},{16,24},{20,28},{1,9},{5,13},{9,17},{1... | collective-permute-start | bytes 147464 | tf_op jit(solution)/shard_map/ppermute | solution.py:53
  25.0 13.8 %collective-permute-start.1 = (bf16[192,128]{1,0:T(8,128)(2,1)}, bf16[192,128]{1,0:T(8,128)(2,1)S(1)}, u32[]{:S(2)}, u32[]{:S(2)}) collective-permute-start(bf16[192,128]{1,0:T(8,128)(2,1)} %refs_4_.1), channel_id=1, source_target_pairs={{0,12},{4,16},{8,20},{12,24},{16,28},{1,13},{5,17},{9,21},{13,25},... | collective-permute-start | bytes 147464 | tf_op jit(solution)/shard_map/ppermute | solution.py:53
  33.3 5.6 %collective-permute-start = (bf16[192,128]{1,0:T(8,128)(2,1)}, bf16[192,128]{1,0:T(8,128)(2,1)S(1)}, u32[]{:S(2)}, u32[]{:S(2)}) collective-permute-start(bf16[192,128]{1,0:T(8,128)(2,1)} %refs_4_.1), channel_id=1, source_target_pairs={{0,16},{4,20},{8,24},{12,28},{1,17},{5,21},{9,25},{13,29},{2,18},{... | collective-permute-start | bytes 147464 | tf_op jit(solution)/shard_map/ppermute | solution.py:53
  36.4 4.5 %collective-permute-start.3 = (bf16[192,128]{1,0:T(8,128)(2,1)}, bf16[192,128]{1,0:T(8,128)(2,1)S(1)}, u32[]{:S(2)}, u32[]{:S(2)}) collective-permute-start(bf16[192,128]{1,0:T(8,128)(2,1)} %refs_4_.1), channel_id=1, source_target_pairs={{0,4},{4,8},{8,12},{12,16},{16,20},{20,24},{24,28},{1,5},{5,9},{9,... | collective-permute-start | bytes 147464 | tf_op jit(solution)/shard_map/ppermute | solution.py:53
  38.9 8.5 %copy-start.5 = (bf16[192,128]{1,0:T(8,128)(2,1)}, bf16[192,128]{1,0:T(8,128)(2,1)S(1)}, u32[]{:S(2)}) copy-start(bf16[192,128]{1,0:T(8,128)(2,1)S(1)} %collective-permute-done.2.refs_2_) | copy-start | bytes 147460
  38.9 8.5 %copy-start.6 = (bf16[192,128]{1,0:T(8,128)(2,1)}, bf16[192,128]{1,0:T(8,128)(2,1)S(1)}, u32[]{:S(2)}) copy-start(bf16[192,128]{1,0:T(8,128)(2,1)S(1)} %collective-permute-done.1.refs_1_) | copy-start | bytes 147460
  38.9 8.5 %copy-start.7 = (bf16[192,128]{1,0:T(8,128)(2,1)}, bf16[192,128]{1,0:T(8,128)(2,1)S(1)}, u32[]{:S(2)}) copy-start(bf16[192,128]{1,0:T(8,128)(2,1)S(1)} %collective-permute-done.refs_0_) | copy-start | bytes 147460
  40.9 6.5 %copy-start.8 = (bf16[192,128]{1,0:T(8,128)(2,1)}, bf16[192,128]{1,0:T(8,128)(2,1)S(1)}, u32[]{:S(2)}) copy-start(bf16[192,128]{1,0:T(8,128)(2,1)S(1)} %collective-permute-done.3.refs_3_) | copy-start | bytes 147460
  42.2 34.0 %all-to-all-start.1 = ((bf16[8,8,64,128]{3,2,1,0:T(8,128)(2,1)}), bf16[8,8,64,128]{3,2,1,0:T(8,128)(2,1)S(1)}, u32[]{:S(2)}, u32[]{:S(2)}) async-start(bf16[8,8,64,128]{3,2,1,0:T(8,128)(2,1)} %broadcast_in_dim.5), calls=%async_computation.1 | async-start | bytes 2097152 | tf_op jit(solution)/shard_map/all_to_all | solution.py:206
  53.1 18.9 %collective-permute-start.4 = (bf16[192,128]{1,0:T(8,128)(2,1)}, bf16[192,128]{1,0:T(8,128)(2,1)S(1)}, u32[]{:S(2)}, u32[]{:S(2)}) collective-permute-start(bf16[192,128]{1,0:T(8,128)(2,1)} %get-tuple-element.45), channel_id=1, source_target_pairs={{4,0},{8,4},{12,8},{16,12},{20,16},{24,20},{28,24},{5,1},{9,5},{13... | collective-permute-start | bytes 147464 | tf_op jit(solution)/shard_map/ppermute | solution.py:57
  54.4 18.8 %collective-permute-start.5 = (bf16[192,128]{1,0:T(8,128)(2,1)}, bf16[192,128]{1,0:T(8,128)(2,1)S(1)}, u32[]{:S(2)}, u32[]{:S(2)}) collective-permute-start(bf16[192,128]{1,0:T(8,128)(2,1)} %get-tuple-element.46), channel_id=1, source_target_pairs={{8,0},{12,4},{16,8},{20,12},{24,16},{28,20},{9,1},{13,5},{17,9},{2... | collective-permute-start | bytes 147464 | tf_op jit(solution)/shard_map/ppermute | solution.py:57
  55.7 20.5 %collective-permute-start.6 = (bf16[192,128]{1,0:T(8,128)(2,1)}, bf16[192,128]{1,0:T(8,128)(2,1)S(1)}, u32[]{:S(2)}, u32[]{:S(2)}) collective-permute-start(bf16[192,128]{1,0:T(8,128)(2,1)} %get-tuple-element.47), channel_id=1, source_target_pairs={{12,0},{16,4},{20,8},{24,12},{28,16},{13,1},{17,5},{21,9},{25,13},... | collective-permute-start | bytes 147464 | tf_op jit(solution)/shard_map/ppermute | solution.py:57
  57.0 19.2 %collective-permute-start.7 = (bf16[192,128]{1,0:T(8,128)(2,1)}, bf16[192,128]{1,0:T(8,128)(2,1)S(1)}, u32[]{:S(2)}, u32[]{:S(2)}) collective-permute-start(bf16[192,128]{1,0:T(8,128)(2,1)} %get-tuple-element.48), channel_id=1, source_target_pairs={{16,0},{20,4},{24,8},{28,12},{17,1},{21,5},{25,9},{29,13},{18,2},{... | collective-permute-start | bytes 147464 | tf_op jit(solution)/shard_map/ppermute | solution.py:57
  76.1 4.5 %collective-permute-start.8 = (bf16[8,8,64,128]{3,2,1,0:T(8,128)(2,1)S(1)}, bf16[8,8,64,128]{3,2,1,0:T(8,128)(2,1)S(1)}, u32[]{:S(2)}, u32[]{:S(2)}) collective-permute-start(bf16[8,8,64,128]{3,2,1,0:T(8,128)(2,1)S(1)} %all-to-all-done.1.own_ref), channel_id=1, source_target_pairs={{0,32},{32,0},{1,33},{33,1},{2,34},{34,2},{3,35},{35,3},{4,36},{36... | collective-permute-start | bytes 3145736 | tf_op jit(solution)/shard_map/ppermute | solution.py:222
  85.3 1.9 %copy-start = (bf16[768,2048]{1,0:T(8,128)(2,1)S(1)}, bf16[768,2048]{1,0:T(8,128)(2,1)}, u32[]{:S(2)}) copy-start(bf16[768,2048]{1,0:T(8,128)(2,1)} %all-gather.3.cloned.1.call-done) | copy-start | bytes 9437188
  87.2 0.9 copy-start.3
  88.1 3.3 %copy-start.1 = (bf16[768,2048]{1,0:T(8,128)(2,1)S(1)}, bf16[768,2048]{1,0:T(8,128)(2,1)}, u32[]{:S(2)}) copy-start(bf16[768,2048]{1,0:T(8,128)(2,1)} %all-gather.3.cloned.1.call-done) | copy-start | bytes 9437188
  89.4 4.6 %collective-permute-start.9 = (bf16[8,8,64,128]{3,2,1,0:T(8,128)(2,1)S(1)}, bf16[8,8,64,128]{3,2,1,0:T(8,128)(2,1)S(1)}, u32[]{:S(2)}, u32[]{:S(2)}) collective-permute-start(bf16[8,8,64,128]{3,2,1,0:T(8,128)(2,1)S(1)} %get-tuple-element.60), channel_id=1, source_target_pairs={{0,32},{32,0},{1,33},{33,1},{2,34},{34,2},{3,35},{35,3},{4,36},{36... | collective-permute-start | bytes 3145736 | tf_op jit(solution)/shard_map/ppermute | solution.py:226
  92.3 29.6 %copy-start.4 = (bf16[192,128]{1,0:T(8,128)(2,1)}, bf16[192,128]{1,0:T(8,128)(2,1)S(1)}, u32[]{:S(2)}) copy-start(bf16[192,128]{1,0:T(8,128)(2,1)S(1)} %project.1.refs_9_) | copy-start | bytes 147460
  95.2 35.9 %all-to-all-start.2 = ((bf16[8,8,64,128]{3,2,1,0:T(8,128)(2,1)}), bf16[8,8,64,128]{3,2,1,0:T(8,128)(2,1)S(1)}, u32[]{:S(2)}, u32[]{:S(2)}) async-start(bf16[8,8,64,128]{3,2,1,0:T(8,128)(2,1)} %add_halves.1), calls=%async_computation.2 | async-start | bytes 2097152 | tf_op jit(solution)/shard_map/all_to_all | solution.py:231
  104.8 15.6 %collective-permute-start.13 = (bf16[192,128]{1,0:T(8,128)(2,1)S(1)}, bf16[192,128]{1,0:T(8,128)(2,1)S(1)}, u32[]{:S(2)}, u32[]{:S(2)}) collective-permute-start(bf16[192,128]{1,0:T(8,128)(2,1)S(1)} %project.1.refs_9_), channel_id=1, source_target_pairs={{0,4},{4,8},{8,12},{12,16},{16,20},{20,24},{24,28},{1,5},{5,9},{9,... | collective-permute-start | bytes 147464 | tf_op jit(solution)/shard_map/ppermute | solution.py:53
  108.9 11.5 %collective-permute-start.12 = (bf16[192,128]{1,0:T(8,128)(2,1)S(1)}, bf16[192,128]{1,0:T(8,128)(2,1)S(1)}, u32[]{:S(2)}, u32[]{:S(2)}) collective-permute-start(bf16[192,128]{1,0:T(8,128)(2,1)S(1)} %project.1.refs_9_), channel_id=1, source_target_pairs={{0,8},{4,12},{8,16},{12,20},{16,24},{20,28},{1,9},{5,13},{9,17},{1... | collective-permute-start | bytes 147464 | tf_op jit(solution)/shard_map/ppermute | solution.py:53
  113.0 7.5 %collective-permute-start.11 = (bf16[192,128]{1,0:T(8,128)(2,1)S(1)}, bf16[192,128]{1,0:T(8,128)(2,1)S(1)}, u32[]{:S(2)}, u32[]{:S(2)}) collective-permute-start(bf16[192,128]{1,0:T(8,128)(2,1)S(1)} %project.1.refs_9_), channel_id=1, source_target_pairs={{0,12},{4,16},{8,20},{12,24},{16,28},{1,13},{5,17},{9,21},{13,25},... | collective-permute-start | bytes 147464 | tf_op jit(solution)/shard_map/ppermute | solution.py:53
  118.1 3.8 %collective-permute-start.10 = (bf16[192,128]{1,0:T(8,128)(2,1)S(1)}, bf16[192,128]{1,0:T(8,128)(2,1)S(1)}, u32[]{:S(2)}, u32[]{:S(2)}) collective-permute-start(bf16[192,128]{1,0:T(8,128)(2,1)S(1)} %project.1.refs_9_), channel_id=1, source_target_pairs={{0,16},{4,20},{8,24},{12,28},{1,17},{5,21},{9,25},{13,29},{2,18},{... | collective-permute-start | bytes 147464 | tf_op jit(solution)/shard_map/ppermute | solution.py:53
  120.4 1.5 copy-start.9
  120.5 1.5 copy-start.10
  120.5 1.5 copy-start.11
  122.0 0.6 copy-start.12
  131.1 1.0 copy-start.2
Sparse Core Ops, SparseCore 0:
  10.1 75.1 all-gather.2

commit v9 on v7

--- a/solution.py
+++ b/solution.py
@@ -13,7 +13,7 @@
 HEADS_AT_ONCE = 2
 LANES = HEADS_AT_ONCE * TOK
 CHUNKS = GROUP // HEADS_AT_ONCE
-CHIPS = ("yh", "x")
+PAIR = [(0, 1), (1, 0)]
 SCALE = HEAD_DIM ** -0.5
 F32 = jnp.float32
 BF16 = jnp.bfloat16
@@ -57,56 +57,74 @@
     return lax.ppermute(block, "ctx", [(i + distance, i) for i in range(8 - distance)])
 
 
-def weight_rows(w_ref, j):
-    return jnp.concatenate([w_ref[ctx, j] for ctx in range(8)], axis=0)
-
-
-def feature_columns(x_ref, j, core):
-    place = pl.multiple_of(((j % 2) * 2 + core) * 512, 512)
-    return x_ref[j // 2, :, pl.ds(place, 512)]
-
-
-def project(x_ref, own_ref, other_ref, out_ref):
-    core = lax.axis_index("core")
-    total = jnp.zeros((TOK, HEAD_DIM), F32)
-    for w_ref, half in ((own_ref, core), (other_ref, 1 - core)):
-        for j in range(8):
-            total += jnp.dot(
-                feature_columns(x_ref, j, half), weight_rows(w_ref, j), preferred_element_type=F32
+def feature_steps(own_ref, near_ref, half):
+    m0 = lax.axis_index("m0")
+    for step in range(4):
+        ref, m = (own_ref, m0) if step < 2 else (near_ref, 1 - m0)
+        place = pl.multiple_of((step % 2) * 1024 + half * 512, 512)
+        yield ref[:, pl.ds(place, 512)], 2 * m + step % 2
+
+
+def project(own_ref, near_ref, mine_ref, other_ref, keep_ref, give_ref):
+    core, m1 = lax.axis_index("core"), lax.axis_index("m1")
+    total = jnp.zeros((TOK, 2 * HEAD_DIM), F32)
+    for w_ref, half in ((mine_ref, core), (other_ref, 1 - core)):
+        for columns, x in feature_steps(own_ref, near_ref, half):
+            weight = jnp.concatenate(
+                [
+                    jnp.concatenate([w_ref[x, ctx, c] for c in range(2)], axis=1)
+                    for ctx in range(8)
+                ],
+                axis=0,
             )
-    out_ref[...] = total.astype(BF16)
-
-
-def weight_grad(x_ref, *refs):
-    dv_refs, out_refs = refs[:5], refs[5:]
-    core = lax.axis_index("core")
-    dv = dv_refs[0][...]
-    for ref in dv_refs[1:]:
-        dv = dv + ref[...].astype(F32)
-    dv = dv.astype(BF16)
+            total += jnp.dot(columns, weight, preferred_element_type=F32)
+    low, high = total[:, :HEAD_DIM], total[:, HEAD_DIM:]
+    keep_ref[...] = jnp.where(m1 == 0, low, high)
+    give_ref[...] = jnp.where(m1 == 0, high, low).astype(BF16)
+
+
+def weight_grad(own_ref, near_ref, dv_ref, far_dv_ref, *out_refs):
+    core, m1 = lax.axis_index("core"), lax.axis_index("m1")
+    mine, far = dv_ref[...], far_dv_ref[...]
+    dv = jnp.concatenate([jnp.where(m1 == 0, mine, far), jnp.where(m1 == 0, far, mine)], axis=1)
     for out_ref, half in zip(out_refs, (core, 1 - core)):
-        for j in range(8):
-            rows = lax.dot_general(
-                feature_columns(x_ref, j, half), dv, TN, preferred_element_type=F32
-            ).astype(BF16)
+        for columns, x in feature_steps(own_ref, near_ref, half):
+            rows = lax.dot_general(columns, dv, TN, preferred_element_type=F32).astype(BF16)
             for ctx in range(8):
-                out_ref[j, ctx] = rows[ctx * 64 : (ctx + 1) * 64]
+                for c in range(2):
+                    out_ref[x, ctx, c] = rows[
+                        ctx * 64 : (ctx + 1) * 64, c * HEAD_DIM : (c + 1) * HEAD_DIM
+                    ]
 
 
 def add_halves(a_ref, b_ref, out_ref):
     out_ref[...] = (a_ref[...].astype(F32) + b_ref[...].astype(F32)).astype(BF16)
 
 
+def sum_of(parts):
+    total = parts[0].astype(F32)
+    for part in parts[1:]:
+        total = total + part.astype(F32)
+    return total
+
+
 def sum_blocks(parts_ref, out_ref):
-    total = parts_ref[0].astype(F32)
-    for i in range(1, parts_ref.shape[0]):
-        total = total + parts_ref[i].astype(F32)
-    out_ref[...] = total.astype(out_ref.dtype)
+    out_ref[...] = sum_of([parts_ref[i] for i in range(parts_ref.shape[0])]).astype(out_ref.dtype)
+
+
+def twice_sum(parts_ref, out_ref):
+    total = sum_of([parts_ref[i] for i in range(8)])
+    for i in range(2):
+        out_ref[i] = total
 
 
 def rows_of_heads(wide_ref, rows_ref):
     for h in range(GROUP):
         rows_ref[h * TOK : (h + 1) * TOK] = wide_ref[:, h * HEAD_DIM : (h + 1) * HEAD_DIM]
+
+
+def slot_owner(slot):
+    return lax.rem(lax.axis_index("ctx") - (REACH - slot) + 8, 8)
 
 
 def fill_bias(len_ref, bias):
@@ -120,7 +138,7 @@
         first = jnp.where(query >= end, end, first)
     offset = lax.broadcasted_iota(jnp.int32, (TOK, LANES), 0)
     for slot in range(REACH + 1):
-        key = lax.rem(ctx - (REACH - slot) + 8, 8) * TOK + offset
+        key = slot_owner(slot) * TOK + offset
         bias[slot * TOK : (slot + 1) * TOK] = jnp.where(
             (key >= first) & (key <= query), F32(0.0), F32(-1e30)
         )
@@ -181,13 +199,12 @@
 
 
 def shards(queries, key_states, normed, value_weight, grad_out, lengths):
-    features = lax.all_gather(normed, "mp", axis=0)
+    yh, m1 = lax.axis_index("yh"), lax.axis_index("m1")
+    corners = to_all(value_weight, ("yh", "m1"), 4)
+    near = lax.ppermute(normed, "m0", PAIR)
     keys = [from_behind(key_states, d) for d in range(REACH, 0, -1)] + [key_states]
-    chips = to_all(value_weight, CHIPS, 8)
-    spread = jnp.broadcast_to(chips[None], (8, 8, 64, HEAD_DIM))
-    spread, keys = lax.optimization_barrier((spread, keys))
-
-    weight = lax.all_to_all(spread, "ctx", 0, 0, tiled=True)
+    corners, keys = lax.optimization_barrier((corners, keys))
+    weight = to_all(lax.dynamic_slice_in_dim(corners, 2 * m1, 2, 0), "ctx", 8)
     heads = GROUP * TOK
     rows = pltpu.VMEM((heads, HEAD_DIM), BF16)
     window = pltpu.VMEM((WINDOW, HEAD_DIM), BF16)
@@ -195,47 +212,58 @@
     pairs = pltpu.VMEM((WINDOW, heads), BF16)
     block = shape((TOK, HEAD_DIM))
     own = shape((TOK, HEAD_DIM), F32)
-    whole = shape((8, 8, 64, HEAD_DIM))
+    whole = shape((4, 8, 2, 64, HEAD_DIM))
     *dv, stats = call(
         soft, (block,) * REACH + (own, shape((8, LANES), F32)), 7, 3 * 10**9, 2 * 10**6,
         (rows, rows, bias, pairs, window), smem=1, vmem=56,
     )(lengths, queries, grad_out, *keys)
+    weight, stats = lax.optimization_barrier((weight, stats))
+    weight = to_all(weight, "x", 4)
     dv = [dv[REACH]] + [from_ahead(dv[REACH - d], d) for d in range(1, REACH + 1)]
-
-    weight, dv = lax.optimization_barrier((weight, dv))
-    other = lax.ppermute(weight, "core", [(0, 1), (1, 0)])
-    other, dv = lax.optimization_barrier((other, dv))
-
-    partial, given = call(weight_grad, (whole, whole), 6, 4 * 10**8, 5 * 10**6)(features, *dv)
-    taken = lax.ppermute(given, "core", [(0, 1), (1, 0)])
-    projected = call(project, block, 3, 4 * 10**8, 5 * 10**6)(features, weight, other)
-    taken, projected = lax.optimization_barrier((taken, projected))
+    dv = sum_of(dv).astype(BF16)
+    far_dv = lax.ppermute(dv, "m1", PAIR)
+    other = lax.ppermute(weight, "core", PAIR)
+
+    partial, given = call(weight_grad, (whole, whole), 4, 4 * 10**8, 5 * 10**6)(
+        normed, near, dv, far_dv
+    )
+    taken = lax.ppermute(given, "core", PAIR)
+    kept, given = call(project, (own, block), 4, 4 * 10**8, 5 * 10**6)(normed, near, weight, other)
+    projected = (kept + lax.ppermute(given, "m1", PAIR).astype(F32)).astype(BF16)
     values = [from_behind(projected, d) for d in range(REACH, 0, -1)] + [projected]
     partial = call(add_halves, whole, 2, 10**6, 3 * 10**6)(partial, taken)
-    partial = lax.all_to_all(partial, CHIPS, 0, 0, tiled=True)
+    partial = lax.all_to_all(partial, "x", 0, 0, tiled=True)
+    partial = call(sum_blocks, shape((8, 2, 64, HEAD_DIM)), 1, 10**6, 10**6)(partial)
+    partial, values = lax.optimization_barrier((partial, values))
+    partial = lax.all_to_all(partial, "ctx", 0, 0, tiled=True)
 
     wide = shape((TOK, GROUP * HEAD_DIM))
     attended, grad_query, *dk = call(
         attend, (wide, wide) + (block,) * REACH + (own,), 13, 6 * 10**9, 4 * 10**6,
         (rows, rows, bias, pairs, window, window), smem=1, vmem=56,
     )(lengths, queries, grad_out, stats, *keys, *values)
+    partial = call(twice_sum, shape((2, 2, 64, HEAD_DIM), F32), 1, 10**6, 10**6)(partial)
     partial, dk = lax.optimization_barrier((partial, dk))
+    partial = lax.all_to_all(partial.reshape(4, 64, HEAD_DIM), ("yh", "m1"), 0, 0, tiled=True)
+    grad_weight = jnp.sum(
+        lax.dynamic_index_in_dim(
+            partial.reshape(2, 2, 64, HEAD_DIM), yh, axis=1, keepdims=False
+        ),
+        axis=0,
+    )
     dk = [dk[REACH]] + [from_ahead(dk[REACH - d], d) for d in range(1, REACH + 1)]
     grad_key = (sum(part.astype(F32) for part in dk) * F32(SCALE)).astype(BF16)
-
-    partial = call(sum_blocks, shape((8, 64, HEAD_DIM)), 1, 10**6, 10**6)(partial)
-    partial = lax.all_to_all(partial, "ctx", 0, 0, tiled=True)
-    grad_weight = call(sum_blocks, shape((64, HEAD_DIM), F32), 1, 10**6, 10**6)(partial)
     return attended, grad_query, grad_key, grad_weight
 
 
 def solution(mesh):
-    fine = Mesh(mesh.devices.reshape(2, 4, 2, 8, 4), ("yh", "x", "core", "ctx", "mp"))
-    tokens = P(("yh", "x", "core", "ctx"), "mp")
+    axes = ("yh", "x", "core", "ctx", "m1", "m0")
+    fine = Mesh(mesh.devices.reshape(2, 4, 2, 8, 2, 2), axes)
+    tokens = P(axes[:4], axes[4:])
     return jax.shard_map(
         shards,
         mesh=fine,
-        in_specs=(tokens,) * 5 + (P(("yh", "x", "core"), None),),
+        in_specs=(tokens,) * 5 + (P(axes[:3], None),),
         out_specs=(tokens,) * 4,
         check_vma=False,
     )

time: 168 us -> 152 us (0.905)
  the two profiles are of different devices: /device:TPU:56 before, /device:TPU:450 now
where the time goes in v9:
time: 152 us; the launch traced here: 151 us
  starting transfers between devices  93 us (61%)
  waiting for transfers between devices  27.8 us (18%)
  Pallas kernels  20.3 us (13%)
  local copies, waits for them, and re-layouts  7.43 us (5%)
    ppermute x8, starting transfers between devices, from_ahead(): lax.ppermute(block, 'ctx', [(i + distance, i) for i in range(8 - distance)])  24.9 us
    all_to_all x3, starting transfers between devices, to_all(): lax.all_to_all(jnp.broadcast_to(block[None], (copies,) + block.shape), ax...  21 us
    ppermute x8, waiting for transfers between devices, from_behind(): lax.ppermute(block, 'ctx', [(i, i + distance) for i in range(8 - distance)])  13.6 us
    ppermute x8, starting transfers between devices, from_behind(): lax.ppermute(block, 'ctx', [(i, i + distance) for i in range(8 - distance)])  10.3 us
    all_to_all x1, starting transfers between devices, shards(): partial = lax.all_to_all(partial, 'ctx', 0, 0, tiled=True)  9.01 us
    pallas_call x1, Pallas kernels, shards(): call(attend, (wide, wide) + (block,) * REACH + (own,), 13, 6 * 10 ** 9, 4...  8.36 us
    all_to_all x1, waiting for transfers between devices, shards(): lax.all_to_all(partial.reshape(4, 64, HEAD_DIM), ('yh', 'm1'), 0, 0, tile...  8.03 us
    all_to_all x1, starting transfers between devices, shards(): lax.all_to_all(partial.reshape(4, 64, HEAD_DIM), ('yh', 'm1'), 0, 0, tile...  7.19 us
  transfers between devices with their start and end apart: 27, of which 11 were waited for; matrix products, arithmetic and copies ran while one was open for 2% of the time, Pallas kernels for 13%

profile of v9, /device:TPU:450, one launch (start us, length us, event | category | flops | bytes accessed | tf_op | source)
XLA Modules:
  0.0 150.8 jit_solution(3072272521957006344)
XLA Ops:
  0.6 1.4 broadcast_in_dim.6
  2.0 7.2 %all-to-all-start = ((bf16[4,64,128]{2,1,0:T(8,128)(2,1)}), bf16[4,64,128]{2,1,0:T(8,128)(2,1)S(1)}, u32[]{:S(2)}, u32[]{:S(2)}) async-start(bf16[4,64,128]{2,1,0:T(8,128)(2,1)} %broadcast_in_dim.6), calls=%async_computation | async-start | bytes 131072 | tf_op jit(solution)/shard_map/all_to_all | solution.py:47
  9.2 1.3 collective-permute-start.2
  10.5 1.3 collective-permute-start.1
  11.8 1.3 collective-permute-start
  13.1 1.3 collective-permute-start.3
  14.4 2.6 %collective-permute-start.4 = (bf16[192,2048]{1,0:T(8,128)(2,1)}, bf16[192,2048]{1,0:T(8,128)(2,1)S(1)}, u32[]{:S(2)}, u32[]{:S(2)}) collective-permute-start(bf16[192,2048]{1,0:T(8,128)(2,1)} %own_ref.3), channel_id=1, source_target_pairs={{0,1},{1,0},{2,3},{3,2},{4,5},{5,4},{6,7},{7,6},{8,9},{9,8},{10,11... | collective-permute-start | bytes 2359304 | tf_op jit(solution)/shard_map/ppermute | solution.py:204
  17.0 0.1 collective-permute-done.2.refs_2_
  17.1 1.7 %collective-permute-done.1.refs_1_ = bf16[192,128]{1,0:T(8,128)(2,1)S(1)} collective-permute-done((bf16[192,128]{1,0:T(8,128)(2,1)S(1)}, bf16[192,128]{1,0:T(8,128)(2,1)S(1)}, u32[]{:S(2)}, u32[]{:S(2)}) %collective-permute-start.1) | collective-permute-done | bytes 49184 | tf_op jit(solution)/shard_map/ppermute | solution.py:53
  18.9 2.8 %collective-permute-done.refs_0_ = bf16[192,128]{1,0:T(8,128)(2,1)S(1)} collective-permute-done((bf16[192,128]{1,0:T(8,128)(2,1)S(1)}, bf16[192,128]{1,0:T(8,128)(2,1)S(1)}, u32[]{:S(2)}, u32[]{:S(2)}) %collective-permute-start) | collective-permute-done | bytes 49184 | tf_op jit(solution)/shard_map/ppermute | solution.py:53
  21.7 0.0 collective-permute-done.3.refs_3_
  21.7 0.0 all-to-all-done
  21.7 0.8 broadcast_in_dim.7
  22.5 8.9 %all-to-all-start.1 = ((bf16[8,2,64,128]{3,2,1,0:T(8,128)(2,1)}), bf16[8,2,64,128]{3,2,1,0:T(8,128)(2,1)S(1)}, u32[]{:S(2)}, u32[]{:S(2)}) async-start(bf16[8,2,64,128]{3,2,1,0:T(8,128)(2,1)} %broadcast_in_dim.7), calls=%async_computation.1 | async-start | bytes 524288 | tf_op jit(solution)/shard_map/all_to_all | solution.py:47
  31.4 5.6 %soft.1 = (bf16[192,128]{1,0:T(8,128)(2,1)}, bf16[192,128]{1,0:T(8,128)(2,1)}, bf16[192,128]{1,0:T(8,128)(2,1)}, bf16[192,128]{1,0:T(8,128)(2,1)}, f32[192,128]{1,0:T(8,128)}, /*index=5*/f32[8,384]{1,0:T(8,128)}) custom-call(s32[1,8]{1,0:T(1,128)} %len_ref.3, bf16[192,1024]{1,0:T(8,128)(2,1)} %q_ref.3, bf16[192,1024]{1,0:T(8,128)(2,1)} %do_ref.3, ...), custom_call_target="tpu_custom_call" | custom-call | flops 3000000000 | bytes 2000000 | tf_op jit(solution)/shard_map/soft/pallas_call | solution.py:216
  37.0 3.4 %collective-permute-start.5 = (bf16[192,128]{1,0:T(8,128)(2,1)}, bf16[192,128]{1,0:T(8,128)(2,1)S(1)}, u32[]{:S(2)}, u32[]{:S(2)}) collective-permute-start(bf16[192,128]{1,0:T(8,128)(2,1)} %get-tuple-element.50), channel_id=1, source_target_pairs={{4,0},{8,4},{12,8},{16,12},{20,16},{24,20},{28,24},{5,1},{9,5},{13... | collective-permute-start | bytes 147464 | tf_op jit(solution)/shard_map/ppermute | solution.py:57
  40.3 4.3 %collective-permute-start.6 = (bf16[192,128]{1,0:T(8,128)(2,1)}, bf16[192,128]{1,0:T(8,128)(2,1)S(1)}, u32[]{:S(2)}, u32[]{:S(2)}) collective-permute-start(bf16[192,128]{1,0:T(8,128)(2,1)} %get-tuple-element.51), channel_id=1, source_target_pairs={{8,0},{12,4},{16,8},{20,12},{24,16},{28,20},{9,1},{13,5},{17,9},{2... | collective-permute-start | bytes 147464 | tf_op jit(solution)/shard_map/ppermute | solution.py:57
  44.6 2.5 %collective-permute-start.7 = (bf16[192,128]{1,0:T(8,128)(2,1)}, bf16[192,128]{1,0:T(8,128)(2,1)S(1)}, u32[]{:S(2)}, u32[]{:S(2)}) collective-permute-start(bf16[192,128]{1,0:T(8,128)(2,1)} %get-tuple-element.52), channel_id=1, source_target_pairs={{12,0},{16,4},{20,8},{24,12},{28,16},{13,1},{17,5},{21,9},{25,13},... | collective-permute-start | bytes 147464 | tf_op jit(solution)/shard_map/ppermute | solution.py:57
  47.1 1.4 collective-permute-start.8
  48.5 0.0 all-to-all-done.1
  48.5 1.3 broadcast_in_dim.8
  49.7 5.0 %all-to-all-start.3 = ((bf16[4,8,2,64,128]{4,3,2,1,0:T(8,128)(2,1)}), bf16[4,8,2,64,128]{4,3,2,1,0:T(8,128)(2,1)S(1)}, u32[]{:S(2)}, u32[]{:S(2)}) async-start(bf16[4,8,2,64,128]{4,3,2,1,0:T(8,128)(2,1)} %broadcast_in_dim.8), calls=%async_computation.3 | async-start | bytes 2097152 | tf_op jit(solution)/shard_map/all_to_all | solution.py:47
  54.7 0.0 collective-permute-done.5
  54.7 0.0 collective-permute-done.8
  54.8 4.7 %collective-permute-start.9 = (bf16[192,128]{1,0:T(8,128)(2,1)S(1)}, bf16[192,128]{1,0:T(8,128)(2,1)S(1)}, u32[]{:S(2)}, u32[]{:S(2)}) collective-permute-start(bf16[192,128]{1,0:T(8,128)(2,1)S(1)} %add_convert_fusion.1.dv_ref), channel_id=1, source_target_pairs={{0,2},{2,0},{1,3},{3,1},{4,6},{6,4},{5,7},{7,5},{8,10},{10,8},{9,1... | collective-permute-start | bytes 147464 | tf_op jit(solution)/shard_map/ppermute | solution.py:224
  59.4 2.7 %collective-permute-done.9.far_dv_ref = bf16[192,128]{1,0:T(8,128)(2,1)S(1)} collective-permute-done((bf16[192,128]{1,0:T(8,128)(2,1)S(1)}, bf16[192,128]{1,0:T(8,128)(2,1)S(1)}, u32[]{:S(2)}, u32[]{:S(2)}) %collective-permute-start.9) | collective-permute-done | bytes 49184 | tf_op jit(solution)/shard_map/ppermute | solution.py:224
  62.2 1.8 %weight_grad.1 = (bf16[4,8,2,64,128]{4,3,2,1,0:T(8,128)(2,1)S(1)}, bf16[4,8,2,64,128]{4,3,2,1,0:T(8,128)(2,1)}) custom-call(bf16[192,2048]{1,0:T(8,128)(2,1)S(1)} %copy-done, bf16[192,2048]{1,0:T(8,128)(2,1)S(1)} %collective-permute-done.4.near_ref, bf16[192,128]{1,0:T(8,128)(2,1)S(1)} %add_convert_fusion.1.dv_ref, ...), custom_call_target="tpu_custom_call" | custom-call | flops 400000000 | bytes 5000000 | tf_op jit(solution)/shard_map/weight_grad/pallas_call | solution.py:227
  64.0 1.0 copy-done.3
  64.9 1.9 %collective-permute-start.10 = (bf16[4,8,2,64,128]{4,3,2,1,0:T(8,128)(2,1)}, bf16[4,8,2,64,128]{4,3,2,1,0:T(8,128)(2,1)S(1)}, u32[]{:S(2)}, u32[]{:S(2)}) collective-permute-start(bf16[4,8,2,64,128]{4,3,2,1,0:T(8,128)(2,1)} %get-tuple-element.55), channel_id=1, source_target_pairs={{0,32},{32,0},{1,33},{33,1},{2,34},{34,2},{3,35},{35,3},{4,36},{36... | collective-permute-start | bytes 3145736 | tf_op jit(solution)/shard_map/ppermute | solution.py:230
  66.8 0.0 all-to-all-done.3.mine_ref
  66.9 2.4 %collective-permute-start.11 = (bf16[4,8,2,64,128]{4,3,2,1,0:T(8,128)(2,1)S(1)}, bf16[4,8,2,64,128]{4,3,2,1,0:T(8,128)(2,1)}, u32[]{:S(2)}, u32[]{:S(2)}) collective-permute-start(bf16[4,8,2,64,128]{4,3,2,1,0:T(8,128)(2,1)S(1)} %all-to-all-done.3.mine_ref), channel_id=1, source_target_pairs={{0,32},{32,0},{1,33},{33,1},{2,34},{34,2},{3,35},{35,3},{4,36},{36... | collective-permute-start | bytes 3145736 | tf_op jit(solution)/shard_map/ppermute | solution.py:225
  69.3 0.4 collective-permute-done.10.b_ref
  69.7 1.2 copy-done.4
  70.9 1.2 add_halves.1
  72.1 4.8 %all-to-all-start.2 = ((bf16[4,8,2,64,128]{4,3,2,1,0:T(8,128)(2,1)}), bf16[4,8,2,64,128]{4,3,2,1,0:T(8,128)(2,1)S(1)}, u32[]{:S(2)}, u32[]{:S(2)}) async-start(bf16[4,8,2,64,128]{4,3,2,1,0:T(8,128)(2,1)} %add_halves.1), calls=%async_computation.2 | async-start | bytes 2097152 | tf_op jit(solution)/shard_map/all_to_all | solution.py:235
  76.9 0.0 collective-permute-done.11.other_ref
  76.9 1.1 copy-done.2
  78.0 1.8 %project.1 = (f32[192,128]{1,0:T(8,128)S(1)}, bf16[192,128]{1,0:T(8,128)(2,1)S(1)}) custom-call(bf16[192,2048]{1,0:T(8,128)(2,1)S(1)} %copy-done, bf16[192,2048]{1,0:T(8,128)(2,1)S(1)} %copy-done.2, bf16[4,8,2,64,128]{4,3,2,1,0:T(8,128)(2,1)S(1)} %all-to-all-done.3.mine_ref, bf16[4,8,2,64,128]{4,3,2,1,0:T(8,128)(2,1)} %collective-permute-done.11.other_ref), custom_call_target="tpu_custom_call" | custom-call | flops 400000000 | bytes 5000000 | tf_op jit(solution)/shard_map/project/pallas_call | solution.py:231
  79.9 4.1 %collective-permute-start.12 = (bf16[192,128]{1,0:T(8,128)(2,1)S(1)}, bf16[192,128]{1,0:T(8,128)(2,1)S(1)}, u32[]{:S(2)}, u32[]{:S(2)}) collective-permute-start(bf16[192,128]{1,0:T(8,128)(2,1)S(1)} %get-tuple-element.58), channel_id=1, source_target_pairs={{0,2},{2,0},{1,3},{3,1},{4,6},{6,4},{5,7},{7,5},{8,10},{10,8},{9,1... | collective-permute-start | bytes 147464 | tf_op jit(solution)/shard_map/ppermute | solution.py:232
  84.0 2.9 %collective-permute-done.12 = bf16[192,128]{1,0:T(8,128)(2,1)S(1)} collective-permute-done((bf16[192,128]{1,0:T(8,128)(2,1)S(1)}, bf16[192,128]{1,0:T(8,128)(2,1)S(1)}, u32[]{:S(2)}, u32[]{:S(2)}) %collective-permute-start.12) | collective-permute-done | bytes 49184 | tf_op jit(solution)/shard_map/ppermute | solution.py:232
  87.0 1.3 collective-permute-start.16
  88.3 1.3 collective-permute-start.15
  89.6 1.3 collective-permute-start.14
  90.9 1.3 collective-permute-start.13
  92.2 0.0 all-to-all-done.2.parts_ref
  92.2 0.8 sum_blocks.1
  93.0 0.3 collective-permute-done.16.refs_8_
  93.3 1.8 %collective-permute-done.15.refs_7_ = bf16[192,128]{1,0:T(8,128)(2,1)S(1)} collective-permute-done((bf16[192,128]{1,0:T(8,128)(2,1)S(1)}, bf16[192,128]{1,0:T(8,128)(2,1)S(1)}, u32[]{:S(2)}, u32[]{:S(2)}) %collective-permute-start.15) | collective-permute-done | bytes 49184 | tf_op jit(solution)/shard_map/ppermute | solution.py:53
  95.2 4.8 %collective-permute-done.14.refs_6_ = bf16[192,128]{1,0:T(8,128)(2,1)S(1)} collective-permute-done((bf16[192,128]{1,0:T(8,128)(2,1)S(1)}, bf16[192,128]{1,0:T(8,128)(2,1)S(1)}, u32[]{:S(2)}, u32[]{:S(2)}) %collective-permute-start.14) | collective-permute-done | bytes 49184 | tf_op jit(solution)/shard_map/ppermute | solution.py:53
  100.0 2.0 %collective-permute-done.13.refs_5_ = bf16[192,128]{1,0:T(8,128)(2,1)S(1)} collective-permute-done((bf16[192,128]{1,0:T(8,128)(2,1)S(1)}, bf16[192,128]{1,0:T(8,128)(2,1)S(1)}, u32[]{:S(2)}, u32[]{:S(2)}) %collective-permute-start.13) | collective-permute-done | bytes 49184 | tf_op jit(solution)/shard_map/ppermute | solution.py:53
  102.0 0.6 copy-done.20
  102.6 9.0 %all-to-all-start.4 = ((bf16[8,2,64,128]{3,2,1,0:T(8,128)(2,1)}), bf16[8,2,64,128]{3,2,1,0:T(8,128)(2,1)S(1)}, u32[]{:S(2)}, u32[]{:S(2)}) async-start(bf16[8,2,64,128]{3,2,1,0:T(8,128)(2,1)} %sum_blocks.1), calls=%async_computation.4 | async-start | bytes 524288 | tf_op jit(solution)/shard_map/all_to_all | solution.py:238
  111.6 8.4 %attend.1 = (bf16[192,1024]{1,0:T(8,128)(2,1)}, bf16[192,1024]{1,0:T(8,128)(2,1)}, bf16[192,128]{1,0:T(8,128)(2,1)}, bf16[192,128]{1,0:T(8,128)(2,1)}, bf16[192,...) custom-call(s32[1,8]{1,0:T(1,128)} %len_ref.3, bf16[192,1024]{1,0:T(8,128)(2,1)} %q_ref.3, ...), custom_call_target="tpu_custom_call" | custom-call | flops 6000000000 | bytes 4000000 | tf_op jit(solution)/shard_map/attend/pallas_call | solution.py:241
  120.0 0.7 twice_sum.1
  120.7 0.1 copy-done.16
  120.8 3.4 %collective-permute-start.17 = (bf16[192,128]{1,0:T(8,128)(2,1)S(1)}, bf16[192,128]{1,0:T(8,128)(2,1)S(1)}, u32[]{:S(2)}, u32[]{:S(2)}) collective-permute-start(bf16[192,128]{1,0:T(8,128)(2,1)S(1)} %copy-done.16), channel_id=1, source_target_pairs={{4,0},{8,4},{12,8},{16,12},{20,16},{24,20},{28,24},{5,1},{9,5},{13... | collective-permute-start | bytes 147464 | tf_op jit(solution)/shard_map/ppermute | solution.py:57
  124.1 4.3 %collective-permute-start.18 = (bf16[192,128]{1,0:T(8,128)(2,1)S(1)}, bf16[192,128]{1,0:T(8,128)(2,1)S(1)}, u32[]{:S(2)}, u32[]{:S(2)}) collective-permute-start(bf16[192,128]{1,0:T(8,128)(2,1)S(1)} %copy-done.15), channel_id=1, source_target_pairs={{8,0},{12,4},{16,8},{20,12},{24,16},{28,20},{9,1},{13,5},{17,9},{2... | collective-permute-start | bytes 147464 | tf_op jit(solution)/shard_map/ppermute | solution.py:57
  128.4 2.7 %collective-permute-start.19 = (bf16[192,128]{1,0:T(8,128)(2,1)S(1)}, bf16[192,128]{1,0:T(8,128)(2,1)S(1)}, u32[]{:S(2)}, u32[]{:S(2)}) collective-permute-start(bf16[192,128]{1,0:T(8,128)(2,1)S(1)} %copy-done.14), channel_id=1, source_target_pairs={{12,0},{16,4},{20,8},{24,12},{28,16},{13,1},{17,5},{21,9},{25,13},... | collective-permute-start | bytes 147464 | tf_op jit(solution)/shard_map/ppermute | solution.py:57
  131.1 3.2 %collective-permute-start.20 = (bf16[192,128]{1,0:T(8,128)(2,1)S(1)}, bf16[192,128]{1,0:T(8,128)(2,1)S(1)}, u32[]{:S(2)}, u32[]{:S(2)}) collective-permute-start(bf16[192,128]{1,0:T(8,128)(2,1)S(1)} %copy-done.13), channel_id=1, source_target_pairs={{16,0},{20,4},{24,8},{28,12},{17,1},{21,5},{25,9},{29,13},{18,2},{... | collective-permute-start | bytes 147464 | tf_op jit(solution)/shard_map/ppermute | solution.py:57
  134.3 7.2 %all-to-all-start.5 = ((f32[4,64,128]{2,1,0:T(8,128)}), f32[4,64,128]{2,1,0:T(8,128)S(1)}, u32[]{:S(2)}, u32[]{:S(2)}) async-start(f32[4,64,128]{2,1,0:T(8,128)} %bitcast), calls=%async_computation.5 | async-start | bytes 262144 | tf_op jit(solution)/shard_map/all_to_all | solution.py:247
  141.5 0.0 collective-permute-done.19
  141.5 0.7 multiply_convert_fusion
  142.2 8.0 %all-to-all-done.5 = f32[4,64,128]{2,1,0:T(8,128)S(1)} async-done(((f32[4,64,128]{2,1,0:T(8,128)}), f32[4,64,128]{2,1,0:T(8,128)S(1)}, u32[]{:S(2)}, u32[]{:S(2)}) %all-to-all-start.5) | async-done | bytes 131104 | tf_op jit(solution)/shard_map/all_to_all | solution.py:247
  150.2 0.6 dynamic-slice_reduce_fusion
  (47 shorter events, 0.1 us)
Async XLA Ops:
  2.0 7.2 %copy-start.8 = (bf16[192,128]{1,0:T(8,128)(2,1)S(1)}, bf16[192,128]{1,0:T(8,128)(2,1)}, u32[]{:S(2)}) copy-start(bf16[192,128]{1,0:T(8,128)(2,1)} %refs_4_.1) | copy-start | bytes 147460
  2.0 19.7 %all-to-all-start = ((bf16[4,64,128]{2,1,0:T(8,128)(2,1)}), bf16[4,64,128]{2,1,0:T(8,128)(2,1)S(1)}, u32[]{:S(2)}, u32[]{:S(2)}) async-start(bf16[4,64,128]{2,1,0:T(8,128)(2,1)} %broadcast_in_dim.6), calls=%async_computation | async-start | bytes 131072 | tf_op jit(solution)/shard_map/all_to_all | solution.py:47
  9.2 7.9 %collective-permute-start.2 = (bf16[192,128]{1,0:T(8,128)(2,1)S(1)}, bf16[192,128]{1,0:T(8,128)(2,1)S(1)}, u32[]{:S(2)}, u32[]{:S(2)}) collective-permute-start(bf16[192,128]{1,0:T(8,128)(2,1)S(1)} %copy-done.8), channel_id=1, source_target_pairs={{0,8},{4,12},{8,16},{12,20},{16,24},{20,28},{1,9},{5,13},{9,17},{1... | collective-permute-start | bytes 147464 | tf_op jit(solution)/shard_map/ppermute | solution.py:53
  10.5 8.4 %collective-permute-start.1 = (bf16[192,128]{1,0:T(8,128)(2,1)S(1)}, bf16[192,128]{1,0:T(8,128)(2,1)S(1)}, u32[]{:S(2)}, u32[]{:S(2)}) collective-permute-start(bf16[192,128]{1,0:T(8,128)(2,1)S(1)} %copy-done.8), channel_id=1, source_target_pairs={{0,12},{4,16},{8,20},{12,24},{16,28},{1,13},{5,17},{9,21},{13,25},... | collective-permute-start | bytes 147464 | tf_op jit(solution)/shard_map/ppermute | solution.py:53
  11.8 9.9 %collective-permute-start = (bf16[192,128]{1,0:T(8,128)(2,1)S(1)}, bf16[192,128]{1,0:T(8,128)(2,1)S(1)}, u32[]{:S(2)}, u32[]{:S(2)}) collective-permute-start(bf16[192,128]{1,0:T(8,128)(2,1)S(1)} %copy-done.8), channel_id=1, source_target_pairs={{0,16},{4,20},{8,24},{12,28},{1,17},{5,21},{9,25},{13,29},{2,18},{... | collective-permute-start | bytes 147464 | tf_op jit(solution)/shard_map/ppermute | solution.py:53
  13.1 8.6 %collective-permute-start.3 = (bf16[192,128]{1,0:T(8,128)(2,1)S(1)}, bf16[192,128]{1,0:T(8,128)(2,1)S(1)}, u32[]{:S(2)}, u32[]{:S(2)}) collective-permute-start(bf16[192,128]{1,0:T(8,128)(2,1)S(1)} %copy-done.8), channel_id=1, source_target_pairs={{0,4},{4,8},{8,12},{12,16},{16,20},{20,24},{24,28},{1,5},{5,9},{9,... | collective-permute-start | bytes 147464 | tf_op jit(solution)/shard_map/ppermute | solution.py:53
  14.4 47.8 %collective-permute-start.4 = (bf16[192,2048]{1,0:T(8,128)(2,1)}, bf16[192,2048]{1,0:T(8,128)(2,1)S(1)}, u32[]{:S(2)}, u32[]{:S(2)}) collective-permute-start(bf16[192,2048]{1,0:T(8,128)(2,1)} %own_ref.3), channel_id=1, source_target_pairs={{0,1},{1,0},{2,3},{3,2},{4,5},{5,4},{6,7},{7,6},{8,9},{9,8},{10,11... | collective-permute-start | bytes 2359304 | tf_op jit(solution)/shard_map/ppermute | solution.py:204
  17.1 5.4 %copy-start.9 = (bf16[192,128]{1,0:T(8,128)(2,1)}, bf16[192,128]{1,0:T(8,128)(2,1)S(1)}, u32[]{:S(2)}) copy-start(bf16[192,128]{1,0:T(8,128)(2,1)S(1)} %collective-permute-done.2.refs_2_) | copy-start | bytes 147460
  18.9 3.6 %copy-start.10 = (bf16[192,128]{1,0:T(8,128)(2,1)}, bf16[192,128]{1,0:T(8,128)(2,1)S(1)}, u32[]{:S(2)}) copy-start(bf16[192,128]{1,0:T(8,128)(2,1)S(1)} %collective-permute-done.1.refs_1_) | copy-start | bytes 147460
  21.7 0.8 copy-start.11
  21.7 0.8 copy-start.12
  22.5 25.9 %all-to-all-start.1 = ((bf16[8,2,64,128]{3,2,1,0:T(8,128)(2,1)}), bf16[8,2,64,128]{3,2,1,0:T(8,128)(2,1)S(1)}, u32[]{:S(2)}, u32[]{:S(2)}) async-start(bf16[8,2,64,128]{3,2,1,0:T(8,128)(2,1)} %broadcast_in_dim.7), calls=%async_computation.1 | async-start | bytes 524288 | tf_op jit(solution)/shard_map/all_to_all | solution.py:47
  37.0 17.7 %collective-permute-start.5 = (bf16[192,128]{1,0:T(8,128)(2,1)}, bf16[192,128]{1,0:T(8,128)(2,1)S(1)}, u32[]{:S(2)}, u32[]{:S(2)}) collective-permute-start(bf16[192,128]{1,0:T(8,128)(2,1)} %get-tuple-element.50), channel_id=1, source_target_pairs={{4,0},{8,4},{12,8},{16,12},{20,16},{24,20},{28,24},{5,1},{9,5},{13... | collective-permute-start | bytes 147464 | tf_op jit(solution)/shard_map/ppermute | solution.py:57
  40.3 14.4 %collective-permute-start.6 = (bf16[192,128]{1,0:T(8,128)(2,1)}, bf16[192,128]{1,0:T(8,128)(2,1)S(1)}, u32[]{:S(2)}, u32[]{:S(2)}) collective-permute-start(bf16[192,128]{1,0:T(8,128)(2,1)} %get-tuple-element.51), channel_id=1, source_target_pairs={{8,0},{12,4},{16,8},{20,12},{24,16},{28,20},{9,1},{13,5},{17,9},{2... | collective-permute-start | bytes 147464 | tf_op jit(solution)/shard_map/ppermute | solution.py:57
  44.6 10.1 %collective-permute-start.7 = (bf16[192,128]{1,0:T(8,128)(2,1)}, bf16[192,128]{1,0:T(8,128)(2,1)S(1)}, u32[]{:S(2)}, u32[]{:S(2)}) collective-permute-start(bf16[192,128]{1,0:T(8,128)(2,1)} %get-tuple-element.52), channel_id=1, source_target_pairs={{12,0},{16,4},{20,8},{24,12},{28,16},{13,1},{17,5},{21,9},{25,13},... | collective-permute-start | bytes 147464 | tf_op jit(solution)/shard_map/ppermute | solution.py:57
  47.1 7.6 %collective-permute-start.8 = (bf16[192,128]{1,0:T(8,128)(2,1)}, bf16[192,128]{1,0:T(8,128)(2,1)S(1)}, u32[]{:S(2)}, u32[]{:S(2)}) collective-permute-start(bf16[192,128]{1,0:T(8,128)(2,1)} %get-tuple-element.53), channel_id=1, source_target_pairs={{16,0},{20,4},{24,8},{28,12},{17,1},{21,5},{25,9},{29,13},{18,2},{... | collective-permute-start | bytes 147464 | tf_op jit(solution)/shard_map/ppermute | solution.py:57
  49.7 5.0 %copy-start.6 = (f32[192,128]{1,0:T(8,128)S(1)}, f32[192,128]{1,0:T(8,128)}, u32[]{:S(2)}) copy-start(f32[192,128]{1,0:T(8,128)} %get-tuple-element.49) | copy-start | bytes 294916
  49.7 12.5 %copy-start = (bf16[192,2048]{1,0:T(8,128)(2,1)S(1)}, bf16[192,2048]{1,0:T(8,128)(2,1)}, u32[]{:S(2)}) copy-start(bf16[192,2048]{1,0:T(8,128)(2,1)} %own_ref.3) | copy-start | bytes 2359300
  49.7 17.1 %all-to-all-start.3 = ((bf16[4,8,2,64,128]{4,3,2,1,0:T(8,128)(2,1)}), bf16[4,8,2,64,128]{4,3,2,1,0:T(8,128)(2,1)S(1)}, u32[]{:S(2)}, u32[]{:S(2)}) async-start(bf16[4,8,2,64,128]{4,3,2,1,0:T(8,128)(2,1)} %broadcast_in_dim.8), calls=%async_computation.3 | async-start | bytes 2097152 | tf_op jit(solution)/shard_map/all_to_all | solution.py:47
  54.8 7.4 %collective-permute-start.9 = (bf16[192,128]{1,0:T(8,128)(2,1)S(1)}, bf16[192,128]{1,0:T(8,128)(2,1)S(1)}, u32[]{:S(2)}, u32[]{:S(2)}) collective-permute-start(bf16[192,128]{1,0:T(8,128)(2,1)S(1)} %add_convert_fusion.1.dv_ref), channel_id=1, source_target_pairs={{0,2},{2,0},{1,3},{3,1},{4,6},{6,4},{5,7},{7,5},{8,10},{10,8},{9,1... | collective-permute-start | bytes 147464 | tf_op jit(solution)/shard_map/ppermute | solution.py:224
  62.2 1.8 %copy-start.1 = (bf16[192,2048]{1,0:T(8,128)(2,1)}, bf16[192,2048]{1,0:T(8,128)(2,1)S(1)}, u32[]{:S(2)}) copy-start(bf16[192,2048]{1,0:T(8,128)(2,1)S(1)} %collective-permute-done.4.near_ref) | copy-start | bytes 2359300
  64.0 1.0 copy-start.3
  64.9 4.8 %collective-permute-start.10 = (bf16[4,8,2,64,128]{4,3,2,1,0:T(8,128)(2,1)}, bf16[4,8,2,64,128]{4,3,2,1,0:T(8,128)(2,1)S(1)}, u32[]{:S(2)}, u32[]{:S(2)}) collective-permute-start(bf16[4,8,2,64,128]{4,3,2,1,0:T(8,128)(2,1)} %get-tuple-element.55), channel_id=1, source_target_pairs={{0,32},{32,0},{1,33},{33,1},{2,34},{34,2},{3,35},{35,3},{4,36},{36... | collective-permute-start | bytes 3145736 | tf_op jit(solution)/shard_map/ppermute | solution.py:230
  66.9 10.1 %collective-permute-start.11 = (bf16[4,8,2,64,128]{4,3,2,1,0:T(8,128)(2,1)S(1)}, bf16[4,8,2,64,128]{4,3,2,1,0:T(8,128)(2,1)}, u32[]{:S(2)}, u32[]{:S(2)}) collective-permute-start(bf16[4,8,2,64,128]{4,3,2,1,0:T(8,128)(2,1)S(1)} %all-to-all-done.3.mine_ref), channel_id=1, source_target_pairs={{0,32},{32,0},{1,33},{33,1},{2,34},{34,2},{3,35},{35,3},{4,36},{36... | collective-permute-start | bytes 3145736 | tf_op jit(solution)/shard_map/ppermute | solution.py:225
  69.7 1.2 copy-start.4
  72.1 20.1 %all-to-all-start.2 = ((bf16[4,8,2,64,128]{4,3,2,1,0:T(8,128)(2,1)}), bf16[4,8,2,64,128]{4,3,2,1,0:T(8,128)(2,1)S(1)}, u32[]{:S(2)}, u32[]{:S(2)}) async-start(bf16[4,8,2,64,128]{4,3,2,1,0:T(8,128)(2,1)} %add_halves.1), calls=%async_computation.2 | async-start | bytes 2097152 | tf_op jit(solution)/shard_map/all_to_all | solution.py:235
  76.9 1.1 copy-start.2
  79.9 7.1 %collective-permute-start.12 = (bf16[192,128]{1,0:T(8,128)(2,1)S(1)}, bf16[192,128]{1,0:T(8,128)(2,1)S(1)}, u32[]{:S(2)}, u32[]{:S(2)}) collective-permute-start(bf16[192,128]{1,0:T(8,128)(2,1)S(1)} %get-tuple-element.58), channel_id=1, source_target_pairs={{0,2},{2,0},{1,3},{3,1},{4,6},{6,4},{5,7},{7,5},{8,10},{10,8},{9,1... | collective-permute-start | bytes 147464 | tf_op jit(solution)/shard_map/ppermute | solution.py:232
  87.0 6.0 %copy-start.7 = (bf16[192,128]{1,0:T(8,128)(2,1)}, bf16[192,128]{1,0:T(8,128)(2,1)S(1)}, u32[]{:S(2)}) copy-start(bf16[192,128]{1,0:T(8,128)(2,1)S(1)} %add_convert_fusion.refs_9_) | copy-start | bytes 147460
  87.0 6.4 %collective-permute-start.16 = (bf16[192,128]{1,0:T(8,128)(2,1)S(1)}, bf16[192,128]{1,0:T(8,128)(2,1)S(1)}, u32[]{:S(2)}, u32[]{:S(2)}) collective-permute-start(bf16[192,128]{1,0:T(8,128)(2,1)S(1)} %add_convert_fusion.refs_9_), channel_id=1, source_target_pairs={{0,4},{4,8},{8,12},{12,16},{16,20},{20,24},{24,28},{1,5},{5,9},{9,... | collective-permute-start | bytes 147464 | tf_op jit(solution)/shard_map/ppermute | solution.py:53
  88.3 6.9 %collective-permute-start.15 = (bf16[192,128]{1,0:T(8,128)(2,1)S(1)}, bf16[192,128]{1,0:T(8,128)(2,1)S(1)}, u32[]{:S(2)}, u32[]{:S(2)}) collective-permute-start(bf16[192,128]{1,0:T(8,128)(2,1)S(1)} %add_convert_fusion.refs_9_), channel_id=1, source_target_pairs={{0,8},{4,12},{8,16},{12,20},{16,24},{20,28},{1,9},{5,13},{9,17},{1... | collective-permute-start | bytes 147464 | tf_op jit(solution)/shard_map/ppermute | solution.py:53
  89.6 10.4 %collective-permute-start.14 = (bf16[192,128]{1,0:T(8,128)(2,1)S(1)}, bf16[192,128]{1,0:T(8,128)(2,1)S(1)}, u32[]{:S(2)}, u32[]{:S(2)}) collective-permute-start(bf16[192,128]{1,0:T(8,128)(2,1)S(1)} %add_convert_fusion.refs_9_), channel_id=1, source_target_pairs={{0,12},{4,16},{8,20},{12,24},{16,28},{1,13},{5,17},{9,21},{13,25},... | collective-permute-start | bytes 147464 | tf_op jit(solution)/shard_map/ppermute | solution.py:53
  90.9 11.1 %collective-permute-start.13 = (bf16[192,128]{1,0:T(8,128)(2,1)S(1)}, bf16[192,128]{1,0:T(8,128)(2,1)S(1)}, u32[]{:S(2)}, u32[]{:S(2)}) collective-permute-start(bf16[192,128]{1,0:T(8,128)(2,1)S(1)} %add_convert_fusion.refs_9_), channel_id=1, source_target_pairs={{0,16},{4,20},{8,24},{12,28},{1,17},{5,21},{9,25},{13,29},{2,18},{... | collective-permute-start | bytes 147464 | tf_op jit(solution)/shard_map/ppermute | solution.py:53
  93.3 8.6 %copy-start.17 = (bf16[192,128]{1,0:T(8,128)(2,1)}, bf16[192,128]{1,0:T(8,128)(2,1)S(1)}, u32[]{:S(2)}) copy-start(bf16[192,128]{1,0:T(8,128)(2,1)S(1)} %collective-permute-done.16.refs_8_) | copy-start | bytes 147460
  95.2 6.8 %copy-start.18 = (bf16[192,128]{1,0:T(8,128)(2,1)}, bf16[192,128]{1,0:T(8,128)(2,1)S(1)}, u32[]{:S(2)}) copy-start(bf16[192,128]{1,0:T(8,128)(2,1)S(1)} %collective-permute-done.15.refs_7_) | copy-start | bytes 147460
  100.0 2.0 %copy-start.19 = (bf16[192,128]{1,0:T(8,128)(2,1)}, bf16[192,128]{1,0:T(8,128)(2,1)S(1)}, u32[]{:S(2)}) copy-start(bf16[192,128]{1,0:T(8,128)(2,1)S(1)} %collective-permute-done.14.refs_6_) | copy-start | bytes 147460
  102.0 0.6 copy-start.20
  102.6 17.4 %all-to-all-start.4 = ((bf16[8,2,64,128]{3,2,1,0:T(8,128)(2,1)}), bf16[8,2,64,128]{3,2,1,0:T(8,128)(2,1)S(1)}, u32[]{:S(2)}, u32[]{:S(2)}) async-start(bf16[8,2,64,128]{3,2,1,0:T(8,128)(2,1)} %sum_blocks.1), calls=%async_computation.4 | async-start | bytes 524288 | tf_op jit(solution)/shard_map/all_to_all | solution.py:238
  120.0 0.8 copy-start.16
  120.0 4.2 %copy-start.15 = (bf16[192,128]{1,0:T(8,128)(2,1)S(1)}, bf16[192,128]{1,0:T(8,128)(2,1)}, u32[]{:S(2)}) copy-start(bf16[192,128]{1,0:T(8,128)(2,1)} %get-tuple-element.74) | copy-start | bytes 147460
  120.0 8.4 %copy-start.14 = (bf16[192,128]{1,0:T(8,128)(2,1)S(1)}, bf16[192,128]{1,0:T(8,128)(2,1)}, u32[]{:S(2)}) copy-start(bf16[192,128]{1,0:T(8,128)(2,1)} %get-tuple-element.75) | copy-start | bytes 147460
  120.0 11.1 %copy-start.13 = (bf16[192,128]{1,0:T(8,128)(2,1)S(1)}, bf16[192,128]{1,0:T(8,128)(2,1)}, u32[]{:S(2)}) copy-start(bf16[192,128]{1,0:T(8,128)(2,1)} %get-tuple-element.76) | copy-start | bytes 147460
  120.8 20.7 %collective-permute-start.17 = (bf16[192,128]{1,0:T(8,128)(2,1)S(1)}, bf16[192,128]{1,0:T(8,128)(2,1)S(1)}, u32[]{:S(2)}, u32[]{:S(2)}) collective-permute-start(bf16[192,128]{1,0:T(8,128)(2,1)S(1)} %copy-done.16), channel_id=1, source_target_pairs={{4,0},{8,4},{12,8},{16,12},{20,16},{24,20},{28,24},{5,1},{9,5},{13... | collective-permute-start | bytes 147464 | tf_op jit(solution)/shard_map/ppermute | solution.py:57
  124.1 17.4 %collective-permute-start.18 = (bf16[192,128]{1,0:T(8,128)(2,1)S(1)}, bf16[192,128]{1,0:T(8,128)(2,1)S(1)}, u32[]{:S(2)}, u32[]{:S(2)}) collective-permute-start(bf16[192,128]{1,0:T(8,128)(2,1)S(1)} %copy-done.15), channel_id=1, source_target_pairs={{8,0},{12,4},{16,8},{20,12},{24,16},{28,20},{9,1},{13,5},{17,9},{2... | collective-permute-start | bytes 147464 | tf_op jit(solution)/shard_map/ppermute | solution.py:57
  128.4 13.1 %collective-permute-start.19 = (bf16[192,128]{1,0:T(8,128)(2,1)S(1)}, bf16[192,128]{1,0:T(8,128)(2,1)S(1)}, u32[]{:S(2)}, u32[]{:S(2)}) collective-permute-start(bf16[192,128]{1,0:T(8,128)(2,1)S(1)} %copy-done.14), channel_id=1, source_target_pairs={{12,0},{16,4},{20,8},{24,12},{28,16},{13,1},{17,5},{21,9},{25,13},... | collective-permute-start | bytes 147464 | tf_op jit(solution)/shard_map/ppermute | solution.py:57
  131.1 10.4 %collective-permute-start.20 = (bf16[192,128]{1,0:T(8,128)(2,1)S(1)}, bf16[192,128]{1,0:T(8,128)(2,1)S(1)}, u32[]{:S(2)}, u32[]{:S(2)}) collective-permute-start(bf16[192,128]{1,0:T(8,128)(2,1)S(1)} %copy-done.13), channel_id=1, source_target_pairs={{16,0},{20,4},{24,8},{28,12},{17,1},{21,5},{25,9},{29,13},{18,2},{... | collective-permute-start | bytes 147464 | tf_op jit(solution)/shard_map/ppermute | solution.py:57
  134.3 7.2 %copy-start.5 = (f32[192,128]{1,0:T(8,128)S(1)}, f32[192,128]{1,0:T(8,128)}, u32[]{:S(2)}) copy-start(f32[192,128]{1,0:T(8,128)} %get-tuple-element.72) | copy-start | bytes 294916
  134.3 15.9 %all-to-all-start.5 = ((f32[4,64,128]{2,1,0:T(8,128)}), f32[4,64,128]{2,1,0:T(8,128)S(1)}, u32[]{:S(2)}, u32[]{:S(2)}) async-start(f32[4,64,128]{2,1,0:T(8,128)} %bitcast), calls=%async_computation.5 | async-start | bytes 262144 | tf_op jit(solution)/shard_map/all_to_all | solution.py:247

commit v10 on v9

--- a/solution.py
+++ b/solution.py
@@ -27,7 +27,7 @@
     return jax.ShapeDtypeStruct(dims, dtype)
 
 
-def call(kernel, out_shape, n_in, flops, n_bytes, scratch=(), smem=0, vmem=48):
+def call(kernel, out_shape, n_in, flops, n_bytes, scratch=(), smem=0, vmem=20):
     outs = out_shape if isinstance(out_shape, tuple) else None
     return pl.pallas_call(
         kernel,
@@ -215,7 +215,7 @@
     whole = shape((4, 8, 2, 64, HEAD_DIM))
     *dv, stats = call(
         soft, (block,) * REACH + (own, shape((8, LANES), F32)), 7, 3 * 10**9, 2 * 10**6,
-        (rows, rows, bias, pairs, window), smem=1, vmem=56,
+        (rows, rows, bias, pairs, window), smem=1, vmem=28,
     )(lengths, queries, grad_out, *keys)
     weight, stats = lax.optimization_barrier((weight, stats))
     weight = to_all(weight, "x", 4)
@@ -240,7 +240,7 @@
     wide = shape((TOK, GROUP * HEAD_DIM))
     attended, grad_query, *dk = call(
         attend, (wide, wide) + (block,) * REACH + (own,), 13, 6 * 10**9, 4 * 10**6,
-        (rows, rows, bias, pairs, window, window), smem=1, vmem=56,
+        (rows, rows, bias, pairs, window, window), smem=1, vmem=28,
     )(lengths, queries, grad_out, stats, *keys, *values)
     partial = call(twice_sum, shape((2, 2, 64, HEAD_DIM), F32), 1, 10**6, 10**6)(partial)
     partial, dk = lax.optimization_barrier((partial, dk))

time: 152 us -> 153 us (level)
  starting transfers between devices: 93 us -> 94.9 us
    ppermute x8, starting transfers between devices: 24.9 us -> 26.9 us  [from_ahead(): lax.ppermute(block, 'ctx', [(i + distance, i) for i in range(8 - distance)])]
    unnamed x42 -> x20, local copies, waits for them, and re-layouts: 4.05 us -> 3.37 us
  transfers between devices with their start and end apart: 27 -> 27, of which waited for: 11 -> 11; matrix products, arithmetic and copies ran while one was open for 2% -> 2% of each run, Pallas kernels for 13% -> 12%
where the time goes in v10:
time: 153 us; the launch traced here: 151 us
  starting transfers between devices  94.9 us (62%)
  waiting for transfers between devices  27.8 us (18%)
  Pallas kernels  18.9 us (12%)
  local copies, waits for them, and re-layouts  6.73 us (4%)
  other arithmetic  2.15 us (1%)
    ppermute x8, starting transfers between devices, from_ahead(): lax.ppermute(block, 'ctx', [(i + distance, i) for i in range(8 - distance)])  26.9 us
    all_to_all x3, starting transfers between devices, to_all(): lax.all_to_all(jnp.broadcast_to(block[None], (copies,) + block.shape), ax...  21.2 us
    ppermute x8, waiting for transfers between devices, from_behind(): lax.ppermute(block, 'ctx', [(i, i + distance) for i in range(8 - distance)])  13.6 us
    ppermute x8, starting transfers between devices, from_behind(): lax.ppermute(block, 'ctx', [(i, i + distance) for i in range(8 - distance)])  10.3 us
    all_to_all x1, starting transfers between devices, shards(): partial = lax.all_to_all(partial, 'ctx', 0, 0, tiled=True)  9.02 us
    all_to_all x1, waiting for transfers between devices, shards(): lax.all_to_all(partial.reshape(4, 64, HEAD_DIM), ('yh', 'm1'), 0, 0, tile...  8.04 us
    pallas_call x1, Pallas kernels, shards(): call(attend, (wide, wide) + (block,) * REACH + (own,), 13, 6 * 10 ** 9, 4...  7.64 us
    all_to_all x1, starting transfers between devices, shards(): lax.all_to_all(partial.reshape(4, 64, HEAD_DIM), ('yh', 'm1'), 0, 0, tile...  7.05 us
  transfers between devices with their start and end apart: 27, of which 11 were waited for; matrix products, arithmetic and copies ran while one was open for 2% of the time, Pallas kernels for 12%

profile of v10, /device:TPU:450, one launch (start us, length us, event | category | flops | bytes accessed | tf_op | source)
XLA Modules:
  0.0 151.4 jit_solution(13219741108937309217)
XLA Ops:
  0.6 1.4 broadcast_in_dim.6
  2.0 7.2 %all-to-all-start = ((bf16[4,64,128]{2,1,0:T(8,128)(2,1)}), bf16[4,64,128]{2,1,0:T(8,128)(2,1)S(1)}, u32[]{:S(2)}, u32[]{:S(2)}) async-start(bf16[4,64,128]{2,1,0:T(8,128)(2,1)} %broadcast_in_dim.6), calls=%async_computation | async-start | bytes 131072 | tf_op jit(solution)/shard_map/all_to_all | solution.py:47
  9.2 1.3 collective-permute-start.2
  10.5 1.3 collective-permute-start.1
  11.8 1.3 collective-permute-start
  13.1 1.3 collective-permute-start.3
  14.4 2.6 %collective-permute-start.4 = (bf16[192,2048]{1,0:T(8,128)(2,1)}, bf16[192,2048]{1,0:T(8,128)(2,1)S(1)}, u32[]{:S(2)}, u32[]{:S(2)}) collective-permute-start(bf16[192,2048]{1,0:T(8,128)(2,1)} %own_ref.3), channel_id=1, source_target_pairs={{0,1},{1,0},{2,3},{3,2},{4,5},{5,4},{6,7},{7,6},{8,9},{9,8},{10,11... | collective-permute-start | bytes 2359304 | tf_op jit(solution)/shard_map/ppermute | solution.py:204
  17.0 0.1 collective-permute-done.2.refs_2_
  17.1 1.7 %collective-permute-done.1.refs_1_ = bf16[192,128]{1,0:T(8,128)(2,1)S(1)} collective-permute-done((bf16[192,128]{1,0:T(8,128)(2,1)S(1)}, bf16[192,128]{1,0:T(8,128)(2,1)S(1)}, u32[]{:S(2)}, u32[]{:S(2)}) %collective-permute-start.1) | collective-permute-done | bytes 49184 | tf_op jit(solution)/shard_map/ppermute | solution.py:53
  18.9 2.8 %collective-permute-done.refs_0_ = bf16[192,128]{1,0:T(8,128)(2,1)S(1)} collective-permute-done((bf16[192,128]{1,0:T(8,128)(2,1)S(1)}, bf16[192,128]{1,0:T(8,128)(2,1)S(1)}, u32[]{:S(2)}, u32[]{:S(2)}) %collective-permute-start) | collective-permute-done | bytes 49184 | tf_op jit(solution)/shard_map/ppermute | solution.py:53
  21.7 0.0 collective-permute-done.3.refs_3_
  21.7 0.0 all-to-all-done
  21.7 0.0 copy-start.5
  21.7 0.0 copy-start.6
  21.7 0.8 broadcast_in_dim.7
  22.5 9.0 %all-to-all-start.1 = ((bf16[8,2,64,128]{3,2,1,0:T(8,128)(2,1)}), bf16[8,2,64,128]{3,2,1,0:T(8,128)(2,1)S(1)}, u32[]{:S(2)}, u32[]{:S(2)}) async-start(bf16[8,2,64,128]{3,2,1,0:T(8,128)(2,1)} %broadcast_in_dim.7), calls=%async_computation.1 | async-start | bytes 524288 | tf_op jit(solution)/shard_map/all_to_all | solution.py:47
  31.5 4.9 %soft.1 = (bf16[192,128]{1,0:T(8,128)(2,1)S(1)}, bf16[192,128]{1,0:T(8,128)(2,1)}, bf16[192,128]{1,0:T(8,128)(2,1)}, bf16[192,128]{1,0:T(8,128)(2,1)}, f32[192,128]{1,0:T(8,128)S(1)}, /*index=5*/f32[8,384]{1,0:T(8,128)S(1)}) custom-call(s32[1,8]{1,0:T(1,128)S(1)} %copy-done.9, bf16[192,1024]{1,0:T(8,128)(2,1)S(1)} %copy-done.5, ...), custom_call_target="tpu_custom_call" | custom-call | flops 3000000000 | bytes 2000000 | tf_op jit(solution)/shard_map/soft/pallas_call | solution.py:216
  36.4 3.4 %collective-permute-start.5 = (bf16[192,128]{1,0:T(8,128)(2,1)}, bf16[192,128]{1,0:T(8,128)(2,1)S(1)}, u32[]{:S(2)}, u32[]{:S(2)}) collective-permute-start(bf16[192,128]{1,0:T(8,128)(2,1)} %get-tuple-element.50), channel_id=1, source_target_pairs={{4,0},{8,4},{12,8},{16,12},{20,16},{24,20},{28,24},{5,1},{9,5},{13... | collective-permute-start | bytes 147464 | tf_op jit(solution)/shard_map/ppermute | solution.py:57
  39.7 4.3 %collective-permute-start.6 = (bf16[192,128]{1,0:T(8,128)(2,1)}, bf16[192,128]{1,0:T(8,128)(2,1)S(1)}, u32[]{:S(2)}, u32[]{:S(2)}) collective-permute-start(bf16[192,128]{1,0:T(8,128)(2,1)} %get-tuple-element.51), channel_id=1, source_target_pairs={{8,0},{12,4},{16,8},{20,12},{24,16},{28,20},{9,1},{13,5},{17,9},{2... | collective-permute-start | bytes 147464 | tf_op jit(solution)/shard_map/ppermute | solution.py:57
  44.0 3.1 %collective-permute-start.7 = (bf16[192,128]{1,0:T(8,128)(2,1)}, bf16[192,128]{1,0:T(8,128)(2,1)}, u32[]{:S(2)}, u32[]{:S(2)}) collective-permute-start(bf16[192,128]{1,0:T(8,128)(2,1)} %get-tuple-element.52), channel_id=1, source_target_pairs={{12,0},{16,4},{20,8},{24,12},{28,16},{13,1},{17,5},{21,9},{25,13},... | collective-permute-start | bytes 147464 | tf_op jit(solution)/shard_map/ppermute | solution.py:57
  47.1 1.9 %collective-permute-start.8 = (bf16[192,128]{1,0:T(8,128)(2,1)S(1)}, bf16[192,128]{1,0:T(8,128)(2,1)}, u32[]{:S(2)}, u32[]{:S(2)}) collective-permute-start(bf16[192,128]{1,0:T(8,128)(2,1)S(1)} %get-tuple-element.53), channel_id=1, source_target_pairs={{16,0},{20,4},{24,8},{28,12},{17,1},{21,5},{25,9},{29,13},{18,2},{... | collective-permute-start | bytes 147464 | tf_op jit(solution)/shard_map/ppermute | solution.py:57
  49.0 0.0 all-to-all-done.1
  49.0 1.2 broadcast_in_dim.8
  50.2 5.0 %all-to-all-start.3 = ((bf16[4,8,2,64,128]{4,3,2,1,0:T(8,128)(2,1)}), bf16[4,8,2,64,128]{4,3,2,1,0:T(8,128)(2,1)S(1)}, u32[]{:S(2)}, u32[]{:S(2)}) async-start(bf16[4,8,2,64,128]{4,3,2,1,0:T(8,128)(2,1)} %broadcast_in_dim.8), calls=%async_computation.3 | async-start | bytes 2097152 | tf_op jit(solution)/shard_map/all_to_all | solution.py:47
  55.2 0.0 collective-permute-done.5
  55.2 0.0 collective-permute-done.8
  55.2 0.9 add_convert_fusion.1.dv_ref
  56.1 4.7 %collective-permute-start.9 = (bf16[192,128]{1,0:T(8,128)(2,1)S(1)}, bf16[192,128]{1,0:T(8,128)(2,1)S(1)}, u32[]{:S(2)}, u32[]{:S(2)}) collective-permute-start(bf16[192,128]{1,0:T(8,128)(2,1)S(1)} %add_convert_fusion.1.dv_ref), channel_id=1, source_target_pairs={{0,2},{2,0},{1,3},{3,1},{4,6},{6,4},{5,7},{7,5},{8,10},{10,8},{9,1... | collective-permute-start | bytes 147464 | tf_op jit(solution)/shard_map/ppermute | solution.py:224
  60.8 2.7 %collective-permute-done.9.far_dv_ref = bf16[192,128]{1,0:T(8,128)(2,1)S(1)} collective-permute-done((bf16[192,128]{1,0:T(8,128)(2,1)S(1)}, bf16[192,128]{1,0:T(8,128)(2,1)S(1)}, u32[]{:S(2)}, u32[]{:S(2)}) %collective-permute-start.9) | collective-permute-done | bytes 49184 | tf_op jit(solution)/shard_map/ppermute | solution.py:224
  63.5 0.0 collective-permute-done.4.near_ref
  63.5 1.8 %weight_grad.1 = (bf16[4,8,2,64,128]{4,3,2,1,0:T(8,128)(2,1)S(1)}, bf16[4,8,2,64,128]{4,3,2,1,0:T(8,128)(2,1)}) custom-call(bf16[192,2048]{1,0:T(8,128)(2,1)S(1)} %copy-done, bf16[192,2048]{1,0:T(8,128)(2,1)S(1)} %collective-permute-done.4.near_ref, bf16[192,128]{1,0:T(8,128)(2,1)S(1)} %add_convert_fusion.1.dv_ref, ...), custom_call_target="tpu_custom_call" | custom-call | flops 400000000 | bytes 5000000 | tf_op jit(solution)/shard_map/weight_grad/pallas_call | solution.py:227
  65.3 1.0 copy-done.3
  66.3 1.9 %collective-permute-start.10 = (bf16[4,8,2,64,128]{4,3,2,1,0:T(8,128)(2,1)}, bf16[4,8,2,64,128]{4,3,2,1,0:T(8,128)(2,1)S(1)}, u32[]{:S(2)}, u32[]{:S(2)}) collective-permute-start(bf16[4,8,2,64,128]{4,3,2,1,0:T(8,128)(2,1)} %get-tuple-element.55), channel_id=1, source_target_pairs={{0,32},{32,0},{1,33},{33,1},{2,34},{34,2},{3,35},{35,3},{4,36},{36... | collective-permute-start | bytes 3145736 | tf_op jit(solution)/shard_map/ppermute | solution.py:230
  68.2 0.0 all-to-all-done.3.mine_ref
  68.2 2.4 %collective-permute-start.11 = (bf16[4,8,2,64,128]{4,3,2,1,0:T(8,128)(2,1)S(1)}, bf16[4,8,2,64,128]{4,3,2,1,0:T(8,128)(2,1)}, u32[]{:S(2)}, u32[]{:S(2)}) collective-permute-start(bf16[4,8,2,64,128]{4,3,2,1,0:T(8,128)(2,1)S(1)} %all-to-all-done.3.mine_ref), channel_id=1, source_target_pairs={{0,32},{32,0},{1,33},{33,1},{2,34},{34,2},{3,35},{35,3},{4,36},{36... | collective-permute-start | bytes 3145736 | tf_op jit(solution)/shard_map/ppermute | solution.py:225
  70.6 0.4 collective-permute-done.10.b_ref
  71.0 1.2 copy-done.4
  72.3 1.2 add_halves.1
  73.5 4.8 %all-to-all-start.2 = ((bf16[4,8,2,64,128]{4,3,2,1,0:T(8,128)(2,1)}), bf16[4,8,2,64,128]{4,3,2,1,0:T(8,128)(2,1)S(1)}, u32[]{:S(2)}, u32[]{:S(2)}) async-start(bf16[4,8,2,64,128]{4,3,2,1,0:T(8,128)(2,1)} %add_halves.1), calls=%async_computation.2 | async-start | bytes 2097152 | tf_op jit(solution)/shard_map/all_to_all | solution.py:235
  78.3 0.0 collective-permute-done.11.other_ref
  78.3 1.1 copy-done.2
  79.4 1.8 %project.1 = (f32[192,128]{1,0:T(8,128)S(1)}, bf16[192,128]{1,0:T(8,128)(2,1)S(1)}) custom-call(bf16[192,2048]{1,0:T(8,128)(2,1)S(1)} %copy-done, bf16[192,2048]{1,0:T(8,128)(2,1)S(1)} %copy-done.2, bf16[4,8,2,64,128]{4,3,2,1,0:T(8,128)(2,1)S(1)} %all-to-all-done.3.mine_ref, bf16[4,8,2,64,128]{4,3,2,1,0:T(8,128)(2,1)} %collective-permute-done.11.other_ref), custom_call_target="tpu_custom_call" | custom-call | flops 400000000 | bytes 5000000 | tf_op jit(solution)/shard_map/project/pallas_call | solution.py:231
  81.2 4.1 %collective-permute-start.12 = (bf16[192,128]{1,0:T(8,128)(2,1)S(1)}, bf16[192,128]{1,0:T(8,128)(2,1)S(1)}, u32[]{:S(2)}, u32[]{:S(2)}) collective-permute-start(bf16[192,128]{1,0:T(8,128)(2,1)S(1)} %get-tuple-element.58), channel_id=1, source_target_pairs={{0,2},{2,0},{1,3},{3,1},{4,6},{6,4},{5,7},{7,5},{8,10},{10,8},{9,1... | collective-permute-start | bytes 147464 | tf_op jit(solution)/shard_map/ppermute | solution.py:232
  85.4 2.9 %collective-permute-done.12 = bf16[192,128]{1,0:T(8,128)(2,1)S(1)} collective-permute-done((bf16[192,128]{1,0:T(8,128)(2,1)S(1)}, bf16[192,128]{1,0:T(8,128)(2,1)S(1)}, u32[]{:S(2)}, u32[]{:S(2)}) %collective-permute-start.12) | collective-permute-done | bytes 49184 | tf_op jit(solution)/shard_map/ppermute | solution.py:232
  88.3 1.3 collective-permute-start.16
  89.6 1.3 collective-permute-start.15
  90.9 1.3 collective-permute-start.14
  92.2 1.3 collective-permute-start.13
  93.6 0.8 sum_blocks.1
  94.4 0.3 collective-permute-done.16.refs_8_
  94.7 1.8 %collective-permute-done.15.refs_7_ = bf16[192,128]{1,0:T(8,128)(2,1)S(1)} collective-permute-done((bf16[192,128]{1,0:T(8,128)(2,1)S(1)}, bf16[192,128]{1,0:T(8,128)(2,1)S(1)}, u32[]{:S(2)}, u32[]{:S(2)}) %collective-permute-start.15) | collective-permute-done | bytes 49184 | tf_op jit(solution)/shard_map/ppermute | solution.py:53
  96.5 4.8 %collective-permute-done.14.refs_6_ = bf16[192,128]{1,0:T(8,128)(2,1)S(1)} collective-permute-done((bf16[192,128]{1,0:T(8,128)(2,1)S(1)}, bf16[192,128]{1,0:T(8,128)(2,1)S(1)}, u32[]{:S(2)}, u32[]{:S(2)}) %collective-permute-start.14) | collective-permute-done | bytes 49184 | tf_op jit(solution)/shard_map/ppermute | solution.py:53
  101.4 1.9 %collective-permute-done.13.refs_5_ = bf16[192,128]{1,0:T(8,128)(2,1)S(1)} collective-permute-done((bf16[192,128]{1,0:T(8,128)(2,1)S(1)}, bf16[192,128]{1,0:T(8,128)(2,1)S(1)}, u32[]{:S(2)}, u32[]{:S(2)}) %collective-permute-start.13) | collective-permute-done | bytes 49184 | tf_op jit(solution)/shard_map/ppermute | solution.py:53
  103.3 9.0 %all-to-all-start.4 = ((bf16[8,2,64,128]{3,2,1,0:T(8,128)(2,1)}), bf16[8,2,64,128]{3,2,1,0:T(8,128)(2,1)S(1)}, u32[]{:S(2)}, u32[]{:S(2)}) async-start(bf16[8,2,64,128]{3,2,1,0:T(8,128)(2,1)} %sum_blocks.1), calls=%async_computation.4 | async-start | bytes 524288 | tf_op jit(solution)/shard_map/all_to_all | solution.py:238
  112.3 7.6 %attend.1 = (bf16[192,1024]{1,0:T(8,128)(2,1)}, bf16[192,1024]{1,0:T(8,128)(2,1)}, bf16[192,128]{1,0:T(8,128)(2,1)S(1)}, bf16[192,128]{1,0:T(8,128)(2,1)S(1)}, b...) custom-call(s32[1,8]{1,0:T(1,128)S(1)} %copy-done.9, ...), custom_call_target="tpu_custom_call" | custom-call | flops 6000000000 | bytes 4000000 | tf_op jit(solution)/shard_map/attend/pallas_call | solution.py:241
  120.0 0.7 twice_sum.1
  120.7 3.4 %collective-permute-start.17 = (bf16[192,128]{1,0:T(8,128)(2,1)S(1)}, bf16[192,128]{1,0:T(8,128)(2,1)S(1)}, u32[]{:S(2)}, u32[]{:S(2)}) collective-permute-start(bf16[192,128]{1,0:T(8,128)(2,1)S(1)} %get-tuple-element.73), channel_id=1, source_target_pairs={{4,0},{8,4},{12,8},{16,12},{20,16},{24,20},{28,24},{5,1},{9,5},{13... | collective-permute-start | bytes 147464 | tf_op jit(solution)/shard_map/ppermute | solution.py:57
  124.0 4.3 %collective-permute-start.18 = (bf16[192,128]{1,0:T(8,128)(2,1)S(1)}, bf16[192,128]{1,0:T(8,128)(2,1)S(1)}, u32[]{:S(2)}, u32[]{:S(2)}) collective-permute-start(bf16[192,128]{1,0:T(8,128)(2,1)S(1)} %get-tuple-element.74), channel_id=1, source_target_pairs={{8,0},{12,4},{16,8},{20,12},{24,16},{28,20},{9,1},{13,5},{17,9},{2... | collective-permute-start | bytes 147464 | tf_op jit(solution)/shard_map/ppermute | solution.py:57
  128.3 3.5 %collective-permute-start.19 = (bf16[192,128]{1,0:T(8,128)(2,1)S(1)}, bf16[192,128]{1,0:T(8,128)(2,1)S(1)}, u32[]{:S(2)}, u32[]{:S(2)}) collective-permute-start(bf16[192,128]{1,0:T(8,128)(2,1)S(1)} %get-tuple-element.75), channel_id=1, source_target_pairs={{12,0},{16,4},{20,8},{24,12},{28,16},{13,1},{17,5},{21,9},{25,13},... | collective-permute-start | bytes 147464 | tf_op jit(solution)/shard_map/ppermute | solution.py:57
  131.8 3.2 %collective-permute-start.20 = (bf16[192,128]{1,0:T(8,128)(2,1)S(1)}, bf16[192,128]{1,0:T(8,128)(2,1)S(1)}, u32[]{:S(2)}, u32[]{:S(2)}) collective-permute-start(bf16[192,128]{1,0:T(8,128)(2,1)S(1)} %get-tuple-element.76), channel_id=1, source_target_pairs={{16,0},{20,4},{24,8},{28,12},{17,1},{21,5},{25,9},{29,13},{18,2},{... | collective-permute-start | bytes 147464 | tf_op jit(solution)/shard_map/ppermute | solution.py:57
  135.0 7.1 %all-to-all-start.5 = ((f32[4,64,128]{2,1,0:T(8,128)}), f32[4,64,128]{2,1,0:T(8,128)S(1)}, u32[]{:S(2)}, u32[]{:S(2)}) async-start(f32[4,64,128]{2,1,0:T(8,128)} %bitcast), calls=%async_computation.5 | async-start | bytes 262144 | tf_op jit(solution)/shard_map/all_to_all | solution.py:247
  142.1 0.7 multiply_convert_fusion
  142.7 8.0 %all-to-all-done.5 = f32[4,64,128]{2,1,0:T(8,128)S(1)} async-done(((f32[4,64,128]{2,1,0:T(8,128)}), f32[4,64,128]{2,1,0:T(8,128)S(1)}, u32[]{:S(2)}, u32[]{:S(2)}) %all-to-all-start.5) | async-done | bytes 131104 | tf_op jit(solution)/shard_map/all_to_all | solution.py:247
  150.8 0.6 dynamic-slice_reduce_fusion
  (25 shorter events, 0.1 us)
Async XLA Ops:
  2.0 7.2 %copy-start.8 = (bf16[192,128]{1,0:T(8,128)(2,1)S(1)}, bf16[192,128]{1,0:T(8,128)(2,1)}, u32[]{:S(2)}) copy-start(bf16[192,128]{1,0:T(8,128)(2,1)} %refs_4_.1) | copy-start | bytes 147460
  2.0 19.7 %all-to-all-start = ((bf16[4,64,128]{2,1,0:T(8,128)(2,1)}), bf16[4,64,128]{2,1,0:T(8,128)(2,1)S(1)}, u32[]{:S(2)}, u32[]{:S(2)}) async-start(bf16[4,64,128]{2,1,0:T(8,128)(2,1)} %broadcast_in_dim.6), calls=%async_computation | async-start | bytes 131072 | tf_op jit(solution)/shard_map/all_to_all | solution.py:47
  9.2 7.9 %collective-permute-start.2 = (bf16[192,128]{1,0:T(8,128)(2,1)S(1)}, bf16[192,128]{1,0:T(8,128)(2,1)S(1)}, u32[]{:S(2)}, u32[]{:S(2)}) collective-permute-start(bf16[192,128]{1,0:T(8,128)(2,1)S(1)} %copy-done.8), channel_id=1, source_target_pairs={{0,8},{4,12},{8,16},{12,20},{16,24},{20,28},{1,9},{5,13},{9,17},{1... | collective-permute-start | bytes 147464 | tf_op jit(solution)/shard_map/ppermute | solution.py:53
  10.5 8.4 %collective-permute-start.1 = (bf16[192,128]{1,0:T(8,128)(2,1)S(1)}, bf16[192,128]{1,0:T(8,128)(2,1)S(1)}, u32[]{:S(2)}, u32[]{:S(2)}) collective-permute-start(bf16[192,128]{1,0:T(8,128)(2,1)S(1)} %copy-done.8), channel_id=1, source_target_pairs={{0,12},{4,16},{8,20},{12,24},{16,28},{1,13},{5,17},{9,21},{13,25},... | collective-permute-start | bytes 147464 | tf_op jit(solution)/shard_map/ppermute | solution.py:53
  11.8 9.9 %collective-permute-start = (bf16[192,128]{1,0:T(8,128)(2,1)S(1)}, bf16[192,128]{1,0:T(8,128)(2,1)S(1)}, u32[]{:S(2)}, u32[]{:S(2)}) collective-permute-start(bf16[192,128]{1,0:T(8,128)(2,1)S(1)} %copy-done.8), channel_id=1, source_target_pairs={{0,16},{4,20},{8,24},{12,28},{1,17},{5,21},{9,25},{13,29},{2,18},{... | collective-permute-start | bytes 147464 | tf_op jit(solution)/shard_map/ppermute | solution.py:53
  13.1 8.6 %collective-permute-start.3 = (bf16[192,128]{1,0:T(8,128)(2,1)S(1)}, bf16[192,128]{1,0:T(8,128)(2,1)S(1)}, u32[]{:S(2)}, u32[]{:S(2)}) collective-permute-start(bf16[192,128]{1,0:T(8,128)(2,1)S(1)} %copy-done.8), channel_id=1, source_target_pairs={{0,4},{4,8},{8,12},{12,16},{16,20},{20,24},{24,28},{1,5},{5,9},{9,... | collective-permute-start | bytes 147464 | tf_op jit(solution)/shard_map/ppermute | solution.py:53
  14.4 49.1 %collective-permute-start.4 = (bf16[192,2048]{1,0:T(8,128)(2,1)}, bf16[192,2048]{1,0:T(8,128)(2,1)S(1)}, u32[]{:S(2)}, u32[]{:S(2)}) collective-permute-start(bf16[192,2048]{1,0:T(8,128)(2,1)} %own_ref.3), channel_id=1, source_target_pairs={{0,1},{1,0},{2,3},{3,2},{4,5},{5,4},{6,7},{7,6},{8,9},{9,8},{10,11... | collective-permute-start | bytes 2359304 | tf_op jit(solution)/shard_map/ppermute | solution.py:204
  21.7 9.8 %copy-start.5 = (bf16[192,1024]{1,0:T(8,128)(2,1)S(1)}, bf16[192,1024]{1,0:T(8,128)(2,1)}, u32[]{:S(2)}) copy-start(bf16[192,1024]{1,0:T(8,128)(2,1)} %q_ref.3) | copy-start | bytes 1179652
  21.7 9.7 %copy-start.6 = (bf16[192,1024]{1,0:T(8,128)(2,1)S(1)}, bf16[192,1024]{1,0:T(8,128)(2,1)}, u32[]{:S(2)}) copy-start(bf16[192,1024]{1,0:T(8,128)(2,1)} %do_ref.3) | copy-start | bytes 1179652
  22.5 9.0 %copy-start.9 = (s32[1,8]{1,0:T(1,128)S(1)}, s32[1,8]{1,0:T(1,128)}, u32[]{:S(2)}) copy-start(s32[1,8]{1,0:T(1,128)} %len_ref.3) | copy-start | bytes 100
  22.5 26.5 %all-to-all-start.1 = ((bf16[8,2,64,128]{3,2,1,0:T(8,128)(2,1)}), bf16[8,2,64,128]{3,2,1,0:T(8,128)(2,1)S(1)}, u32[]{:S(2)}, u32[]{:S(2)}) async-start(bf16[8,2,64,128]{3,2,1,0:T(8,128)(2,1)} %broadcast_in_dim.7), calls=%async_computation.1 | async-start | bytes 524288 | tf_op jit(solution)/shard_map/all_to_all | solution.py:47
  36.4 18.8 %collective-permute-start.5 = (bf16[192,128]{1,0:T(8,128)(2,1)}, bf16[192,128]{1,0:T(8,128)(2,1)S(1)}, u32[]{:S(2)}, u32[]{:S(2)}) collective-permute-start(bf16[192,128]{1,0:T(8,128)(2,1)} %get-tuple-element.50), channel_id=1, source_target_pairs={{4,0},{8,4},{12,8},{16,12},{20,16},{24,20},{28,24},{5,1},{9,5},{13... | collective-permute-start | bytes 147464 | tf_op jit(solution)/shard_map/ppermute | solution.py:57
  39.7 15.5 %collective-permute-start.6 = (bf16[192,128]{1,0:T(8,128)(2,1)}, bf16[192,128]{1,0:T(8,128)(2,1)S(1)}, u32[]{:S(2)}, u32[]{:S(2)}) collective-permute-start(bf16[192,128]{1,0:T(8,128)(2,1)} %get-tuple-element.51), channel_id=1, source_target_pairs={{8,0},{12,4},{16,8},{20,12},{24,16},{28,20},{9,1},{13,5},{17,9},{2... | collective-permute-start | bytes 147464 | tf_op jit(solution)/shard_map/ppermute | solution.py:57
  44.0 11.2 %collective-permute-start.7 = (bf16[192,128]{1,0:T(8,128)(2,1)}, bf16[192,128]{1,0:T(8,128)(2,1)}, u32[]{:S(2)}, u32[]{:S(2)}) collective-permute-start(bf16[192,128]{1,0:T(8,128)(2,1)} %get-tuple-element.52), channel_id=1, source_target_pairs={{12,0},{16,4},{20,8},{24,12},{28,16},{13,1},{17,5},{21,9},{25,13},... | collective-permute-start | bytes 147464 | tf_op jit(solution)/shard_map/ppermute | solution.py:57
  47.1 8.1 %collective-permute-start.8 = (bf16[192,128]{1,0:T(8,128)(2,1)S(1)}, bf16[192,128]{1,0:T(8,128)(2,1)}, u32[]{:S(2)}, u32[]{:S(2)}) collective-permute-start(bf16[192,128]{1,0:T(8,128)(2,1)S(1)} %get-tuple-element.53), channel_id=1, source_target_pairs={{16,0},{20,4},{24,8},{28,12},{17,1},{21,5},{25,9},{29,13},{18,2},{... | collective-permute-start | bytes 147464 | tf_op jit(solution)/shard_map/ppermute | solution.py:57
  50.2 13.3 %copy-start = (bf16[192,2048]{1,0:T(8,128)(2,1)S(1)}, bf16[192,2048]{1,0:T(8,128)(2,1)}, u32[]{:S(2)}) copy-start(bf16[192,2048]{1,0:T(8,128)(2,1)} %own_ref.3) | copy-start | bytes 2359300
  50.2 17.9 %all-to-all-start.3 = ((bf16[4,8,2,64,128]{4,3,2,1,0:T(8,128)(2,1)}), bf16[4,8,2,64,128]{4,3,2,1,0:T(8,128)(2,1)S(1)}, u32[]{:S(2)}, u32[]{:S(2)}) async-start(bf16[4,8,2,64,128]{4,3,2,1,0:T(8,128)(2,1)} %broadcast_in_dim.8), calls=%async_computation.3 | async-start | bytes 2097152 | tf_op jit(solution)/shard_map/all_to_all | solution.py:47
  56.1 7.4 %collective-permute-start.9 = (bf16[192,128]{1,0:T(8,128)(2,1)S(1)}, bf16[192,128]{1,0:T(8,128)(2,1)S(1)}, u32[]{:S(2)}, u32[]{:S(2)}) collective-permute-start(bf16[192,128]{1,0:T(8,128)(2,1)S(1)} %add_convert_fusion.1.dv_ref), channel_id=1, source_target_pairs={{0,2},{2,0},{1,3},{3,1},{4,6},{6,4},{5,7},{7,5},{8,10},{10,8},{9,1... | collective-permute-start | bytes 147464 | tf_op jit(solution)/shard_map/ppermute | solution.py:224
  63.5 1.8 %copy-start.1 = (bf16[192,2048]{1,0:T(8,128)(2,1)}, bf16[192,2048]{1,0:T(8,128)(2,1)S(1)}, u32[]{:S(2)}) copy-start(bf16[192,2048]{1,0:T(8,128)(2,1)S(1)} %collective-permute-done.4.near_ref) | copy-start | bytes 2359300
  65.3 1.0 copy-start.3
  66.3 4.8 %collective-permute-start.10 = (bf16[4,8,2,64,128]{4,3,2,1,0:T(8,128)(2,1)}, bf16[4,8,2,64,128]{4,3,2,1,0:T(8,128)(2,1)S(1)}, u32[]{:S(2)}, u32[]{:S(2)}) collective-permute-start(bf16[4,8,2,64,128]{4,3,2,1,0:T(8,128)(2,1)} %get-tuple-element.55), channel_id=1, source_target_pairs={{0,32},{32,0},{1,33},{33,1},{2,34},{34,2},{3,35},{35,3},{4,36},{36... | collective-permute-start | bytes 3145736 | tf_op jit(solution)/shard_map/ppermute | solution.py:230
  68.2 10.1 %collective-permute-start.11 = (bf16[4,8,2,64,128]{4,3,2,1,0:T(8,128)(2,1)S(1)}, bf16[4,8,2,64,128]{4,3,2,1,0:T(8,128)(2,1)}, u32[]{:S(2)}, u32[]{:S(2)}) collective-permute-start(bf16[4,8,2,64,128]{4,3,2,1,0:T(8,128)(2,1)S(1)} %all-to-all-done.3.mine_ref), channel_id=1, source_target_pairs={{0,32},{32,0},{1,33},{33,1},{2,34},{34,2},{3,35},{35,3},{4,36},{36... | collective-permute-start | bytes 3145736 | tf_op jit(solution)/shard_map/ppermute | solution.py:225
  71.0 1.2 copy-start.4
  73.5 20.1 %all-to-all-start.2 = ((bf16[4,8,2,64,128]{4,3,2,1,0:T(8,128)(2,1)}), bf16[4,8,2,64,128]{4,3,2,1,0:T(8,128)(2,1)S(1)}, u32[]{:S(2)}, u32[]{:S(2)}) async-start(bf16[4,8,2,64,128]{4,3,2,1,0:T(8,128)(2,1)} %add_halves.1), calls=%async_computation.2 | async-start | bytes 2097152 | tf_op jit(solution)/shard_map/all_to_all | solution.py:235
  78.3 1.1 copy-start.2
  81.2 7.1 %collective-permute-start.12 = (bf16[192,128]{1,0:T(8,128)(2,1)S(1)}, bf16[192,128]{1,0:T(8,128)(2,1)S(1)}, u32[]{:S(2)}, u32[]{:S(2)}) collective-permute-start(bf16[192,128]{1,0:T(8,128)(2,1)S(1)} %get-tuple-element.58), channel_id=1, source_target_pairs={{0,2},{2,0},{1,3},{3,1},{4,6},{6,4},{5,7},{7,5},{8,10},{10,8},{9,1... | collective-permute-start | bytes 147464 | tf_op jit(solution)/shard_map/ppermute | solution.py:232
  88.3 6.4 %collective-permute-start.16 = (bf16[192,128]{1,0:T(8,128)(2,1)S(1)}, bf16[192,128]{1,0:T(8,128)(2,1)S(1)}, u32[]{:S(2)}, u32[]{:S(2)}) collective-permute-start(bf16[192,128]{1,0:T(8,128)(2,1)S(1)} %add_convert_fusion.refs_9_), channel_id=1, source_target_pairs={{0,4},{4,8},{8,12},{12,16},{16,20},{20,24},{24,28},{1,5},{5,9},{9,... | collective-permute-start | bytes 147464 | tf_op jit(solution)/shard_map/ppermute | solution.py:53
  89.6 6.9 %collective-permute-start.15 = (bf16[192,128]{1,0:T(8,128)(2,1)S(1)}, bf16[192,128]{1,0:T(8,128)(2,1)S(1)}, u32[]{:S(2)}, u32[]{:S(2)}) collective-permute-start(bf16[192,128]{1,0:T(8,128)(2,1)S(1)} %add_convert_fusion.refs_9_), channel_id=1, source_target_pairs={{0,8},{4,12},{8,16},{12,20},{16,24},{20,28},{1,9},{5,13},{9,17},{1... | collective-permute-start | bytes 147464 | tf_op jit(solution)/shard_map/ppermute | solution.py:53
  90.9 10.4 %collective-permute-start.14 = (bf16[192,128]{1,0:T(8,128)(2,1)S(1)}, bf16[192,128]{1,0:T(8,128)(2,1)S(1)}, u32[]{:S(2)}, u32[]{:S(2)}) collective-permute-start(bf16[192,128]{1,0:T(8,128)(2,1)S(1)} %add_convert_fusion.refs_9_), channel_id=1, source_target_pairs={{0,12},{4,16},{8,20},{12,24},{16,28},{1,13},{5,17},{9,21},{13,25},... | collective-permute-start | bytes 147464 | tf_op jit(solution)/shard_map/ppermute | solution.py:53
  92.2 11.1 %collective-permute-start.13 = (bf16[192,128]{1,0:T(8,128)(2,1)S(1)}, bf16[192,128]{1,0:T(8,128)(2,1)S(1)}, u32[]{:S(2)}, u32[]{:S(2)}) collective-permute-start(bf16[192,128]{1,0:T(8,128)(2,1)S(1)} %add_convert_fusion.refs_9_), channel_id=1, source_target_pairs={{0,16},{4,20},{8,24},{12,28},{1,17},{5,21},{9,25},{13,29},{2,18},{... | collective-permute-start | bytes 147464 | tf_op jit(solution)/shard_map/ppermute | solution.py:53
  94.4 18.0 %copy-start.7 = (bf16[192,1024]{1,0:T(8,128)(2,1)S(1)}, bf16[192,1024]{1,0:T(8,128)(2,1)}, u32[]{:S(2)}) copy-start(bf16[192,1024]{1,0:T(8,128)(2,1)} %do_ref.3) | copy-start | bytes 1179652
  103.3 16.7 %all-to-all-start.4 = ((bf16[8,2,64,128]{3,2,1,0:T(8,128)(2,1)}), bf16[8,2,64,128]{3,2,1,0:T(8,128)(2,1)S(1)}, u32[]{:S(2)}, u32[]{:S(2)}) async-start(bf16[8,2,64,128]{3,2,1,0:T(8,128)(2,1)} %sum_blocks.1), calls=%async_computation.4 | async-start | bytes 524288 | tf_op jit(solution)/shard_map/all_to_all | solution.py:238
  120.7 21.4 %collective-permute-start.17 = (bf16[192,128]{1,0:T(8,128)(2,1)S(1)}, bf16[192,128]{1,0:T(8,128)(2,1)S(1)}, u32[]{:S(2)}, u32[]{:S(2)}) collective-permute-start(bf16[192,128]{1,0:T(8,128)(2,1)S(1)} %get-tuple-element.73), channel_id=1, source_target_pairs={{4,0},{8,4},{12,8},{16,12},{20,16},{24,20},{28,24},{5,1},{9,5},{13... | collective-permute-start | bytes 147464 | tf_op jit(solution)/shard_map/ppermute | solution.py:57
  124.0 18.0 %collective-permute-start.18 = (bf16[192,128]{1,0:T(8,128)(2,1)S(1)}, bf16[192,128]{1,0:T(8,128)(2,1)S(1)}, u32[]{:S(2)}, u32[]{:S(2)}) collective-permute-start(bf16[192,128]{1,0:T(8,128)(2,1)S(1)} %get-tuple-element.74), channel_id=1, source_target_pairs={{8,0},{12,4},{16,8},{20,12},{24,16},{28,20},{9,1},{13,5},{17,9},{2... | collective-permute-start | bytes 147464 | tf_op jit(solution)/shard_map/ppermute | solution.py:57
  128.3 13.8 %collective-permute-start.19 = (bf16[192,128]{1,0:T(8,128)(2,1)S(1)}, bf16[192,128]{1,0:T(8,128)(2,1)S(1)}, u32[]{:S(2)}, u32[]{:S(2)}) collective-permute-start(bf16[192,128]{1,0:T(8,128)(2,1)S(1)} %get-tuple-element.75), channel_id=1, source_target_pairs={{12,0},{16,4},{20,8},{24,12},{28,16},{13,1},{17,5},{21,9},{25,13},... | collective-permute-start | bytes 147464 | tf_op jit(solution)/shard_map/ppermute | solution.py:57
  131.8 10.3 %collective-permute-start.20 = (bf16[192,128]{1,0:T(8,128)(2,1)S(1)}, bf16[192,128]{1,0:T(8,128)(2,1)S(1)}, u32[]{:S(2)}, u32[]{:S(2)}) collective-permute-start(bf16[192,128]{1,0:T(8,128)(2,1)S(1)} %get-tuple-element.76), channel_id=1, source_target_pairs={{16,0},{20,4},{24,8},{28,12},{17,1},{21,5},{25,9},{29,13},{18,2},{... | collective-permute-start | bytes 147464 | tf_op jit(solution)/shard_map/ppermute | solution.py:57
  135.0 15.8 %all-to-all-start.5 = ((f32[4,64,128]{2,1,0:T(8,128)}), f32[4,64,128]{2,1,0:T(8,128)S(1)}, u32[]{:S(2)}, u32[]{:S(2)}) async-start(f32[4,64,128]{2,1,0:T(8,128)} %bitcast), calls=%async_computation.5 | async-start | bytes 262144 | tf_op jit(solution)/shard_map/all_to_all | solution.py:247

commit v11 on v10

--- a/solution.py
+++ b/solution.py
@@ -1,3 +1,5 @@
+import math
+
 import jax
 import jax.numpy as jnp
 from jax import lax
@@ -15,6 +17,7 @@
 CHUNKS = GROUP // HEADS_AT_ONCE
 PAIR = [(0, 1), (1, 0)]
 SCALE = HEAD_DIM ** -0.5
+LOG2_SCALE = SCALE * math.log2(math.e)
 F32 = jnp.float32
 BF16 = jnp.bfloat16
 NT = (((1,), (1,)), ((), ()))
@@ -92,7 +95,7 @@
             rows = lax.dot_general(columns, dv, TN, preferred_element_type=F32).astype(BF16)
             for ctx in range(8):
                 for c in range(2):
-                    out_ref[x, ctx, c] = rows[
+                    out_ref[x, c, ctx] = rows[
                         ctx * 64 : (ctx + 1) * 64, c * HEAD_DIM : (c + 1) * HEAD_DIM
                     ]
 
@@ -108,12 +111,13 @@
     return total
 
 
-def sum_blocks(parts_ref, out_ref):
-    out_ref[...] = sum_of([parts_ref[i] for i in range(parts_ref.shape[0])]).astype(out_ref.dtype)
+def last_sum(parts_ref, out_ref):
+    yh = lax.axis_index("yh")
+    out_ref[...] = sum_of([parts_ref[i, yh, ctx] for i in range(2) for ctx in range(8)])
 
 
 def twice_sum(parts_ref, out_ref):
-    total = sum_of([parts_ref[i] for i in range(8)])
+    total = sum_of([parts_ref[i] for i in range(4)]).astype(BF16)
     for i in range(2):
         out_ref[i] = total
 
@@ -155,13 +159,12 @@
     for i in range(CHUNKS):
         cols = slice(i * LANES, (i + 1) * LANES)
         scores = lax.dot_general(keys[...], q_rows[cols], NT, preferred_element_type=F32)
-        scores = scores * F32(SCALE) + bias[...]
+        scores = scores * F32(LOG2_SCALE) + bias[...]
         top = jnp.max(scores, axis=0, keepdims=True)
-        weights = jnp.exp(scores - top)
-        inverse = 1.0 / jnp.sum(weights, axis=0, keepdims=True)
-        probs[:, cols] = (weights * inverse).astype(BF16)
-        stat_ref[i : i + 1] = top
-        stat_ref[CHUNKS + i : CHUNKS + i + 1] = inverse
+        weights = jnp.exp2(scores - top)
+        total = jnp.sum(weights, axis=0, keepdims=True)
+        probs[:, cols] = (weights * (1.0 / total)).astype(BF16)
+        stat_ref[i : i + 1] = top + jnp.log2(total)
     total = jnp.dot(probs[...], do_rows[...], preferred_element_type=F32)
     for slot, ref in enumerate(dv_refs):
         ref[...] = total[slot * TOK : (slot + 1) * TOK].astype(ref.dtype)
@@ -179,8 +182,8 @@
     for i in range(CHUNKS):
         cols = slice(i * LANES, (i + 1) * LANES)
         scores = lax.dot_general(keys[...], q_rows[cols], NT, preferred_element_type=F32)
-        scores = scores * F32(SCALE) + bias[...]
-        p = jnp.exp(scores - stat_ref[i : i + 1]) * stat_ref[CHUNKS + i : CHUNKS + i + 1]
+        scores = scores * F32(LOG2_SCALE) + bias[...]
+        p = jnp.exp2(scores - stat_ref[i : i + 1])
         att = lax.dot_general(values[...], p.astype(BF16), TN, preferred_element_type=F32)
         dp = lax.dot_general(values[...], do_rows[cols], NT, preferred_element_type=F32)
         dots = jnp.sum(p * dp, axis=0, keepdims=True)
@@ -199,7 +202,7 @@
 
 
 def shards(queries, key_states, normed, value_weight, grad_out, lengths):
-    yh, m1 = lax.axis_index("yh"), lax.axis_index("m1")
+    m1 = lax.axis_index("m1")
     corners = to_all(value_weight, ("yh", "m1"), 4)
     near = lax.ppermute(normed, "m0", PAIR)
     keys = [from_behind(key_states, d) for d in range(REACH, 0, -1)] + [key_states]
@@ -212,7 +215,7 @@
     pairs = pltpu.VMEM((WINDOW, heads), BF16)
     block = shape((TOK, HEAD_DIM))
     own = shape((TOK, HEAD_DIM), F32)
-    whole = shape((4, 8, 2, 64, HEAD_DIM))
+    whole = shape((4, 2, 8, 64, HEAD_DIM))
     *dv, stats = call(
         soft, (block,) * REACH + (own, shape((8, LANES), F32)), 7, 3 * 10**9, 2 * 10**6,
         (rows, rows, bias, pairs, window), smem=1, vmem=28,
@@ -233,26 +236,22 @@
     values = [from_behind(projected, d) for d in range(REACH, 0, -1)] + [projected]
     partial = call(add_halves, whole, 2, 10**6, 3 * 10**6)(partial, taken)
     partial = lax.all_to_all(partial, "x", 0, 0, tiled=True)
-    partial = call(sum_blocks, shape((8, 2, 64, HEAD_DIM)), 1, 10**6, 10**6)(partial)
+    partial = call(twice_sum, shape((2, 2, 8, 64, HEAD_DIM)), 1, 10**6, 10**6)(partial)
     partial, values = lax.optimization_barrier((partial, values))
-    partial = lax.all_to_all(partial, "ctx", 0, 0, tiled=True)
+    partial = lax.all_to_all(
+        partial.reshape(32, 64, HEAD_DIM), ("yh", "m1", "ctx"), 0, 0, tiled=True
+    )
 
     wide = shape((TOK, GROUP * HEAD_DIM))
     attended, grad_query, *dk = call(
         attend, (wide, wide) + (block,) * REACH + (own,), 13, 6 * 10**9, 4 * 10**6,
         (rows, rows, bias, pairs, window, window), smem=1, vmem=28,
     )(lengths, queries, grad_out, stats, *keys, *values)
-    partial = call(twice_sum, shape((2, 2, 64, HEAD_DIM), F32), 1, 10**6, 10**6)(partial)
-    partial, dk = lax.optimization_barrier((partial, dk))
-    partial = lax.all_to_all(partial.reshape(4, 64, HEAD_DIM), ("yh", "m1"), 0, 0, tiled=True)
-    grad_weight = jnp.sum(
-        lax.dynamic_index_in_dim(
-            partial.reshape(2, 2, 64, HEAD_DIM), yh, axis=1, keepdims=False
-        ),
-        axis=0,
-    )
     dk = [dk[REACH]] + [from_ahead(dk[REACH - d], d) for d in range(1, REACH + 1)]
     grad_key = (sum(part.astype(F32) for part in dk) * F32(SCALE)).astype(BF16)
+    grad_weight = call(last_sum, shape((64, HEAD_DIM), F32), 1, 10**6, 10**6)(
+        partial.reshape(2, 2, 8, 64, HEAD_DIM)
+    )
     return attended, grad_query, grad_key, grad_weight
 
 

time: 153 us -> 150 us (0.980)
  the two profiles are of different devices: /device:TPU:450 before, /device:TPU:64 now
where the time goes in v11:
time: 150 us; the launch traced here: 149 us
  starting transfers between devices  97 us (65%)
  waiting for transfers between devices  23.7 us (16%)
  Pallas kernels  18.7 us (12%)
  local copies, waits for them, and re-layouts  6.72 us (4%)
  other arithmetic  1.53 us (1%)
    ppermute x8, starting transfers between devices, from_behind(): lax.ppermute(block, 'ctx', [(i, i + distance) for i in range(8 - distance)])  33.1 us
    all_to_all x3, starting transfers between devices, to_all(): lax.all_to_all(jnp.broadcast_to(block[None], (copies,) + block.shape), ax...  17 us
    ppermute x8, waiting for transfers between devices, from_ahead(): lax.ppermute(block, 'ctx', [(i + distance, i) for i in range(8 - distance)])  15.8 us
    all_to_all x1, starting transfers between devices, shards(): lax.all_to_all(partial.reshape(32, 64, HEAD_DIM), ('yh', 'm1', 'ctx'), 0,...  15.1 us
    ppermute x8, starting transfers between devices, from_ahead(): lax.ppermute(block, 'ctx', [(i + distance, i) for i in range(8 - distance)])  12 us
    pallas_call x1, Pallas kernels, shards(): call(attend, (wide, wide) + (block,) * REACH + (own,), 13, 6 * 10 ** 9, 4...  7.52 us
    pallas_call x1, Pallas kernels, shards(): call(soft, (block,) * REACH + (own, shape((8, LANES), F32)), 7, 3 * 10 **...  4.77 us
    ppermute x1, starting transfers between devices, shards(): far_dv = lax.ppermute(dv, 'm1', PAIR)  4.58 us
  transfers between devices with their start and end apart: 26, of which 10 were waited for; matrix products, arithmetic and copies ran while one was open for 2% of the time, Pallas kernels for 12%

profile of v11, /device:TPU:64, one launch (start us, length us, event | category | flops | bytes accessed | tf_op | source)
XLA Modules:
  0.0 148.6 jit_solution(13176443285360099810)
XLA Ops:
  0.6 1.4 broadcast_in_dim.6
  2.0 7.2 %all-to-all-start = ((bf16[4,64,128]{2,1,0:T(8,128)(2,1)}), bf16[4,64,128]{2,1,0:T(8,128)(2,1)S(1)}, u32[]{:S(2)}, u32[]{:S(2)}) async-start(bf16[4,64,128]{2,1,0:T(8,128)(2,1)} %broadcast_in_dim.6), calls=%async_computation | async-start | bytes 131072 | tf_op jit(solution)/shard_map/all_to_all | solution.py:50
  9.2 6.1 %collective-permute-start.2 = (bf16[192,128]{1,0:T(8,128)(2,1)S(1)}, bf16[192,128]{1,0:T(8,128)(2,1)S(1)}, u32[]{:S(2)}, u32[]{:S(2)}) collective-permute-start(bf16[192,128]{1,0:T(8,128)(2,1)S(1)} %copy-done.8), channel_id=1, source_target_pairs={{0,8},{4,12},{8,16},{12,20},{16,24},{20,28},{1,9},{5,13},{9,17},{1... | collective-permute-start | bytes 147464 | tf_op jit(solution)/shard_map/ppermute | solution.py:56
  15.3 7.3 %collective-permute-start.1 = (bf16[192,128]{1,0:T(8,128)(2,1)S(1)}, bf16[192,128]{1,0:T(8,128)(2,1)S(1)}, u32[]{:S(2)}, u32[]{:S(2)}) collective-permute-start(bf16[192,128]{1,0:T(8,128)(2,1)S(1)} %copy-done.8), channel_id=1, source_target_pairs={{0,12},{4,16},{8,20},{12,24},{16,28},{1,13},{5,17},{9,21},{13,25},... | collective-permute-start | bytes 147464 | tf_op jit(solution)/shard_map/ppermute | solution.py:56
  22.6 2.2 %collective-permute-start = (bf16[192,128]{1,0:T(8,128)(2,1)S(1)}, bf16[192,128]{1,0:T(8,128)(2,1)S(1)}, u32[]{:S(2)}, u32[]{:S(2)}) collective-permute-start(bf16[192,128]{1,0:T(8,128)(2,1)S(1)} %copy-done.8), channel_id=1, source_target_pairs={{0,16},{4,20},{8,24},{12,28},{1,17},{5,21},{9,25},{13,29},{2,18},{... | collective-permute-start | bytes 147464 | tf_op jit(solution)/shard_map/ppermute | solution.py:56
  24.8 2.5 %collective-permute-start.3 = (bf16[192,128]{1,0:T(8,128)(2,1)S(1)}, bf16[192,128]{1,0:T(8,128)(2,1)S(1)}, u32[]{:S(2)}, u32[]{:S(2)}) collective-permute-start(bf16[192,128]{1,0:T(8,128)(2,1)S(1)} %copy-done.8), channel_id=1, source_target_pairs={{0,4},{4,8},{8,12},{12,16},{16,20},{20,24},{24,28},{1,5},{5,9},{9,... | collective-permute-start | bytes 147464 | tf_op jit(solution)/shard_map/ppermute | solution.py:56
  27.3 2.6 %collective-permute-start.4 = (bf16[192,2048]{1,0:T(8,128)(2,1)}, bf16[192,2048]{1,0:T(8,128)(2,1)S(1)}, u32[]{:S(2)}, u32[]{:S(2)}) collective-permute-start(bf16[192,2048]{1,0:T(8,128)(2,1)} %own_ref.3), channel_id=1, source_target_pairs={{0,1},{1,0},{2,3},{3,2},{4,5},{5,4},{6,7},{7,6},{8,9},{9,8},{10,11... | collective-permute-start | bytes 2359304 | tf_op jit(solution)/shard_map/ppermute | solution.py:207
  29.9 0.0 collective-permute-done.2.refs_2_
  29.9 0.9 collective-permute-done.3.refs_3_
  30.8 0.0 all-to-all-done
  30.8 0.0 copy-start.6
  30.8 0.8 broadcast_in_dim.7
  31.6 5.3 %all-to-all-start.1 = ((bf16[8,2,64,128]{3,2,1,0:T(8,128)(2,1)}), bf16[8,2,64,128]{3,2,1,0:T(8,128)(2,1)S(1)}, u32[]{:S(2)}, u32[]{:S(2)}) async-start(bf16[8,2,64,128]{3,2,1,0:T(8,128)(2,1)} %broadcast_in_dim.7), calls=%async_computation.1 | async-start | bytes 524288 | tf_op jit(solution)/shard_map/all_to_all | solution.py:50
  36.9 4.8 %soft.1 = (bf16[192,128]{1,0:T(8,128)(2,1)S(1)}, bf16[192,128]{1,0:T(8,128)(2,1)}, bf16[192,128]{1,0:T(8,128)(2,1)}, bf16[192,128]{1,0:T(8,128)(2,1)}, f32[192,128]{1,0:T(8,128)S(1)}, /*index=5*/f32[8,384]{1,0:T(8,128)S(1)}) custom-call(s32[1,8]{1,0:T(1,128)S(1)} %copy-done.9, bf16[192,1024]{1,0:T(8,128)(2,1)S(1)} %copy-done.5, ...), custom_call_target="tpu_custom_call" | custom-call | flops 3000000000 | bytes 2000000 | tf_op jit(solution)/shard_map/soft/pallas_call | solution.py:219
  41.7 1.9 %collective-permute-start.5 = (bf16[192,128]{1,0:T(8,128)(2,1)}, bf16[192,128]{1,0:T(8,128)(2,1)S(1)}, u32[]{:S(2)}, u32[]{:S(2)}) collective-permute-start(bf16[192,128]{1,0:T(8,128)(2,1)} %get-tuple-element.44), channel_id=1, source_target_pairs={{4,0},{8,4},{12,8},{16,12},{20,16},{24,20},{28,24},{5,1},{9,5},{13... | collective-permute-start | bytes 147464 | tf_op jit(solution)/shard_map/ppermute | solution.py:60
  43.6 1.3 collective-permute-start.6
  44.9 1.3 collective-permute-start.7
  46.2 1.3 collective-permute-start.8
  47.5 0.0 all-to-all-done.1
  47.5 1.2 broadcast_in_dim.8
  48.8 4.4 %all-to-all-start.3 = ((bf16[4,8,2,64,128]{4,3,2,1,0:T(8,128)(2,1)}), bf16[4,8,2,64,128]{4,3,2,1,0:T(8,128)(2,1)S(1)}, u32[]{:S(2)}, u32[]{:S(2)}) async-start(bf16[4,8,2,64,128]{4,3,2,1,0:T(8,128)(2,1)} %broadcast_in_dim.8), calls=%async_computation.3 | async-start | bytes 2097152 | tf_op jit(solution)/shard_map/all_to_all | solution.py:50
  53.2 0.0 collective-permute-done.5
  53.2 0.0 collective-permute-done.6
  53.2 4.9 %collective-permute-done.7 = bf16[192,128]{1,0:T(8,128)(2,1)} collective-permute-done((bf16[192,128]{1,0:T(8,128)(2,1)}, bf16[192,128]{1,0:T(8,128)(2,1)}, u32[]{:S(2)}, u32[]{:S(2)}) %collective-permute-start.7) | collective-permute-done | bytes 49184 | tf_op jit(solution)/shard_map/ppermute | solution.py:60
  58.1 0.0 collective-permute-done.8
  58.1 0.9 add_convert_fusion.1.dv_ref
  59.0 4.6 %collective-permute-start.9 = (bf16[192,128]{1,0:T(8,128)(2,1)S(1)}, bf16[192,128]{1,0:T(8,128)(2,1)S(1)}, u32[]{:S(2)}, u32[]{:S(2)}) collective-permute-start(bf16[192,128]{1,0:T(8,128)(2,1)S(1)} %add_convert_fusion.1.dv_ref), channel_id=1, source_target_pairs={{0,2},{2,0},{1,3},{3,1},{4,6},{6,4},{5,7},{7,5},{8,10},{10,8},{9,1... | collective-permute-start | bytes 147464 | tf_op jit(solution)/shard_map/ppermute | solution.py:227
  63.5 2.8 %collective-permute-done.9.far_dv_ref = bf16[192,128]{1,0:T(8,128)(2,1)S(1)} collective-permute-done((bf16[192,128]{1,0:T(8,128)(2,1)S(1)}, bf16[192,128]{1,0:T(8,128)(2,1)S(1)}, u32[]{:S(2)}, u32[]{:S(2)}) %collective-permute-start.9) | collective-permute-done | bytes 49184 | tf_op jit(solution)/shard_map/ppermute | solution.py:227
  66.4 0.0 collective-permute-done.4.near_ref
  66.4 1.8 %weight_grad.1 = (bf16[4,2,8,64,128]{4,3,2,1,0:T(8,128)(2,1)S(1)}, bf16[4,2,8,64,128]{4,3,2,1,0:T(8,128)(2,1)}) custom-call(bf16[192,2048]{1,0:T(8,128)(2,1)S(1)} %copy-done, bf16[192,2048]{1,0:T(8,128)(2,1)S(1)} %collective-permute-done.4.near_ref, bf16[192,128]{1,0:T(8,128)(2,1)S(1)} %add_convert_fusion.1.dv_ref, ...), custom_call_target="tpu_custom_call" | custom-call | flops 400000000 | bytes 5000000 | tf_op jit(solution)/shard_map/weight_grad/pallas_call | solution.py:230
  68.2 1.0 copy-done.3
  69.1 1.9 %collective-permute-start.10 = (bf16[4,2,8,64,128]{4,3,2,1,0:T(8,128)(2,1)}, bf16[4,2,8,64,128]{4,3,2,1,0:T(8,128)(2,1)S(1)}, u32[]{:S(2)}, u32[]{:S(2)}) collective-permute-start(bf16[4,2,8,64,128]{4,3,2,1,0:T(8,128)(2,1)} %get-tuple-element.49), channel_id=1, source_target_pairs={{0,32},{32,0},{1,33},{33,1},{2,34},{34,2},{3,35},{35,3},{4,36},{36... | collective-permute-start | bytes 3145736 | tf_op jit(solution)/shard_map/ppermute | solution.py:233
  71.1 0.0 all-to-all-done.3.mine_ref
  71.1 2.4 %collective-permute-start.11 = (bf16[4,8,2,64,128]{4,3,2,1,0:T(8,128)(2,1)S(1)}, bf16[4,8,2,64,128]{4,3,2,1,0:T(8,128)(2,1)}, u32[]{:S(2)}, u32[]{:S(2)}) collective-permute-start(bf16[4,8,2,64,128]{4,3,2,1,0:T(8,128)(2,1)S(1)} %all-to-all-done.3.mine_ref), channel_id=1, source_target_pairs={{0,32},{32,0},{1,33},{33,1},{2,34},{34,2},{3,35},{35,3},{4,36},{36... | collective-permute-start | bytes 3145736 | tf_op jit(solution)/shard_map/ppermute | solution.py:228
  73.5 0.4 collective-permute-done.10.b_ref
  73.9 1.2 copy-done.4
  75.1 1.2 add_halves.1
  76.3 4.3 %all-to-all-start.2 = ((bf16[4,2,8,64,128]{4,3,2,1,0:T(8,128)(2,1)}), bf16[4,2,8,64,128]{4,3,2,1,0:T(8,128)(2,1)S(1)}, u32[]{:S(2)}, u32[]{:S(2)}) async-start(bf16[4,2,8,64,128]{4,3,2,1,0:T(8,128)(2,1)} %add_halves.1), calls=%async_computation.2 | async-start | bytes 2097152 | tf_op jit(solution)/shard_map/all_to_all | solution.py:238
  80.6 0.0 collective-permute-done.11.other_ref
  80.6 1.1 copy-done.2
  81.8 1.8 %project.1 = (f32[192,128]{1,0:T(8,128)S(1)}, bf16[192,128]{1,0:T(8,128)(2,1)S(1)}) custom-call(bf16[192,2048]{1,0:T(8,128)(2,1)S(1)} %copy-done, bf16[192,2048]{1,0:T(8,128)(2,1)S(1)} %copy-done.2, bf16[4,8,2,64,128]{4,3,2,1,0:T(8,128)(2,1)S(1)} %all-to-all-done.3.mine_ref, bf16[4,8,2,64,128]{4,3,2,1,0:T(8,128)(2,1)} %collective-permute-done.11.other_ref), custom_call_target="tpu_custom_call" | custom-call | flops 400000000 | bytes 5000000 | tf_op jit(solution)/shard_map/project/pallas_call | solution.py:234
  83.6 4.0 %collective-permute-start.12 = (bf16[192,128]{1,0:T(8,128)(2,1)S(1)}, bf16[192,128]{1,0:T(8,128)(2,1)S(1)}, u32[]{:S(2)}, u32[]{:S(2)}) collective-permute-start(bf16[192,128]{1,0:T(8,128)(2,1)S(1)} %get-tuple-element.52), channel_id=1, source_target_pairs={{0,2},{2,0},{1,3},{3,1},{4,6},{6,4},{5,7},{7,5},{8,10},{10,8},{9,1... | collective-permute-start | bytes 147464 | tf_op jit(solution)/shard_map/ppermute | solution.py:235
  87.6 3.0 %collective-permute-done.12 = bf16[192,128]{1,0:T(8,128)(2,1)S(1)} collective-permute-done((bf16[192,128]{1,0:T(8,128)(2,1)S(1)}, bf16[192,128]{1,0:T(8,128)(2,1)S(1)}, u32[]{:S(2)}, u32[]{:S(2)}) %collective-permute-start.12) | collective-permute-done | bytes 49184 | tf_op jit(solution)/shard_map/ppermute | solution.py:235
  90.7 3.3 %collective-permute-start.16 = (bf16[192,128]{1,0:T(8,128)(2,1)S(1)}, bf16[192,128]{1,0:T(8,128)(2,1)S(1)}, u32[]{:S(2)}, u32[]{:S(2)}) collective-permute-start(bf16[192,128]{1,0:T(8,128)(2,1)S(1)} %add_convert_fusion.refs_9_), channel_id=1, source_target_pairs={{0,4},{4,8},{8,12},{12,16},{16,20},{20,24},{24,28},{1,5},{5,9},{9,... | collective-permute-start | bytes 147464 | tf_op jit(solution)/shard_map/ppermute | solution.py:56
  94.0 4.2 %collective-permute-start.15 = (bf16[192,128]{1,0:T(8,128)(2,1)S(1)}, bf16[192,128]{1,0:T(8,128)(2,1)S(1)}, u32[]{:S(2)}, u32[]{:S(2)}) collective-permute-start(bf16[192,128]{1,0:T(8,128)(2,1)S(1)} %add_convert_fusion.refs_9_), channel_id=1, source_target_pairs={{0,8},{4,12},{8,16},{12,20},{16,24},{20,28},{1,9},{5,13},{9,17},{1... | collective-permute-start | bytes 147464 | tf_op jit(solution)/shard_map/ppermute | solution.py:56
  98.2 6.3 %collective-permute-start.14 = (bf16[192,128]{1,0:T(8,128)(2,1)S(1)}, bf16[192,128]{1,0:T(8,128)(2,1)S(1)}, u32[]{:S(2)}, u32[]{:S(2)}) collective-permute-start(bf16[192,128]{1,0:T(8,128)(2,1)S(1)} %add_convert_fusion.refs_9_), channel_id=1, source_target_pairs={{0,12},{4,16},{8,20},{12,24},{16,28},{1,13},{5,17},{9,21},{13,25},... | collective-permute-start | bytes 147464 | tf_op jit(solution)/shard_map/ppermute | solution.py:56
  104.5 1.3 collective-permute-start.13
  105.8 0.0 all-to-all-done.2.parts_ref
  105.8 0.9 twice_sum.1
  106.7 0.0 collective-permute-done.16.refs_8_
  106.7 0.0 collective-permute-done.15.refs_7_
  106.7 0.8 collective-permute-done.13.refs_5_
  107.5 15.1 %all-to-all-start.4 = ((bf16[32,64,128]{2,1,0:T(8,128)(2,1)}), bf16[32,64,128]{2,1,0:T(8,128)(2,1)S(1)}, u32[]{:S(2)}, u32[]{:S(2)}) async-start(bf16[32,64,128]{2,1,0:T(8,128)(2,1)} %bitcast), calls=%async_computation.4 | async-start | bytes 1048576 | tf_op jit(solution)/shard_map/all_to_all | solution.py:241
  122.7 7.5 %attend.1 = (bf16[192,1024]{1,0:T(8,128)(2,1)}, bf16[192,1024]{1,0:T(8,128)(2,1)}, bf16[192,128]{1,0:T(8,128)(2,1)S(1)}, bf16[192,128]{1,0:T(8,128)(2,1)S(1)}, b...) custom-call(s32[1,8]{1,0:T(1,128)S(1)} %copy-done.9, ...), custom_call_target="tpu_custom_call" | custom-call | flops 6000000000 | bytes 4000000 | tf_op jit(solution)/shard_map/attend/pallas_call | solution.py:246
  130.2 2.3 %collective-permute-start.17 = (bf16[192,128]{1,0:T(8,128)(2,1)S(1)}, bf16[192,128]{1,0:T(8,128)(2,1)S(1)}, u32[]{:S(2)}, u32[]{:S(2)}) collective-permute-start(bf16[192,128]{1,0:T(8,128)(2,1)S(1)} %get-tuple-element.61), channel_id=1, source_target_pairs={{4,0},{8,4},{12,8},{16,12},{20,16},{24,20},{28,24},{5,1},{9,5},{13... | collective-permute-start | bytes 147464 | tf_op jit(solution)/shard_map/ppermute | solution.py:60
  132.5 1.3 collective-permute-start.18
  133.8 1.3 collective-permute-start.19
  135.1 1.3 collective-permute-start.20
  136.4 1.9 %collective-permute-done.17 = bf16[192,128]{1,0:T(8,128)(2,1)S(1)} collective-permute-done((bf16[192,128]{1,0:T(8,128)(2,1)S(1)}, bf16[192,128]{1,0:T(8,128)(2,1)S(1)}, u32[]{:S(2)}, u32[]{:S(2)}) %collective-permute-start.17) | collective-permute-done | bytes 49184 | tf_op jit(solution)/shard_map/ppermute | solution.py:60
  138.3 2.2 %collective-permute-done.18 = bf16[192,128]{1,0:T(8,128)(2,1)S(1)} collective-permute-done((bf16[192,128]{1,0:T(8,128)(2,1)S(1)}, bf16[192,128]{1,0:T(8,128)(2,1)S(1)}, u32[]{:S(2)}, u32[]{:S(2)}) %collective-permute-start.18) | collective-permute-done | bytes 49184 | tf_op jit(solution)/shard_map/ppermute | solution.py:60
  140.5 6.2 %collective-permute-done.19 = bf16[192,128]{1,0:T(8,128)(2,1)S(1)} collective-permute-done((bf16[192,128]{1,0:T(8,128)(2,1)S(1)}, bf16[192,128]{1,0:T(8,128)(2,1)S(1)}, u32[]{:S(2)}, u32[]{:S(2)}) %collective-permute-start.19) | collective-permute-done | bytes 49184 | tf_op jit(solution)/shard_map/ppermute | solution.py:60
  146.7 0.6 collective-permute-done.20
  147.3 0.7 multiply_convert_fusion
  148.0 0.7 last_sum.1
  (22 shorter events, 0.1 us)
Async XLA Ops:
  2.0 7.2 %copy-start.8 = (bf16[192,128]{1,0:T(8,128)(2,1)S(1)}, bf16[192,128]{1,0:T(8,128)(2,1)}, u32[]{:S(2)}) copy-start(bf16[192,128]{1,0:T(8,128)(2,1)} %refs_4_.1) | copy-start | bytes 147460
  2.0 28.8 %all-to-all-start = ((bf16[4,64,128]{2,1,0:T(8,128)(2,1)}), bf16[4,64,128]{2,1,0:T(8,128)(2,1)S(1)}, u32[]{:S(2)}, u32[]{:S(2)}) async-start(bf16[4,64,128]{2,1,0:T(8,128)(2,1)} %broadcast_in_dim.6), calls=%async_computation | async-start | bytes 131072 | tf_op jit(solution)/shard_map/all_to_all | solution.py:50
  9.2 20.7 %collective-permute-start.2 = (bf16[192,128]{1,0:T(8,128)(2,1)S(1)}, bf16[192,128]{1,0:T(8,128)(2,1)S(1)}, u32[]{:S(2)}, u32[]{:S(2)}) collective-permute-start(bf16[192,128]{1,0:T(8,128)(2,1)S(1)} %copy-done.8), channel_id=1, source_target_pairs={{0,8},{4,12},{8,16},{12,20},{16,24},{20,28},{1,9},{5,13},{9,17},{1... | collective-permute-start | bytes 147464 | tf_op jit(solution)/shard_map/ppermute | solution.py:56
  15.3 14.6 %collective-permute-start.1 = (bf16[192,128]{1,0:T(8,128)(2,1)S(1)}, bf16[192,128]{1,0:T(8,128)(2,1)S(1)}, u32[]{:S(2)}, u32[]{:S(2)}) collective-permute-start(bf16[192,128]{1,0:T(8,128)(2,1)S(1)} %copy-done.8), channel_id=1, source_target_pairs={{0,12},{4,16},{8,20},{12,24},{16,28},{1,13},{5,17},{9,21},{13,25},... | collective-permute-start | bytes 147464 | tf_op jit(solution)/shard_map/ppermute | solution.py:56
  22.6 7.3 %collective-permute-start = (bf16[192,128]{1,0:T(8,128)(2,1)S(1)}, bf16[192,128]{1,0:T(8,128)(2,1)S(1)}, u32[]{:S(2)}, u32[]{:S(2)}) collective-permute-start(bf16[192,128]{1,0:T(8,128)(2,1)S(1)} %copy-done.8), channel_id=1, source_target_pairs={{0,16},{4,20},{8,24},{12,28},{1,17},{5,21},{9,25},{13,29},{2,18},{... | collective-permute-start | bytes 147464 | tf_op jit(solution)/shard_map/ppermute | solution.py:56
  24.8 6.0 %collective-permute-start.3 = (bf16[192,128]{1,0:T(8,128)(2,1)S(1)}, bf16[192,128]{1,0:T(8,128)(2,1)S(1)}, u32[]{:S(2)}, u32[]{:S(2)}) collective-permute-start(bf16[192,128]{1,0:T(8,128)(2,1)S(1)} %copy-done.8), channel_id=1, source_target_pairs={{0,4},{4,8},{8,12},{12,16},{16,20},{20,24},{24,28},{1,5},{5,9},{9,... | collective-permute-start | bytes 147464 | tf_op jit(solution)/shard_map/ppermute | solution.py:56
  27.3 39.1 %collective-permute-start.4 = (bf16[192,2048]{1,0:T(8,128)(2,1)}, bf16[192,2048]{1,0:T(8,128)(2,1)S(1)}, u32[]{:S(2)}, u32[]{:S(2)}) collective-permute-start(bf16[192,2048]{1,0:T(8,128)(2,1)} %own_ref.3), channel_id=1, source_target_pairs={{0,1},{1,0},{2,3},{3,2},{4,5},{5,4},{6,7},{7,6},{8,9},{9,8},{10,11... | collective-permute-start | bytes 2359304 | tf_op jit(solution)/shard_map/ppermute | solution.py:207
  30.8 6.1 %copy-start.5 = (bf16[192,1024]{1,0:T(8,128)(2,1)S(1)}, bf16[192,1024]{1,0:T(8,128)(2,1)}, u32[]{:S(2)}) copy-start(bf16[192,1024]{1,0:T(8,128)(2,1)} %q_ref.3) | copy-start | bytes 1179652
  30.8 6.1 %copy-start.6 = (bf16[192,1024]{1,0:T(8,128)(2,1)S(1)}, bf16[192,1024]{1,0:T(8,128)(2,1)}, u32[]{:S(2)}) copy-start(bf16[192,1024]{1,0:T(8,128)(2,1)} %do_ref.3) | copy-start | bytes 1179652
  31.6 5.3 %copy-start.9 = (s32[1,8]{1,0:T(1,128)S(1)}, s32[1,8]{1,0:T(1,128)}, u32[]{:S(2)}) copy-start(s32[1,8]{1,0:T(1,128)} %len_ref.3) | copy-start | bytes 100
  31.6 15.9 %all-to-all-start.1 = ((bf16[8,2,64,128]{3,2,1,0:T(8,128)(2,1)}), bf16[8,2,64,128]{3,2,1,0:T(8,128)(2,1)S(1)}, u32[]{:S(2)}, u32[]{:S(2)}) async-start(bf16[8,2,64,128]{3,2,1,0:T(8,128)(2,1)} %broadcast_in_dim.7), calls=%async_computation.1 | async-start | bytes 524288 | tf_op jit(solution)/shard_map/all_to_all | solution.py:50
  41.7 11.5 %collective-permute-start.5 = (bf16[192,128]{1,0:T(8,128)(2,1)}, bf16[192,128]{1,0:T(8,128)(2,1)S(1)}, u32[]{:S(2)}, u32[]{:S(2)}) collective-permute-start(bf16[192,128]{1,0:T(8,128)(2,1)} %get-tuple-element.44), channel_id=1, source_target_pairs={{4,0},{8,4},{12,8},{16,12},{20,16},{24,20},{28,24},{5,1},{9,5},{13... | collective-permute-start | bytes 147464 | tf_op jit(solution)/shard_map/ppermute | solution.py:60
  43.6 9.6 %collective-permute-start.6 = (bf16[192,128]{1,0:T(8,128)(2,1)}, bf16[192,128]{1,0:T(8,128)(2,1)S(1)}, u32[]{:S(2)}, u32[]{:S(2)}) collective-permute-start(bf16[192,128]{1,0:T(8,128)(2,1)} %get-tuple-element.45), channel_id=1, source_target_pairs={{8,0},{12,4},{16,8},{20,12},{24,16},{28,20},{9,1},{13,5},{17,9},{2... | collective-permute-start | bytes 147464 | tf_op jit(solution)/shard_map/ppermute | solution.py:60
  44.9 13.2 %collective-permute-start.7 = (bf16[192,128]{1,0:T(8,128)(2,1)}, bf16[192,128]{1,0:T(8,128)(2,1)}, u32[]{:S(2)}, u32[]{:S(2)}) collective-permute-start(bf16[192,128]{1,0:T(8,128)(2,1)} %get-tuple-element.46), channel_id=1, source_target_pairs={{12,0},{16,4},{20,8},{24,12},{28,16},{13,1},{17,5},{21,9},{25,13},... | collective-permute-start | bytes 147464 | tf_op jit(solution)/shard_map/ppermute | solution.py:60
  46.2 11.9 %collective-permute-start.8 = (bf16[192,128]{1,0:T(8,128)(2,1)S(1)}, bf16[192,128]{1,0:T(8,128)(2,1)}, u32[]{:S(2)}, u32[]{:S(2)}) collective-permute-start(bf16[192,128]{1,0:T(8,128)(2,1)S(1)} %get-tuple-element.47), channel_id=1, source_target_pairs={{16,0},{20,4},{24,8},{28,12},{17,1},{21,5},{25,9},{29,13},{18,2},{... | collective-permute-start | bytes 147464 | tf_op jit(solution)/shard_map/ppermute | solution.py:60
  48.8 17.6 %copy-start = (bf16[192,2048]{1,0:T(8,128)(2,1)S(1)}, bf16[192,2048]{1,0:T(8,128)(2,1)}, u32[]{:S(2)}) copy-start(bf16[192,2048]{1,0:T(8,128)(2,1)} %own_ref.3) | copy-start | bytes 2359300
  48.8 22.3 %all-to-all-start.3 = ((bf16[4,8,2,64,128]{4,3,2,1,0:T(8,128)(2,1)}), bf16[4,8,2,64,128]{4,3,2,1,0:T(8,128)(2,1)S(1)}, u32[]{:S(2)}, u32[]{:S(2)}) async-start(bf16[4,8,2,64,128]{4,3,2,1,0:T(8,128)(2,1)} %broadcast_in_dim.8), calls=%async_computation.3 | async-start | bytes 2097152 | tf_op jit(solution)/shard_map/all_to_all | solution.py:50
  59.0 7.4 %collective-permute-start.9 = (bf16[192,128]{1,0:T(8,128)(2,1)S(1)}, bf16[192,128]{1,0:T(8,128)(2,1)S(1)}, u32[]{:S(2)}, u32[]{:S(2)}) collective-permute-start(bf16[192,128]{1,0:T(8,128)(2,1)S(1)} %add_convert_fusion.1.dv_ref), channel_id=1, source_target_pairs={{0,2},{2,0},{1,3},{3,1},{4,6},{6,4},{5,7},{7,5},{8,10},{10,8},{9,1... | collective-permute-start | bytes 147464 | tf_op jit(solution)/shard_map/ppermute | solution.py:227
  66.4 1.8 %copy-start.1 = (bf16[192,2048]{1,0:T(8,128)(2,1)}, bf16[192,2048]{1,0:T(8,128)(2,1)S(1)}, u32[]{:S(2)}) copy-start(bf16[192,2048]{1,0:T(8,128)(2,1)S(1)} %collective-permute-done.4.near_ref) | copy-start | bytes 2359300
  68.2 1.0 copy-start.3
  69.1 4.8 %collective-permute-start.10 = (bf16[4,2,8,64,128]{4,3,2,1,0:T(8,128)(2,1)}, bf16[4,2,8,64,128]{4,3,2,1,0:T(8,128)(2,1)S(1)}, u32[]{:S(2)}, u32[]{:S(2)}) collective-permute-start(bf16[4,2,8,64,128]{4,3,2,1,0:T(8,128)(2,1)} %get-tuple-element.49), channel_id=1, source_target_pairs={{0,32},{32,0},{1,33},{33,1},{2,34},{34,2},{3,35},{35,3},{4,36},{36... | collective-permute-start | bytes 3145736 | tf_op jit(solution)/shard_map/ppermute | solution.py:233
  71.1 9.6 %collective-permute-start.11 = (bf16[4,8,2,64,128]{4,3,2,1,0:T(8,128)(2,1)S(1)}, bf16[4,8,2,64,128]{4,3,2,1,0:T(8,128)(2,1)}, u32[]{:S(2)}, u32[]{:S(2)}) collective-permute-start(bf16[4,8,2,64,128]{4,3,2,1,0:T(8,128)(2,1)S(1)} %all-to-all-done.3.mine_ref), channel_id=1, source_target_pairs={{0,32},{32,0},{1,33},{33,1},{2,34},{34,2},{3,35},{35,3},{4,36},{36... | collective-permute-start | bytes 3145736 | tf_op jit(solution)/shard_map/ppermute | solution.py:228
  73.9 1.2 copy-start.4
  76.3 29.5 %all-to-all-start.2 = ((bf16[4,2,8,64,128]{4,3,2,1,0:T(8,128)(2,1)}), bf16[4,2,8,64,128]{4,3,2,1,0:T(8,128)(2,1)S(1)}, u32[]{:S(2)}, u32[]{:S(2)}) async-start(bf16[4,2,8,64,128]{4,3,2,1,0:T(8,128)(2,1)} %add_halves.1), calls=%async_computation.2 | async-start | bytes 2097152 | tf_op jit(solution)/shard_map/all_to_all | solution.py:238
  80.6 1.1 copy-start.2
  83.6 7.1 %collective-permute-start.12 = (bf16[192,128]{1,0:T(8,128)(2,1)S(1)}, bf16[192,128]{1,0:T(8,128)(2,1)S(1)}, u32[]{:S(2)}, u32[]{:S(2)}) collective-permute-start(bf16[192,128]{1,0:T(8,128)(2,1)S(1)} %get-tuple-element.52), channel_id=1, source_target_pairs={{0,2},{2,0},{1,3},{3,1},{4,6},{6,4},{5,7},{7,5},{8,10},{10,8},{9,1... | collective-permute-start | bytes 147464 | tf_op jit(solution)/shard_map/ppermute | solution.py:235
  90.7 16.0 %collective-permute-start.16 = (bf16[192,128]{1,0:T(8,128)(2,1)S(1)}, bf16[192,128]{1,0:T(8,128)(2,1)S(1)}, u32[]{:S(2)}, u32[]{:S(2)}) collective-permute-start(bf16[192,128]{1,0:T(8,128)(2,1)S(1)} %add_convert_fusion.refs_9_), channel_id=1, source_target_pairs={{0,4},{4,8},{8,12},{12,16},{16,20},{20,24},{24,28},{1,5},{5,9},{9,... | collective-permute-start | bytes 147464 | tf_op jit(solution)/shard_map/ppermute | solution.py:56
  94.0 12.7 %collective-permute-start.15 = (bf16[192,128]{1,0:T(8,128)(2,1)S(1)}, bf16[192,128]{1,0:T(8,128)(2,1)S(1)}, u32[]{:S(2)}, u32[]{:S(2)}) collective-permute-start(bf16[192,128]{1,0:T(8,128)(2,1)S(1)} %add_convert_fusion.refs_9_), channel_id=1, source_target_pairs={{0,8},{4,12},{8,16},{12,20},{16,24},{20,28},{1,9},{5,13},{9,17},{1... | collective-permute-start | bytes 147464 | tf_op jit(solution)/shard_map/ppermute | solution.py:56
  98.2 8.6 %collective-permute-start.14 = (bf16[192,128]{1,0:T(8,128)(2,1)S(1)}, bf16[192,128]{1,0:T(8,128)(2,1)S(1)}, u32[]{:S(2)}, u32[]{:S(2)}) collective-permute-start(bf16[192,128]{1,0:T(8,128)(2,1)S(1)} %add_convert_fusion.refs_9_), channel_id=1, source_target_pairs={{0,12},{4,16},{8,20},{12,24},{16,28},{1,13},{5,17},{9,21},{13,25},... | collective-permute-start | bytes 147464 | tf_op jit(solution)/shard_map/ppermute | solution.py:56
  104.5 3.0 %collective-permute-start.13 = (bf16[192,128]{1,0:T(8,128)(2,1)S(1)}, bf16[192,128]{1,0:T(8,128)(2,1)S(1)}, u32[]{:S(2)}, u32[]{:S(2)}) collective-permute-start(bf16[192,128]{1,0:T(8,128)(2,1)S(1)} %add_convert_fusion.refs_9_), channel_id=1, source_target_pairs={{0,16},{4,20},{8,24},{12,28},{1,17},{5,21},{9,25},{13,29},{2,18},{... | collective-permute-start | bytes 147464 | tf_op jit(solution)/shard_map/ppermute | solution.py:56
  107.5 15.1 %copy-start.7 = (bf16[192,1024]{1,0:T(8,128)(2,1)S(1)}, bf16[192,1024]{1,0:T(8,128)(2,1)}, u32[]{:S(2)}) copy-start(bf16[192,1024]{1,0:T(8,128)(2,1)} %do_ref.3) | copy-start | bytes 1179652
  107.5 40.4 %all-to-all-start.4 = ((bf16[32,64,128]{2,1,0:T(8,128)(2,1)}), bf16[32,64,128]{2,1,0:T(8,128)(2,1)S(1)}, u32[]{:S(2)}, u32[]{:S(2)}) async-start(bf16[32,64,128]{2,1,0:T(8,128)(2,1)} %bitcast), calls=%async_computation.4 | async-start | bytes 1048576 | tf_op jit(solution)/shard_map/all_to_all | solution.py:241
  130.2 8.1 %collective-permute-start.17 = (bf16[192,128]{1,0:T(8,128)(2,1)S(1)}, bf16[192,128]{1,0:T(8,128)(2,1)S(1)}, u32[]{:S(2)}, u32[]{:S(2)}) collective-permute-start(bf16[192,128]{1,0:T(8,128)(2,1)S(1)} %get-tuple-element.61), channel_id=1, source_target_pairs={{4,0},{8,4},{12,8},{16,12},{20,16},{24,20},{28,24},{5,1},{9,5},{13... | collective-permute-start | bytes 147464 | tf_op jit(solution)/shard_map/ppermute | solution.py:60
  132.5 8.0 %collective-permute-start.18 = (bf16[192,128]{1,0:T(8,128)(2,1)S(1)}, bf16[192,128]{1,0:T(8,128)(2,1)S(1)}, u32[]{:S(2)}, u32[]{:S(2)}) collective-permute-start(bf16[192,128]{1,0:T(8,128)(2,1)S(1)} %get-tuple-element.62), channel_id=1, source_target_pairs={{8,0},{12,4},{16,8},{20,12},{24,16},{28,20},{9,1},{13,5},{17,9},{2... | collective-permute-start | bytes 147464 | tf_op jit(solution)/shard_map/ppermute | solution.py:60
  133.8 12.9 %collective-permute-start.19 = (bf16[192,128]{1,0:T(8,128)(2,1)S(1)}, bf16[192,128]{1,0:T(8,128)(2,1)S(1)}, u32[]{:S(2)}, u32[]{:S(2)}) collective-permute-start(bf16[192,128]{1,0:T(8,128)(2,1)S(1)} %get-tuple-element.63), channel_id=1, source_target_pairs={{12,0},{16,4},{20,8},{24,12},{28,16},{13,1},{17,5},{21,9},{25,13},... | collective-permute-start | bytes 147464 | tf_op jit(solution)/shard_map/ppermute | solution.py:60
  135.1 12.2 %collective-permute-start.20 = (bf16[192,128]{1,0:T(8,128)(2,1)S(1)}, bf16[192,128]{1,0:T(8,128)(2,1)S(1)}, u32[]{:S(2)}, u32[]{:S(2)}) collective-permute-start(bf16[192,128]{1,0:T(8,128)(2,1)S(1)} %get-tuple-element.64), channel_id=1, source_target_pairs={{16,0},{20,4},{24,8},{28,12},{17,1},{21,5},{25,9},{29,13},{18,2},{... | collective-permute-start | bytes 147464 | tf_op jit(solution)/shard_map/ppermute | solution.py:60
